TPU v7x, 32 devices: a whole 2x2x4 slice. The times are simulated.
32 devices in a mesh: replica: 2 (over x), tile: 16 (over z, y, core).
Axes of the slice: x: 2, y: 2, z: 4, core: 2. Of those that a mesh axis runs over, the one named last changes fastest.
Arguments:
- fields: bfloat16 [2, 64, 64, 8, 128], P('replica', None, 'tile'), may hold values from -6 to 6
- convolution_weight: bfloat16 [64, 1728], replicated, may hold values from -0.15625 to 0.15625
- convolution_bias: float32 [64], replicated, may hold values from -3 to 3
- query_owner: int32 [2, 2048, 1], P('replica', 'tile'), may hold values from 0 to 15; in each aligned block of 128 rows (0 to 127, 128 to 255, ..., all dimensions but the last counted through in order) at most 16 rows name the same one
- query_cell: int32 [2, 2048], P('replica', 'tile'), may hold values from 0 to 4095
- query_frac: float32 [2, 3, 2048], P('replica', None, 'tile'), may hold values from 0 to 1
- target: float32 [2, 5, 2048], P('replica', None, 'tile'), may hold values from -6 to 6
- w_latent: float32 [64, 512], replicated, may hold values from -3 to 3
- w_pos: float32 [3, 512], replicated, may hold values from -3.5 to 3.5
- bias_one: float32 [512], replicated, may hold values from -2 to 2
- w_mid: float32 [512, 512], replicated, may hold values from -0.5 to 0.5
- bias_two: float32 [512], replicated, may hold values from -2 to 2
- w_out: float32 [5, 512], replicated, may hold values from -0.25 to 0.25
- bias_out: float32 [5], replicated, may hold values from -3 to 3
Outputs:
- prediction: float32 [2, 5, 2048], P('replica', None, 'tile')
- grad_latent: float32 [64, 512], replicated
- grad_pos: float32 [3, 512], replicated
- grad_bias_one: float32 [512], replicated
- grad_mid: float32 [512, 512], replicated
- grad_bias_two: float32 [512], replicated
- grad_out: float32 [5, 512], replicated
- grad_bias_out: float32 [5], replicated
- loss: float32 [], replicated
Inputs may be any that keep to these rules, and one draw needn't show every extreme that they name: `query_owner`: among the query points of one device, no tile is named more than 16 times; in every draw some device names some tile exactly 16 times.
All inputs are finite; a program needn't handle non-finite values.
Results may differ from a plain program's by a relative error of at most 0.0009.
The roundings to bfloat16 on the way count: a program that leaves them out, or rounds other values in their place, can miss the bound.
Values may be sent and summed in bfloat16 or wider, within the bound.
No kernel may reach another device: no remote copies, remote signals or barrier semaphores. Data moves between devices by JAX's collectives and lax.ppermute only.
A program may use at most 64 MiB of HBM per device.

v0:
```python
import functools

import jax
import jax.numpy as jnp
from jax import lax
from jax.experimental import pallas as pl
from jax.experimental.pallas import tpu as pltpu
from jax.sharding import PartitionSpec as P

DILATION_RATE = 2
VISCOSITY = 0.05
DIFFUSIVITY = 0.05
RESIDUAL_WEIGHT = 0.5

F32 = jnp.float32
BF16 = jnp.bfloat16
LANES = 128
BLOCK = 32
WORDS = 128
MISC = 16
NN = (((1,), (0,)), ((), ()))
NT = (((1,), (1,)), ((), ()))
TN = (((0,), (0,)), ((), ()))
VMEM = pl.BlockSpec(memory_space=pltpu.VMEM)
SMEM = pl.BlockSpec(memory_space=pltpu.SMEM)


def mul(left, right, dims=NN):
    return lax.dot_general(left, right, dims, preferred_element_type=F32)


def halves(value):
    high = value.astype(BF16)
    return high, (value - high.astype(F32)).astype(BF16)


def thirds(value):
    high = value.astype(BF16)
    rest = value - high.astype(F32)
    middle = rest.astype(BF16)
    return high, middle, (rest - middle.astype(F32)).astype(BF16)


def mul3(left, right, dims=NN):
    return mul(left[0], right[0], dims) + mul(left[0], right[1], dims) + mul(left[1], right[0], dims)


def route_kernel(tiles, slots, owner_ref, cell_ref, frac_ref, target_ref, out_ref, words):
    queries = owner_ref.shape[1]
    owner = owner_ref[...]
    hits = (lax.broadcasted_iota(jnp.int32, (tiles, queries), 0) == owner).astype(F32)
    before = lax.broadcasted_iota(jnp.int32, (queries, queries), 0) < lax.broadcasted_iota(
        jnp.int32, (queries, queries), 1
    )
    earlier = mul(hits.astype(BF16), before.astype(F32).astype(BF16))
    slot = jnp.sum(hits * earlier, axis=0, keepdims=True)
    place = owner * slots + slot.astype(jnp.int32)
    chosen = (lax.broadcasted_iota(jnp.int32, (tiles * slots, queries), 0) == place).astype(F32).astype(BF16)
    words[...] = jnp.zeros_like(words)
    words[0:1, :] = cell_ref[...].astype(F32)
    words[1:4, :] = frac_ref[...]
    words[4:9, :] = target_ref[...]
    words[9:10, :] = jnp.ones((1, queries), F32)
    words[10:11, :] = lax.broadcasted_iota(jnp.int32, (1, queries), 1).astype(F32)
    high, middle, low = thirds(words[...])
    out_ref[...] = mul(chosen, high, NT) + mul(chosen, middle, NT) + mul(chosen, low, NT)


def route(owner, cell, frac, target, tiles, slots):
    queries = owner.shape[1]
    return pl.pallas_call(
        functools.partial(route_kernel, tiles, slots),
        out_shape=jax.ShapeDtypeStruct((tiles * slots, WORDS), F32),
        in_specs=[VMEM] * 4,
        out_specs=VMEM,
        scratch_shapes=[pltpu.VMEM((WORDS, queries), F32)],
        name="route",
    )(owner, cell, frac, target)


def convolve(left_ref, here_ref, right_ref, weight_ref, bias_ref, lat):
    planes, rows_y = here_ref.shape[0], here_ref.shape[1]
    channels = here_ref.shape[2]
    behind = left_ref.shape[0]

    def plane(index):
        if index < behind:
            return left_ref, index
        if index < behind + planes:
            return here_ref, index - behind
        return right_ref, index - behind - planes

    weight = weight_ref[...]
    bias = bias_ref[...]
    for x in range(planes + 1):
        for pair in range(rows_y // 2):
            blocks = []
            for step_x in range(3):
                ref, index = plane(x + DILATION_RATE * step_x)
                for step_y in (-1, 0, 1):
                    blocks.append(
                        jnp.concatenate(
                            [ref[index, (2 * pair + half + step_y) % rows_y] for half in (0, 1)],
                            axis=1,
                        )
                    )
            partial = mul(weight, jnp.concatenate(blocks, axis=0))
            for half in (0, 1):
                part = partial[:, half * LANES : (half + 1) * LANES]
                summed = (
                    part[channels : 2 * channels]
                    + pltpu.roll(part[:channels], 1, 1)
                    + pltpu.roll(part[2 * channels :], LANES - 1, 1)
                    + bias
                )
                lat[x * (rows_y // 2) + pair, :, half * LANES : (half + 1) * LANES] = jax.nn.gelu(
                    summed
                ).astype(BF16)


def interpolate(words, lat, planes, rows_y, rows_z):
    rows = words.shape[0]
    cell = jnp.broadcast_to(words[:, 0:1], (rows, LANES)).astype(jnp.int32)
    frac = [jnp.broadcast_to(words[:, 1 + d : 2 + d], (rows, LANES)) for d in range(3)]
    shift_z = rows_z.bit_length() - 1
    shift_y = rows_y.bit_length() - 1
    base_x = cell >> (shift_z + shift_y)
    base_y = (cell >> shift_z) & (rows_y - 1)
    base_z = cell & (rows_z - 1)
    spot = lax.broadcasted_iota(jnp.int32, (rows, rows_z), 1)
    part_z = jnp.where(spot == base_z, 1.0 - frac[2], 0.0) + jnp.where(
        spot == ((base_z + 1) & (rows_z - 1)), frac[2], 0.0
    )
    total = None
    for x in range(planes + 1):
        part_x = jnp.where(base_x == x, 1.0 - frac[0], jnp.where(base_x == x - 1, frac[0], 0.0))
        for pair in range(rows_y // 2):
            sides = []
            for y in (2 * pair, 2 * pair + 1):
                part_y = jnp.where(
                    base_y == y, 1.0 - frac[1], jnp.where(base_y == (y - 1) % rows_y, frac[1], 0.0)
                )
                sides.append((part_x * part_y * part_z).astype(BF16))
            term = mul(jnp.concatenate(sides, axis=1), lat[x * (rows_y // 2) + pair], NT)
            total = term if total is None else total + term
    return total.astype(BF16), base_x, base_y, base_z, frac


def folded(value):
    return jnp.sum(value.reshape(value.shape[0] // 8, 8, value.shape[1]), axis=0)


def main_kernel(
    plan,
    place_ref,
    left_ref,
    here_ref,
    right_ref,
    conv_weight_ref,
    conv_bias_ref,
    words_ref,
    w_latent_ref,
    w_pos_ref,
    bias_one_ref,
    w_mid_ref,
    bias_two_ref,
    w_out_ref,
    bias_out_ref,
    send_ref,
    keep_ref,
    lat,
    code,
    pos,
    z_one,
    mid_high,
    mid_low,
    one_high,
    one_low,
    mixed,
    two_high,
    two_low,
    back,
    d_high,
    d_low,
    out_t,
    d_out_t,
    packed,
):
    rows = words_ref.shape[0]
    hidden = w_mid_ref.shape[0]
    latents = w_latent_ref.shape[0]
    planes, rows_y, rows_z = here_ref.shape[0], here_ref.shape[1], here_ref.shape[3]
    my_chunk = place_ref[0]
    my_tile = place_ref[1]
    my_replica = place_ref[2]

    convolve(left_ref, here_ref, right_ref, conv_weight_ref, conv_bias_ref, lat)
    words = words_ref[...]
    interp, base_x, base_y, base_z, frac = interpolate(words, lat, planes, rows_y, rows_z)
    code[...] = interp
    global_x = my_tile * planes + base_x
    lane = lax.broadcasted_iota(jnp.int32, (rows, LANES), 1)
    pos[...] = jnp.where(
        lane == 0,
        (global_x.astype(F32) + frac[0]) / (planes * plan.tiles),
        jnp.where(
            lane == 1,
            (base_y.astype(F32) + frac[1]) / rows_y,
            (base_z.astype(F32) + frac[2]) / rows_z,
        ),
    )

    wl_high, wl_low = halves(w_latent_ref[...])
    z_one[...] = mul(interp, wl_high) + mul(interp, wl_low)
    high, low = halves(w_mid_ref[...])
    mid_high[...] = high
    mid_low[...] = low
    w_pos = [w_pos_ref[d : d + 1, :] for d in range(3)]
    square = w_pos[0] * w_pos[0] + w_pos[1] * w_pos[1] + w_pos[2] * w_pos[2]
    bias_one = bias_one_ref[...]
    bias_two = bias_two_ref[...]

    def store(index, block, refs, value):
        high, low = halves(value)
        refs[0][pl.ds(pl.multiple_of(index * rows + block * BLOCK, BLOCK), BLOCK), :] = high
        refs[1][pl.ds(pl.multiple_of(index * rows + block * BLOCK, BLOCK), BLOCK), :] = low

    def fetch(ref, index, block):
        return ref[pl.ds(pl.multiple_of(index * rows + block * BLOCK, BLOCK), BLOCK), :]

    def layer_one(block, carry):
        where = fetch(pos, 0, block)
        pre = (
            fetch(z_one, 0, block)
            + (where[:, 0:1] * w_pos[0] + where[:, 1:2] * w_pos[1] + where[:, 2:3] * w_pos[2])
            + bias_one
        )
        act = jnp.tanh(pre)
        slope = 1.0 - act * act
        curve = -2.0 * act * slope
        z_one[pl.ds(pl.multiple_of(block * BLOCK, BLOCK), BLOCK), :] = act
        refs = (one_high, one_low)
        store(0, block, refs, act)
        for d in range(3):
            store(1 + d, block, refs, slope * w_pos[d])
        store(4, block, refs, curve * square)
        return carry

    lax.fori_loop(0, rows // BLOCK, layer_one, 0)

    def times_mid(dims, source, result, index, carry):
        span = pl.ds(pl.multiple_of(index * rows, rows), rows)
        result[span, :] = mul3((source[0][span, :], source[1][span, :]), (mid_high[...], mid_low[...]), dims)
        return carry

    lax.fori_loop(0, 5, functools.partial(times_mid, NN, (one_high, one_low), mixed), 0)

    def layer_two(block, carry):
        act = jnp.tanh(fetch(mixed, 0, block) + bias_two)
        slope = 1.0 - act * act
        curve = -2.0 * act * slope
        refs = (two_high, two_low)
        store(0, block, refs, act)
        mixed[pl.ds(pl.multiple_of(block * BLOCK, BLOCK), BLOCK), :] = act
        norm = None
        for d in range(3):
            tangent = fetch(mixed, 1 + d, block)
            store(1 + d, block, refs, slope * tangent)
            norm = tangent * tangent if norm is None else norm + tangent * tangent
        store(4, block, refs, slope * fetch(mixed, 4, block) + curve * norm)
        return carry

    lax.fori_loop(0, rows // BLOCK, layer_two, 0)

    out_fields = jnp.concatenate([w_out_ref[...], jnp.zeros((3, hidden), F32)], axis=0)
    wo_high, wo_low = halves(out_fields)
    wo_both = jnp.concatenate([out_fields, wo_low.astype(F32)], axis=0).astype(BF16)
    for s in range(5):
        span = slice(s * rows, (s + 1) * rows)
        both = mul(wo_both, two_high[span, :], NT)
        out_t[8 * s : 8 * s + 8, :] = both[:8] + both[8:] + mul(wo_high, two_low[span, :], NT)

    words_t = words.T
    target = [words_t[4 + f : 5 + f, :] for f in range(5)]
    valid = words_t[9:10, :]
    value = [out_t[f : f + 1, :] + bias_out_ref[f] for f in range(5)]
    grad = [[out_t[8 * (d + 1) + f : 8 * (d + 1) + f + 1, :] for f in range(5)] for d in range(3)]
    laplace = [out_t[32 + f : 33 + f, :] for f in range(5)]
    velocity = value[2:5]
    advection = [
        velocity[0] * grad[0][f] + velocity[1] * grad[1][f] + velocity[2] * grad[2][f] for f in range(5)
    ]
    continuity = grad[0][2] + grad[1][3] + grad[2][4]
    momentum = [advection[2 + j] + grad[j][1] - VISCOSITY * laplace[2 + j] for j in range(3)]
    momentum[2] = momentum[2] - value[0]
    energy = advection[0] - DIFFUSIVITY * laplace[0]
    misfit = [value[f] - target[f] for f in range(5)]
    physics = (
        continuity * continuity
        + (momentum[0] * momentum[0] + momentum[1] * momentum[1] + momentum[2] * momentum[2])
        + energy * energy
    )
    squares = (
        misfit[0] * misfit[0]
        + misfit[1] * misfit[1]
        + misfit[2] * misfit[2]
        + misfit[3] * misfit[3]
        + misfit[4] * misfit[4]
    )
    point_loss = valid * (squares + RESIDUAL_WEIGHT * physics) * (1.0 / plan.query_total)

    rate = valid * (1.0 / plan.query_total)
    twice = RESIDUAL_WEIGHT * 2.0
    d_cont = rate * twice * continuity
    d_mom = [rate * twice * m for m in momentum]
    d_energy = rate * twice * energy
    d_value = [2.0 * rate * m for m in misfit]
    for d in range(3):
        d_value[2 + d] = d_value[2 + d] + (
            d_mom[0] * grad[d][2] + d_mom[1] * grad[d][3] + d_mom[2] * grad[d][4] + d_energy * grad[d][0]
        )
    d_value[0] = d_value[0] - d_mom[2]
    d_out_t[...] = jnp.zeros_like(d_out_t)
    for f in range(5):
        d_out_t[f : f + 1, :] = d_value[f]
    for d in range(3):
        first = 8 * (d + 1)
        d_out_t[first : first + 1, :] = d_energy * velocity[d]
        d_out_t[first + 1 : first + 2, :] = d_mom[d]
        for j in range(3):
            term = d_mom[j] * velocity[d]
            if j == d:
                term = term + d_cont
            d_out_t[first + 2 + j : first + 3 + j, :] = term
    d_out_t[32:33, :] = -DIFFUSIVITY * d_energy
    for j in range(3):
        d_out_t[34 + j : 35 + j, :] = -VISCOSITY * d_mom[j]

    for s in range(5):
        span = slice(s * rows, (s + 1) * rows)
        wanted = d_out_t[8 * s : 8 * s + 8, :]
        do_high, do_low = halves(wanted)
        back[span, :] = mul3((do_high, do_low), (wo_high, wo_low), TN)

    def second_back(block, total):
        act = fetch(mixed, 0, block)
        slope = 1.0 - act * act
        curve = -2.0 * act * slope
        tangent = [fetch(mixed, 1 + d, block) for d in range(3)]
        cot_t = [fetch(back, 1 + d, block) for d in range(3)]
        cot_l = fetch(back, 4, block)
        refs = (d_high, d_low)
        d_slope = cot_l * fetch(mixed, 4, block)
        norm = None
        bent = 2.0 * curve * cot_l
        for d in range(3):
            store(1 + d, block, refs, slope * cot_t[d] + bent * tangent[d])
            d_slope = d_slope + cot_t[d] * tangent[d]
            norm = tangent[d] * tangent[d] if norm is None else norm + tangent[d] * tangent[d]
        store(4, block, refs, slope * cot_l)
        d_curve = cot_l * norm
        d_slope = d_slope - 2.0 * act * d_curve
        d_act = fetch(back, 0, block) - 2.0 * slope * d_curve - 2.0 * act * d_slope
        d_pre = slope * d_act
        store(0, block, refs, d_pre)
        return total + folded(d_pre)

    grad_two = lax.fori_loop(0, rows // BLOCK, second_back, jnp.zeros((8, hidden), F32))

    packed[...] = jnp.zeros_like(packed)
    main_rows = hidden + latents + MISC
    wide = 2 * LANES
    for left in range(hidden // wide):
        for right in range(hidden // wide):
            lefts = slice(left * wide, (left + 1) * wide)
            rights = slice(right * wide, (right + 1) * wide)
            part = mul3(
                (one_high[:, lefts], one_low[:, lefts]), (d_high[:, rights], d_low[:, rights]), TN
            )
            for side in range(2):
                first = (2 * right + side) * main_rows + left * wide
                packed[first : first + wide, :] = part[:, side * LANES : (side + 1) * LANES]

    lax.fori_loop(0, 5, functools.partial(times_mid, NT, (d_high, d_low), back), 0)

    def first_back(block, totals):
        act = fetch(z_one, 0, block)
        slope = 1.0 - act * act
        curve = -2.0 * act * slope
        where = fetch(pos, 0, block)
        cot_t = [fetch(back, 1 + d, block) for d in range(3)]
        cot_l = fetch(back, 4, block)
        d_curve = cot_l * square
        d_slope = cot_t[0] * w_pos[0] + cot_t[1] * w_pos[1] + cot_t[2] * w_pos[2] - 2.0 * act * d_curve
        d_act = fetch(back, 0, block) - 2.0 * slope * d_curve - 2.0 * act * d_slope
        d_pre = slope * d_act
        store(0, block, (d_high, d_low), d_pre)
        sums = [totals[0] + folded(d_pre)]
        for d in range(3):
            sums.append(totals[1 + d] + folded(where[:, d : d + 1] * d_pre + slope * cot_t[d]))
        sums.append(totals[4] + folded(curve * cot_l))
        return tuple(sums)

    sums = lax.fori_loop(
        0, rows // BLOCK, first_back, tuple(jnp.zeros((8, hidden), F32) for _ in range(5))
    )
    d_square = jnp.sum(sums[4], axis=0, keepdims=True)
    grad_latent = mul(code[...], d_high[0:rows, :], TN) + mul(code[...], d_low[0:rows, :], TN)

    grad_out = None
    for s in range(5):
        span = slice(s * rows, (s + 1) * rows)
        wanted = d_out_t[8 * s : 8 * s + 8, :]
        do_high, do_low = halves(wanted)
        do_both = jnp.concatenate([wanted, do_low.astype(F32)], axis=0).astype(BF16)
        both = mul(do_both, two_high[span, :])
        term = both[:8] + both[8:] + mul(do_high, two_low[span, :])
        grad_out = term if grad_out is None else grad_out + term

    lane_row = lax.broadcasted_iota(jnp.int32, (1, hidden), 1)
    last = jnp.where(lane_row == 5, jnp.sum(point_loss), 0.0)
    for f in range(5):
        last = last + jnp.where(lane_row == f, jnp.sum(d_value[f]), 0.0)
    grad_pos = [jnp.sum(sums[1 + d], axis=0, keepdims=True) + 2.0 * w_pos[d] * d_square for d in range(3)]
    misc = grad_pos + [
        jnp.sum(sums[0], axis=0, keepdims=True),
        jnp.sum(grad_two, axis=0, keepdims=True),
        last,
    ]
    for part in range(hidden // LANES):
        lanes = slice(part * LANES, (part + 1) * LANES)
        first = part * main_rows + hidden
        packed[first : first + latents, :] = grad_latent[:, lanes]
        first = first + latents
        for number, row in enumerate(misc):
            packed[first + number : first + number + 1, :] = row[:, lanes]
        packed[first + 8 : first + 16, :] = grad_out[:, lanes]

    slots = rows // plan.tiles
    chosen = jnp.where(
        lane == jnp.broadcast_to(words[:, 10:11], (rows, LANES)).astype(jnp.int32), words[:, 9:10], 0.0
    ).astype(BF16)
    source = lax.broadcasted_iota(jnp.int32, (plan.tiles, rows), 0)
    inside = lax.broadcasted_iota(jnp.int32, (plan.tiles, rows), 1)
    mine = (inside >= source * slots) & (inside < (source + 1) * slots)
    for f in range(5):
        high, middle, low = thirds(jnp.where(mine, jnp.broadcast_to(value[f], (plan.tiles, rows)), 0.0))
        first = pl.multiple_of((hidden // LANES) * main_rows + f * plan.devices + my_replica * plan.tiles, 16)
        packed[pl.ds(first, plan.tiles), :] = mul(high, chosen) + mul(middle, chosen) + mul(low, chosen)

    half = plan.devices // 2
    chunk = plan.chunk
    my_half = my_chunk // half
    for number in range(plan.devices):
        spot = jnp.bitwise_xor(number, my_chunk) & (half - 1)

        @pl.when(my_half == number // half)
        def _():
            keep_ref[spot] = packed[number * chunk : (number + 1) * chunk, :]

        @pl.when(my_half != number // half)
        def _():
            send_ref[spot] = packed[number * chunk : (number + 1) * chunk, :]


class Plan:
    def __init__(self, tiles, replicas, queries, hidden, latents):
        self.tiles, self.replicas = tiles, replicas
        self.devices = tiles * replicas
        self.query_total = float(queries * self.devices)
        self.main_rows = hidden + latents + MISC
        needed = (hidden // LANES) * self.main_rows + 5 * self.devices
        self.chunk = -(-needed // (8 * self.devices)) * 8
        bits = self.devices.bit_length() - 1
        middle = list(range(2, bits - 1))
        self.stages = [[0], [1, bits - 1]] + [middle[i : i + 2] for i in range(0, len(middle), 2)]

    def mask(self, bits, steps):
        return sum(1 << bit for number, bit in enumerate(bits) if steps >> number & 1)

    def my_chunk(self, device):
        chunk = 0
        for bits in self.stages:
            for bit in reversed(bits):
                chunk = chunk * 2 + (device >> bit & 1)
        return chunk


def swapped(value, plan, bits, steps):
    mask = plan.mask(bits, steps)
    return lax.ppermute(value, ("replica", "tile"), [(i, i ^ mask) for i in range(plan.devices)])


def main(place, left, here, right, conv_weight, conv_bias, words, params, plan):
    w_latent, w_pos, bias_one, w_mid, bias_two, w_out, bias_out = params
    rows = words.shape[0]
    hidden = w_mid.shape[0]
    channels = here.shape[2]
    outs = jax.ShapeDtypeStruct((plan.devices // 2, plan.chunk, LANES), F32)
    pairs = (here.shape[0] + 1) * here.shape[1] // 2
    wide = lambda kind: pltpu.VMEM((5 * rows, hidden), kind)
    return pl.pallas_call(
        functools.partial(main_kernel, plan),
        out_shape=(outs, outs),
        in_specs=[SMEM] + [VMEM] * 12 + [SMEM],
        out_specs=(VMEM, VMEM),
        scratch_shapes=[
            pltpu.VMEM((pairs, channels, 2 * LANES), BF16),
            pltpu.VMEM((rows, channels), BF16),
            pltpu.VMEM((rows, LANES), F32),
            pltpu.VMEM((rows, hidden), F32),
            pltpu.VMEM((hidden, hidden), BF16),
            pltpu.VMEM((hidden, hidden), BF16),
            wide(BF16),
            wide(BF16),
            wide(F32),
            wide(BF16),
            wide(BF16),
            wide(F32),
            wide(BF16),
            wide(BF16),
            pltpu.VMEM((40, rows), F32),
            pltpu.VMEM((40, rows), F32),
            pltpu.VMEM((plan.devices * plan.chunk, LANES), F32),
        ],
        compiler_params=pltpu.CompilerParams(vmem_limit_bytes=48 << 20),
        name="encode_decode",
    )(place, left, here, right, conv_weight, conv_bias, words, w_latent, w_pos, bias_one, w_mid, bias_two, w_out, bias_out)


def unpack_kernel(
    plan,
    place_ref,
    mine_ref,
    other_ref,
    prediction_ref,
    latent_ref,
    pos_ref,
    one_ref,
    mid_ref,
    two_ref,
    out_ref,
    tail_ref,
    packed,
):
    my_chunk = place_ref[0]
    device = place_ref[2] * plan.tiles + place_ref[1]
    half = plan.devices // 2
    chunk = plan.chunk
    my_half = my_chunk // half
    for number in range(plan.devices):
        spot = jnp.bitwise_xor(number, my_chunk) & (half - 1)

        @pl.when(my_half == number // half)
        def _():
            packed[number * chunk : (number + 1) * chunk, :] = mine_ref[spot]

        @pl.when(my_half != number // half)
        def _():
            packed[number * chunk : (number + 1) * chunk, :] = other_ref[spot]

    hidden = mid_ref.shape[0]
    latents = latent_ref.shape[0]
    for part in range(hidden // LANES):
        lanes = slice(part * LANES, (part + 1) * LANES)
        first = part * plan.main_rows
        mid_ref[:, lanes] = packed[first : first + hidden, :]
        first = first + hidden
        latent_ref[:, lanes] = packed[first : first + latents, :]
        first = first + latents
        pos_ref[:, lanes] = packed[first : first + 3, :]
        one_ref[:, lanes] = packed[first + 3 : first + 4, :]
        two_ref[:, lanes] = packed[first + 4 : first + 5, :]
        out_ref[:, lanes] = packed[first + 8 : first + 13, :]
        if part == 0:
            tail_ref[...] = packed[first + 5 : first + 6, :]
    first = (hidden // LANES) * plan.main_rows
    for f in range(5):
        prediction_ref[0, f : f + 1, :] = packed[pl.ds(first + f * plan.devices + device, 1), :]


def unpack(place, mine, other, plan, hidden, latents):
    shapes = [(1, 5, LANES), (latents, hidden), (3, hidden), (1, hidden), (hidden, hidden), (1, hidden), (5, hidden), (1, LANES)]
    return pl.pallas_call(
        functools.partial(unpack_kernel, plan),
        out_shape=tuple(jax.ShapeDtypeStruct(shape, F32) for shape in shapes),
        in_specs=[SMEM, VMEM, VMEM],
        out_specs=tuple([VMEM] * len(shapes)),
        scratch_shapes=[pltpu.VMEM((plan.devices * plan.chunk, LANES), F32)],
        compiler_params=pltpu.CompilerParams(vmem_limit_bytes=16 << 20),
        name="unpack",
    )(place, mine, other)


def body(
    fields,
    convolution_weight,
    convolution_bias,
    query_owner,
    query_cell,
    query_frac,
    target,
    w_latent,
    w_pos,
    bias_one,
    w_mid,
    bias_two,
    w_out,
    bias_out,
):
    tiles = lax.axis_size("tile")
    replicas = lax.axis_size("replica")
    my_tile = lax.axis_index("tile")
    my_replica = lax.axis_index("replica")
    channels = fields.shape[1]
    queries = query_cell.shape[1]
    hidden = w_mid.shape[0]
    slots = 2 * queries // tiles
    plan = Plan(tiles, replicas, queries, hidden, channels)
    device = my_replica * tiles + my_tile
    place = jnp.stack([plan.my_chunk(device), my_tile, my_replica]).astype(jnp.int32)

    words = route(query_owner[:, :, 0], query_cell, query_frac[0], target[0], tiles, slots)
    words = lax.all_to_all(
        words.reshape(tiles, slots, WORDS), "tile", split_axis=0, concat_axis=0, tiled=True
    ).reshape(tiles * slots, WORDS)

    here = fields[0].transpose(1, 2, 0, 3)
    up = [(i, (i + 1) % tiles) for i in range(tiles)]
    down = [((i + 1) % tiles, i) for i in range(tiles)]
    left = lax.ppermute(here[-DILATION_RATE:], "tile", up)
    right = lax.ppermute(here[: DILATION_RATE + 1], "tile", down)
    taps = convolution_weight.reshape(channels, 9, 3, channels)
    taps = taps.transpose(2, 0, 1, 3).reshape(3 * channels, 9 * channels)

    params = (w_latent, w_pos, bias_one[None], w_mid, bias_two[None], w_out, bias_out)
    send, keep = main(place, left, here, right, taps, convolution_bias[:, None], words, params, plan)

    keep = keep + swapped(send, plan, plan.stages[0], 1)
    for bits in plan.stages[1:]:
        group = 1 << len(bits)
        keep = keep.reshape(group, keep.shape[0] // group, plan.chunk, LANES)
        arrived = [swapped(keep[step], plan, bits, step) for step in range(1, group)]
        keep = keep[0]
        for block in arrived:
            keep = keep + block
    for bits in reversed(plan.stages[1:]):
        group = 1 << len(bits)
        keep = jnp.concatenate([keep] + [swapped(keep, plan, bits, step) for step in range(1, group)], axis=0)
    other = swapped(keep, plan, plan.stages[0], 1)
    prediction, g_latent, g_pos, g_one, g_mid, g_two, g_out, tail = unpack(
        place, keep, other, plan, hidden, channels
    )
    return (prediction, g_latent, g_pos, g_one[0], g_mid, g_two[0], g_out, tail[0, :5], tail[0, 5])


def solution(mesh):
    return jax.shard_map(
        body,
        mesh=mesh,
        in_specs=(
            P("replica", None, "tile", None, None),
            P(),
            P(),
            P("replica", "tile", None),
            P("replica", "tile"),
            P("replica", None, "tile"),
            P("replica", None, "tile"),
            P(),
            P(),
            P(),
            P(),
            P(),
            P(),
            P(),
        ),
        out_specs=(P("replica", None, "tile"), P(), P(), P(), P(), P(), P(), P(), P()),
        check_vma=False,
    )
```

profile of v0, /device:TPU:0, one launch (start us, length us, event | category | flops | bytes accessed | tf_op | source)
XLA Modules:
  0.0 85.6 jit_solution(18439432835016959700)
XLA Ops:
  0.6 1.2 %copy.39 = bf16[1,64,4,8,128]{4,1,3,2,0:T(8,128)(2,1)S(1)} copy(bf16[1,64,4,8,128]{4,3,2,1,0:T(8,128)(2,1)} %param.14) | data formatting | bytes 1048576 | tf_op args[0]
  1.9 0.0 copy-start.9
  1.9 5.5 %collective-permute-start.1 = (bf16[3,8,64,128]{3,2,1,0:T(8,128)(2,1)S(1)}, bf16[3,8,64,128]{3,2,1,0:T(8,128)(2,1)S(1)}, u32[]{:S(2)}, u32[]{:S(2)}) collective-permute-start(bf16[3,8,64,128]{3,2,1,0:T(8,128)(2,1)S(1)} %slice.57), channel_id=1, source_target_pairs={{1,0},{2,1},{3,2},{4,3},{5,4},{6,5},{7,6},{8,7},{9,8},{10,9},{11,1... | collective-permute-start | bytes 1179656 | tf_op jit(solution)/shard_map/ppermute | solution.py:632
  7.4 0.7 slice.56
  8.1 0.6 copy.41
  8.7 0.1 copy-done.8
  8.8 0.6 copy.40
  9.4 1.8 %route.1 = f32[256,128]{1,0:T(8,128)} custom-call(s32[1,128]{1,0:T(1,128)} %bitcast.36, s32[1,128]{1,0:T(1,128)} %cell_ref.1, f32[3,128]{1,0:T(4,128)} %bitcast.35, f32[5,128]{1,0:T(8,128)} %bitcast.34), custom_call_target="tpu_custom_call" | custom-call | tf_op jit(solution)/shard_map/route/pallas_call | solution.py:71
  11.2 5.7 %all-to-all-start = ((f32[16,16,128]{2,1,0:T(8,128)}), f32[16,16,128]{2,1,0:T(8,128)S(1)}, u32[]{:S(2)}, u32[]{:S(2)}) async-start(f32[16,16,128]{2,1,0:T(8,128)} %bitcast.33), calls=%async_computation | async-start | bytes 262144 | tf_op jit(solution)/shard_map/all_to_all | solution.py:624
  16.9 0.0 copy-start.10
  17.0 0.6 copy-done.10
  17.6 0.1 copy.30.conv_bias_ref
  17.7 0.3 reshape.48
  18.1 1.0 %copy.32 = bf16[3,64,9,64]{3,2,1,0:T(8,128)(2,1)} copy(bf16[3,64,9,64]{3,0,2,1:T(4,128)(2,1)S(1)} %bitcast.32) | data formatting | bytes 442368 | tf_op jit(solution)/shard_map/reshape | solution.py:634
  19.1 1.6 %reshape.52.conv_weight_ref = bf16[192,576]{1,0:T(8,128)(2,1)S(1)} reshape(bf16[3,64,9,64]{3,2,1,0:T(8,128)(2,1)} %copy.32) | data formatting | bytes 442368 | tf_op jit(solution)/shard_map/reshape | solution.py:634
  20.7 0.1 pad_add_fusion.place_ref
  20.8 4.1 %all-to-all-done = f32[16,16,128]{2,1,0:T(8,128)S(1)} async-done(((f32[16,16,128]{2,1,0:T(8,128)}), f32[16,16,128]{2,1,0:T(8,128)S(1)}, u32[]{:S(2)}, u32[]{:S(2)}) %all-to-all-start) | async-done | bytes 131104 | tf_op jit(solution)/shard_map/all_to_all | solution.py:624
  24.9 0.6 copy-done.5
  25.6 0.0 copy-done.4
  25.6 18.8 %encode_decode.1 = (f32[16,80,128]{2,1,0:T(8,128)S(1)}, f32[16,80,128]{2,1,0:T(8,128)S(1)}) custom-call(s32[3]{0:T(128)S(1)} %pad_add_fusion.place_ref, bf16[2,8,64,128]{3,2,1,0:T(8,128)(2,1)S(1)} %collective-permute-done.left_ref, bf16[4,8,64,128]{3,2,1,0:T(8,128)(2,1)S(1)} %bitcast.28, bf16[3,8,64,128]{3,2,1,0:T(8,128)(2,1)S(1)} %collective-permute-done.1.right_ref, ...), custom_call_target="tpu_custom_call" | custom-call | tf_op jit(solution)/shard_map/encode_decode/pallas_call | solution.py:502
  44.3 0.1 collective-permute-start.2
  44.4 2.1 %collective-permute-done.2 = f32[16,80,128]{2,1,0:T(8,128)S(1)} collective-permute-done((f32[16,80,128]{2,1,0:T(8,128)S(1)}, f32[16,80,128]{2,1,0:T(8,128)S(1)}, u32[]{:S(2)}, u32[]{:S(2)}) %collective-permute-start.2) | collective-permute-done | bytes 655392 | tf_op jit(solution)/shard_map/ppermute | solution.py:491
  46.5 0.1 add.41
  46.6 0.1 collective-permute-start.3
  46.7 2.9 %collective-permute-start.5 = (f32[4,80,128]{2,1,0:T(8,128)S(1)}, f32[4,80,128]{2,1,0:T(8,128)S(1)}, u32[]{:S(2)}, u32[]{:S(2)}) collective-permute-start(f32[4,80,128]{2,1,0:T(8,128)S(1)} %get-tuple-element.50), channel_id=1, source_target_pairs={{0,18},{1,19},{2,16},{3,17},{4,22},{5,23},{6,20},{7,21},{8,26},{9,... | collective-permute-start | bytes 491528 | tf_op jit(solution)/shard_map/ppermute | solution.py:491
  49.6 0.5 collective-permute-start.4
  50.2 6.3 %collective-permute-done.3 = f32[4,80,128]{2,1,0:T(8,128)S(1)} collective-permute-done((f32[4,80,128]{2,1,0:T(8,128)S(1)}, f32[4,80,128]{2,1,0:T(8,128)S(1)}, u32[]{:S(2)}, u32[]{:S(2)}) %collective-permute-start.3) | collective-permute-done | bytes 163872 | tf_op jit(solution)/shard_map/ppermute | solution.py:491
  56.4 1.2 %collective-permute-done.4 = f32[4,80,128]{2,1,0:T(8,128)S(1)} collective-permute-done((f32[4,80,128]{2,1,0:T(8,128)S(1)}, f32[4,80,128]{2,1,0:T(8,128)S(1)}, u32[]{:S(2)}, u32[]{:S(2)}) %collective-permute-start.4) | collective-permute-done | bytes 163872 | tf_op jit(solution)/shard_map/ppermute | solution.py:491
  57.7 0.1 collective-permute-start.6
  57.8 1.9 %collective-permute-start.8 = (f32[1,80,128]{2,1,0:T(8,128)S(1)}, f32[1,80,128]{2,1,0:T(8,128)S(1)}, u32[]{:S(2)}, u32[]{:S(2)}) collective-permute-start(f32[1,80,128]{2,1,0:T(8,128)S(1)} %get-tuple-element.53), channel_id=1, source_target_pairs={{0,12},{1,13},{2,14},{3,15},{4,8},{5,9},{6,10},{7,11},{8,4},{9,5},... | collective-permute-start | bytes 122888 | tf_op jit(solution)/shard_map/ppermute | solution.py:491
  59.7 1.6 %collective-permute-start.7 = (f32[1,80,128]{2,1,0:T(8,128)S(1)}, f32[1,80,128]{2,1,0:T(8,128)S(1)}, u32[]{:S(2)}, u32[]{:S(2)}) collective-permute-start(f32[1,80,128]{2,1,0:T(8,128)S(1)} %get-tuple-element.54), channel_id=1, source_target_pairs={{0,8},{1,9},{2,10},{3,11},{4,12},{5,13},{6,14},{7,15},{8,0},{9,1},... | collective-permute-start | bytes 122888 | tf_op jit(solution)/shard_map/ppermute | solution.py:491
  61.3 1.2 %collective-permute-done.6 = f32[1,80,128]{2,1,0:T(8,128)S(1)} collective-permute-done((f32[1,80,128]{2,1,0:T(8,128)S(1)}, f32[1,80,128]{2,1,0:T(8,128)S(1)}, u32[]{:S(2)}, u32[]{:S(2)}) %collective-permute-start.6) | collective-permute-done | bytes 40992 | tf_op jit(solution)/shard_map/ppermute | solution.py:491
  62.5 1.2 %collective-permute-done.8 = f32[1,80,128]{2,1,0:T(8,128)S(1)} collective-permute-done((f32[1,80,128]{2,1,0:T(8,128)S(1)}, f32[1,80,128]{2,1,0:T(8,128)S(1)}, u32[]{:S(2)}, u32[]{:S(2)}) %collective-permute-start.8) | collective-permute-done | bytes 40992 | tf_op jit(solution)/shard_map/ppermute | solution.py:491
  63.7 0.9 %collective-permute-done.7 = f32[1,80,128]{2,1,0:T(8,128)S(1)} collective-permute-done((f32[1,80,128]{2,1,0:T(8,128)S(1)}, f32[1,80,128]{2,1,0:T(8,128)S(1)}, u32[]{:S(2)}, u32[]{:S(2)}) %collective-permute-start.7) | collective-permute-done | bytes 40992 | tf_op jit(solution)/shard_map/ppermute | solution.py:491
  64.6 2.1 %collective-permute-start.11 = (f32[1,80,128]{2,1,0:T(8,128)S(1)}, f32[1,80,128]{2,1,0:T(8,128)S(1)}, u32[]{:S(2)}, u32[]{:S(2)}) collective-permute-start(f32[1,80,128]{2,1,0:T(8,128)S(1)} %get-tuple-element.48), channel_id=1, source_target_pairs={{0,12},{1,13},{2,14},{3,15},{4,8},{5,9},{6,10},{7,11},{8,4},{9,5},... | collective-permute-start | bytes 122888 | tf_op jit(solution)/shard_map/ppermute | solution.py:491
  66.7 2.4 %collective-permute-start.9 = (f32[1,80,128]{2,1,0:T(8,128)S(1)}, f32[1,80,128]{2,1,0:T(8,128)S(1)}, u32[]{:S(2)}, u32[]{:S(2)}) collective-permute-start(f32[1,80,128]{2,1,0:T(8,128)S(1)} %get-tuple-element.48), channel_id=1, source_target_pairs={{0,4},{1,5},{2,6},{3,7},{4,0},{5,1},{6,2},{7,3},{8,12},{9,13},{10,... | collective-permute-start | bytes 122888 | tf_op jit(solution)/shard_map/ppermute | solution.py:491
  69.1 1.4 %collective-permute-done.11 = f32[1,80,128]{2,1,0:T(8,128)S(1)} collective-permute-done((f32[1,80,128]{2,1,0:T(8,128)S(1)}, f32[1,80,128]{2,1,0:T(8,128)S(1)}, u32[]{:S(2)}, u32[]{:S(2)}) %collective-permute-start.11) | collective-permute-done | bytes 40992 | tf_op jit(solution)/shard_map/ppermute | solution.py:491
  70.5 1.1 %collective-permute-done.10 = f32[1,80,128]{2,1,0:T(8,128)S(1)} collective-permute-done((f32[1,80,128]{2,1,0:T(8,128)S(1)}, f32[1,80,128]{2,1,0:T(8,128)S(1)}, u32[]{:S(2)}, u32[]{:S(2)}) %collective-permute-start.10) | collective-permute-done | bytes 40992 | tf_op jit(solution)/shard_map/ppermute | solution.py:491
  71.6 2.0 %collective-permute-start.14 = (f32[4,80,128]{2,1,0:T(8,128)S(1)}, f32[4,80,128]{2,1,0:T(8,128)S(1)}, u32[]{:S(2)}, u32[]{:S(2)}) collective-permute-start(f32[4,80,128]{2,1,0:T(8,128)S(1)} %pad_maximum_fusion), channel_id=1, source_target_pairs={{0,18},{1,19},{2,16},{3,17},{4,22},{5,23},{6,20},{7,21},{8,26},{9,... | collective-permute-start | bytes 491528 | tf_op jit(solution)/shard_map/ppermute | solution.py:491
  73.6 0.5 collective-permute-start.13
  74.1 1.1 %collective-permute-start.12 = (f32[4,80,128]{2,1,0:T(8,128)S(1)}, f32[4,80,128]{2,1,0:T(8,128)S(1)}, u32[]{:S(2)}, u32[]{:S(2)}) collective-permute-start(f32[4,80,128]{2,1,0:T(8,128)S(1)} %pad_maximum_fusion), channel_id=1, source_target_pairs={{0,2},{1,3},{2,0},{3,1},{4,6},{5,7},{6,4},{7,5},{8,10},{9,11},{10,... | collective-permute-start | bytes 491528 | tf_op jit(solution)/shard_map/ppermute | solution.py:491
  75.2 4.5 %collective-permute-done.12 = f32[4,80,128]{2,1,0:T(8,128)S(1)} collective-permute-done((f32[4,80,128]{2,1,0:T(8,128)S(1)}, f32[4,80,128]{2,1,0:T(8,128)S(1)}, u32[]{:S(2)}, u32[]{:S(2)}) %collective-permute-start.12) | collective-permute-done | bytes 163872 | tf_op jit(solution)/shard_map/ppermute | solution.py:491
  79.7 0.1 collective-permute-start.15
  79.8 2.1 %collective-permute-done.15.other_ref = f32[16,80,128]{2,1,0:T(8,128)S(1)} collective-permute-done((f32[16,80,128]{2,1,0:T(8,128)S(1)}, f32[16,80,128]{2,1,0:T(8,128)S(1)}, u32[]{:S(2)}, u32[]{:S(2)}) %collective-permute-start.15) | collective-permute-done | bytes 655392 | tf_op jit(solution)/shard_map/ppermute | solution.py:491
  81.9 2.0 %unpack.1 = (f32[1,5,128]{2,1,0:T(8,128)S(1)}, f32[64,512]{1,0:T(8,128)}, f32[3,512]{1,0:T(4,128)}, f32[1,512]{1,0:T(1,128)}, f32[512,512]{1,0:T(8,128)}, /*inde...) custom-call(s32[3]{0:T(128)S(1)} %pad_add_fusion.place_ref, ...), custom_call_target="tpu_custom_call" | custom-call | tf_op jit(solution)/shard_map/unpack/pallas_call | solution.py:584
  83.9 0.6 slice.55
  84.5 0.5 slice_bitcast_fusion
  85.0 0.6 copy.31
  (36 shorter events, 0.3 us)
Async XLA Ops:
  1.9 6.2 %copy-start.9 = (f32[1,3,128]{2,0,1:T(1,128)S(1)}, f32[1,3,128]{2,0,1:T(1,128)}, u32[]{:S(2)}) copy-start(f32[1,3,128]{2,0,1:T(1,128)} %param.19) | copy-start | bytes 4612
  1.9 22.9 %collective-permute-start.1 = (bf16[3,8,64,128]{3,2,1,0:T(8,128)(2,1)S(1)}, bf16[3,8,64,128]{3,2,1,0:T(8,128)(2,1)S(1)}, u32[]{:S(2)}, u32[]{:S(2)}) collective-permute-start(bf16[3,8,64,128]{3,2,1,0:T(8,128)(2,1)S(1)} %slice.57), channel_id=1, source_target_pairs={{1,0},{2,1},{3,2},{4,3},{5,4},{6,5},{7,6},{8,7},{9,8},{10,9},{11,1... | collective-permute-start | bytes 1179656 | tf_op jit(solution)/shard_map/ppermute | solution.py:632
  8.1 0.7 copy-start.8
  8.1 16.7 %collective-permute-start = (bf16[2,8,64,128]{3,2,1,0:T(8,128)(2,1)}, bf16[2,8,64,128]{3,2,1,0:T(8,128)(2,1)S(1)}, u32[]{:S(2)}, u32[]{:S(2)}) collective-permute-start(bf16[2,8,64,128]{3,2,1,0:T(8,128)(2,1)} %slice.56), channel_id=1, source_target_pairs={{0,1},{1,2},{2,3},{3,4},{4,5},{5,6},{6,7},{7,8},{8,9},{9,10},{10,1... | collective-permute-start | bytes 786440 | tf_op jit(solution)/shard_map/ppermute | solution.py:631
  9.4 8.3 %copy-start.7 = (bf16[64,1728]{1,0:T(8,128)(2,1)S(1)}, bf16[64,1728]{1,0:T(8,128)(2,1)}, u32[]{:S(2)}) copy-start(bf16[64,1728]{1,0:T(8,128)(2,1)} %param.15) | copy-start | bytes 663556
  11.2 13.7 %all-to-all-start = ((f32[16,16,128]{2,1,0:T(8,128)}), f32[16,16,128]{2,1,0:T(8,128)S(1)}, u32[]{:S(2)}, u32[]{:S(2)}) async-start(f32[16,16,128]{2,1,0:T(8,128)} %bitcast.33), calls=%async_computation | async-start | bytes 262144 | tf_op jit(solution)/shard_map/all_to_all | solution.py:624
  16.9 0.7 copy-start.10
  18.0 6.9 %copy-start = (f32[512,512]{1,0:T(8,128)S(1)}, f32[512,512]{1,0:T(8,128)}, u32[]{:S(2)}) copy-start(f32[512,512]{1,0:T(8,128)} %w_mid_ref.1) | copy-start | bytes 3145732
  19.1 5.8 %copy-start.1 = (f32[64,512]{1,0:T(8,128)S(1)}, f32[64,512]{1,0:T(8,128)}, u32[]{:S(2)}) copy-start(f32[64,512]{1,0:T(8,128)} %w_latent_ref.1) | copy-start | bytes 393220
  19.1 5.8 %copy-start.2 = (f32[5,512]{1,0:T(8,128)S(1)}, f32[5,512]{1,0:T(8,128)}, u32[]{:S(2)}) copy-start(f32[5,512]{1,0:T(8,128)} %w_out_ref.1) | copy-start | bytes 30724
  20.7 4.3 %copy-start.3 = (f32[3,512]{1,0:T(4,128)S(1)}, f32[3,512]{1,0:T(4,128)}, u32[]{:S(2)}) copy-start(f32[3,512]{1,0:T(4,128)} %w_pos_ref.1) | copy-start | bytes 18436
  24.9 0.7 copy-start.5
  24.9 0.7 copy-start.4
  24.9 0.7 copy-start.6
  44.3 2.2 %collective-permute-start.2 = (f32[16,80,128]{2,1,0:T(8,128)S(1)}, f32[16,80,128]{2,1,0:T(8,128)S(1)}, u32[]{:S(2)}, u32[]{:S(2)}) collective-permute-start(f32[16,80,128]{2,1,0:T(8,128)S(1)} %get-tuple-element.20), channel_id=1, source_target_pairs={{0,1},{1,0},{2,3},{3,2},{4,5},{5,4},{6,7},{7,6},{8,9},{9,8},{10,11... | collective-permute-start | bytes 1966088 | tf_op jit(solution)/shard_map/ppermute | solution.py:491
  46.6 9.8 %collective-permute-start.3 = (f32[4,80,128]{2,1,0:T(8,128)S(1)}, f32[4,80,128]{2,1,0:T(8,128)S(1)}, u32[]{:S(2)}, u32[]{:S(2)}) collective-permute-start(f32[4,80,128]{2,1,0:T(8,128)S(1)} %get-tuple-element.49), channel_id=1, source_target_pairs={{0,2},{1,3},{2,0},{3,1},{4,6},{5,7},{6,4},{7,5},{8,10},{9,11},{10,... | collective-permute-start | bytes 491528 | tf_op jit(solution)/shard_map/ppermute | solution.py:491
  46.7 9.7 %collective-permute-start.5 = (f32[4,80,128]{2,1,0:T(8,128)S(1)}, f32[4,80,128]{2,1,0:T(8,128)S(1)}, u32[]{:S(2)}, u32[]{:S(2)}) collective-permute-start(f32[4,80,128]{2,1,0:T(8,128)S(1)} %get-tuple-element.50), channel_id=1, source_target_pairs={{0,18},{1,19},{2,16},{3,17},{4,22},{5,23},{6,20},{7,21},{8,26},{9,... | collective-permute-start | bytes 491528 | tf_op jit(solution)/shard_map/ppermute | solution.py:491
  49.6 8.0 %collective-permute-start.4 = (f32[4,80,128]{2,1,0:T(8,128)S(1)}, f32[4,80,128]{2,1,0:T(8,128)S(1)}, u32[]{:S(2)}, u32[]{:S(2)}) collective-permute-start(f32[4,80,128]{2,1,0:T(8,128)S(1)} %get-tuple-element.51), channel_id=1, source_target_pairs={{0,16},{1,17},{2,18},{3,19},{4,20},{5,21},{6,22},{7,23},{8,24},{9,... | collective-permute-start | bytes 491528 | tf_op jit(solution)/shard_map/ppermute | solution.py:491
  57.7 4.8 %collective-permute-start.6 = (f32[1,80,128]{2,1,0:T(8,128)S(1)}, f32[1,80,128]{2,1,0:T(8,128)S(1)}, u32[]{:S(2)}, u32[]{:S(2)}) collective-permute-start(f32[1,80,128]{2,1,0:T(8,128)S(1)} %get-tuple-element.52), channel_id=1, source_target_pairs={{0,4},{1,5},{2,6},{3,7},{4,0},{5,1},{6,2},{7,3},{8,12},{9,13},{10,... | collective-permute-start | bytes 122888 | tf_op jit(solution)/shard_map/ppermute | solution.py:491
  57.8 5.9 %collective-permute-start.8 = (f32[1,80,128]{2,1,0:T(8,128)S(1)}, f32[1,80,128]{2,1,0:T(8,128)S(1)}, u32[]{:S(2)}, u32[]{:S(2)}) collective-permute-start(f32[1,80,128]{2,1,0:T(8,128)S(1)} %get-tuple-element.53), channel_id=1, source_target_pairs={{0,12},{1,13},{2,14},{3,15},{4,8},{5,9},{6,10},{7,11},{8,4},{9,5},... | collective-permute-start | bytes 122888 | tf_op jit(solution)/shard_map/ppermute | solution.py:491
  59.7 4.9 %collective-permute-start.7 = (f32[1,80,128]{2,1,0:T(8,128)S(1)}, f32[1,80,128]{2,1,0:T(8,128)S(1)}, u32[]{:S(2)}, u32[]{:S(2)}) collective-permute-start(f32[1,80,128]{2,1,0:T(8,128)S(1)} %get-tuple-element.54), channel_id=1, source_target_pairs={{0,8},{1,9},{2,10},{3,11},{4,12},{5,13},{6,14},{7,15},{8,0},{9,1},... | collective-permute-start | bytes 122888 | tf_op jit(solution)/shard_map/ppermute | solution.py:491
  64.6 5.9 %collective-permute-start.11 = (f32[1,80,128]{2,1,0:T(8,128)S(1)}, f32[1,80,128]{2,1,0:T(8,128)S(1)}, u32[]{:S(2)}, u32[]{:S(2)}) collective-permute-start(f32[1,80,128]{2,1,0:T(8,128)S(1)} %get-tuple-element.48), channel_id=1, source_target_pairs={{0,12},{1,13},{2,14},{3,15},{4,8},{5,9},{6,10},{7,11},{8,4},{9,5},... | collective-permute-start | bytes 122888 | tf_op jit(solution)/shard_map/ppermute | solution.py:491
  66.7 4.9 %collective-permute-start.10 = (f32[1,80,128]{2,1,0:T(8,128)S(1)}, f32[1,80,128]{2,1,0:T(8,128)S(1)}, u32[]{:S(2)}, u32[]{:S(2)}) collective-permute-start(f32[1,80,128]{2,1,0:T(8,128)S(1)} %get-tuple-element.48), channel_id=1, source_target_pairs={{0,8},{1,9},{2,10},{3,11},{4,12},{5,13},{6,14},{7,15},{8,0},{9,1},... | collective-permute-start | bytes 122888 | tf_op jit(solution)/shard_map/ppermute | solution.py:491
  66.7 4.9 %collective-permute-start.9 = (f32[1,80,128]{2,1,0:T(8,128)S(1)}, f32[1,80,128]{2,1,0:T(8,128)S(1)}, u32[]{:S(2)}, u32[]{:S(2)}) collective-permute-start(f32[1,80,128]{2,1,0:T(8,128)S(1)} %get-tuple-element.48), channel_id=1, source_target_pairs={{0,4},{1,5},{2,6},{3,7},{4,0},{5,1},{6,2},{7,3},{8,12},{9,13},{10,... | collective-permute-start | bytes 122888 | tf_op jit(solution)/shard_map/ppermute | solution.py:491
  71.6 8.1 %collective-permute-start.14 = (f32[4,80,128]{2,1,0:T(8,128)S(1)}, f32[4,80,128]{2,1,0:T(8,128)S(1)}, u32[]{:S(2)}, u32[]{:S(2)}) collective-permute-start(f32[4,80,128]{2,1,0:T(8,128)S(1)} %pad_maximum_fusion), channel_id=1, source_target_pairs={{0,18},{1,19},{2,16},{3,17},{4,22},{5,23},{6,20},{7,21},{8,26},{9,... | collective-permute-start | bytes 491528 | tf_op jit(solution)/shard_map/ppermute | solution.py:491
  73.6 6.1 %collective-permute-start.13 = (f32[4,80,128]{2,1,0:T(8,128)S(1)}, f32[4,80,128]{2,1,0:T(8,128)S(1)}, u32[]{:S(2)}, u32[]{:S(2)}) collective-permute-start(f32[4,80,128]{2,1,0:T(8,128)S(1)} %pad_maximum_fusion), channel_id=1, source_target_pairs={{0,16},{1,17},{2,18},{3,19},{4,20},{5,21},{6,22},{7,23},{8,24},{9,... | collective-permute-start | bytes 491528 | tf_op jit(solution)/shard_map/ppermute | solution.py:491
  74.1 5.5 %collective-permute-start.12 = (f32[4,80,128]{2,1,0:T(8,128)S(1)}, f32[4,80,128]{2,1,0:T(8,128)S(1)}, u32[]{:S(2)}, u32[]{:S(2)}) collective-permute-start(f32[4,80,128]{2,1,0:T(8,128)S(1)} %pad_maximum_fusion), channel_id=1, source_target_pairs={{0,2},{1,3},{2,0},{3,1},{4,6},{5,7},{6,4},{7,5},{8,10},{9,11},{10,... | collective-permute-start | bytes 491528 | tf_op jit(solution)/shard_map/ppermute | solution.py:491
  79.7 2.2 %collective-permute-start.15 = (f32[16,80,128]{2,1,0:T(8,128)S(1)}, f32[16,80,128]{2,1,0:T(8,128)S(1)}, u32[]{:S(2)}, u32[]{:S(2)}) collective-permute-start(f32[16,80,128]{2,1,0:T(8,128)S(1)} %constant_dynamic-update-slice_fusion.mine_ref), channel_id=1, source_target_pairs={{0,1},{1,0},{2,3},{3,2},{4,5},{5,4},{6,7},{7,6},{8,9},{9,8},{10,11... | collective-permute-start | bytes 1966088 | tf_op jit(solution)/shard_map/ppermute | solution.py:491
where the time goes:
time: 85.9 us; the launch traced here: 85.6 us
  starting transfers between devices  26.5 us (31%)
  waiting for transfers between devices  26.1 us (30%)
  Pallas kernels  22.5 us (26%)
  local copies, waits for them, and re-layouts  9.38 us (11%)
  between operations  0.91 us (1%)
    ppermute x14, waiting for transfers between devices, swapped(): lax.ppermute(value, ('replica', 'tile'), [(i, i ^ mask) for i in range(pl...  22 us
    pallas_call x1, Pallas kernels, main(): pl.pallas_call(functools.partial(main_kernel, plan), out_shape=(outs, out...  18.8 us
    ppermute x14, starting transfers between devices, swapped(): lax.ppermute(value, ('replica', 'tile'), [(i, i ^ mask) for i in range(pl...  15.2 us
    all_to_all x1, starting transfers between devices, body(): lax.all_to_all(words.reshape(tiles, slots, WORDS), 'tile', split_axis=0,...  5.73 us
    ppermute x1, starting transfers between devices, body(): right = lax.ppermute(here[:DILATION_RATE + 1], 'tile', down)  5.5 us
    unnamed x31, local copies, waits for them, and re-layouts  4.46 us
    all_to_all x1, waiting for transfers between devices, body(): lax.all_to_all(words.reshape(tiles, slots, WORDS), 'tile', split_axis=0,...  4.1 us
    reshape x2, local copies, waits for them, and re-layouts, body(): taps = taps.transpose(2, 0, 1, 3).reshape(3 * channels, 9 * channels)  2.6 us
  transfers between devices with their start and end apart: 17, of which 11 were waited for; matrix products, arithmetic and copies ran while one was open for 6% of the time, Pallas kernels for 2%

commit v1 on v0

--- a/solution.py
+++ b/solution.py
@@ -45,83 +45,100 @@
     return mul(left[0], right[0], dims) + mul(left[0], right[1], dims) + mul(left[1], right[0], dims)
 
 
-def route_kernel(tiles, slots, owner_ref, cell_ref, frac_ref, target_ref, out_ref, words):
-    queries = owner_ref.shape[1]
-    owner = owner_ref[...]
-    hits = (lax.broadcasted_iota(jnp.int32, (tiles, queries), 0) == owner).astype(F32)
+def select(gathered_ref, my_tile, slots, words_ref):
+    tiles, kinds, queries = gathered_ref.shape
+    owner = jnp.concatenate([gathered_ref[r, 0:1, :] for r in range(tiles)], axis=0)
+    hits = jnp.where(owner == my_tile.astype(F32), 1.0, 0.0)
     before = lax.broadcasted_iota(jnp.int32, (queries, queries), 0) < lax.broadcasted_iota(
         jnp.int32, (queries, queries), 1
     )
-    earlier = mul(hits.astype(BF16), before.astype(F32).astype(BF16))
-    slot = jnp.sum(hits * earlier, axis=0, keepdims=True)
-    place = owner * slots + slot.astype(jnp.int32)
-    chosen = (lax.broadcasted_iota(jnp.int32, (tiles * slots, queries), 0) == place).astype(F32).astype(BF16)
-    words[...] = jnp.zeros_like(words)
-    words[0:1, :] = cell_ref[...].astype(F32)
-    words[1:4, :] = frac_ref[...]
-    words[4:9, :] = target_ref[...]
-    words[9:10, :] = jnp.ones((1, queries), F32)
-    words[10:11, :] = lax.broadcasted_iota(jnp.int32, (1, queries), 1).astype(F32)
-    high, middle, low = thirds(words[...])
-    out_ref[...] = mul(chosen, high, NT) + mul(chosen, middle, NT) + mul(chosen, low, NT)
-
-
-def route(owner, cell, frac, target, tiles, slots):
-    queries = owner.shape[1]
+    earlier = mul(hits.astype(BF16), jnp.where(before, 1.0, 0.0).astype(BF16))
+    place = jnp.where(hits > 0.0, earlier, -1.0)
+    slot = lax.broadcasted_iota(jnp.int32, (slots, queries), 0).astype(F32)
+    chosen = jnp.concatenate([jnp.where(slot == place[r : r + 1, :], 1.0, 0.0) for r in range(tiles)], axis=0)
+    chosen = chosen.astype(BF16)
+    high, middle, low = thirds(gathered_ref[...].reshape(tiles * kinds, queries))
+    picked = mul(chosen, high, NT) + mul(chosen, middle, NT) + mul(chosen, low, NT)
+    words_ref[...] = jnp.zeros_like(words_ref)
+    for r in range(tiles):
+        words_ref[r * slots : (r + 1) * slots, 0:kinds] = picked[
+            r * slots : (r + 1) * slots, r * kinds : (r + 1) * kinds
+        ]
+
+
+def tap_sum(weight_ref, planes, pair):
+    total = None
+    for step_x, ref, index in planes:
+        rows_y = ref.shape[1]
+        blocks = [
+            jnp.concatenate([ref[index, (2 * pair + half + step_y) % rows_y] for half in (0, 1)], axis=1)
+            for step_y in (-1, 0, 1)
+        ]
+        term = mul(weight_ref[step_x], jnp.concatenate(blocks, axis=0))
+        total = term if total is None else total + term
+    channels = total.shape[0] // 3
+    sides = []
+    for half in (0, 1):
+        part = total[:, half * LANES : (half + 1) * LANES]
+        sides.append(
+            part[channels : 2 * channels]
+            + pltpu.roll(part[:channels], 1, 1)
+            + pltpu.roll(part[2 * channels :], LANES - 1, 1)
+        )
+    return jnp.concatenate(sides, axis=1)
+
+
+def local_kernel(here_ref, weight_ref, w_mid_ref, partial_ref, high_ref, low_ref):
+    planes, rows_y = here_ref.shape[0], here_ref.shape[1]
+    for x in range(planes + 1):
+        taps = [
+            (step, here_ref, x + DILATION_RATE * (step - 1))
+            for step in range(3)
+            if 0 <= x + DILATION_RATE * (step - 1) < planes
+        ]
+        for pair in range(rows_y // 2):
+            partial_ref[x * (rows_y // 2) + pair] = tap_sum(weight_ref, taps, pair)
+    high, low = halves(w_mid_ref[...])
+    high_ref[...] = high
+    low_ref[...] = low
+
+
+def local_part(here, taps, w_mid):
+    planes, rows_y, channels, rows_z = here.shape
+    pairs = (planes + 1) * rows_y // 2
+    split = jax.ShapeDtypeStruct(w_mid.shape, BF16)
     return pl.pallas_call(
-        functools.partial(route_kernel, tiles, slots),
-        out_shape=jax.ShapeDtypeStruct((tiles * slots, WORDS), F32),
-        in_specs=[VMEM] * 4,
-        out_specs=VMEM,
-        scratch_shapes=[pltpu.VMEM((WORDS, queries), F32)],
-        name="route",
-    )(owner, cell, frac, target)
-
-
-def convolve(left_ref, here_ref, right_ref, weight_ref, bias_ref, lat):
-    planes, rows_y = here_ref.shape[0], here_ref.shape[1]
-    channels = here_ref.shape[2]
-    behind = left_ref.shape[0]
-
-    def plane(index):
-        if index < behind:
-            return left_ref, index
-        if index < behind + planes:
-            return here_ref, index - behind
-        return right_ref, index - behind - planes
-
-    weight = weight_ref[...]
+        local_kernel,
+        out_shape=(jax.ShapeDtypeStruct((pairs, channels, 2 * rows_z), F32), split, split),
+        in_specs=[VMEM] * 3,
+        out_specs=(VMEM, VMEM, VMEM),
+        compiler_params=pltpu.CompilerParams(vmem_limit_bytes=16 << 20),
+        cost_estimate=pl.CostEstimate(flops=3 << 30, bytes_accessed=4 << 20, transcendentals=0),
+        name="conv_local",
+    )(here, taps, w_mid)
+
+
+def finish_latent(left_ref, right_ref, partial_ref, weight_ref, bias_ref, planes, lat):
+    rows_y = left_ref.shape[1]
     bias = bias_ref[...]
     for x in range(planes + 1):
+        taps = []
+        for step in range(3):
+            plane = x + DILATION_RATE * (step - 1)
+            if plane < 0:
+                taps.append((step, left_ref, plane + left_ref.shape[0]))
+            elif plane >= planes:
+                taps.append((step, right_ref, plane - planes))
         for pair in range(rows_y // 2):
-            blocks = []
-            for step_x in range(3):
-                ref, index = plane(x + DILATION_RATE * step_x)
-                for step_y in (-1, 0, 1):
-                    blocks.append(
-                        jnp.concatenate(
-                            [ref[index, (2 * pair + half + step_y) % rows_y] for half in (0, 1)],
-                            axis=1,
-                        )
-                    )
-            partial = mul(weight, jnp.concatenate(blocks, axis=0))
-            for half in (0, 1):
-                part = partial[:, half * LANES : (half + 1) * LANES]
-                summed = (
-                    part[channels : 2 * channels]
-                    + pltpu.roll(part[:channels], 1, 1)
-                    + pltpu.roll(part[2 * channels :], LANES - 1, 1)
-                    + bias
-                )
-                lat[x * (rows_y // 2) + pair, :, half * LANES : (half + 1) * LANES] = jax.nn.gelu(
-                    summed
-                ).astype(BF16)
+            number = x * (rows_y // 2) + pair
+            summed = partial_ref[number] + tap_sum(weight_ref, taps, pair) + bias
+            lat[number] = jax.nn.gelu(summed).astype(BF16)
 
 
 def interpolate(words, lat, planes, rows_y, rows_z):
     rows = words.shape[0]
-    cell = jnp.broadcast_to(words[:, 0:1], (rows, LANES)).astype(jnp.int32)
-    frac = [jnp.broadcast_to(words[:, 1 + d : 2 + d], (rows, LANES)) for d in range(3)]
+    cell = jnp.broadcast_to(words[:, 1:2], (rows, LANES)).astype(jnp.int32)
+    frac = [jnp.broadcast_to(words[:, 2 + d : 3 + d], (rows, LANES)) for d in range(3)]
     shift_z = rows_z.bit_length() - 1
     shift_y = rows_y.bit_length() - 1
     base_x = cell >> (shift_z + shift_y)
@@ -154,15 +171,16 @@
     plan,
     place_ref,
     left_ref,
-    here_ref,
     right_ref,
+    partial_ref,
     conv_weight_ref,
     conv_bias_ref,
-    words_ref,
+    gathered_ref,
     w_latent_ref,
     w_pos_ref,
     bias_one_ref,
-    w_mid_ref,
+    mid_high,
+    mid_low,
     bias_two_ref,
     w_out_ref,
     bias_out_ref,
@@ -172,8 +190,7 @@
     code,
     pos,
     z_one,
-    mid_high,
-    mid_low,
+    words_ref,
     one_high,
     one_low,
     mixed,
@@ -186,15 +203,17 @@
     d_out_t,
     packed,
 ):
-    rows = words_ref.shape[0]
-    hidden = w_mid_ref.shape[0]
+    rows = plan.tiles * plan.slots
+    hidden = mid_high.shape[0]
     latents = w_latent_ref.shape[0]
-    planes, rows_y, rows_z = here_ref.shape[0], here_ref.shape[1], here_ref.shape[3]
+    planes, rows_y, rows_z = plan.planes, left_ref.shape[1], left_ref.shape[3]
+    slots = rows // plan.tiles
     my_chunk = place_ref[0]
     my_tile = place_ref[1]
     my_replica = place_ref[2]
 
-    convolve(left_ref, here_ref, right_ref, conv_weight_ref, conv_bias_ref, lat)
+    select(gathered_ref, my_tile, slots, words_ref)
+    finish_latent(left_ref, right_ref, partial_ref, conv_weight_ref, conv_bias_ref, planes, lat)
     words = words_ref[...]
     interp, base_x, base_y, base_z, frac = interpolate(words, lat, planes, rows_y, rows_z)
     code[...] = interp
@@ -212,9 +231,6 @@
 
     wl_high, wl_low = halves(w_latent_ref[...])
     z_one[...] = mul(interp, wl_high) + mul(interp, wl_low)
-    high, low = halves(w_mid_ref[...])
-    mid_high[...] = high
-    mid_low[...] = low
     w_pos = [w_pos_ref[d : d + 1, :] for d in range(3)]
     square = w_pos[0] * w_pos[0] + w_pos[1] * w_pos[1] + w_pos[2] * w_pos[2]
     bias_one = bias_one_ref[...]
@@ -281,8 +297,8 @@
         out_t[8 * s : 8 * s + 8, :] = both[:8] + both[8:] + mul(wo_high, two_low[span, :], NT)
 
     words_t = words.T
-    target = [words_t[4 + f : 5 + f, :] for f in range(5)]
-    valid = words_t[9:10, :]
+    target = [words_t[5 + f : 6 + f, :] for f in range(5)]
+    valid = words_t[10:11, :]
     value = [out_t[f : f + 1, :] + bias_out_ref[f] for f in range(5)]
     grad = [[out_t[8 * (d + 1) + f : 8 * (d + 1) + f + 1, :] for f in range(5)] for d in range(3)]
     laplace = [out_t[32 + f : 33 + f, :] for f in range(5)]
@@ -436,13 +452,12 @@
             packed[first + number : first + number + 1, :] = row[:, lanes]
         packed[first + 8 : first + 16, :] = grad_out[:, lanes]
 
-    slots = rows // plan.tiles
     chosen = jnp.where(
-        lane == jnp.broadcast_to(words[:, 10:11], (rows, LANES)).astype(jnp.int32), words[:, 9:10], 0.0
+        lane == jnp.broadcast_to(words[:, 11:12], (rows, LANES)).astype(jnp.int32), words[:, 10:11], 0.0
     ).astype(BF16)
     source = lax.broadcasted_iota(jnp.int32, (plan.tiles, rows), 0)
     inside = lax.broadcasted_iota(jnp.int32, (plan.tiles, rows), 1)
-    mine = (inside >= source * slots) & (inside < (source + 1) * slots)
+    mine = jnp.bitwise_xor(inside >> (slots.bit_length() - 1), my_tile) == source
     for f in range(5):
         high, middle, low = thirds(jnp.where(mine, jnp.broadcast_to(value[f], (plan.tiles, rows)), 0.0))
         first = pl.multiple_of((hidden // LANES) * main_rows + f * plan.devices + my_replica * plan.tiles, 16)
@@ -464,8 +479,9 @@
 
 
 class Plan:
-    def __init__(self, tiles, replicas, queries, hidden, latents):
-        self.tiles, self.replicas = tiles, replicas
+    def __init__(self, tiles, replicas, queries, planes, hidden, latents):
+        self.tiles, self.replicas, self.planes = tiles, replicas, planes
+        self.slots = 2 * queries // tiles
         self.devices = tiles * replicas
         self.query_total = float(queries * self.devices)
         self.main_rows = hidden + latents + MISC
@@ -473,6 +489,9 @@
         self.chunk = -(-needed // (8 * self.devices)) * 8
         bits = self.devices.bit_length() - 1
         middle = list(range(2, bits - 1))
+        along = list(range(1, tiles.bit_length() - 1))
+        odd = len(along) % 2
+        self.tile_stages = [[0]] + [along[:1]] * odd + [along[i : i + 2] for i in range(odd, len(along), 2)]
         self.stages = [[0], [1, bits - 1]] + [middle[i : i + 2] for i in range(0, len(middle), 2)]
 
     def mask(self, bits, steps):
@@ -491,26 +510,24 @@
     return lax.ppermute(value, ("replica", "tile"), [(i, i ^ mask) for i in range(plan.devices)])
 
 
-def main(place, left, here, right, conv_weight, conv_bias, words, params, plan):
-    w_latent, w_pos, bias_one, w_mid, bias_two, w_out, bias_out = params
-    rows = words.shape[0]
-    hidden = w_mid.shape[0]
-    channels = here.shape[2]
+def main(place, left, right, partial, taps, conv_bias, gathered, params, plan):
+    w_latent, w_pos, bias_one, mid_high, mid_low, bias_two, w_out, bias_out = params
+    rows = plan.tiles * plan.slots
+    hidden = mid_high.shape[0]
+    channels = left.shape[2]
     outs = jax.ShapeDtypeStruct((plan.devices // 2, plan.chunk, LANES), F32)
-    pairs = (here.shape[0] + 1) * here.shape[1] // 2
     wide = lambda kind: pltpu.VMEM((5 * rows, hidden), kind)
     return pl.pallas_call(
         functools.partial(main_kernel, plan),
         out_shape=(outs, outs),
-        in_specs=[SMEM] + [VMEM] * 12 + [SMEM],
+        in_specs=[SMEM] + [VMEM] * 13 + [SMEM],
         out_specs=(VMEM, VMEM),
         scratch_shapes=[
-            pltpu.VMEM((pairs, channels, 2 * LANES), BF16),
+            pltpu.VMEM((partial.shape[0], channels, 2 * LANES), BF16),
             pltpu.VMEM((rows, channels), BF16),
             pltpu.VMEM((rows, LANES), F32),
             pltpu.VMEM((rows, hidden), F32),
-            pltpu.VMEM((hidden, hidden), BF16),
-            pltpu.VMEM((hidden, hidden), BF16),
+            pltpu.VMEM((rows, WORDS), F32),
             wide(BF16),
             wide(BF16),
             wide(F32),
@@ -525,7 +542,7 @@
         ],
         compiler_params=pltpu.CompilerParams(vmem_limit_bytes=48 << 20),
         name="encode_decode",
-    )(place, left, here, right, conv_weight, conv_bias, words, w_latent, w_pos, bias_one, w_mid, bias_two, w_out, bias_out)
+    )(place, left, right, partial, taps, conv_bias, gathered, *params)
 
 
 def unpack_kernel(
@@ -540,7 +557,8 @@
     mid_ref,
     two_ref,
     out_ref,
-    tail_ref,
+    bias_out_ref,
+    loss_ref,
     packed,
 ):
     my_chunk = place_ref[0]
@@ -573,14 +591,25 @@
         two_ref[:, lanes] = packed[first + 4 : first + 5, :]
         out_ref[:, lanes] = packed[first + 8 : first + 13, :]
         if part == 0:
-            tail_ref[...] = packed[first + 5 : first + 6, :]
+            bias_out_ref[...] = packed[first + 5 : first + 6, 0:5]
+            loss_ref[...] = packed[first + 5 : first + 6, 5:6]
     first = (hidden // LANES) * plan.main_rows
     for f in range(5):
-        prediction_ref[0, f : f + 1, :] = packed[pl.ds(first + f * plan.devices + device, 1), :]
+        prediction_ref[f] = packed[pl.ds(first + f * plan.devices + device, 1), :]
 
 
 def unpack(place, mine, other, plan, hidden, latents):
-    shapes = [(1, 5, LANES), (latents, hidden), (3, hidden), (1, hidden), (hidden, hidden), (1, hidden), (5, hidden), (1, LANES)]
+    shapes = [
+        (5, 1, LANES),
+        (latents, hidden),
+        (3, hidden),
+        (1, hidden),
+        (hidden, hidden),
+        (1, hidden),
+        (5, hidden),
+        (1, 5),
+        (1, 1),
+    ]
     return pl.pallas_call(
         functools.partial(unpack_kernel, plan),
         out_shape=tuple(jax.ShapeDtypeStruct(shape, F32) for shape in shapes),
@@ -615,26 +644,37 @@
     channels = fields.shape[1]
     queries = query_cell.shape[1]
     hidden = w_mid.shape[0]
-    slots = 2 * queries // tiles
-    plan = Plan(tiles, replicas, queries, hidden, channels)
+    plan = Plan(tiles, replicas, queries, fields.shape[2], hidden, channels)
     device = my_replica * tiles + my_tile
     place = jnp.stack([plan.my_chunk(device), my_tile, my_replica]).astype(jnp.int32)
 
-    words = route(query_owner[:, :, 0], query_cell, query_frac[0], target[0], tiles, slots)
-    words = lax.all_to_all(
-        words.reshape(tiles, slots, WORDS), "tile", split_axis=0, concat_axis=0, tiled=True
-    ).reshape(tiles * slots, WORDS)
+    gathered = jnp.concatenate(
+        [
+            query_owner[:, :, 0].astype(F32),
+            query_cell.astype(F32),
+            query_frac[0],
+            target[0],
+            jnp.ones((1, queries), F32),
+            lax.broadcasted_iota(jnp.int32, (1, queries), 1).astype(F32),
+            jnp.zeros((4, queries), F32),
+        ],
+        axis=0,
+    )[None]
+    for bits in plan.tile_stages:
+        moved = [swapped(gathered, plan, bits, step) for step in range(1, 1 << len(bits))]
+        gathered = jnp.concatenate([gathered] + moved, axis=0)
 
     here = fields[0].transpose(1, 2, 0, 3)
     up = [(i, (i + 1) % tiles) for i in range(tiles)]
     down = [((i + 1) % tiles, i) for i in range(tiles)]
     left = lax.ppermute(here[-DILATION_RATE:], "tile", up)
     right = lax.ppermute(here[: DILATION_RATE + 1], "tile", down)
-    taps = convolution_weight.reshape(channels, 9, 3, channels)
-    taps = taps.transpose(2, 0, 1, 3).reshape(3 * channels, 9 * channels)
-
-    params = (w_latent, w_pos, bias_one[None], w_mid, bias_two[None], w_out, bias_out)
-    send, keep = main(place, left, here, right, taps, convolution_bias[:, None], words, params, plan)
+    taps = convolution_weight.reshape(channels, 3, 3, 3, channels)
+    taps = taps.transpose(1, 3, 0, 2, 4).reshape(3, 3 * channels, 3 * channels)
+    partial, mid_high, mid_low = local_part(here, taps, w_mid)
+
+    params = (w_latent, w_pos, bias_one[None], mid_high, mid_low, bias_two[None], w_out, bias_out)
+    send, keep = main(place, left, right, partial, taps, convolution_bias[:, None], gathered, params, plan)
 
     keep = keep + swapped(send, plan, plan.stages[0], 1)
     for bits in plan.stages[1:]:
@@ -648,10 +688,20 @@
         group = 1 << len(bits)
         keep = jnp.concatenate([keep] + [swapped(keep, plan, bits, step) for step in range(1, group)], axis=0)
     other = swapped(keep, plan, plan.stages[0], 1)
-    prediction, g_latent, g_pos, g_one, g_mid, g_two, g_out, tail = unpack(
+    prediction, g_latent, g_pos, g_one, g_mid, g_two, g_out, g_bias, loss = unpack(
         place, keep, other, plan, hidden, channels
     )
-    return (prediction, g_latent, g_pos, g_one[0], g_mid, g_two[0], g_out, tail[0, :5], tail[0, 5])
+    return (
+        prediction.transpose(1, 0, 2),
+        g_latent,
+        g_pos,
+        g_one.reshape(hidden),
+        g_mid,
+        g_two.reshape(hidden),
+        g_out,
+        g_bias.reshape(5),
+        loss.reshape(()),
+    )
 
 
 def solution(mesh):

time: 85.9 us -> 91.3 us (1.063)
  local copies, waits for them, and re-layouts: 9.38 us -> 12.1 us
  waiting for transfers between devices: 26.1 us -> 28.6 us
  other arithmetic: 0.22 us -> 1.57 us
    ppermute x14 -> x19, waiting for transfers between devices: 22 us -> 28.6 us  [swapped(): lax.ppermute(value, ('replica', 'tile'), [(i, i ^ mask) for i in range(pl...]
    all_to_all x1 -> x0, starting transfers between devices: 5.73 us -> none  [body(): lax.all_to_all(words.reshape(tiles, slots, WORDS), 'tile', split_axis=0,...]
    ppermute x14 -> x19, starting transfers between devices: 15.2 us -> 20.2 us  [swapped(): lax.ppermute(value, ('replica', 'tile'), [(i, i ^ mask) for i in range(pl...]
    unnamed x31 -> x33, local copies, waits for them, and re-layouts: 4.46 us -> 8.75 us
    all_to_all x1 -> x0, waiting for transfers between devices: 4.1 us -> none  [body(): lax.all_to_all(words.reshape(tiles, slots, WORDS), 'tile', split_axis=0,...]
    reshape x3 -> x2, local copies, waits for them, and re-layouts: 2.94 us -> 0.69 us  [the longest x1 0.35 us: body(): taps = taps.transpose(1, 3, 0, 2, 4).reshape(3, 3 * channels, 3 * channels)]
    convert_element_type x0 -> x3, other arithmetic: none -> 1.36 us  [the longest x1 0.7 us: body(): query_owner[:, :, 0].astype(F32)]
  transfers between devices with their start and end apart: 17 -> 21, of which waited for: 11 -> 12; matrix products, arithmetic and copies ran while one was open for 6% -> 8% of each run, Pallas kernels for 2% -> 2%
where the time goes in v1:
time: 91.3 us; the launch traced here: 91 us
  waiting for transfers between devices  28.6 us (31%)
  starting transfers between devices  25.9 us (28%)
  Pallas kernels  21.9 us (24%)
  local copies, waits for them, and re-layouts  12.1 us (13%)
  other arithmetic  1.57 us (2%)
    ppermute x19, waiting for transfers between devices, swapped(): lax.ppermute(value, ('replica', 'tile'), [(i, i ^ mask) for i in range(pl...  28.6 us
    ppermute x19, starting transfers between devices, swapped(): lax.ppermute(value, ('replica', 'tile'), [(i, i ^ mask) for i in range(pl...  20.2 us
    pallas_call x1, Pallas kernels, main(): pl.pallas_call(functools.partial(main_kernel, plan), out_shape=(outs, out...  18.5 us
    unnamed x33, local copies, waits for them, and re-layouts  8.75 us
    ppermute x1, starting transfers between devices, body(): right = lax.ppermute(here[:DILATION_RATE + 1], 'tile', down)  5.61 us
    pallas_call x1, Pallas kernels, unpack(): pl.pallas_call(functools.partial(unpack_kernel, plan), out_shape=tuple((j...  1.98 us
  transfers between devices with their start and end apart: 21, of which 12 were waited for; matrix products, arithmetic and copies ran while one was open for 8% of the time, Pallas kernels for 2%

profile of v1, /device:TPU:0, one launch (start us, length us, event | category | flops | bytes accessed | tf_op | source)
XLA Modules:
  0.0 91.0 jit_solution(11246349125352861526)
XLA Ops:
  0.7 0.7 convert_bitcast_fusion
  1.4 0.7 convert_element_type.30
  2.0 0.7 copy.36
  2.7 0.7 copy.35
  3.5 0.5 collective-permute-start.2
  4.0 1.2 %copy.34 = bf16[1,64,4,8,128]{4,1,3,2,0:T(8,128)(2,1)S(1)} copy(bf16[1,64,4,8,128]{4,3,2,1,0:T(8,128)(2,1)} %param.14) | data formatting | bytes 1048576 | tf_op args[0]
  5.3 0.7 slice.48
  6.1 0.8 slice.49
  6.8 5.6 %collective-permute-start.1 = (bf16[3,8,64,128]{3,2,1,0:T(8,128)(2,1)}, bf16[3,8,64,128]{3,2,1,0:T(8,128)(2,1)}, u32[]{:S(2)}, u32[]{:S(2)}) collective-permute-start(bf16[3,8,64,128]{3,2,1,0:T(8,128)(2,1)} %slice.49), channel_id=1, source_target_pairs={{1,0},{2,1},{3,2},{4,3},{5,4},{6,5},{7,6},{8,7},{9,8},{10,9},{11,1... | collective-permute-start | bytes 1179656 | tf_op jit(solution)/shard_map/ppermute | solution.py:671
  12.4 0.6 constant_dynamic-update-slice_fusion.5
  13.0 0.3 reshape.75
  13.4 0.3 copy.27
  13.7 0.4 reshape.76.weight_ref.conv_weight_ref
  14.0 1.2 %copy-done.7 = f32[512,512]{1,0:T(8,128)S(1)} copy-done((f32[512,512]{1,0:T(8,128)S(1)}, f32[512,512]{1,0:T(8,128)}, u32[]{:S(2)}) %copy-start.7) | copy-done | bytes 1048600
  15.3 1.4 %conv_local.1 = (f32[20,64,256]{2,1,0:T(8,128)S(1)}, bf16[512,512]{1,0:T(8,128)(2,1)S(1)}, bf16[512,512]{1,0:T(8,128)(2,1)S(1)}) custom-call(bf16[4,8,64,128]{3,2,1,0:T(8,128)(2,1)S(1)} %bitcast.29, bf16[3,192,192]{2,1,0:T(8,128)(2,1)S(1)} %reshape.76.weight_ref.conv_weight_ref, f32[512,512]{1,0:T(8,128)S(1)} %copy-done.7), custom_call_target="tpu_custom_call" | custom-call | flops 3221225472 | bytes 4194304 | tf_op jit(solution)/shard_map/conv_local/pallas_call | solution.py:110
  17.0 0.6 constant_dynamic-update-slice_fusion.4
  17.6 3.1 %collective-permute-done.3 = f32[2,16,128]{2,1,0:T(8,128)S(1)} collective-permute-done((f32[2,16,128]{2,1,0:T(8,128)S(1)}, f32[2,16,128]{2,1,0:T(8,128)S(1)}, u32[]{:S(2)}, u32[]{:S(2)}) %collective-permute-start.3) | collective-permute-done | bytes 16416 | tf_op jit(solution)/shard_map/ppermute | solution.py:510
  20.7 1.6 %collective-permute-start.6 = (f32[4,16,128]{2,1,0:T(8,128)S(1)}, f32[4,16,128]{2,1,0:T(8,128)S(1)}, u32[]{:S(2)}, u32[]{:S(2)}) collective-permute-start(f32[4,16,128]{2,1,0:T(8,128)S(1)} %pad_maximum_fusion.1), channel_id=1, source_target_pairs={{0,12},{1,13},{2,14},{3,15},{4,8},{5,9},{6,10},{7,11},{8,4},{9,5},... | collective-permute-start | bytes 98312 | tf_op jit(solution)/shard_map/ppermute | solution.py:510
  22.3 2.8 %collective-permute-start.4 = (f32[4,16,128]{2,1,0:T(8,128)S(1)}, f32[4,16,128]{2,1,0:T(8,128)S(1)}, u32[]{:S(2)}, u32[]{:S(2)}) collective-permute-start(f32[4,16,128]{2,1,0:T(8,128)S(1)} %pad_maximum_fusion.1), channel_id=1, source_target_pairs={{0,4},{1,5},{2,6},{3,7},{4,0},{5,1},{6,2},{7,3},{8,12},{9,13},{10,... | collective-permute-start | bytes 98312 | tf_op jit(solution)/shard_map/ppermute | solution.py:510
  25.1 0.6 constant_dynamic-update-slice_fusion.3
  25.7 1.6 %collective-permute-done.4 = f32[4,16,128]{2,1,0:T(8,128)S(1)} collective-permute-done((f32[4,16,128]{2,1,0:T(8,128)S(1)}, f32[4,16,128]{2,1,0:T(8,128)S(1)}, u32[]{:S(2)}, u32[]{:S(2)}) %collective-permute-start.4) | collective-permute-done | bytes 32800 | tf_op jit(solution)/shard_map/ppermute | solution.py:510
  27.3 0.6 constant_dynamic-update-slice_fusion.2
  28.0 0.6 constant_dynamic-update-slice_fusion.1
  28.6 0.6 constant_dynamic-update-slice_fusion.gathered_ref
  29.3 0.9 copy-done
  30.2 0.9 copy-done.1
  31.1 18.5 %encode_decode.1 = (f32[16,80,128]{2,1,0:T(8,128)S(1)}, f32[16,80,128]{2,1,0:T(8,128)S(1)}) custom-call(s32[3]{0:T(128)S(1)} %pad_add_fusion.place_ref, bf16[2,8,64,128]{3,2,1,0:T(8,128)(2,1)S(1)} %collective-permute-done.left_ref, bf16[3,8,64,128]{3,2,1,0:T(8,128)(2,1)} %collective-permute-done.1.right_ref, ...), custom_call_target="tpu_custom_call" | custom-call | tf_op jit(solution)/shard_map/encode_decode/pallas_call | solution.py:520
  49.6 2.1 %collective-permute-done.7 = f32[16,80,128]{2,1,0:T(8,128)S(1)} collective-permute-done((f32[16,80,128]{2,1,0:T(8,128)S(1)}, f32[16,80,128]{2,1,0:T(8,128)S(1)}, u32[]{:S(2)}, u32[]{:S(2)}) %collective-permute-start.7) | collective-permute-done | bytes 655392 | tf_op jit(solution)/shard_map/ppermute | solution.py:510
  51.8 1.0 %collective-permute-start.8 = (f32[4,80,128]{2,1,0:T(8,128)S(1)}, f32[4,80,128]{2,1,0:T(8,128)S(1)}, u32[]{:S(2)}, u32[]{:S(2)}) collective-permute-start(f32[4,80,128]{2,1,0:T(8,128)S(1)} %get-tuple-element.39), channel_id=1, source_target_pairs={{0,2},{1,3},{2,0},{3,1},{4,6},{5,7},{6,4},{7,5},{8,10},{9,11},{10,... | collective-permute-start | bytes 491528 | tf_op jit(solution)/shard_map/ppermute | solution.py:510
  52.8 2.0 %collective-permute-start.10 = (f32[4,80,128]{2,1,0:T(8,128)S(1)}, f32[4,80,128]{2,1,0:T(8,128)S(1)}, u32[]{:S(2)}, u32[]{:S(2)}) collective-permute-start(f32[4,80,128]{2,1,0:T(8,128)S(1)} %get-tuple-element.40), channel_id=1, source_target_pairs={{0,18},{1,19},{2,16},{3,17},{4,22},{5,23},{6,20},{7,21},{8,26},{9,... | collective-permute-start | bytes 491528 | tf_op jit(solution)/shard_map/ppermute | solution.py:510
  54.8 0.5 collective-permute-start.9
  55.4 6.3 %collective-permute-done.8 = f32[4,80,128]{2,1,0:T(8,128)S(1)} collective-permute-done((f32[4,80,128]{2,1,0:T(8,128)S(1)}, f32[4,80,128]{2,1,0:T(8,128)S(1)}, u32[]{:S(2)}, u32[]{:S(2)}) %collective-permute-start.8) | collective-permute-done | bytes 163872 | tf_op jit(solution)/shard_map/ppermute | solution.py:510
  61.6 1.2 %collective-permute-done.9 = f32[4,80,128]{2,1,0:T(8,128)S(1)} collective-permute-done((f32[4,80,128]{2,1,0:T(8,128)S(1)}, f32[4,80,128]{2,1,0:T(8,128)S(1)}, u32[]{:S(2)}, u32[]{:S(2)}) %collective-permute-start.9) | collective-permute-done | bytes 163872 | tf_op jit(solution)/shard_map/ppermute | solution.py:510
  62.9 1.7 %collective-permute-start.11 = (f32[1,80,128]{2,1,0:T(8,128)S(1)}, f32[1,80,128]{2,1,0:T(8,128)S(1)}, u32[]{:S(2)}, u32[]{:S(2)}) collective-permute-start(f32[1,80,128]{2,1,0:T(8,128)S(1)} %get-tuple-element.42), channel_id=1, source_target_pairs={{0,4},{1,5},{2,6},{3,7},{4,0},{5,1},{6,2},{7,3},{8,12},{9,13},{10,... | collective-permute-start | bytes 122888 | tf_op jit(solution)/shard_map/ppermute | solution.py:510
  64.7 1.7 %collective-permute-start.13 = (f32[1,80,128]{2,1,0:T(8,128)S(1)}, f32[1,80,128]{2,1,0:T(8,128)S(1)}, u32[]{:S(2)}, u32[]{:S(2)}) collective-permute-start(f32[1,80,128]{2,1,0:T(8,128)S(1)} %get-tuple-element.43), channel_id=1, source_target_pairs={{0,12},{1,13},{2,14},{3,15},{4,8},{5,9},{6,10},{7,11},{8,4},{9,5},... | collective-permute-start | bytes 122888 | tf_op jit(solution)/shard_map/ppermute | solution.py:510
  66.5 0.5 collective-permute-done.11
  67.0 3.5 %collective-permute-done.13 = f32[1,80,128]{2,1,0:T(8,128)S(1)} collective-permute-done((f32[1,80,128]{2,1,0:T(8,128)S(1)}, f32[1,80,128]{2,1,0:T(8,128)S(1)}, u32[]{:S(2)}, u32[]{:S(2)}) %collective-permute-start.13) | collective-permute-done | bytes 40992 | tf_op jit(solution)/shard_map/ppermute | solution.py:510
  70.5 0.9 collective-permute-done.12
  71.4 2.1 %collective-permute-start.16 = (f32[1,80,128]{2,1,0:T(8,128)S(1)}, f32[1,80,128]{2,1,0:T(8,128)S(1)}, u32[]{:S(2)}, u32[]{:S(2)}) collective-permute-start(f32[1,80,128]{2,1,0:T(8,128)S(1)} %get-tuple-element.38), channel_id=1, source_target_pairs={{0,12},{1,13},{2,14},{3,15},{4,8},{5,9},{6,10},{7,11},{8,4},{9,5},... | collective-permute-start | bytes 122888 | tf_op jit(solution)/shard_map/ppermute | solution.py:510
  73.5 2.3 %collective-permute-start.14 = (f32[1,80,128]{2,1,0:T(8,128)S(1)}, f32[1,80,128]{2,1,0:T(8,128)S(1)}, u32[]{:S(2)}, u32[]{:S(2)}) collective-permute-start(f32[1,80,128]{2,1,0:T(8,128)S(1)} %get-tuple-element.38), channel_id=1, source_target_pairs={{0,4},{1,5},{2,6},{3,7},{4,0},{5,1},{6,2},{7,3},{8,12},{9,13},{10,... | collective-permute-start | bytes 122888 | tf_op jit(solution)/shard_map/ppermute | solution.py:510
  75.8 1.4 %collective-permute-done.16 = f32[1,80,128]{2,1,0:T(8,128)S(1)} collective-permute-done((f32[1,80,128]{2,1,0:T(8,128)S(1)}, f32[1,80,128]{2,1,0:T(8,128)S(1)}, u32[]{:S(2)}, u32[]{:S(2)}) %collective-permute-start.16) | collective-permute-done | bytes 40992 | tf_op jit(solution)/shard_map/ppermute | solution.py:510
  77.2 1.1 %collective-permute-done.15 = f32[1,80,128]{2,1,0:T(8,128)S(1)} collective-permute-done((f32[1,80,128]{2,1,0:T(8,128)S(1)}, f32[1,80,128]{2,1,0:T(8,128)S(1)}, u32[]{:S(2)}, u32[]{:S(2)}) %collective-permute-start.15) | collective-permute-done | bytes 40992 | tf_op jit(solution)/shard_map/ppermute | solution.py:510
  78.4 2.5 %collective-permute-start.19 = (f32[4,80,128]{2,1,0:T(8,128)S(1)}, f32[4,80,128]{2,1,0:T(8,128)S(1)}, u32[]{:S(2)}, u32[]{:S(2)}) collective-permute-start(f32[4,80,128]{2,1,0:T(8,128)S(1)} %pad_maximum_fusion), channel_id=1, source_target_pairs={{0,18},{1,19},{2,16},{3,17},{4,22},{5,23},{6,20},{7,21},{8,26},{9,... | collective-permute-start | bytes 491528 | tf_op jit(solution)/shard_map/ppermute | solution.py:510
  80.9 0.5 collective-permute-start.18
  81.4 0.5 collective-permute-start.17
  82.0 4.8 %collective-permute-done.17 = f32[4,80,128]{2,1,0:T(8,128)S(1)} collective-permute-done((f32[4,80,128]{2,1,0:T(8,128)S(1)}, f32[4,80,128]{2,1,0:T(8,128)S(1)}, u32[]{:S(2)}, u32[]{:S(2)}) %collective-permute-start.17) | collective-permute-done | bytes 163872 | tf_op jit(solution)/shard_map/ppermute | solution.py:510
  86.9 2.1 %collective-permute-done.20.other_ref = f32[16,80,128]{2,1,0:T(8,128)S(1)} collective-permute-done((f32[16,80,128]{2,1,0:T(8,128)S(1)}, f32[16,80,128]{2,1,0:T(8,128)S(1)}, u32[]{:S(2)}, u32[]{:S(2)}) %collective-permute-start.20) | collective-permute-done | bytes 655392 | tf_op jit(solution)/shard_map/ppermute | solution.py:510
  89.0 2.0 %unpack.1 = (f32[5,1,128]{2,1,0:T(1,128)}, f32[64,512]{1,0:T(8,128)}, f32[3,512]{1,0:T(4,128)}, f32[1,512]{1,0:T(1,128)}, f32[512,512]{1,0:T(8,128)}, /*index=5*...) custom-call(s32[3]{0:T(128)S(1)} %pad_add_fusion.place_ref, ...), custom_call_target="tpu_custom_call" | custom-call | tf_op jit(solution)/shard_map/unpack/pallas_call | solution.py:613
  (53 shorter events, 1.0 us)
Async XLA Ops:
  0.6 12.4 %copy-start.8 = (bf16[64,1728]{1,0:T(8,128)(2,1)S(1)}, bf16[64,1728]{1,0:T(8,128)(2,1)}, u32[]{:S(2)}) copy-start(bf16[64,1728]{1,0:T(8,128)(2,1)} %param.15) | copy-start | bytes 663556
  3.5 13.4 %collective-permute-start.2 = (f32[1,16,128]{2,1,0:T(8,128)S(1)}, f32[1,16,128]{2,1,0:T(8,128)S(1)}, u32[]{:S(2)}, u32[]{:S(2)}) collective-permute-start(f32[1,16,128]{2,1,0:T(8,128)S(1)} %bitcast.33), channel_id=1, source_target_pairs={{0,1},{1,0},{2,3},{3,2},{4,5},{5,4},{6,7},{7,6},{8,9},{9,8},{10,11... | collective-permute-start | bytes 24584 | tf_op jit(solution)/shard_map/ppermute | solution.py:510
  6.0 23.2 %collective-permute-start = (bf16[2,8,64,128]{3,2,1,0:T(8,128)(2,1)}, bf16[2,8,64,128]{3,2,1,0:T(8,128)(2,1)S(1)}, u32[]{:S(2)}, u32[]{:S(2)}) collective-permute-start(bf16[2,8,64,128]{3,2,1,0:T(8,128)(2,1)} %slice.48), channel_id=1, source_target_pairs={{0,1},{1,2},{2,3},{3,4},{4,5},{5,6},{6,7},{7,8},{8,9},{9,10},{10,1... | collective-permute-start | bytes 786440 | tf_op jit(solution)/shard_map/ppermute | solution.py:670
  6.8 22.4 %collective-permute-start.1 = (bf16[3,8,64,128]{3,2,1,0:T(8,128)(2,1)}, bf16[3,8,64,128]{3,2,1,0:T(8,128)(2,1)}, u32[]{:S(2)}, u32[]{:S(2)}) collective-permute-start(bf16[3,8,64,128]{3,2,1,0:T(8,128)(2,1)} %slice.49), channel_id=1, source_target_pairs={{1,0},{2,1},{3,2},{4,3},{5,4},{6,5},{7,6},{8,7},{9,8},{10,9},{11,1... | collective-permute-start | bytes 1179656 | tf_op jit(solution)/shard_map/ppermute | solution.py:671
  14.0 1.2 %copy-start.7 = (f32[512,512]{1,0:T(8,128)S(1)}, f32[512,512]{1,0:T(8,128)}, u32[]{:S(2)}) copy-start(f32[512,512]{1,0:T(8,128)} %w_mid_ref.1) | copy-start | bytes 3145732
  15.2 1.5 %copy-start.9 = (f32[64]{0:T(128)S(1)}, f32[64]{0:T(128)}, u32[]{:S(2)}) copy-start(f32[64]{0:T(128)} %param.16) | copy-start | bytes 772
  15.2 14.0 %copy-start.2 = (f32[5,512]{1,0:T(8,128)S(1)}, f32[5,512]{1,0:T(8,128)}, u32[]{:S(2)}) copy-start(f32[5,512]{1,0:T(8,128)} %w_out_ref.1) | copy-start | bytes 30724
  15.2 14.0 %copy-start.3 = (f32[3,512]{1,0:T(4,128)S(1)}, f32[3,512]{1,0:T(4,128)}, u32[]{:S(2)}) copy-start(f32[3,512]{1,0:T(4,128)} %w_pos_ref.1) | copy-start | bytes 18436
  15.2 14.0 %copy-start.4 = (f32[512]{0:T(512)S(1)}, f32[512]{0:T(512)}, u32[]{:S(2)}) copy-start(f32[512]{0:T(512)} %param.23) | copy-start | bytes 6148
  15.2 14.0 %copy-start.5 = (f32[512]{0:T(512)S(1)}, f32[512]{0:T(512)}, u32[]{:S(2)}) copy-start(f32[512]{0:T(512)} %param.25) | copy-start | bytes 6148
  15.3 14.0 %copy-start.6 = (f32[5]{0:T(128)S(1)}, f32[5]{0:T(128)}, u32[]{:S(2)}) copy-start(f32[5]{0:T(128)} %bias_out_ref.1) | copy-start | bytes 64
  16.9 3.8 %collective-permute-start.3 = (f32[2,16,128]{2,1,0:T(8,128)S(1)}, f32[2,16,128]{2,1,0:T(8,128)S(1)}, u32[]{:S(2)}, u32[]{:S(2)}) collective-permute-start(f32[2,16,128]{2,1,0:T(8,128)S(1)} %pad_maximum_fusion.2), channel_id=1, source_target_pairs={{0,2},{1,3},{2,0},{3,1},{4,6},{5,7},{6,4},{7,5},{8,10},{9,11},{10,... | collective-permute-start | bytes 49160 | tf_op jit(solution)/shard_map/ppermute | solution.py:510
  20.7 7.9 %collective-permute-start.6 = (f32[4,16,128]{2,1,0:T(8,128)S(1)}, f32[4,16,128]{2,1,0:T(8,128)S(1)}, u32[]{:S(2)}, u32[]{:S(2)}) collective-permute-start(f32[4,16,128]{2,1,0:T(8,128)S(1)} %pad_maximum_fusion.1), channel_id=1, source_target_pairs={{0,12},{1,13},{2,14},{3,15},{4,8},{5,9},{6,10},{7,11},{8,4},{9,5},... | collective-permute-start | bytes 98312 | tf_op jit(solution)/shard_map/ppermute | solution.py:510
  22.3 5.7 %collective-permute-start.5 = (f32[4,16,128]{2,1,0:T(8,128)S(1)}, f32[4,16,128]{2,1,0:T(8,128)S(1)}, u32[]{:S(2)}, u32[]{:S(2)}) collective-permute-start(f32[4,16,128]{2,1,0:T(8,128)S(1)} %pad_maximum_fusion.1), channel_id=1, source_target_pairs={{0,8},{1,9},{2,10},{3,11},{4,12},{5,13},{6,14},{7,15},{8,0},{9,1},... | collective-permute-start | bytes 98312 | tf_op jit(solution)/shard_map/ppermute | solution.py:510
  22.3 5.0 %collective-permute-start.4 = (f32[4,16,128]{2,1,0:T(8,128)S(1)}, f32[4,16,128]{2,1,0:T(8,128)S(1)}, u32[]{:S(2)}, u32[]{:S(2)}) collective-permute-start(f32[4,16,128]{2,1,0:T(8,128)S(1)} %pad_maximum_fusion.1), channel_id=1, source_target_pairs={{0,4},{1,5},{2,6},{3,7},{4,0},{5,1},{6,2},{7,3},{8,12},{9,13},{10,... | collective-permute-start | bytes 98312 | tf_op jit(solution)/shard_map/ppermute | solution.py:510
  29.2 0.9 copy-start
  30.2 0.9 copy-start.1
  49.5 2.2 %collective-permute-start.7 = (f32[16,80,128]{2,1,0:T(8,128)S(1)}, f32[16,80,128]{2,1,0:T(8,128)S(1)}, u32[]{:S(2)}, u32[]{:S(2)}) collective-permute-start(f32[16,80,128]{2,1,0:T(8,128)S(1)} %get-tuple-element.27), channel_id=1, source_target_pairs={{0,1},{1,0},{2,3},{3,2},{4,5},{5,4},{6,7},{7,6},{8,9},{9,8},{10,11... | collective-permute-start | bytes 1966088 | tf_op jit(solution)/shard_map/ppermute | solution.py:510
  51.8 9.8 %collective-permute-start.8 = (f32[4,80,128]{2,1,0:T(8,128)S(1)}, f32[4,80,128]{2,1,0:T(8,128)S(1)}, u32[]{:S(2)}, u32[]{:S(2)}) collective-permute-start(f32[4,80,128]{2,1,0:T(8,128)S(1)} %get-tuple-element.39), channel_id=1, source_target_pairs={{0,2},{1,3},{2,0},{3,1},{4,6},{5,7},{6,4},{7,5},{8,10},{9,11},{10,... | collective-permute-start | bytes 491528 | tf_op jit(solution)/shard_map/ppermute | solution.py:510
  52.8 8.9 %collective-permute-start.10 = (f32[4,80,128]{2,1,0:T(8,128)S(1)}, f32[4,80,128]{2,1,0:T(8,128)S(1)}, u32[]{:S(2)}, u32[]{:S(2)}) collective-permute-start(f32[4,80,128]{2,1,0:T(8,128)S(1)} %get-tuple-element.40), channel_id=1, source_target_pairs={{0,18},{1,19},{2,16},{3,17},{4,22},{5,23},{6,20},{7,21},{8,26},{9,... | collective-permute-start | bytes 491528 | tf_op jit(solution)/shard_map/ppermute | solution.py:510
  54.8 8.0 %collective-permute-start.9 = (f32[4,80,128]{2,1,0:T(8,128)S(1)}, f32[4,80,128]{2,1,0:T(8,128)S(1)}, u32[]{:S(2)}, u32[]{:S(2)}) collective-permute-start(f32[4,80,128]{2,1,0:T(8,128)S(1)} %get-tuple-element.41), channel_id=1, source_target_pairs={{0,16},{1,17},{2,18},{3,19},{4,20},{5,21},{6,22},{7,23},{8,24},{9,... | collective-permute-start | bytes 491528 | tf_op jit(solution)/shard_map/ppermute | solution.py:510
  62.9 4.1 %collective-permute-start.11 = (f32[1,80,128]{2,1,0:T(8,128)S(1)}, f32[1,80,128]{2,1,0:T(8,128)S(1)}, u32[]{:S(2)}, u32[]{:S(2)}) collective-permute-start(f32[1,80,128]{2,1,0:T(8,128)S(1)} %get-tuple-element.42), channel_id=1, source_target_pairs={{0,4},{1,5},{2,6},{3,7},{4,0},{5,1},{6,2},{7,3},{8,12},{9,13},{10,... | collective-permute-start | bytes 122888 | tf_op jit(solution)/shard_map/ppermute | solution.py:510
  64.7 5.8 %collective-permute-start.13 = (f32[1,80,128]{2,1,0:T(8,128)S(1)}, f32[1,80,128]{2,1,0:T(8,128)S(1)}, u32[]{:S(2)}, u32[]{:S(2)}) collective-permute-start(f32[1,80,128]{2,1,0:T(8,128)S(1)} %get-tuple-element.43), channel_id=1, source_target_pairs={{0,12},{1,13},{2,14},{3,15},{4,8},{5,9},{6,10},{7,11},{8,4},{9,5},... | collective-permute-start | bytes 122888 | tf_op jit(solution)/shard_map/ppermute | solution.py:510
  66.3 5.0 %collective-permute-start.12 = (f32[1,80,128]{2,1,0:T(8,128)S(1)}, f32[1,80,128]{2,1,0:T(8,128)S(1)}, u32[]{:S(2)}, u32[]{:S(2)}) collective-permute-start(f32[1,80,128]{2,1,0:T(8,128)S(1)} %get-tuple-element.44), channel_id=1, source_target_pairs={{0,8},{1,9},{2,10},{3,11},{4,12},{5,13},{6,14},{7,15},{8,0},{9,1},... | collective-permute-start | bytes 122888 | tf_op jit(solution)/shard_map/ppermute | solution.py:510
  71.4 5.9 %collective-permute-start.16 = (f32[1,80,128]{2,1,0:T(8,128)S(1)}, f32[1,80,128]{2,1,0:T(8,128)S(1)}, u32[]{:S(2)}, u32[]{:S(2)}) collective-permute-start(f32[1,80,128]{2,1,0:T(8,128)S(1)} %get-tuple-element.38), channel_id=1, source_target_pairs={{0,12},{1,13},{2,14},{3,15},{4,8},{5,9},{6,10},{7,11},{8,4},{9,5},... | collective-permute-start | bytes 122888 | tf_op jit(solution)/shard_map/ppermute | solution.py:510
  73.5 4.9 %collective-permute-start.15 = (f32[1,80,128]{2,1,0:T(8,128)S(1)}, f32[1,80,128]{2,1,0:T(8,128)S(1)}, u32[]{:S(2)}, u32[]{:S(2)}) collective-permute-start(f32[1,80,128]{2,1,0:T(8,128)S(1)} %get-tuple-element.38), channel_id=1, source_target_pairs={{0,8},{1,9},{2,10},{3,11},{4,12},{5,13},{6,14},{7,15},{8,0},{9,1},... | collective-permute-start | bytes 122888 | tf_op jit(solution)/shard_map/ppermute | solution.py:510
  73.5 4.9 %collective-permute-start.14 = (f32[1,80,128]{2,1,0:T(8,128)S(1)}, f32[1,80,128]{2,1,0:T(8,128)S(1)}, u32[]{:S(2)}, u32[]{:S(2)}) collective-permute-start(f32[1,80,128]{2,1,0:T(8,128)S(1)} %get-tuple-element.38), channel_id=1, source_target_pairs={{0,4},{1,5},{2,6},{3,7},{4,0},{5,1},{6,2},{7,3},{8,12},{9,13},{10,... | collective-permute-start | bytes 122888 | tf_op jit(solution)/shard_map/ppermute | solution.py:510
  78.4 8.4 %collective-permute-start.19 = (f32[4,80,128]{2,1,0:T(8,128)S(1)}, f32[4,80,128]{2,1,0:T(8,128)S(1)}, u32[]{:S(2)}, u32[]{:S(2)}) collective-permute-start(f32[4,80,128]{2,1,0:T(8,128)S(1)} %pad_maximum_fusion), channel_id=1, source_target_pairs={{0,18},{1,19},{2,16},{3,17},{4,22},{5,23},{6,20},{7,21},{8,26},{9,... | collective-permute-start | bytes 491528 | tf_op jit(solution)/shard_map/ppermute | solution.py:510
  80.9 5.9 %collective-permute-start.18 = (f32[4,80,128]{2,1,0:T(8,128)S(1)}, f32[4,80,128]{2,1,0:T(8,128)S(1)}, u32[]{:S(2)}, u32[]{:S(2)}) collective-permute-start(f32[4,80,128]{2,1,0:T(8,128)S(1)} %pad_maximum_fusion), channel_id=1, source_target_pairs={{0,16},{1,17},{2,18},{3,19},{4,20},{5,21},{6,22},{7,23},{8,24},{9,... | collective-permute-start | bytes 491528 | tf_op jit(solution)/shard_map/ppermute | solution.py:510
  81.4 5.3 %collective-permute-start.17 = (f32[4,80,128]{2,1,0:T(8,128)S(1)}, f32[4,80,128]{2,1,0:T(8,128)S(1)}, u32[]{:S(2)}, u32[]{:S(2)}) collective-permute-start(f32[4,80,128]{2,1,0:T(8,128)S(1)} %pad_maximum_fusion), channel_id=1, source_target_pairs={{0,2},{1,3},{2,0},{3,1},{4,6},{5,7},{6,4},{7,5},{8,10},{9,11},{10,... | collective-permute-start | bytes 491528 | tf_op jit(solution)/shard_map/ppermute | solution.py:510
  86.8 2.2 %collective-permute-start.20 = (f32[16,80,128]{2,1,0:T(8,128)S(1)}, f32[16,80,128]{2,1,0:T(8,128)S(1)}, u32[]{:S(2)}, u32[]{:S(2)}) collective-permute-start(f32[16,80,128]{2,1,0:T(8,128)S(1)} %constant_dynamic-update-slice_fusion.6.mine_ref), channel_id=1, source_target_pairs={{0,1},{1,0},{2,3},{3,2},{4,5},{5,4},{6,7},{7,6},{8,9},{9,8},{10,11... | collective-permute-start | bytes 1966088 | tf_op jit(solution)/shard_map/ppermute | solution.py:510

commit v2 on v1

--- a/solution.py
+++ b/solution.py
@@ -45,25 +45,39 @@
     return mul(left[0], right[0], dims) + mul(left[0], right[1], dims) + mul(left[1], right[0], dims)
 
 
-def select(gathered_ref, my_tile, slots, words_ref):
-    tiles, kinds, queries = gathered_ref.shape
-    owner = jnp.concatenate([gathered_ref[r, 0:1, :] for r in range(tiles)], axis=0)
-    hits = jnp.where(owner == my_tile.astype(F32), 1.0, 0.0)
+def route_kernel(tiles, slots, owner_ref, cell_ref, frac_ref, target_ref, out_ref, words):
+    queries = owner_ref.shape[1]
+    owner = owner_ref[...]
+    hits = (lax.broadcasted_iota(jnp.int32, (tiles, queries), 0) == owner).astype(F32)
     before = lax.broadcasted_iota(jnp.int32, (queries, queries), 0) < lax.broadcasted_iota(
         jnp.int32, (queries, queries), 1
     )
-    earlier = mul(hits.astype(BF16), jnp.where(before, 1.0, 0.0).astype(BF16))
-    place = jnp.where(hits > 0.0, earlier, -1.0)
-    slot = lax.broadcasted_iota(jnp.int32, (slots, queries), 0).astype(F32)
-    chosen = jnp.concatenate([jnp.where(slot == place[r : r + 1, :], 1.0, 0.0) for r in range(tiles)], axis=0)
-    chosen = chosen.astype(BF16)
-    high, middle, low = thirds(gathered_ref[...].reshape(tiles * kinds, queries))
-    picked = mul(chosen, high, NT) + mul(chosen, middle, NT) + mul(chosen, low, NT)
-    words_ref[...] = jnp.zeros_like(words_ref)
-    for r in range(tiles):
-        words_ref[r * slots : (r + 1) * slots, 0:kinds] = picked[
-            r * slots : (r + 1) * slots, r * kinds : (r + 1) * kinds
-        ]
+    earlier = mul(hits.astype(BF16), before.astype(F32).astype(BF16))
+    slot = jnp.sum(hits * earlier, axis=0, keepdims=True)
+    place = owner * slots + slot.astype(jnp.int32)
+    chosen = (lax.broadcasted_iota(jnp.int32, (tiles * slots, queries), 0) == place).astype(F32).astype(BF16)
+    words[...] = jnp.zeros_like(words)
+    words[0:1, :] = cell_ref[...].astype(F32)
+    for d in range(3):
+        words[1 + d : 2 + d, :] = frac_ref[d]
+    for f in range(5):
+        words[4 + f : 5 + f, :] = target_ref[f]
+    words[9:10, :] = jnp.ones((1, queries), F32)
+    words[10:11, :] = lax.broadcasted_iota(jnp.int32, (1, queries), 1).astype(F32)
+    high, middle, low = thirds(words[...])
+    out_ref[...] = mul(chosen, high, NT) + mul(chosen, middle, NT) + mul(chosen, low, NT)
+
+
+def route(owner, cell, frac, target, tiles, slots):
+    queries = owner.shape[1]
+    return pl.pallas_call(
+        functools.partial(route_kernel, tiles, slots),
+        out_shape=jax.ShapeDtypeStruct((tiles * slots, WORDS), F32),
+        in_specs=[VMEM] * 4,
+        out_specs=VMEM,
+        scratch_shapes=[pltpu.VMEM((WORDS, queries), F32)],
+        name="route",
+    )(owner, cell, frac, target)
 
 
 def tap_sum(weight_ref, planes, pair):
@@ -88,8 +102,26 @@
     return jnp.concatenate(sides, axis=1)
 
 
-def local_kernel(here_ref, weight_ref, w_mid_ref, partial_ref, high_ref, low_ref):
+def local_kernel(
+    here_ref,
+    weight_ref,
+    bias_ref,
+    w_latent_ref,
+    w_pos_ref,
+    bias_one_ref,
+    w_mid_ref,
+    bias_two_ref,
+    w_out_ref,
+    bias_out_ref,
+    partial_ref,
+    latent_high_ref,
+    latent_low_ref,
+    mid_high_ref,
+    mid_low_ref,
+    small_ref,
+):
     planes, rows_y = here_ref.shape[0], here_ref.shape[1]
+    bias = bias_ref[...]
     for x in range(planes + 1):
         taps = [
             (step, here_ref, x + DILATION_RATE * (step - 1))
@@ -97,30 +129,45 @@
             if 0 <= x + DILATION_RATE * (step - 1) < planes
         ]
         for pair in range(rows_y // 2):
-            partial_ref[x * (rows_y // 2) + pair] = tap_sum(weight_ref, taps, pair)
-    high, low = halves(w_mid_ref[...])
-    high_ref[...] = high
-    low_ref[...] = low
-
-
-def local_part(here, taps, w_mid):
+            partial_ref[x * (rows_y // 2) + pair] = tap_sum(weight_ref, taps, pair) + bias
+    for source, high_ref, low_ref in (
+        (w_latent_ref, latent_high_ref, latent_low_ref),
+        (w_mid_ref, mid_high_ref, mid_low_ref),
+    ):
+        high, low = halves(source[...])
+        high_ref[...] = high
+        low_ref[...] = low
+    small_ref[...] = jnp.zeros_like(small_ref)
+    small_ref[0:3, :] = w_pos_ref[...]
+    small_ref[3:4, :] = bias_one_ref[...]
+    small_ref[4:5, :] = bias_two_ref[...]
+    small_ref[5:6, 0:5] = bias_out_ref[...]
+    small_ref[8:13, :] = w_out_ref[...]
+
+
+def local_part(here, taps, conv_bias, params):
+    w_latent, w_mid = params[0], params[3]
     planes, rows_y, channels, rows_z = here.shape
     pairs = (planes + 1) * rows_y // 2
-    split = jax.ShapeDtypeStruct(w_mid.shape, BF16)
+    split = lambda array: [jax.ShapeDtypeStruct(array.shape, BF16)] * 2
     return pl.pallas_call(
         local_kernel,
-        out_shape=(jax.ShapeDtypeStruct((pairs, channels, 2 * rows_z), F32), split, split),
-        in_specs=[VMEM] * 3,
-        out_specs=(VMEM, VMEM, VMEM),
+        out_shape=tuple(
+            [jax.ShapeDtypeStruct((pairs, channels, 2 * rows_z), F32)]
+            + split(w_latent)
+            + split(w_mid)
+            + [jax.ShapeDtypeStruct((16, w_mid.shape[0]), F32)]
+        ),
+        in_specs=[VMEM] * 10,
+        out_specs=tuple([VMEM] * 6),
         compiler_params=pltpu.CompilerParams(vmem_limit_bytes=16 << 20),
         cost_estimate=pl.CostEstimate(flops=3 << 30, bytes_accessed=4 << 20, transcendentals=0),
         name="conv_local",
-    )(here, taps, w_mid)
-
-
-def finish_latent(left_ref, right_ref, partial_ref, weight_ref, bias_ref, planes, lat):
+    )(here, taps, conv_bias, *params)
+
+
+def finish_latent(left_ref, right_ref, partial_ref, weight_ref, planes, lat):
     rows_y = left_ref.shape[1]
-    bias = bias_ref[...]
     for x in range(planes + 1):
         taps = []
         for step in range(3):
@@ -131,14 +178,14 @@
                 taps.append((step, right_ref, plane - planes))
         for pair in range(rows_y // 2):
             number = x * (rows_y // 2) + pair
-            summed = partial_ref[number] + tap_sum(weight_ref, taps, pair) + bias
+            summed = partial_ref[number] + tap_sum(weight_ref, taps, pair)
             lat[number] = jax.nn.gelu(summed).astype(BF16)
 
 
 def interpolate(words, lat, planes, rows_y, rows_z):
     rows = words.shape[0]
-    cell = jnp.broadcast_to(words[:, 1:2], (rows, LANES)).astype(jnp.int32)
-    frac = [jnp.broadcast_to(words[:, 2 + d : 3 + d], (rows, LANES)) for d in range(3)]
+    cell = jnp.broadcast_to(words[:, 0:1], (rows, LANES)).astype(jnp.int32)
+    frac = [jnp.broadcast_to(words[:, 1 + d : 2 + d], (rows, LANES)) for d in range(3)]
     shift_z = rows_z.bit_length() - 1
     shift_y = rows_y.bit_length() - 1
     base_x = cell >> (shift_z + shift_y)
@@ -174,23 +221,18 @@
     right_ref,
     partial_ref,
     conv_weight_ref,
-    conv_bias_ref,
-    gathered_ref,
-    w_latent_ref,
-    w_pos_ref,
-    bias_one_ref,
+    words_ref,
+    latent_high,
+    latent_low,
     mid_high,
     mid_low,
-    bias_two_ref,
-    w_out_ref,
-    bias_out_ref,
+    small_ref,
     send_ref,
     keep_ref,
     lat,
     code,
     pos,
     z_one,
-    words_ref,
     one_high,
     one_low,
     mixed,
@@ -205,15 +247,14 @@
 ):
     rows = plan.tiles * plan.slots
     hidden = mid_high.shape[0]
-    latents = w_latent_ref.shape[0]
+    latents = latent_high.shape[0]
     planes, rows_y, rows_z = plan.planes, left_ref.shape[1], left_ref.shape[3]
     slots = rows // plan.tiles
     my_chunk = place_ref[0]
     my_tile = place_ref[1]
     my_replica = place_ref[2]
 
-    select(gathered_ref, my_tile, slots, words_ref)
-    finish_latent(left_ref, right_ref, partial_ref, conv_weight_ref, conv_bias_ref, planes, lat)
+    finish_latent(left_ref, right_ref, partial_ref, conv_weight_ref, planes, lat)
     words = words_ref[...]
     interp, base_x, base_y, base_z, frac = interpolate(words, lat, planes, rows_y, rows_z)
     code[...] = interp
@@ -229,12 +270,11 @@
         ),
     )
 
-    wl_high, wl_low = halves(w_latent_ref[...])
-    z_one[...] = mul(interp, wl_high) + mul(interp, wl_low)
-    w_pos = [w_pos_ref[d : d + 1, :] for d in range(3)]
+    z_one[...] = mul(interp, latent_high[...]) + mul(interp, latent_low[...])
+    w_pos = [small_ref[d : d + 1, :] for d in range(3)]
     square = w_pos[0] * w_pos[0] + w_pos[1] * w_pos[1] + w_pos[2] * w_pos[2]
-    bias_one = bias_one_ref[...]
-    bias_two = bias_two_ref[...]
+    bias_one = small_ref[3:4, :]
+    bias_two = small_ref[4:5, :]
 
     def store(index, block, refs, value):
         high, low = halves(value)
@@ -288,7 +328,7 @@
 
     lax.fori_loop(0, rows // BLOCK, layer_two, 0)
 
-    out_fields = jnp.concatenate([w_out_ref[...], jnp.zeros((3, hidden), F32)], axis=0)
+    out_fields = small_ref[8:16, :]
     wo_high, wo_low = halves(out_fields)
     wo_both = jnp.concatenate([out_fields, wo_low.astype(F32)], axis=0).astype(BF16)
     for s in range(5):
@@ -297,9 +337,9 @@
         out_t[8 * s : 8 * s + 8, :] = both[:8] + both[8:] + mul(wo_high, two_low[span, :], NT)
 
     words_t = words.T
-    target = [words_t[5 + f : 6 + f, :] for f in range(5)]
-    valid = words_t[10:11, :]
-    value = [out_t[f : f + 1, :] + bias_out_ref[f] for f in range(5)]
+    target = [words_t[4 + f : 5 + f, :] for f in range(5)]
+    valid = words_t[9:10, :]
+    value = [out_t[f : f + 1, :] + small_ref[5:6, f : f + 1] for f in range(5)]
     grad = [[out_t[8 * (d + 1) + f : 8 * (d + 1) + f + 1, :] for f in range(5)] for d in range(3)]
     laplace = [out_t[32 + f : 33 + f, :] for f in range(5)]
     velocity = value[2:5]
@@ -453,11 +493,11 @@
         packed[first + 8 : first + 16, :] = grad_out[:, lanes]
 
     chosen = jnp.where(
-        lane == jnp.broadcast_to(words[:, 11:12], (rows, LANES)).astype(jnp.int32), words[:, 10:11], 0.0
+        lane == jnp.broadcast_to(words[:, 10:11], (rows, LANES)).astype(jnp.int32), words[:, 9:10], 0.0
     ).astype(BF16)
     source = lax.broadcasted_iota(jnp.int32, (plan.tiles, rows), 0)
     inside = lax.broadcasted_iota(jnp.int32, (plan.tiles, rows), 1)
-    mine = jnp.bitwise_xor(inside >> (slots.bit_length() - 1), my_tile) == source
+    mine = (inside >> (slots.bit_length() - 1)) == source
     for f in range(5):
         high, middle, low = thirds(jnp.where(mine, jnp.broadcast_to(value[f], (plan.tiles, rows)), 0.0))
         first = pl.multiple_of((hidden // LANES) * main_rows + f * plan.devices + my_replica * plan.tiles, 16)
@@ -489,9 +529,6 @@
         self.chunk = -(-needed // (8 * self.devices)) * 8
         bits = self.devices.bit_length() - 1
         middle = list(range(2, bits - 1))
-        along = list(range(1, tiles.bit_length() - 1))
-        odd = len(along) % 2
-        self.tile_stages = [[0]] + [along[:1]] * odd + [along[i : i + 2] for i in range(odd, len(along), 2)]
         self.stages = [[0], [1, bits - 1]] + [middle[i : i + 2] for i in range(0, len(middle), 2)]
 
     def mask(self, bits, steps):
@@ -510,24 +547,22 @@
     return lax.ppermute(value, ("replica", "tile"), [(i, i ^ mask) for i in range(plan.devices)])
 
 
-def main(place, left, right, partial, taps, conv_bias, gathered, params, plan):
-    w_latent, w_pos, bias_one, mid_high, mid_low, bias_two, w_out, bias_out = params
+def main(place, left, right, partial, taps, words, weights, plan):
     rows = plan.tiles * plan.slots
-    hidden = mid_high.shape[0]
+    hidden = weights[-1].shape[1]
     channels = left.shape[2]
     outs = jax.ShapeDtypeStruct((plan.devices // 2, plan.chunk, LANES), F32)
     wide = lambda kind: pltpu.VMEM((5 * rows, hidden), kind)
     return pl.pallas_call(
         functools.partial(main_kernel, plan),
         out_shape=(outs, outs),
-        in_specs=[SMEM] + [VMEM] * 13 + [SMEM],
+        in_specs=[SMEM] + [VMEM] * 10,
         out_specs=(VMEM, VMEM),
         scratch_shapes=[
             pltpu.VMEM((partial.shape[0], channels, 2 * LANES), BF16),
             pltpu.VMEM((rows, channels), BF16),
             pltpu.VMEM((rows, LANES), F32),
             pltpu.VMEM((rows, hidden), F32),
-            pltpu.VMEM((rows, WORDS), F32),
             wide(BF16),
             wide(BF16),
             wide(F32),
@@ -542,7 +577,7 @@
         ],
         compiler_params=pltpu.CompilerParams(vmem_limit_bytes=48 << 20),
         name="encode_decode",
-    )(place, left, right, partial, taps, conv_bias, gathered, *params)
+    )(place, left, right, partial, taps, words, *weights)
 
 
 def unpack_kernel(
@@ -648,21 +683,18 @@
     device = my_replica * tiles + my_tile
     place = jnp.stack([plan.my_chunk(device), my_tile, my_replica]).astype(jnp.int32)
 
-    gathered = jnp.concatenate(
-        [
-            query_owner[:, :, 0].astype(F32),
-            query_cell.astype(F32),
-            query_frac[0],
-            target[0],
-            jnp.ones((1, queries), F32),
-            lax.broadcasted_iota(jnp.int32, (1, queries), 1).astype(F32),
-            jnp.zeros((4, queries), F32),
-        ],
-        axis=0,
-    )[None]
-    for bits in plan.tile_stages:
-        moved = [swapped(gathered, plan, bits, step) for step in range(1, 1 << len(bits))]
-        gathered = jnp.concatenate([gathered] + moved, axis=0)
+    words = route(
+        query_owner[:, :, 0],
+        query_cell,
+        query_frac.transpose(1, 0, 2),
+        target.transpose(1, 0, 2),
+        tiles,
+        plan.slots,
+    )
+    words, fields = lax.optimization_barrier((words, fields))
+    words = lax.all_to_all(
+        words.reshape(tiles, plan.slots, WORDS), "tile", split_axis=0, concat_axis=0, tiled=True
+    ).reshape(tiles * plan.slots, WORDS)
 
     here = fields[0].transpose(1, 2, 0, 3)
     up = [(i, (i + 1) % tiles) for i in range(tiles)]
@@ -671,10 +703,9 @@
     right = lax.ppermute(here[: DILATION_RATE + 1], "tile", down)
     taps = convolution_weight.reshape(channels, 3, 3, 3, channels)
     taps = taps.transpose(1, 3, 0, 2, 4).reshape(3, 3 * channels, 3 * channels)
-    partial, mid_high, mid_low = local_part(here, taps, w_mid)
-
-    params = (w_latent, w_pos, bias_one[None], mid_high, mid_low, bias_two[None], w_out, bias_out)
-    send, keep = main(place, left, right, partial, taps, convolution_bias[:, None], gathered, params, plan)
+    params = (w_latent, w_pos, bias_one[None], w_mid, bias_two[None], w_out, bias_out[None])
+    partial, *weights = local_part(here, taps, convolution_bias[:, None], params)
+    send, keep = main(place, left, right, partial, taps, words, weights, plan)
 
     keep = keep + swapped(send, plan, plan.stages[0], 1)
     for bits in plan.stages[1:]:

time: 91.3 us -> 84 us (0.920)
  local copies, waits for them, and re-layouts: 12.1 us -> 6.04 us
  waiting for transfers between devices: 28.6 us -> 23.6 us
  starting transfers between devices: 25.9 us -> 29.3 us
  Pallas kernels: 21.9 us -> 23.7 us
  other arithmetic: 1.57 us -> 0.22 us
    all_to_all x0 -> x1, starting transfers between devices: none -> 7.52 us  [body(): lax.all_to_all(words.reshape(tiles, plan.slots, WORDS), 'tile', split_axi...]
    unnamed x33 -> x23, local copies, waits for them, and re-layouts: 8.75 us -> 2.2 us
    ppermute x19 -> x14, waiting for transfers between devices: 28.6 us -> 22.8 us  [swapped(): lax.ppermute(value, ('replica', 'tile'), [(i, i ^ mask) for i in range(pl...]
    ppermute x19 -> x14, starting transfers between devices: 20.2 us -> 17.3 us  [swapped(): lax.ppermute(value, ('replica', 'tile'), [(i, i ^ mask) for i in range(pl...]
    pallas_call x1 -> x2, Pallas kernels: 1.42 us -> 3.21 us  [the longest x1 1.72 us: route(): pl.pallas_call(functools.partial(route_kernel, tiles, slots), out_shape=j...]
    ppermute x1, starting transfers between devices: 5.61 us -> 4.04 us  [body(): right = lax.ppermute(here[:DILATION_RATE + 1], 'tile', down)]
    convert_element_type x3 -> x0, other arithmetic: 1.36 us -> none  [the longest x1 0.7 us: body(): query_owner[:, :, 0].astype(F32)]
    optimization_barrier x0 -> x1, local copies, waits for them, and re-layouts: none -> 1.25 us  [body(): words, fields = lax.optimization_barrier((words, fields))]
  transfers between devices with their start and end apart: 21 -> 17, of which waited for: 12 -> 11; matrix products, arithmetic and copies ran while one was open for 8% -> 5% of each run, Pallas kernels for 2% -> 2%
where the time goes in v2:
time: 84 us; the launch traced here: 83.7 us
  starting transfers between devices  29.3 us (35%)
  Pallas kernels  23.7 us (28%)
  waiting for transfers between devices  23.6 us (28%)
  local copies, waits for them, and re-layouts  6.04 us (7%)
  between operations  0.87 us (1%)
    ppermute x14, waiting for transfers between devices, swapped(): lax.ppermute(value, ('replica', 'tile'), [(i, i ^ mask) for i in range(pl...  22.8 us
    pallas_call x1, Pallas kernels, main(): pl.pallas_call(functools.partial(main_kernel, plan), out_shape=(outs, out...  18.5 us
    ppermute x14, starting transfers between devices, swapped(): lax.ppermute(value, ('replica', 'tile'), [(i, i ^ mask) for i in range(pl...  17.3 us
    all_to_all x1, starting transfers between devices, body(): lax.all_to_all(words.reshape(tiles, plan.slots, WORDS), 'tile', split_axi...  7.52 us
    ppermute x1, starting transfers between devices, body(): right = lax.ppermute(here[:DILATION_RATE + 1], 'tile', down)  4.04 us
    unnamed x23, local copies, waits for them, and re-layouts  2.2 us
    pallas_call x1, Pallas kernels, unpack(): pl.pallas_call(functools.partial(unpack_kernel, plan), out_shape=tuple((j...  1.98 us
    pallas_call x1, Pallas kernels, route(): pl.pallas_call(functools.partial(route_kernel, tiles, slots), out_shape=j...  1.72 us
  transfers between devices with their start and end apart: 17, of which 11 were waited for; matrix products, arithmetic and copies ran while one was open for 5% of the time, Pallas kernels for 2%

profile of v2, /device:TPU:0, one launch (start us, length us, event | category | flops | bytes accessed | tf_op | source)
XLA Modules:
  0.0 83.7 jit_solution(6446605600689014347)
XLA Ops:
  0.6 1.7 %route.1 = f32[256,128]{1,0:T(8,128)} custom-call(s32[1,128]{1,0:T(1,128)} %bitcast.34, s32[1,128]{1,0:T(1,128)} %cell_ref.1, f32[3,1,128]{2,1,0:T(1,128)} %bitcast.33, f32[5,1,128]{2,1,0:T(1,128)} %bitcast.32), custom_call_target="tpu_custom_call" | custom-call | tf_op jit(solution)/shard_map/route/pallas_call | solution.py:73
  2.4 7.5 %all-to-all-start = ((f32[16,16,128]{2,1,0:T(8,128)}), f32[16,16,128]{2,1,0:T(8,128)S(1)}, u32[]{:S(2)}, u32[]{:S(2)}) async-start(f32[16,16,128]{2,1,0:T(8,128)} %bitcast.31), calls=%async_computation | async-start | bytes 262144 | tf_op jit(solution)/shard_map/all_to_all | solution.py:695
  9.9 1.2 %copy.30 = bf16[1,64,4,8,128]{4,1,3,2,0:T(8,128)(2,1)S(1)} copy(bf16[1,64,4,8,128]{4,3,2,1,0:T(8,128)(2,1)} %param.14) | data formatting | bytes 1048576 | tf_op jit(solution)/shard_map/optimization_barrier | solution.py:694
  11.1 0.7 slice.48
  11.9 0.4 collective-permute-start
  12.3 0.8 slice.49
  13.0 4.0 %collective-permute-start.1 = (bf16[3,8,64,128]{3,2,1,0:T(8,128)(2,1)}, bf16[3,8,64,128]{3,2,1,0:T(8,128)(2,1)}, u32[]{:S(2)}, u32[]{:S(2)}) collective-permute-start(bf16[3,8,64,128]{3,2,1,0:T(8,128)(2,1)} %slice.49), channel_id=1, source_target_pairs={{1,0},{2,1},{3,2},{4,3},{5,4},{6,5},{7,6},{8,7},{9,8},{10,9},{11,1... | collective-permute-start | bytes 1179656 | tf_op jit(solution)/shard_map/ppermute | solution.py:703
  17.1 0.1 copy.28.bias_ref
  17.2 0.0 copy-start.3
  17.2 0.0 copy-start.4
  17.2 0.0 copy-start.5
  17.2 0.0 copy-start.6
  17.2 0.3 reshape.60
  17.6 0.3 copy.27
  17.9 0.4 reshape.61.weight_ref.conv_weight_ref
  18.2 0.1 pad_add_fusion.place_ref
  18.3 0.0 copy-start
  18.3 1.2 %copy-done = f32[512,512]{1,0:T(8,128)S(1)} copy-done((f32[512,512]{1,0:T(8,128)S(1)}, f32[512,512]{1,0:T(8,128)}, u32[]{:S(2)}) %copy-start) | copy-done | bytes 1048600
  19.6 0.9 %copy-done.1 = f32[64,512]{1,0:T(8,128)S(1)} copy-done((f32[64,512]{1,0:T(8,128)S(1)}, f32[64,512]{1,0:T(8,128)}, u32[]{:S(2)}) %copy-start.1) | copy-done | bytes 131096
  20.5 1.5 %conv_local.1 = (f32[20,64,256]{2,1,0:T(8,128)S(1)}, bf16[64,512]{1,0:T(8,128)(2,1)S(1)}, bf16[64,512]{1,0:T(8,128)(2,1)S(1)}, bf16[512,512]{1,0:T(8,128)(2,1)S(...) custom-call(bf16[4,8,64,128]{3,2,1,0:T(8,128)(2,1)S(1)} %bitcast.25, ...), custom_call_target="tpu_custom_call" | custom-call | flops 3221225472 | bytes 4194304 | tf_op jit(solution)/shard_map/conv_local/pallas_call | solution.py:153
  22.0 0.7 collective-permute-done.1.right_ref
  22.7 18.5 %encode_decode.1 = (f32[16,80,128]{2,1,0:T(8,128)S(1)}, f32[16,80,128]{2,1,0:T(8,128)S(1)}) custom-call(s32[3]{0:T(128)S(1)} %pad_add_fusion.place_ref, bf16[2,8,64,128]{3,2,1,0:T(8,128)(2,1)} %collective-permute-done.left_ref, bf16[3,8,64,128]{3,2,1,0:T(8,128)(2,1)} %collective-permute-done.1.right_ref, f32[20,64,256]{2,1,0:T(8,128)S(1)} %get-tuple-element.29.partial_ref, ...), custom_call_target="tpu_custom_call" | custom-call | tf_op jit(solution)/shard_map/encode_decode/pallas_call | solution.py:556
  41.2 2.1 %collective-permute-start.2 = (f32[16,80,128]{2,1,0:T(8,128)S(1)}, f32[16,80,128]{2,1,0:T(8,128)S(1)}, u32[]{:S(2)}, u32[]{:S(2)}) collective-permute-start(f32[16,80,128]{2,1,0:T(8,128)S(1)} %get-tuple-element.37), channel_id=1, source_target_pairs={{0,1},{1,0},{2,3},{3,2},{4,5},{5,4},{6,7},{7,6},{8,9},{9,8},{10,11... | collective-permute-start | bytes 1966088 | tf_op jit(solution)/shard_map/ppermute | solution.py:547
  43.3 1.7 %collective-permute-done.2 = f32[16,80,128]{2,1,0:T(8,128)S(1)} collective-permute-done((f32[16,80,128]{2,1,0:T(8,128)S(1)}, f32[16,80,128]{2,1,0:T(8,128)S(1)}, u32[]{:S(2)}, u32[]{:S(2)}) %collective-permute-start.2) | collective-permute-done | bytes 655392 | tf_op jit(solution)/shard_map/ppermute | solution.py:547
  45.0 0.1 add.41
  45.2 0.2 collective-permute-start.3
  45.3 2.9 %collective-permute-start.5 = (f32[4,80,128]{2,1,0:T(8,128)S(1)}, f32[4,80,128]{2,1,0:T(8,128)S(1)}, u32[]{:S(2)}, u32[]{:S(2)}) collective-permute-start(f32[4,80,128]{2,1,0:T(8,128)S(1)} %get-tuple-element.50), channel_id=1, source_target_pairs={{0,18},{1,19},{2,16},{3,17},{4,22},{5,23},{6,20},{7,21},{8,26},{9,... | collective-permute-start | bytes 491528 | tf_op jit(solution)/shard_map/ppermute | solution.py:547
  48.2 0.5 collective-permute-start.4
  48.7 6.5 %collective-permute-done.3 = f32[4,80,128]{2,1,0:T(8,128)S(1)} collective-permute-done((f32[4,80,128]{2,1,0:T(8,128)S(1)}, f32[4,80,128]{2,1,0:T(8,128)S(1)}, u32[]{:S(2)}, u32[]{:S(2)}) %collective-permute-start.3) | collective-permute-done | bytes 163872 | tf_op jit(solution)/shard_map/ppermute | solution.py:547
  55.2 1.2 %collective-permute-done.4 = f32[4,80,128]{2,1,0:T(8,128)S(1)} collective-permute-done((f32[4,80,128]{2,1,0:T(8,128)S(1)}, f32[4,80,128]{2,1,0:T(8,128)S(1)}, u32[]{:S(2)}, u32[]{:S(2)}) %collective-permute-start.4) | collective-permute-done | bytes 163872 | tf_op jit(solution)/shard_map/ppermute | solution.py:547
  56.5 0.2 collective-permute-start.6
  56.7 2.3 %collective-permute-start.8 = (f32[1,80,128]{2,1,0:T(8,128)S(1)}, f32[1,80,128]{2,1,0:T(8,128)S(1)}, u32[]{:S(2)}, u32[]{:S(2)}) collective-permute-start(f32[1,80,128]{2,1,0:T(8,128)S(1)} %get-tuple-element.53), channel_id=1, source_target_pairs={{0,12},{1,13},{2,14},{3,15},{4,8},{5,9},{6,10},{7,11},{8,4},{9,5},... | collective-permute-start | bytes 122888 | tf_op jit(solution)/shard_map/ppermute | solution.py:547
  59.0 1.1 %collective-permute-start.7 = (f32[1,80,128]{2,1,0:T(8,128)S(1)}, f32[1,80,128]{2,1,0:T(8,128)S(1)}, u32[]{:S(2)}, u32[]{:S(2)}) collective-permute-start(f32[1,80,128]{2,1,0:T(8,128)S(1)} %get-tuple-element.54), channel_id=1, source_target_pairs={{0,8},{1,9},{2,10},{3,11},{4,12},{5,13},{6,14},{7,15},{8,0},{9,1},... | collective-permute-start | bytes 122888 | tf_op jit(solution)/shard_map/ppermute | solution.py:547
  60.1 1.0 %collective-permute-done.6 = f32[1,80,128]{2,1,0:T(8,128)S(1)} collective-permute-done((f32[1,80,128]{2,1,0:T(8,128)S(1)}, f32[1,80,128]{2,1,0:T(8,128)S(1)}, u32[]{:S(2)}, u32[]{:S(2)}) %collective-permute-start.6) | collective-permute-done | bytes 40992 | tf_op jit(solution)/shard_map/ppermute | solution.py:547
  61.0 1.5 %collective-permute-done.8 = f32[1,80,128]{2,1,0:T(8,128)S(1)} collective-permute-done((f32[1,80,128]{2,1,0:T(8,128)S(1)}, f32[1,80,128]{2,1,0:T(8,128)S(1)}, u32[]{:S(2)}, u32[]{:S(2)}) %collective-permute-start.8) | collective-permute-done | bytes 40992 | tf_op jit(solution)/shard_map/ppermute | solution.py:547
  62.5 2.0 %collective-permute-done.7 = f32[1,80,128]{2,1,0:T(8,128)S(1)} collective-permute-done((f32[1,80,128]{2,1,0:T(8,128)S(1)}, f32[1,80,128]{2,1,0:T(8,128)S(1)}, u32[]{:S(2)}, u32[]{:S(2)}) %collective-permute-start.7) | collective-permute-done | bytes 40992 | tf_op jit(solution)/shard_map/ppermute | solution.py:547
  64.6 1.0 %collective-permute-start.11 = (f32[1,80,128]{2,1,0:T(8,128)S(1)}, f32[1,80,128]{2,1,0:T(8,128)S(1)}, u32[]{:S(2)}, u32[]{:S(2)}) collective-permute-start(f32[1,80,128]{2,1,0:T(8,128)S(1)} %get-tuple-element.48), channel_id=1, source_target_pairs={{0,12},{1,13},{2,14},{3,15},{4,8},{5,9},{6,10},{7,11},{8,4},{9,5},... | collective-permute-start | bytes 122888 | tf_op jit(solution)/shard_map/ppermute | solution.py:547
  65.5 0.5 collective-permute-start.10
  66.1 2.9 %collective-permute-start.9 = (f32[1,80,128]{2,1,0:T(8,128)S(1)}, f32[1,80,128]{2,1,0:T(8,128)S(1)}, u32[]{:S(2)}, u32[]{:S(2)}) collective-permute-start(f32[1,80,128]{2,1,0:T(8,128)S(1)} %get-tuple-element.48), channel_id=1, source_target_pairs={{0,4},{1,5},{2,6},{3,7},{4,0},{5,1},{6,2},{7,3},{8,12},{9,13},{10,... | collective-permute-start | bytes 122888 | tf_op jit(solution)/shard_map/ppermute | solution.py:547
  69.0 1.5 %collective-permute-done.11 = f32[1,80,128]{2,1,0:T(8,128)S(1)} collective-permute-done((f32[1,80,128]{2,1,0:T(8,128)S(1)}, f32[1,80,128]{2,1,0:T(8,128)S(1)}, u32[]{:S(2)}, u32[]{:S(2)}) %collective-permute-start.11) | collective-permute-done | bytes 40992 | tf_op jit(solution)/shard_map/ppermute | solution.py:547
  70.5 0.9 %collective-permute-done.10 = f32[1,80,128]{2,1,0:T(8,128)S(1)} collective-permute-done((f32[1,80,128]{2,1,0:T(8,128)S(1)}, f32[1,80,128]{2,1,0:T(8,128)S(1)}, u32[]{:S(2)}, u32[]{:S(2)}) %collective-permute-start.10) | collective-permute-done | bytes 40992 | tf_op jit(solution)/shard_map/ppermute | solution.py:547
  71.4 1.7 %collective-permute-start.14 = (f32[4,80,128]{2,1,0:T(8,128)S(1)}, f32[4,80,128]{2,1,0:T(8,128)S(1)}, u32[]{:S(2)}, u32[]{:S(2)}) collective-permute-start(f32[4,80,128]{2,1,0:T(8,128)S(1)} %pad_maximum_fusion), channel_id=1, source_target_pairs={{0,18},{1,19},{2,16},{3,17},{4,22},{5,23},{6,20},{7,21},{8,26},{9,... | collective-permute-start | bytes 491528 | tf_op jit(solution)/shard_map/ppermute | solution.py:547
  73.1 0.5 collective-permute-start.13
  73.6 1.3 %collective-permute-start.12 = (f32[4,80,128]{2,1,0:T(8,128)S(1)}, f32[4,80,128]{2,1,0:T(8,128)S(1)}, u32[]{:S(2)}, u32[]{:S(2)}) collective-permute-start(f32[4,80,128]{2,1,0:T(8,128)S(1)} %pad_maximum_fusion), channel_id=1, source_target_pairs={{0,2},{1,3},{2,0},{3,1},{4,6},{5,7},{6,4},{7,5},{8,10},{9,11},{10,... | collective-permute-start | bytes 491528 | tf_op jit(solution)/shard_map/ppermute | solution.py:547
  75.0 4.5 %collective-permute-done.12 = f32[4,80,128]{2,1,0:T(8,128)S(1)} collective-permute-done((f32[4,80,128]{2,1,0:T(8,128)S(1)}, f32[4,80,128]{2,1,0:T(8,128)S(1)}, u32[]{:S(2)}, u32[]{:S(2)}) %collective-permute-start.12) | collective-permute-done | bytes 163872 | tf_op jit(solution)/shard_map/ppermute | solution.py:547
  79.5 0.1 collective-permute-start.15
  79.6 2.1 %collective-permute-done.15.other_ref = f32[16,80,128]{2,1,0:T(8,128)S(1)} collective-permute-done((f32[16,80,128]{2,1,0:T(8,128)S(1)}, f32[16,80,128]{2,1,0:T(8,128)S(1)}, u32[]{:S(2)}, u32[]{:S(2)}) %collective-permute-start.15) | collective-permute-done | bytes 655392 | tf_op jit(solution)/shard_map/ppermute | solution.py:547
  81.7 2.0 %unpack.1 = (f32[5,1,128]{2,1,0:T(1,128)}, f32[64,512]{1,0:T(8,128)}, f32[3,512]{1,0:T(4,128)}, f32[1,512]{1,0:T(1,128)}, f32[512,512]{1,0:T(8,128)}, /*index=5*...) custom-call(s32[3]{0:T(128)S(1)} %pad_add_fusion.place_ref, ...), custom_call_target="tpu_custom_call" | custom-call | tf_op jit(solution)/shard_map/unpack/pallas_call | solution.py:648
  (28 shorter events, 0.2 us)
Async XLA Ops:
  2.4 14.7 %copy-start.8 = (f32[64]{0:T(128)S(1)}, f32[64]{0:T(128)}, u32[]{:S(2)}) copy-start(f32[64]{0:T(128)} %param.16) | copy-start | bytes 772
  2.4 14.8 %copy-start.7 = (bf16[64,1728]{1,0:T(8,128)(2,1)S(1)}, bf16[64,1728]{1,0:T(8,128)(2,1)}, u32[]{:S(2)}) copy-start(bf16[64,1728]{1,0:T(8,128)(2,1)} %param.15) | copy-start | bytes 663556
  2.4 19.6 %all-to-all-start = ((f32[16,16,128]{2,1,0:T(8,128)}), f32[16,16,128]{2,1,0:T(8,128)S(1)}, u32[]{:S(2)}, u32[]{:S(2)}) async-start(f32[16,16,128]{2,1,0:T(8,128)} %bitcast.31), calls=%async_computation | async-start | bytes 262144 | tf_op jit(solution)/shard_map/all_to_all | solution.py:695
  11.9 10.1 %collective-permute-start = (bf16[2,8,64,128]{3,2,1,0:T(8,128)(2,1)}, bf16[2,8,64,128]{3,2,1,0:T(8,128)(2,1)}, u32[]{:S(2)}, u32[]{:S(2)}) collective-permute-start(bf16[2,8,64,128]{3,2,1,0:T(8,128)(2,1)} %slice.48), channel_id=1, source_target_pairs={{0,1},{1,2},{2,3},{3,4},{4,5},{5,6},{6,7},{7,8},{8,9},{9,10},{10,1... | collective-permute-start | bytes 786440 | tf_op jit(solution)/shard_map/ppermute | solution.py:702
  13.0 9.6 %collective-permute-start.1 = (bf16[3,8,64,128]{3,2,1,0:T(8,128)(2,1)}, bf16[3,8,64,128]{3,2,1,0:T(8,128)(2,1)}, u32[]{:S(2)}, u32[]{:S(2)}) collective-permute-start(bf16[3,8,64,128]{3,2,1,0:T(8,128)(2,1)} %slice.49), channel_id=1, source_target_pairs={{1,0},{2,1},{3,2},{4,3},{5,4},{6,5},{7,6},{8,7},{9,8},{10,9},{11,1... | collective-permute-start | bytes 1179656 | tf_op jit(solution)/shard_map/ppermute | solution.py:703
  17.2 1.1 %copy-start.2 = (f32[5,512]{1,0:T(8,128)S(1)}, f32[5,512]{1,0:T(8,128)}, u32[]{:S(2)}) copy-start(f32[5,512]{1,0:T(8,128)} %w_out_ref.1) | copy-start | bytes 30724
  17.2 1.1 %copy-start.3 = (f32[3,512]{1,0:T(4,128)S(1)}, f32[3,512]{1,0:T(4,128)}, u32[]{:S(2)}) copy-start(f32[3,512]{1,0:T(4,128)} %w_pos_ref.1) | copy-start | bytes 18436
  17.2 1.1 %copy-start.4 = (f32[512]{0:T(512)S(1)}, f32[512]{0:T(512)}, u32[]{:S(2)}) copy-start(f32[512]{0:T(512)} %param.23) | copy-start | bytes 6148
  17.2 1.1 %copy-start.5 = (f32[512]{0:T(512)S(1)}, f32[512]{0:T(512)}, u32[]{:S(2)}) copy-start(f32[512]{0:T(512)} %param.25) | copy-start | bytes 6148
  17.2 1.1 %copy-start.6 = (f32[5]{0:T(128)S(1)}, f32[5]{0:T(128)}, u32[]{:S(2)}) copy-start(f32[5]{0:T(128)} %param.27) | copy-start | bytes 64
  18.3 1.2 %copy-start = (f32[512,512]{1,0:T(8,128)S(1)}, f32[512,512]{1,0:T(8,128)}, u32[]{:S(2)}) copy-start(f32[512,512]{1,0:T(8,128)} %w_mid_ref.1) | copy-start | bytes 3145732
  19.6 0.9 %copy-start.1 = (f32[64,512]{1,0:T(8,128)S(1)}, f32[64,512]{1,0:T(8,128)}, u32[]{:S(2)}) copy-start(f32[64,512]{1,0:T(8,128)} %w_latent_ref.1) | copy-start | bytes 393220
  41.2 3.9 %collective-permute-start.2 = (f32[16,80,128]{2,1,0:T(8,128)S(1)}, f32[16,80,128]{2,1,0:T(8,128)S(1)}, u32[]{:S(2)}, u32[]{:S(2)}) collective-permute-start(f32[16,80,128]{2,1,0:T(8,128)S(1)} %get-tuple-element.37), channel_id=1, source_target_pairs={{0,1},{1,0},{2,3},{3,2},{4,5},{5,4},{6,7},{7,6},{8,9},{9,8},{10,11... | collective-permute-start | bytes 1966088 | tf_op jit(solution)/shard_map/ppermute | solution.py:547
  45.2 10.1 %collective-permute-start.3 = (f32[4,80,128]{2,1,0:T(8,128)S(1)}, f32[4,80,128]{2,1,0:T(8,128)S(1)}, u32[]{:S(2)}, u32[]{:S(2)}) collective-permute-start(f32[4,80,128]{2,1,0:T(8,128)S(1)} %get-tuple-element.49), channel_id=1, source_target_pairs={{0,2},{1,3},{2,0},{3,1},{4,6},{5,7},{6,4},{7,5},{8,10},{9,11},{10,... | collective-permute-start | bytes 491528 | tf_op jit(solution)/shard_map/ppermute | solution.py:547
  45.3 9.9 %collective-permute-start.5 = (f32[4,80,128]{2,1,0:T(8,128)S(1)}, f32[4,80,128]{2,1,0:T(8,128)S(1)}, u32[]{:S(2)}, u32[]{:S(2)}) collective-permute-start(f32[4,80,128]{2,1,0:T(8,128)S(1)} %get-tuple-element.50), channel_id=1, source_target_pairs={{0,18},{1,19},{2,16},{3,17},{4,22},{5,23},{6,20},{7,21},{8,26},{9,... | collective-permute-start | bytes 491528 | tf_op jit(solution)/shard_map/ppermute | solution.py:547
  48.2 8.3 %collective-permute-start.4 = (f32[4,80,128]{2,1,0:T(8,128)S(1)}, f32[4,80,128]{2,1,0:T(8,128)S(1)}, u32[]{:S(2)}, u32[]{:S(2)}) collective-permute-start(f32[4,80,128]{2,1,0:T(8,128)S(1)} %get-tuple-element.51), channel_id=1, source_target_pairs={{0,16},{1,17},{2,18},{3,19},{4,20},{5,21},{6,22},{7,23},{8,24},{9,... | collective-permute-start | bytes 491528 | tf_op jit(solution)/shard_map/ppermute | solution.py:547
  56.5 4.5 %collective-permute-start.6 = (f32[1,80,128]{2,1,0:T(8,128)S(1)}, f32[1,80,128]{2,1,0:T(8,128)S(1)}, u32[]{:S(2)}, u32[]{:S(2)}) collective-permute-start(f32[1,80,128]{2,1,0:T(8,128)S(1)} %get-tuple-element.52), channel_id=1, source_target_pairs={{0,4},{1,5},{2,6},{3,7},{4,0},{5,1},{6,2},{7,3},{8,12},{9,13},{10,... | collective-permute-start | bytes 122888 | tf_op jit(solution)/shard_map/ppermute | solution.py:547
  56.7 5.8 %collective-permute-start.8 = (f32[1,80,128]{2,1,0:T(8,128)S(1)}, f32[1,80,128]{2,1,0:T(8,128)S(1)}, u32[]{:S(2)}, u32[]{:S(2)}) collective-permute-start(f32[1,80,128]{2,1,0:T(8,128)S(1)} %get-tuple-element.53), channel_id=1, source_target_pairs={{0,12},{1,13},{2,14},{3,15},{4,8},{5,9},{6,10},{7,11},{8,4},{9,5},... | collective-permute-start | bytes 122888 | tf_op jit(solution)/shard_map/ppermute | solution.py:547
  59.0 5.5 %collective-permute-start.7 = (f32[1,80,128]{2,1,0:T(8,128)S(1)}, f32[1,80,128]{2,1,0:T(8,128)S(1)}, u32[]{:S(2)}, u32[]{:S(2)}) collective-permute-start(f32[1,80,128]{2,1,0:T(8,128)S(1)} %get-tuple-element.54), channel_id=1, source_target_pairs={{0,8},{1,9},{2,10},{3,11},{4,12},{5,13},{6,14},{7,15},{8,0},{9,1},... | collective-permute-start | bytes 122888 | tf_op jit(solution)/shard_map/ppermute | solution.py:547
  64.6 5.9 %collective-permute-start.11 = (f32[1,80,128]{2,1,0:T(8,128)S(1)}, f32[1,80,128]{2,1,0:T(8,128)S(1)}, u32[]{:S(2)}, u32[]{:S(2)}) collective-permute-start(f32[1,80,128]{2,1,0:T(8,128)S(1)} %get-tuple-element.48), channel_id=1, source_target_pairs={{0,12},{1,13},{2,14},{3,15},{4,8},{5,9},{6,10},{7,11},{8,4},{9,5},... | collective-permute-start | bytes 122888 | tf_op jit(solution)/shard_map/ppermute | solution.py:547
  65.5 5.8 %collective-permute-start.10 = (f32[1,80,128]{2,1,0:T(8,128)S(1)}, f32[1,80,128]{2,1,0:T(8,128)S(1)}, u32[]{:S(2)}, u32[]{:S(2)}) collective-permute-start(f32[1,80,128]{2,1,0:T(8,128)S(1)} %get-tuple-element.48), channel_id=1, source_target_pairs={{0,8},{1,9},{2,10},{3,11},{4,12},{5,13},{6,14},{7,15},{8,0},{9,1},... | collective-permute-start | bytes 122888 | tf_op jit(solution)/shard_map/ppermute | solution.py:547
  66.1 5.3 %collective-permute-start.9 = (f32[1,80,128]{2,1,0:T(8,128)S(1)}, f32[1,80,128]{2,1,0:T(8,128)S(1)}, u32[]{:S(2)}, u32[]{:S(2)}) collective-permute-start(f32[1,80,128]{2,1,0:T(8,128)S(1)} %get-tuple-element.48), channel_id=1, source_target_pairs={{0,4},{1,5},{2,6},{3,7},{4,0},{5,1},{6,2},{7,3},{8,12},{9,13},{10,... | collective-permute-start | bytes 122888 | tf_op jit(solution)/shard_map/ppermute | solution.py:547
  71.4 8.1 %collective-permute-start.14 = (f32[4,80,128]{2,1,0:T(8,128)S(1)}, f32[4,80,128]{2,1,0:T(8,128)S(1)}, u32[]{:S(2)}, u32[]{:S(2)}) collective-permute-start(f32[4,80,128]{2,1,0:T(8,128)S(1)} %pad_maximum_fusion), channel_id=1, source_target_pairs={{0,18},{1,19},{2,16},{3,17},{4,22},{5,23},{6,20},{7,21},{8,26},{9,... | collective-permute-start | bytes 491528 | tf_op jit(solution)/shard_map/ppermute | solution.py:547
  73.1 6.4 %collective-permute-start.13 = (f32[4,80,128]{2,1,0:T(8,128)S(1)}, f32[4,80,128]{2,1,0:T(8,128)S(1)}, u32[]{:S(2)}, u32[]{:S(2)}) collective-permute-start(f32[4,80,128]{2,1,0:T(8,128)S(1)} %pad_maximum_fusion), channel_id=1, source_target_pairs={{0,16},{1,17},{2,18},{3,19},{4,20},{5,21},{6,22},{7,23},{8,24},{9,... | collective-permute-start | bytes 491528 | tf_op jit(solution)/shard_map/ppermute | solution.py:547
  73.6 5.8 %collective-permute-start.12 = (f32[4,80,128]{2,1,0:T(8,128)S(1)}, f32[4,80,128]{2,1,0:T(8,128)S(1)}, u32[]{:S(2)}, u32[]{:S(2)}) collective-permute-start(f32[4,80,128]{2,1,0:T(8,128)S(1)} %pad_maximum_fusion), channel_id=1, source_target_pairs={{0,2},{1,3},{2,0},{3,1},{4,6},{5,7},{6,4},{7,5},{8,10},{9,11},{10,... | collective-permute-start | bytes 491528 | tf_op jit(solution)/shard_map/ppermute | solution.py:547
  79.5 2.2 %collective-permute-start.15 = (f32[16,80,128]{2,1,0:T(8,128)S(1)}, f32[16,80,128]{2,1,0:T(8,128)S(1)}, u32[]{:S(2)}, u32[]{:S(2)}) collective-permute-start(f32[16,80,128]{2,1,0:T(8,128)S(1)} %constant_dynamic-update-slice_fusion.mine_ref), channel_id=1, source_target_pairs={{0,1},{1,0},{2,3},{3,2},{4,5},{5,4},{6,7},{7,6},{8,9},{9,8},{10,11... | collective-permute-start | bytes 1966088 | tf_op jit(solution)/shard_map/ppermute | solution.py:547

commit v3 on v2

--- a/solution.py
+++ b/solution.py
@@ -17,7 +17,7 @@
 LANES = 128
 BLOCK = 32
 WORDS = 128
-MISC = 16
+SUB = 32
 NN = (((1,), (0,)), ((), ()))
 NT = (((1,), (1,)), ((), ()))
 TN = (((0,), (0,)), ((), ()))
@@ -250,7 +250,7 @@
     latents = latent_high.shape[0]
     planes, rows_y, rows_z = plan.planes, left_ref.shape[1], left_ref.shape[3]
     slots = rows // plan.tiles
-    my_chunk = place_ref[0]
+    my_block = place_ref[0]
     my_tile = place_ref[1]
     my_replica = place_ref[2]
 
@@ -423,8 +423,13 @@
 
     grad_two = lax.fori_loop(0, rows // BLOCK, second_back, jnp.zeros((8, hidden), F32))
 
-    packed[...] = jnp.zeros_like(packed)
-    main_rows = hidden + latents + MISC
+    def put(part, first, value):
+        while value.shape[0]:
+            block, row = first // plan.main_rows, first % plan.main_rows
+            count = min(value.shape[0], plan.main_rows - row)
+            packed[2 * part + block, row : row + count, :] = value[:count]
+            first, value = first + count, value[count:]
+
     wide = 2 * LANES
     for left in range(hidden // wide):
         for right in range(hidden // wide):
@@ -434,8 +439,7 @@
                 (one_high[:, lefts], one_low[:, lefts]), (d_high[:, rights], d_low[:, rights]), TN
             )
             for side in range(2):
-                first = (2 * right + side) * main_rows + left * wide
-                packed[first : first + wide, :] = part[:, side * LANES : (side + 1) * LANES]
+                put(2 * right + side, left * wide, part[:, side * LANES : (side + 1) * LANES])
 
     lax.fori_loop(0, 5, functools.partial(times_mid, NT, (d_high, d_low), back), 0)
 
@@ -483,39 +487,36 @@
         jnp.sum(grad_two, axis=0, keepdims=True),
         last,
     ]
+    misc = jnp.concatenate(misc + [jnp.zeros((2, hidden), F32)], axis=0)
     for part in range(hidden // LANES):
         lanes = slice(part * LANES, (part + 1) * LANES)
-        first = part * main_rows + hidden
-        packed[first : first + latents, :] = grad_latent[:, lanes]
-        first = first + latents
-        for number, row in enumerate(misc):
-            packed[first + number : first + number + 1, :] = row[:, lanes]
-        packed[first + 8 : first + 16, :] = grad_out[:, lanes]
+        put(part, hidden, grad_latent[:, lanes])
+        packed[2 * part, plan.coded_rows :, :] = misc[:, lanes]
+        packed[2 * part + 1, plan.coded_rows :, :] = grad_out[:, lanes]
 
     chosen = jnp.where(
         lane == jnp.broadcast_to(words[:, 10:11], (rows, LANES)).astype(jnp.int32), words[:, 9:10], 0.0
     ).astype(BF16)
-    source = lax.broadcasted_iota(jnp.int32, (plan.tiles, rows), 0)
-    inside = lax.broadcasted_iota(jnp.int32, (plan.tiles, rows), 1)
-    mine = (inside >> (slots.bit_length() - 1)) == source
-    for f in range(5):
-        high, middle, low = thirds(jnp.where(mine, jnp.broadcast_to(value[f], (plan.tiles, rows)), 0.0))
-        first = pl.multiple_of((hidden // LANES) * main_rows + f * plan.devices + my_replica * plan.tiles, 16)
-        packed[pl.ds(first, plan.tiles), :] = mul(high, chosen) + mul(middle, chosen) + mul(low, chosen)
-
-    half = plan.devices // 2
-    chunk = plan.chunk
-    my_half = my_chunk // half
-    for number in range(plan.devices):
-        spot = jnp.bitwise_xor(number, my_chunk) & (half - 1)
-
-        @pl.when(my_half == number // half)
+    fields = jnp.concatenate(value + [jnp.zeros((3, rows), F32)], axis=0)
+    source = lax.broadcasted_iota(jnp.int32, (8, rows), 1) >> (slots.bit_length() - 1)
+    spread = jnp.concatenate([jnp.where(source == t, fields, 0.0) for t in range(plan.tiles)], axis=0)
+    high, middle, low = thirds(spread)
+    spread = mul(high, chosen) + mul(middle, chosen) + mul(low, chosen)
+    packed[:, plan.main_rows : plan.coded_rows, :] = jnp.zeros((8, plan.devices, LANES), F32)
+    for t in range(plan.tiles):
+        row = plan.main_rows + (my_replica * (plan.tiles // 8) + t // 8) * 8
+        packed[t % 8, pl.ds(pl.multiple_of(row, 8), 8), :] = spread[8 * t : 8 * t + 8]
+
+    for block in range(8):
+        spot = jnp.bitwise_xor(block, my_block) & 3
+
+        @pl.when((my_block >> 2) == block // 4)
         def _():
-            keep_ref[spot] = packed[number * chunk : (number + 1) * chunk, :]
-
-        @pl.when(my_half != number // half)
+            keep_ref[spot] = packed[block]
+
+        @pl.when((my_block >> 2) != block // 4)
         def _():
-            send_ref[spot] = packed[number * chunk : (number + 1) * chunk, :]
+            send_ref[spot] = packed[block]
 
 
 class Plan:
@@ -524,34 +525,123 @@
         self.slots = 2 * queries // tiles
         self.devices = tiles * replicas
         self.query_total = float(queries * self.devices)
-        self.main_rows = hidden + latents + MISC
-        needed = (hidden // LANES) * self.main_rows + 5 * self.devices
-        self.chunk = -(-needed // (8 * self.devices)) * 8
-        bits = self.devices.bit_length() - 1
-        middle = list(range(2, bits - 1))
-        self.stages = [[0], [1, bits - 1]] + [middle[i : i + 2] for i in range(0, len(middle), 2)]
+        self.main_rows = (hidden + latents) // 2
+        self.coded_rows = self.main_rows + self.devices
+        self.rows = self.coded_rows + 8
+        self.scales = -(-(self.coded_rows // SUB + 1) // 16) * 16
+        self.sent_rows = self.coded_rows + 16 + self.scales
+        top = self.devices.bit_length() - 1
+        self.core, self.plane, self.rest = [0], [1, top - 1], list(range(2, top - 1))
 
     def mask(self, bits, steps):
         return sum(1 << bit for number, bit in enumerate(bits) if steps >> number & 1)
 
-    def my_chunk(self, device):
-        chunk = 0
-        for bits in self.stages:
-            for bit in reversed(bits):
-                chunk = chunk * 2 + (device >> bit & 1)
-        return chunk
+    def my_block(self, device):
+        return (device & 1) * 4 + (device >> 1 & 1) + 2 * (device >> self.plane[1] & 1)
 
 
 def swapped(value, plan, bits, steps):
     mask = plan.mask(bits, steps)
     return lax.ppermute(value, ("replica", "tile"), [(i, i ^ mask) for i in range(plan.devices)])
+
+
+def encode(plan, read, out_ref):
+    starts = list(range(0, plan.coded_rows, SUB))
+    parts = [read(start, SUB) for start in starts] + [read(plan.coded_rows, 8)]
+    tops = [jnp.max(jnp.abs(part), axis=0, keepdims=True) for part in parts]
+    tops = tops + [jnp.zeros_like(tops[0])] * (plan.scales - len(tops))
+    power = jnp.floor(jnp.log2(jnp.maximum(jnp.concatenate(tops, axis=0), 1e-30)))
+    scale = jnp.exp2(14.0 - power)
+
+    def whole(value):
+        return jnp.clip(jnp.round(value), -32767.0, 32767.0)
+
+    def narrow(value):
+        return value.astype(jnp.int32).astype(jnp.int16)
+
+    for number, start in enumerate(starts):
+        out_ref[start : start + SUB, :] = narrow(whole(parts[number] * scale[number : number + 1]))
+    last = len(starts)
+    exact = parts[last] * scale[last : last + 1]
+    high = whole(exact)
+    low = whole((exact - high) * 32768.0)
+    out_ref[plan.coded_rows : plan.coded_rows + 16, :] = narrow(jnp.concatenate([high, low], axis=0))
+    out_ref[plan.coded_rows + 16 :, :] = narrow(power)
+
+
+def decoder(plan, ref):
+    def widen(value):
+        return value.astype(jnp.int32).astype(F32)
+
+    scale = jnp.exp2(widen(ref[plan.coded_rows + 16 :, :]) - 14.0)
+
+    def read(start, count):
+        if start < plan.coded_rows:
+            number = start // SUB
+            return widen(ref[start : start + count, :]) * scale[number : number + 1]
+        both = widen(ref[plan.coded_rows : plan.coded_rows + 16, :])
+        number = plan.coded_rows // SUB
+        return (both[:8] + both[8:] * (1.0 / 32768.0)) * scale[number : number + 1]
+
+    return read
+
+
+def added(readers):
+    def read(start, count):
+        total = readers[0](start, count)
+        for reader in readers[1:]:
+            total = total + reader(start, count)
+        return total
+
+    return read
+
+
+def first_kernel(plan, keep_ref, got_ref, mine_ref, *out_refs):
+    def reader(block):
+        return lambda start, count: (
+            keep_ref[block, start : start + count, :] + got_ref[block, start : start + count, :]
+        )
+
+    for number, out_ref in enumerate(out_refs):
+        encode(plan, reader(number + 1), out_ref)
+    mine_ref[...] = keep_ref[0] + got_ref[0]
+
+
+def first_sum(keep, got, plan):
+    sent = jax.ShapeDtypeStruct((plan.sent_rows, LANES), jnp.int16)
+    return pl.pallas_call(
+        functools.partial(first_kernel, plan),
+        out_shape=(jax.ShapeDtypeStruct(keep.shape[1:], F32), sent, sent, sent),
+        in_specs=[VMEM] * 2,
+        out_specs=tuple([VMEM] * 4),
+        name="sum_core",
+    )(keep, got)
+
+
+def plane_kernel(plan, mine_ref, *refs):
+    readers = [lambda start, count: mine_ref[start : start + count, :]]
+    encode(plan, added(readers + [decoder(plan, ref) for ref in refs[:-1]]), refs[-1])
+
+
+def pair_kernel(plan, mine_ref, other_ref, out_ref):
+    encode(plan, added([decoder(plan, mine_ref), decoder(plan, other_ref)]), out_ref)
+
+
+def coded_sum(kernel, blocks, plan, name):
+    return pl.pallas_call(
+        functools.partial(kernel, plan),
+        out_shape=jax.ShapeDtypeStruct((plan.sent_rows, LANES), jnp.int16),
+        in_specs=[VMEM] * len(blocks),
+        out_specs=VMEM,
+        name=name,
+    )(*blocks)
 
 
 def main(place, left, right, partial, taps, words, weights, plan):
     rows = plan.tiles * plan.slots
     hidden = weights[-1].shape[1]
     channels = left.shape[2]
-    outs = jax.ShapeDtypeStruct((plan.devices // 2, plan.chunk, LANES), F32)
+    outs = jax.ShapeDtypeStruct((4, plan.rows, LANES), F32)
     wide = lambda kind: pltpu.VMEM((5 * rows, hidden), kind)
     return pl.pallas_call(
         functools.partial(main_kernel, plan),
@@ -573,67 +663,49 @@
             wide(BF16),
             pltpu.VMEM((40, rows), F32),
             pltpu.VMEM((40, rows), F32),
-            pltpu.VMEM((plan.devices * plan.chunk, LANES), F32),
+            pltpu.VMEM((8, plan.rows, LANES), F32),
         ],
         compiler_params=pltpu.CompilerParams(vmem_limit_bytes=48 << 20),
         name="encode_decode",
     )(place, left, right, partial, taps, words, *weights)
 
 
-def unpack_kernel(
-    plan,
-    place_ref,
-    mine_ref,
-    other_ref,
-    prediction_ref,
-    latent_ref,
-    pos_ref,
-    one_ref,
-    mid_ref,
-    two_ref,
-    out_ref,
-    bias_out_ref,
-    loss_ref,
-    packed,
-):
-    my_chunk = place_ref[0]
+def unpack_kernel(plan, place_ref, *refs):
+    sources, outs, packed = refs[:8], refs[8:-1], refs[-1]
+    prediction_ref, latent_ref, pos_ref, one_ref, mid_ref, two_ref, out_ref, bias_out_ref, loss_ref = outs
+    my_block = place_ref[0]
     device = place_ref[2] * plan.tiles + place_ref[1]
-    half = plan.devices // 2
-    chunk = plan.chunk
-    my_half = my_chunk // half
-    for number in range(plan.devices):
-        spot = jnp.bitwise_xor(number, my_chunk) & (half - 1)
-
-        @pl.when(my_half == number // half)
-        def _():
-            packed[number * chunk : (number + 1) * chunk, :] = mine_ref[spot]
-
-        @pl.when(my_half != number // half)
-        def _():
-            packed[number * chunk : (number + 1) * chunk, :] = other_ref[spot]
+    starts = list(range(0, plan.coded_rows, SUB))
+    for number, ref in enumerate(sources):
+        read = decoder(plan, ref)
+        block = jnp.bitwise_xor(number, my_block)
+        for start in starts:
+            packed[block, start : start + SUB, :] = read(start, SUB)
+        packed[block, plan.coded_rows :, :] = read(plan.coded_rows, 8)
 
     hidden = mid_ref.shape[0]
     latents = latent_ref.shape[0]
+    split = plan.main_rows
     for part in range(hidden // LANES):
         lanes = slice(part * LANES, (part + 1) * LANES)
-        first = part * plan.main_rows
-        mid_ref[:, lanes] = packed[first : first + hidden, :]
-        first = first + hidden
-        latent_ref[:, lanes] = packed[first : first + latents, :]
-        first = first + latents
-        pos_ref[:, lanes] = packed[first : first + 3, :]
-        one_ref[:, lanes] = packed[first + 3 : first + 4, :]
-        two_ref[:, lanes] = packed[first + 4 : first + 5, :]
-        out_ref[:, lanes] = packed[first + 8 : first + 13, :]
+        mid_ref[0:split, lanes] = packed[2 * part, 0:split, :]
+        mid_ref[split:, lanes] = packed[2 * part + 1, 0 : hidden - split, :]
+        latent_ref[:, lanes] = packed[2 * part + 1, hidden - split : split, :]
+        misc = packed[2 * part, plan.coded_rows :, :]
+        pos_ref[:, lanes] = misc[0:3]
+        one_ref[:, lanes] = misc[3:4]
+        two_ref[:, lanes] = misc[4:5]
+        out_ref[:, lanes] = packed[2 * part + 1, plan.coded_rows : plan.coded_rows + 5, :]
         if part == 0:
-            bias_out_ref[...] = packed[first + 5 : first + 6, 0:5]
-            loss_ref[...] = packed[first + 5 : first + 6, 5:6]
-    first = (hidden // LANES) * plan.main_rows
+            bias_out_ref[...] = misc[5:6, 0:5]
+            loss_ref[...] = misc[5:6, 5:6]
+    row = pl.multiple_of(plan.main_rows + (device >> 3) * 8, 8)
+    fields = packed[device & 7, pl.ds(row, 8), :]
     for f in range(5):
-        prediction_ref[f] = packed[pl.ds(first + f * plan.devices + device, 1), :]
-
-
-def unpack(place, mine, other, plan, hidden, latents):
+        prediction_ref[f] = fields[f : f + 1]
+
+
+def unpack(place, blocks, plan, hidden, latents):
     shapes = [
         (5, 1, LANES),
         (latents, hidden),
@@ -648,12 +720,12 @@
     return pl.pallas_call(
         functools.partial(unpack_kernel, plan),
         out_shape=tuple(jax.ShapeDtypeStruct(shape, F32) for shape in shapes),
-        in_specs=[SMEM, VMEM, VMEM],
+        in_specs=[SMEM] + [VMEM] * 8,
         out_specs=tuple([VMEM] * len(shapes)),
-        scratch_shapes=[pltpu.VMEM((plan.devices * plan.chunk, LANES), F32)],
+        scratch_shapes=[pltpu.VMEM((8, plan.rows, LANES), F32)],
         compiler_params=pltpu.CompilerParams(vmem_limit_bytes=16 << 20),
         name="unpack",
-    )(place, mine, other)
+    )(place, *blocks)
 
 
 def body(
@@ -681,7 +753,7 @@
     hidden = w_mid.shape[0]
     plan = Plan(tiles, replicas, queries, fields.shape[2], hidden, channels)
     device = my_replica * tiles + my_tile
-    place = jnp.stack([plan.my_chunk(device), my_tile, my_replica]).astype(jnp.int32)
+    place = jnp.stack([plan.my_block(device), my_tile, my_replica]).astype(jnp.int32)
 
     words = route(
         query_owner[:, :, 0],
@@ -707,20 +779,15 @@
     partial, *weights = local_part(here, taps, convolution_bias[:, None], params)
     send, keep = main(place, left, right, partial, taps, words, weights, plan)
 
-    keep = keep + swapped(send, plan, plan.stages[0], 1)
-    for bits in plan.stages[1:]:
-        group = 1 << len(bits)
-        keep = keep.reshape(group, keep.shape[0] // group, plan.chunk, LANES)
-        arrived = [swapped(keep[step], plan, bits, step) for step in range(1, group)]
-        keep = keep[0]
-        for block in arrived:
-            keep = keep + block
-    for bits in reversed(plan.stages[1:]):
-        group = 1 << len(bits)
-        keep = jnp.concatenate([keep] + [swapped(keep, plan, bits, step) for step in range(1, group)], axis=0)
-    other = swapped(keep, plan, plan.stages[0], 1)
+    mine, *others = first_sum(keep, swapped(send, plan, plan.core, 1), plan)
+    arrived = [swapped(block, plan, plan.plane, step + 1) for step, block in enumerate(others)]
+    block = coded_sum(plane_kernel, [mine] + arrived, plan, "sum_plane")
+    for bit in plan.rest:
+        block = coded_sum(pair_kernel, [block, swapped(block, plan, [bit], 1)], plan, "sum_line")
+    blocks = [block] + [swapped(block, plan, plan.plane, step) for step in range(1, 4)]
+    blocks = blocks + [swapped(block, plan, plan.core, 1) for block in blocks]
     prediction, g_latent, g_pos, g_one, g_mid, g_two, g_out, g_bias, loss = unpack(
-        place, keep, other, plan, hidden, channels
+        place, blocks, plan, hidden, channels
     )
     return (
         prediction.transpose(1, 0, 2),

time: 84 us -> 86.6 us (1.031)
  starting transfers between devices: 29.3 us -> 22.3 us
  Pallas kernels: 23.7 us -> 30.5 us
  local copies, waits for them, and re-layouts: 6.04 us -> 10.4 us
  waiting for transfers between devices: 23.6 us -> 22 us
    pallas_call x0 -> x4, Pallas kernels: none -> 7.3 us  [the longest x3 5.16 us: coded_sum(): pl.pallas_call(functools.partial(kernel, plan), out_shape=jax.ShapeDtypeS...]
    ppermute x14 -> x13, starting transfers between devices: 17.3 us -> 10.3 us  [swapped(): lax.ppermute(value, ('replica', 'tile'), [(i, i ^ mask) for i in range(pl...]
    unnamed x23 -> x34, local copies, waits for them, and re-layouts: 2.2 us -> 6.66 us
    ppermute x14 -> x13, waiting for transfers between devices: 22.8 us -> 21.2 us  [swapped(): lax.ppermute(value, ('replica', 'tile'), [(i, i ^ mask) for i in range(pl...]
  transfers between devices with their start and end apart: 17 -> 16, of which waited for: 11 -> 11; matrix products, arithmetic and copies ran while one was open for 5% -> 4% of each run, Pallas kernels for 2% -> 2%
where the time goes in v3:
time: 86.6 us; the launch traced here: 86.1 us
  Pallas kernels  30.5 us (35%)
  starting transfers between devices  22.3 us (26%)
  waiting for transfers between devices  22 us (25%)
  local copies, waits for them, and re-layouts  10.4 us (12%)
    ppermute x13, waiting for transfers between devices, swapped(): lax.ppermute(value, ('replica', 'tile'), [(i, i ^ mask) for i in range(pl...  21.2 us
    pallas_call x1, Pallas kernels, main(): pl.pallas_call(functools.partial(main_kernel, plan), out_shape=(outs, out...  18.2 us
    ppermute x13, starting transfers between devices, swapped(): lax.ppermute(value, ('replica', 'tile'), [(i, i ^ mask) for i in range(pl...  10.3 us
    all_to_all x1, starting transfers between devices, body(): lax.all_to_all(words.reshape(tiles, plan.slots, WORDS), 'tile', split_axi...  7.52 us
    unnamed x34, local copies, waits for them, and re-layouts  6.66 us
    pallas_call x3, Pallas kernels, coded_sum(): pl.pallas_call(functools.partial(kernel, plan), out_shape=jax.ShapeDtypeS...  5.16 us
    ppermute x1, starting transfers between devices, body(): right = lax.ppermute(here[:DILATION_RATE + 1], 'tile', down)  4.04 us
    pallas_call x1, Pallas kernels, first_sum(): pl.pallas_call(functools.partial(first_kernel, plan), out_shape=(jax.Shap...  2.14 us
  transfers between devices with their start and end apart: 16, of which 11 were waited for; matrix products, arithmetic and copies ran while one was open for 4% of the time, Pallas kernels for 2%

profile of v3, /device:TPU:0, one launch (start us, length us, event | category | flops | bytes accessed | tf_op | source)
XLA Modules:
  0.0 86.1 jit_solution(1154394604670496195)
XLA Ops:
  0.6 1.7 %route.1 = f32[256,128]{1,0:T(8,128)} custom-call(s32[1,128]{1,0:T(1,128)} %bitcast.34, s32[1,128]{1,0:T(1,128)} %cell_ref.1, f32[3,1,128]{2,1,0:T(1,128)} %bitcast.33, f32[5,1,128]{2,1,0:T(1,128)} %bitcast.32), custom_call_target="tpu_custom_call" | custom-call | tf_op jit(solution)/shard_map/route/pallas_call | solution.py:73
  2.4 7.5 %all-to-all-start = ((f32[16,16,128]{2,1,0:T(8,128)}), f32[16,16,128]{2,1,0:T(8,128)S(1)}, u32[]{:S(2)}, u32[]{:S(2)}) async-start(f32[16,16,128]{2,1,0:T(8,128)} %bitcast.31), calls=%async_computation | async-start | bytes 262144 | tf_op jit(solution)/shard_map/all_to_all | solution.py:767
  9.9 1.2 %copy.30 = bf16[1,64,4,8,128]{4,1,3,2,0:T(8,128)(2,1)S(1)} copy(bf16[1,64,4,8,128]{4,3,2,1,0:T(8,128)(2,1)} %param.14) | data formatting | bytes 1048576 | tf_op jit(solution)/shard_map/optimization_barrier | solution.py:766
  11.1 0.7 slice.8
  11.9 0.4 collective-permute-start
  12.3 0.8 slice.9
  13.1 4.0 %collective-permute-start.1 = (bf16[3,8,64,128]{3,2,1,0:T(8,128)(2,1)}, bf16[3,8,64,128]{3,2,1,0:T(8,128)(2,1)}, u32[]{:S(2)}, u32[]{:S(2)}) collective-permute-start(bf16[3,8,64,128]{3,2,1,0:T(8,128)(2,1)} %slice.9), channel_id=1, source_target_pairs={{1,0},{2,1},{3,2},{4,3},{5,4},{6,5},{7,6},{8,7},{9,8},{10,9},{11,1... | collective-permute-start | bytes 1179656 | tf_op jit(solution)/shard_map/ppermute | solution.py:775
  17.1 0.1 copy.28.bias_ref
  17.2 0.0 copy-start.7
  17.3 0.3 reshape.42
  17.6 0.3 copy.27
  17.9 0.3 reshape.43.weight_ref.conv_weight_ref
  18.2 0.1 pad_add_fusion.place_ref
  18.3 1.2 %copy-done.2 = f32[512,512]{1,0:T(8,128)S(1)} copy-done((f32[512,512]{1,0:T(8,128)S(1)}, f32[512,512]{1,0:T(8,128)}, u32[]{:S(2)}) %copy-start.2) | copy-done | bytes 1048600
  19.6 0.9 %copy-done.3 = f32[64,512]{1,0:T(8,128)S(1)} copy-done((f32[64,512]{1,0:T(8,128)S(1)}, f32[64,512]{1,0:T(8,128)}, u32[]{:S(2)}) %copy-start.3) | copy-done | bytes 131096
  20.5 1.5 %conv_local.1 = (f32[20,64,256]{2,1,0:T(8,128)S(1)}, bf16[64,512]{1,0:T(8,128)(2,1)S(1)}, bf16[64,512]{1,0:T(8,128)(2,1)S(1)}, bf16[512,512]{1,0:T(8,128)(2,1)S(...) custom-call(bf16[4,8,64,128]{3,2,1,0:T(8,128)(2,1)S(1)} %bitcast.25, ...), custom_call_target="tpu_custom_call" | custom-call | flops 3221225472 | bytes 4194304 | tf_op jit(solution)/shard_map/conv_local/pallas_call | solution.py:153
  22.0 0.7 collective-permute-done.1.right_ref
  22.7 18.2 %encode_decode.1 = (f32[4,328,128]{2,1,0:T(8,128)S(1)}, f32[4,328,128]{2,1,0:T(8,128)S(1)}) custom-call(s32[3]{0:T(128)S(1)} %pad_add_fusion.place_ref, bf16[2,8,64,128]{3,2,1,0:T(8,128)(2,1)} %collective-permute-done.left_ref, bf16[3,8,64,128]{3,2,1,0:T(8,128)(2,1)} %collective-permute-done.1.right_ref, f32[20,64,256]{2,1,0:T(8,128)S(1)} %get-tuple-element.33.partial_ref, ...), custom_call_target="tpu_custom_call" | custom-call | tf_op jit(solution)/shard_map/encode_decode/pallas_call | solution.py:646
  40.9 0.8 copy-done
  41.8 2.1 %collective-permute-start.2 = (f32[4,328,128]{2,1,0:T(8,128)S(1)}, f32[4,328,128]{2,1,0:T(8,128)S(1)}, u32[]{:S(2)}, u32[]{:S(2)}) collective-permute-start(f32[4,328,128]{2,1,0:T(8,128)S(1)} %get-tuple-element.41), channel_id=1, source_target_pairs={{0,1},{1,0},{2,3},{3,2},{4,5},{5,4},{6,7},{7,6},{8,9},{9,8},{10,11... | collective-permute-start | bytes 2015240 | tf_op jit(solution)/shard_map/ppermute | solution.py:545
  43.8 1.7 %collective-permute-done.2.got_ref = f32[4,328,128]{2,1,0:T(8,128)S(1)} collective-permute-done((f32[4,328,128]{2,1,0:T(8,128)S(1)}, f32[4,328,128]{2,1,0:T(8,128)S(1)}, u32[]{:S(2)}, u32[]{:S(2)}) %collective-permute-start.2) | collective-permute-done | bytes 671776 | tf_op jit(solution)/shard_map/ppermute | solution.py:545
  45.6 0.9 %copy-done.9 = f32[4,328,128]{2,1,0:T(8,128)} copy-done((f32[4,328,128]{2,1,0:T(8,128)}, f32[4,328,128]{2,1,0:T(8,128)S(1)}, u32[]{:S(2)}) %copy-start.9) | copy-done | bytes 671768
  46.4 2.1 %sum_core.1 = (f32[328,128]{1,0:T(8,128)}, s16[352,128]{1,0:T(8,128)(2,1)}, s16[352,128]{1,0:T(8,128)(2,1)}, s16[352,128]{1,0:T(8,128)(2,1)}) custom-call(f32[4,328,128]{2,1,0:T(8,128)} %copy-done, f32[4,328,128]{2,1,0:T(8,128)} %copy-done.9), custom_call_target="tpu_custom_call" | custom-call | tf_op jit(solution)/shard_map/sum_core/pallas_call | solution.py:612
  48.6 0.1 collective-permute-start.3
  48.7 1.5 %collective-permute-start.4 = (s16[352,128]{1,0:T(8,128)(2,1)}, s16[352,128]{1,0:T(8,128)(2,1)S(1)}, u32[]{:S(2)}, u32[]{:S(2)}) collective-permute-start(s16[352,128]{1,0:T(8,128)(2,1)} %get-tuple-element.44), channel_id=1, source_target_pairs={{0,16},{1,17},{2,18},{3,19},{4,20},{5,21},{6,22},{7,23},{8,24},{9,... | collective-permute-start | bytes 270344 | tf_op jit(solution)/shard_map/ppermute | solution.py:545
  50.2 1.9 %collective-permute-start.5 = (s16[352,128]{1,0:T(8,128)(2,1)}, s16[352,128]{1,0:T(8,128)(2,1)S(1)}, u32[]{:S(2)}, u32[]{:S(2)}) collective-permute-start(s16[352,128]{1,0:T(8,128)(2,1)} %get-tuple-element.45), channel_id=1, source_target_pairs={{0,18},{1,19},{2,16},{3,17},{4,22},{5,23},{6,20},{7,21},{8,26},{9,... | collective-permute-start | bytes 270344 | tf_op jit(solution)/shard_map/ppermute | solution.py:545
  52.1 1.6 %collective-permute-done.3.refs_0_ = s16[352,128]{1,0:T(8,128)(2,1)S(1)} collective-permute-done((s16[352,128]{1,0:T(8,128)(2,1)}, s16[352,128]{1,0:T(8,128)(2,1)S(1)}, u32[]{:S(2)}, u32[]{:S(2)}) %collective-permute-start.3) | collective-permute-done | bytes 90144 | tf_op jit(solution)/shard_map/ppermute | solution.py:545
  53.7 3.1 %collective-permute-done.5.refs_2_ = s16[352,128]{1,0:T(8,128)(2,1)S(1)} collective-permute-done((s16[352,128]{1,0:T(8,128)(2,1)}, s16[352,128]{1,0:T(8,128)(2,1)S(1)}, u32[]{:S(2)}, u32[]{:S(2)}) %collective-permute-start.5) | collective-permute-done | bytes 90144 | tf_op jit(solution)/shard_map/ppermute | solution.py:545
  56.8 0.6 copy-done.15
  57.4 1.8 %sum_plane.1.mine_ref = s16[352,128]{1,0:T(8,128)(2,1)} custom-call(f32[328,128]{1,0:T(8,128)} %get-tuple-element.42.mine_ref, s16[352,128]{1,0:T(8,128)(2,1)} %copy-done.13, s16[352,128]{1,0:T(8,128)(2,1)} %copy-done.14, s16[352,128]{1,0:T(8,128)(2,1)} %copy-done.15), custom_call_target="tpu_custom_call" | custom-call | tf_op jit(solution)/shard_map/sum_plane/pallas_call | solution.py:631
  59.2 0.2 collective-permute-start.6
  59.4 4.6 %collective-permute-done.6.other_ref = s16[352,128]{1,0:T(8,128)(2,1)S(1)} collective-permute-done((s16[352,128]{1,0:T(8,128)(2,1)}, s16[352,128]{1,0:T(8,128)(2,1)S(1)}, u32[]{:S(2)}, u32[]{:S(2)}) %collective-permute-start.6) | collective-permute-done | bytes 90144 | tf_op jit(solution)/shard_map/ppermute | solution.py:545
  64.0 0.6 copy-done.11
  64.6 1.7 %sum_line.2.mine_ref = s16[352,128]{1,0:T(8,128)(2,1)} custom-call(s16[352,128]{1,0:T(8,128)(2,1)} %sum_plane.1.mine_ref, s16[352,128]{1,0:T(8,128)(2,1)} %copy-done.11), custom_call_target="tpu_custom_call" | custom-call | tf_op jit(solution)/shard_map/sum_line/pallas_call | solution.py:631
  66.3 1.1 %collective-permute-start.7 = (s16[352,128]{1,0:T(8,128)(2,1)}, s16[352,128]{1,0:T(8,128)(2,1)S(1)}, u32[]{:S(2)}, u32[]{:S(2)}) collective-permute-start(s16[352,128]{1,0:T(8,128)(2,1)} %sum_line.2.mine_ref), channel_id=1, source_target_pairs={{0,8},{1,9},{2,10},{3,11},{4,12},{5,13},{6,14},{7,15},{8,0},{9,1},... | collective-permute-start | bytes 270344 | tf_op jit(solution)/shard_map/ppermute | solution.py:545
  67.4 5.1 %collective-permute-done.7.other_ref = s16[352,128]{1,0:T(8,128)(2,1)S(1)} collective-permute-done((s16[352,128]{1,0:T(8,128)(2,1)}, s16[352,128]{1,0:T(8,128)(2,1)S(1)}, u32[]{:S(2)}, u32[]{:S(2)}) %collective-permute-start.7) | collective-permute-done | bytes 90144 | tf_op jit(solution)/shard_map/ppermute | solution.py:545
  72.5 0.6 copy-done.12
  73.1 1.7 %sum_line.3.refs_0_ = s16[352,128]{1,0:T(8,128)(2,1)} custom-call(s16[352,128]{1,0:T(8,128)(2,1)} %sum_line.2.mine_ref, s16[352,128]{1,0:T(8,128)(2,1)} %copy-done.12), custom_call_target="tpu_custom_call" | custom-call | tf_op jit(solution)/shard_map/sum_line/pallas_call | solution.py:631
  74.8 1.6 %collective-permute-start.10 = (s16[352,128]{1,0:T(8,128)(2,1)}, s16[352,128]{1,0:T(8,128)(2,1)S(1)}, u32[]{:S(2)}, u32[]{:S(2)}) collective-permute-start(s16[352,128]{1,0:T(8,128)(2,1)} %sum_line.3.refs_0_), channel_id=1, source_target_pairs={{0,18},{1,19},{2,16},{3,17},{4,22},{5,23},{6,20},{7,21},{8,26},{9,... | collective-permute-start | bytes 270344 | tf_op jit(solution)/shard_map/ppermute | solution.py:545
  76.4 1.0 %collective-permute-start.9 = (s16[352,128]{1,0:T(8,128)(2,1)}, s16[352,128]{1,0:T(8,128)(2,1)S(1)}, u32[]{:S(2)}, u32[]{:S(2)}) collective-permute-start(s16[352,128]{1,0:T(8,128)(2,1)} %sum_line.3.refs_0_), channel_id=1, source_target_pairs={{0,16},{1,17},{2,18},{3,19},{4,20},{5,21},{6,22},{7,23},{8,24},{9,... | collective-permute-start | bytes 270344 | tf_op jit(solution)/shard_map/ppermute | solution.py:545
  77.4 0.9 %collective-permute-start.8 = (s16[352,128]{1,0:T(8,128)(2,1)}, s16[352,128]{1,0:T(8,128)(2,1)S(1)}, u32[]{:S(2)}, u32[]{:S(2)}) collective-permute-start(s16[352,128]{1,0:T(8,128)(2,1)} %sum_line.3.refs_0_), channel_id=1, source_target_pairs={{0,2},{1,3},{2,0},{3,1},{4,6},{5,7},{6,4},{7,5},{8,10},{9,11},{10,... | collective-permute-start | bytes 270344 | tf_op jit(solution)/shard_map/ppermute | solution.py:545
  78.3 2.1 %collective-permute-done.10.refs_3_ = s16[352,128]{1,0:T(8,128)(2,1)S(1)} collective-permute-done((s16[352,128]{1,0:T(8,128)(2,1)}, s16[352,128]{1,0:T(8,128)(2,1)S(1)}, u32[]{:S(2)}, u32[]{:S(2)}) %collective-permute-start.10) | collective-permute-done | bytes 90144 | tf_op jit(solution)/shard_map/ppermute | solution.py:545
  80.5 0.7 collective-permute-done.9.refs_2_
  81.2 0.9 %collective-permute-done.8.refs_1_ = s16[352,128]{1,0:T(8,128)(2,1)S(1)} collective-permute-done((s16[352,128]{1,0:T(8,128)(2,1)}, s16[352,128]{1,0:T(8,128)(2,1)S(1)}, u32[]{:S(2)}, u32[]{:S(2)}) %collective-permute-start.8) | collective-permute-done | bytes 90144 | tf_op jit(solution)/shard_map/ppermute | solution.py:545
  82.1 0.3 collective-permute-done.13.refs_6_
  82.4 1.0 %collective-permute-done.12.refs_5_ = s16[352,128]{1,0:T(8,128)(2,1)S(1)} collective-permute-done((s16[352,128]{1,0:T(8,128)(2,1)S(1)}, s16[352,128]{1,0:T(8,128)(2,1)S(1)}, u32[]{:S(2)}, u32[]{:S(2)}) %collective-permute-start.12) | collective-permute-done | bytes 90144 | tf_op jit(solution)/shard_map/ppermute | solution.py:545
  83.4 0.9 %copy-done.1 = s16[352,128]{1,0:T(8,128)(2,1)S(1)} copy-done((s16[352,128]{1,0:T(8,128)(2,1)S(1)}, s16[352,128]{1,0:T(8,128)(2,1)}, u32[]{:S(2)}) %copy-start.1) | copy-done | bytes 90136
  84.3 1.8 %unpack.1 = (f32[5,1,128]{2,1,0:T(1,128)}, f32[64,512]{1,0:T(8,128)}, f32[3,512]{1,0:T(4,128)}, f32[1,512]{1,0:T(1,128)}, f32[512,512]{1,0:T(8,128)}, /*index=5*...) custom-call(s32[3]{0:T(128)S(1)} %pad_add_fusion.place_ref, s16[352,128]{1,0:T(8,128)(2,1)S(1)} %copy-done.1, ...), custom_call_target="tpu_custom_call" | custom-call | tf_op jit(solution)/shard_map/unpack/pallas_call | solution.py:720
  (34 shorter events, 0.1 us)
Async XLA Ops:
  2.4 14.7 %copy-start.16 = (f32[64]{0:T(128)S(1)}, f32[64]{0:T(128)}, u32[]{:S(2)}) copy-start(f32[64]{0:T(128)} %param.16) | copy-start | bytes 772
  2.4 14.8 %copy-start.10 = (bf16[64,1728]{1,0:T(8,128)(2,1)S(1)}, bf16[64,1728]{1,0:T(8,128)(2,1)}, u32[]{:S(2)}) copy-start(bf16[64,1728]{1,0:T(8,128)(2,1)} %param.15) | copy-start | bytes 663556
  2.4 19.6 %all-to-all-start = ((f32[16,16,128]{2,1,0:T(8,128)}), f32[16,16,128]{2,1,0:T(8,128)S(1)}, u32[]{:S(2)}, u32[]{:S(2)}) async-start(f32[16,16,128]{2,1,0:T(8,128)} %bitcast.31), calls=%async_computation | async-start | bytes 262144 | tf_op jit(solution)/shard_map/all_to_all | solution.py:767
  11.9 10.1 %collective-permute-start = (bf16[2,8,64,128]{3,2,1,0:T(8,128)(2,1)}, bf16[2,8,64,128]{3,2,1,0:T(8,128)(2,1)}, u32[]{:S(2)}, u32[]{:S(2)}) collective-permute-start(bf16[2,8,64,128]{3,2,1,0:T(8,128)(2,1)} %slice.8), channel_id=1, source_target_pairs={{0,1},{1,2},{2,3},{3,4},{4,5},{5,6},{6,7},{7,8},{8,9},{9,10},{10,1... | collective-permute-start | bytes 786440 | tf_op jit(solution)/shard_map/ppermute | solution.py:774
  13.1 9.6 %collective-permute-start.1 = (bf16[3,8,64,128]{3,2,1,0:T(8,128)(2,1)}, bf16[3,8,64,128]{3,2,1,0:T(8,128)(2,1)}, u32[]{:S(2)}, u32[]{:S(2)}) collective-permute-start(bf16[3,8,64,128]{3,2,1,0:T(8,128)(2,1)} %slice.9), channel_id=1, source_target_pairs={{1,0},{2,1},{3,2},{4,3},{5,4},{6,5},{7,6},{8,7},{9,8},{10,9},{11,1... | collective-permute-start | bytes 1179656 | tf_op jit(solution)/shard_map/ppermute | solution.py:775
  17.2 1.1 %copy-start.4 = (f32[5,512]{1,0:T(8,128)S(1)}, f32[5,512]{1,0:T(8,128)}, u32[]{:S(2)}) copy-start(f32[5,512]{1,0:T(8,128)} %w_out_ref.1) | copy-start | bytes 30724
  17.2 1.1 %copy-start.5 = (f32[3,512]{1,0:T(4,128)S(1)}, f32[3,512]{1,0:T(4,128)}, u32[]{:S(2)}) copy-start(f32[3,512]{1,0:T(4,128)} %w_pos_ref.1) | copy-start | bytes 18436
  17.2 1.1 %copy-start.6 = (f32[512]{0:T(512)S(1)}, f32[512]{0:T(512)}, u32[]{:S(2)}) copy-start(f32[512]{0:T(512)} %param.23) | copy-start | bytes 6148
  17.2 1.1 %copy-start.7 = (f32[512]{0:T(512)S(1)}, f32[512]{0:T(512)}, u32[]{:S(2)}) copy-start(f32[512]{0:T(512)} %param.25) | copy-start | bytes 6148
  17.2 1.1 %copy-start.8 = (f32[5]{0:T(128)S(1)}, f32[5]{0:T(128)}, u32[]{:S(2)}) copy-start(f32[5]{0:T(128)} %param.27) | copy-start | bytes 64
  18.3 1.2 %copy-start.2 = (f32[512,512]{1,0:T(8,128)S(1)}, f32[512,512]{1,0:T(8,128)}, u32[]{:S(2)}) copy-start(f32[512,512]{1,0:T(8,128)} %w_mid_ref.1) | copy-start | bytes 3145732
  19.6 0.9 %copy-start.3 = (f32[64,512]{1,0:T(8,128)S(1)}, f32[64,512]{1,0:T(8,128)}, u32[]{:S(2)}) copy-start(f32[64,512]{1,0:T(8,128)} %w_latent_ref.1) | copy-start | bytes 393220
  40.9 0.8 copy-start
  41.8 3.8 %collective-permute-start.2 = (f32[4,328,128]{2,1,0:T(8,128)S(1)}, f32[4,328,128]{2,1,0:T(8,128)S(1)}, u32[]{:S(2)}, u32[]{:S(2)}) collective-permute-start(f32[4,328,128]{2,1,0:T(8,128)S(1)} %get-tuple-element.41), channel_id=1, source_target_pairs={{0,1},{1,0},{2,3},{3,2},{4,5},{5,4},{6,7},{7,6},{8,9},{9,8},{10,11... | collective-permute-start | bytes 2015240 | tf_op jit(solution)/shard_map/ppermute | solution.py:545
  45.6 0.9 %copy-start.9 = (f32[4,328,128]{2,1,0:T(8,128)}, f32[4,328,128]{2,1,0:T(8,128)S(1)}, u32[]{:S(2)}) copy-start(f32[4,328,128]{2,1,0:T(8,128)S(1)} %collective-permute-done.2.got_ref) | copy-start | bytes 2015236
  48.6 5.1 %collective-permute-start.3 = (s16[352,128]{1,0:T(8,128)(2,1)}, s16[352,128]{1,0:T(8,128)(2,1)S(1)}, u32[]{:S(2)}, u32[]{:S(2)}) collective-permute-start(s16[352,128]{1,0:T(8,128)(2,1)} %get-tuple-element.43), channel_id=1, source_target_pairs={{0,2},{1,3},{2,0},{3,1},{4,6},{5,7},{6,4},{7,5},{8,10},{9,11},{10,... | collective-permute-start | bytes 270344 | tf_op jit(solution)/shard_map/ppermute | solution.py:545
  48.7 5.0 %collective-permute-start.4 = (s16[352,128]{1,0:T(8,128)(2,1)}, s16[352,128]{1,0:T(8,128)(2,1)S(1)}, u32[]{:S(2)}, u32[]{:S(2)}) collective-permute-start(s16[352,128]{1,0:T(8,128)(2,1)} %get-tuple-element.44), channel_id=1, source_target_pairs={{0,16},{1,17},{2,18},{3,19},{4,20},{5,21},{6,22},{7,23},{8,24},{9,... | collective-permute-start | bytes 270344 | tf_op jit(solution)/shard_map/ppermute | solution.py:545
  50.2 6.6 %collective-permute-start.5 = (s16[352,128]{1,0:T(8,128)(2,1)}, s16[352,128]{1,0:T(8,128)(2,1)S(1)}, u32[]{:S(2)}, u32[]{:S(2)}) collective-permute-start(s16[352,128]{1,0:T(8,128)(2,1)} %get-tuple-element.45), channel_id=1, source_target_pairs={{0,18},{1,19},{2,16},{3,17},{4,22},{5,23},{6,20},{7,21},{8,26},{9,... | collective-permute-start | bytes 270344 | tf_op jit(solution)/shard_map/ppermute | solution.py:545
  53.7 3.1 %copy-start.13 = (s16[352,128]{1,0:T(8,128)(2,1)}, s16[352,128]{1,0:T(8,128)(2,1)S(1)}, u32[]{:S(2)}) copy-start(s16[352,128]{1,0:T(8,128)(2,1)S(1)} %collective-permute-done.3.refs_0_) | copy-start | bytes 270340
  53.7 3.1 %copy-start.14 = (s16[352,128]{1,0:T(8,128)(2,1)}, s16[352,128]{1,0:T(8,128)(2,1)S(1)}, u32[]{:S(2)}) copy-start(s16[352,128]{1,0:T(8,128)(2,1)S(1)} %collective-permute-done.4.refs_1_) | copy-start | bytes 270340
  56.8 0.6 copy-start.15
  59.2 4.7 %collective-permute-start.6 = (s16[352,128]{1,0:T(8,128)(2,1)}, s16[352,128]{1,0:T(8,128)(2,1)S(1)}, u32[]{:S(2)}, u32[]{:S(2)}) collective-permute-start(s16[352,128]{1,0:T(8,128)(2,1)} %sum_plane.1.mine_ref), channel_id=1, source_target_pairs={{0,4},{1,5},{2,6},{3,7},{4,0},{5,1},{6,2},{7,3},{8,12},{9,13},{10,... | collective-permute-start | bytes 270344 | tf_op jit(solution)/shard_map/ppermute | solution.py:545
  64.0 0.6 copy-start.11
  66.3 6.2 %collective-permute-start.7 = (s16[352,128]{1,0:T(8,128)(2,1)}, s16[352,128]{1,0:T(8,128)(2,1)S(1)}, u32[]{:S(2)}, u32[]{:S(2)}) collective-permute-start(s16[352,128]{1,0:T(8,128)(2,1)} %sum_line.2.mine_ref), channel_id=1, source_target_pairs={{0,8},{1,9},{2,10},{3,11},{4,12},{5,13},{6,14},{7,15},{8,0},{9,1},... | collective-permute-start | bytes 270344 | tf_op jit(solution)/shard_map/ppermute | solution.py:545
  72.5 0.6 copy-start.12
  74.8 5.6 %collective-permute-start.10 = (s16[352,128]{1,0:T(8,128)(2,1)}, s16[352,128]{1,0:T(8,128)(2,1)S(1)}, u32[]{:S(2)}, u32[]{:S(2)}) collective-permute-start(s16[352,128]{1,0:T(8,128)(2,1)} %sum_line.3.refs_0_), channel_id=1, source_target_pairs={{0,18},{1,19},{2,16},{3,17},{4,22},{5,23},{6,20},{7,21},{8,26},{9,... | collective-permute-start | bytes 270344 | tf_op jit(solution)/shard_map/ppermute | solution.py:545
  76.4 4.7 %collective-permute-start.9 = (s16[352,128]{1,0:T(8,128)(2,1)}, s16[352,128]{1,0:T(8,128)(2,1)S(1)}, u32[]{:S(2)}, u32[]{:S(2)}) collective-permute-start(s16[352,128]{1,0:T(8,128)(2,1)} %sum_line.3.refs_0_), channel_id=1, source_target_pairs={{0,16},{1,17},{2,18},{3,19},{4,20},{5,21},{6,22},{7,23},{8,24},{9,... | collective-permute-start | bytes 270344 | tf_op jit(solution)/shard_map/ppermute | solution.py:545
  77.4 4.7 %collective-permute-start.8 = (s16[352,128]{1,0:T(8,128)(2,1)}, s16[352,128]{1,0:T(8,128)(2,1)S(1)}, u32[]{:S(2)}, u32[]{:S(2)}) collective-permute-start(s16[352,128]{1,0:T(8,128)(2,1)} %sum_line.3.refs_0_), channel_id=1, source_target_pairs={{0,2},{1,3},{2,0},{3,1},{4,6},{5,7},{6,4},{7,5},{8,10},{9,11},{10,... | collective-permute-start | bytes 270344 | tf_op jit(solution)/shard_map/ppermute | solution.py:545
  78.3 3.8 %collective-permute-start.11 = (s16[352,128]{1,0:T(8,128)(2,1)}, s16[352,128]{1,0:T(8,128)(2,1)S(1)}, u32[]{:S(2)}, u32[]{:S(2)}) collective-permute-start(s16[352,128]{1,0:T(8,128)(2,1)} %sum_line.3.refs_0_), channel_id=1, source_target_pairs={{0,1},{1,0},{2,3},{3,2},{4,5},{5,4},{6,7},{7,6},{8,9},{9,8},{10,11... | collective-permute-start | bytes 270344 | tf_op jit(solution)/shard_map/ppermute | solution.py:545
  80.5 1.7 %collective-permute-start.14 = (s16[352,128]{1,0:T(8,128)(2,1)S(1)}, s16[352,128]{1,0:T(8,128)(2,1)S(1)}, u32[]{:S(2)}, u32[]{:S(2)}) collective-permute-start(s16[352,128]{1,0:T(8,128)(2,1)S(1)} %collective-permute-done.10.refs_3_), channel_id=1, source_target_pairs={{0,1},{1,0},{2,3},{3,2},{4,5},{5,4},{6,7},{7,6},{8,9},{9,8},{10,11... | collective-permute-start | bytes 270344 | tf_op jit(solution)/shard_map/ppermute | solution.py:545
  81.2 1.3 %collective-permute-start.13 = (s16[352,128]{1,0:T(8,128)(2,1)S(1)}, s16[352,128]{1,0:T(8,128)(2,1)S(1)}, u32[]{:S(2)}, u32[]{:S(2)}) collective-permute-start(s16[352,128]{1,0:T(8,128)(2,1)S(1)} %collective-permute-done.9.refs_2_), channel_id=1, source_target_pairs={{0,1},{1,0},{2,3},{3,2},{4,5},{5,4},{6,7},{7,6},{8,9},{9,8},{10,11... | collective-permute-start | bytes 270344 | tf_op jit(solution)/shard_map/ppermute | solution.py:545
  82.1 1.3 %collective-permute-start.12 = (s16[352,128]{1,0:T(8,128)(2,1)S(1)}, s16[352,128]{1,0:T(8,128)(2,1)S(1)}, u32[]{:S(2)}, u32[]{:S(2)}) collective-permute-start(s16[352,128]{1,0:T(8,128)(2,1)S(1)} %collective-permute-done.8.refs_1_), channel_id=1, source_target_pairs={{0,1},{1,0},{2,3},{3,2},{4,5},{5,4},{6,7},{7,6},{8,9},{9,8},{10,11... | collective-permute-start | bytes 270344 | tf_op jit(solution)/shard_map/ppermute | solution.py:545
  83.4 0.9 %copy-start.1 = (s16[352,128]{1,0:T(8,128)(2,1)S(1)}, s16[352,128]{1,0:T(8,128)(2,1)}, u32[]{:S(2)}) copy-start(s16[352,128]{1,0:T(8,128)(2,1)} %sum_line.3.refs_0_) | copy-start | bytes 270340

commit v4 on v3

--- a/solution.py
+++ b/solution.py
@@ -76,6 +76,7 @@
         in_specs=[VMEM] * 4,
         out_specs=VMEM,
         scratch_shapes=[pltpu.VMEM((WORDS, queries), F32)],
+        compiler_params=pltpu.CompilerParams(vmem_limit_bytes=4 << 20),
         name="route",
     )(owner, cell, frac, target)
 
@@ -614,6 +615,7 @@
         out_shape=(jax.ShapeDtypeStruct(keep.shape[1:], F32), sent, sent, sent),
         in_specs=[VMEM] * 2,
         out_specs=tuple([VMEM] * 4),
+        compiler_params=pltpu.CompilerParams(vmem_limit_bytes=6 << 20),
         name="sum_core",
     )(keep, got)
 
@@ -633,6 +635,7 @@
         out_shape=jax.ShapeDtypeStruct((plan.sent_rows, LANES), jnp.int16),
         in_specs=[VMEM] * len(blocks),
         out_specs=VMEM,
+        compiler_params=pltpu.CompilerParams(vmem_limit_bytes=4 << 20),
         name=name,
     )(*blocks)
 
@@ -665,7 +668,7 @@
             pltpu.VMEM((40, rows), F32),
             pltpu.VMEM((8, plan.rows, LANES), F32),
         ],
-        compiler_params=pltpu.CompilerParams(vmem_limit_bytes=48 << 20),
+        compiler_params=pltpu.CompilerParams(vmem_limit_bytes=32 << 20),
         name="encode_decode",
     )(place, left, right, partial, taps, words, *weights)
 
@@ -755,6 +758,12 @@
     device = my_replica * tiles + my_tile
     place = jnp.stack([plan.my_block(device), my_tile, my_replica]).astype(jnp.int32)
 
+    here = fields[0].transpose(1, 2, 0, 3)
+    here, query_owner = lax.optimization_barrier((here, query_owner))
+    up = [(i, (i + 1) % tiles) for i in range(tiles)]
+    down = [((i + 1) % tiles, i) for i in range(tiles)]
+    left = lax.ppermute(here[-DILATION_RATE:], "tile", up)
+    right = lax.ppermute(here[: DILATION_RATE + 1], "tile", down)
     words = route(
         query_owner[:, :, 0],
         query_cell,
@@ -763,16 +772,10 @@
         tiles,
         plan.slots,
     )
-    words, fields = lax.optimization_barrier((words, fields))
     words = lax.all_to_all(
         words.reshape(tiles, plan.slots, WORDS), "tile", split_axis=0, concat_axis=0, tiled=True
     ).reshape(tiles * plan.slots, WORDS)
 
-    here = fields[0].transpose(1, 2, 0, 3)
-    up = [(i, (i + 1) % tiles) for i in range(tiles)]
-    down = [((i + 1) % tiles, i) for i in range(tiles)]
-    left = lax.ppermute(here[-DILATION_RATE:], "tile", up)
-    right = lax.ppermute(here[: DILATION_RATE + 1], "tile", down)
     taps = convolution_weight.reshape(channels, 3, 3, 3, channels)
     taps = taps.transpose(1, 3, 0, 2, 4).reshape(3, 3 * channels, 3 * channels)
     params = (w_latent, w_pos, bias_one[None], w_mid, bias_two[None], w_out, bias_out[None])

time: 86.6 us -> 76.7 us (0.89)
  Pallas kernels: 30.5 us -> 22.9 us
  local copies, waits for them, and re-layouts: 10.4 us -> 8.64 us
  waiting for transfers between devices: 22 us -> 20.9 us
    pallas_call x3, Pallas kernels: 5.16 us -> 0.34 us  [coded_sum(): pl.pallas_call(functools.partial(kernel, plan), out_shape=jax.ShapeDtypeS...]
    pallas_call x1, Pallas kernels: 2.14 us -> 0.16 us  [first_sum(): pl.pallas_call(functools.partial(first_kernel, plan), out_shape=(jax.Shap...]
    optimization_barrier x1 -> x0, local copies, waits for them, and re-layouts: 1.25 us -> none  [body(): words, fields = lax.optimization_barrier((words, fields))]
    ppermute x13, waiting for transfers between devices: 21.2 us -> 20.1 us  [swapped(): lax.ppermute(value, ('replica', 'tile'), [(i, i ^ mask) for i in range(pl...]
    unnamed x34 -> x27, local copies, waits for them, and re-layouts: 6.66 us -> 6.12 us
  transfers between devices with their start and end apart: 16 -> 16, of which waited for: 11 -> 13; matrix products, arithmetic and copies ran while one was open for 4% -> 3% of each run, Pallas kernels for 2% -> 2%
where the time goes in v4:
time: 76.7 us; the launch traced here: 76.3 us
  Pallas kernels  22.9 us (30%)
  starting transfers between devices  22.9 us (30%)
  waiting for transfers between devices  20.9 us (27%)
  local copies, waits for them, and re-layouts  8.64 us (11%)
  between operations  0.85 us (1%)
    ppermute x13, waiting for transfers between devices, swapped(): lax.ppermute(value, ('replica', 'tile'), [(i, i ^ mask) for i in range(pl...  20.1 us
    pallas_call x1, Pallas kernels, main(): pl.pallas_call(functools.partial(main_kernel, plan), out_shape=(outs, out...  18.1 us
    ppermute x13, starting transfers between devices, swapped(): lax.ppermute(value, ('replica', 'tile'), [(i, i ^ mask) for i in range(pl...  11.1 us
    all_to_all x1, starting transfers between devices, body(): lax.all_to_all(words.reshape(tiles, plan.slots, WORDS), 'tile', split_axi...  7.39 us
    unnamed x27, local copies, waits for them, and re-layouts  6.12 us
    ppermute x1, starting transfers between devices, body(): right = lax.ppermute(here[:DILATION_RATE + 1], 'tile', down)  4.03 us
    pallas_call x1, Pallas kernels, unpack(): pl.pallas_call(functools.partial(unpack_kernel, plan), out_shape=tuple((j...  1.83 us
  transfers between devices with their start and end apart: 16, of which 13 were waited for; matrix products, arithmetic and copies ran while one was open for 3% of the time, Pallas kernels for 2%

profile of v4, /device:TPU:0, one launch (start us, length us, event | category | flops | bytes accessed | tf_op | source)
XLA Modules:
  0.0 76.3 jit_solution(14745298671314720273)
XLA Ops:
  0.7 1.3 %copy.30 = bf16[1,64,4,8,128]{4,1,3,2,0:T(8,128)(2,1)S(1)} copy(bf16[1,64,4,8,128]{4,3,2,1,0:T(8,128)(2,1)} %param.14) | data formatting | bytes 1048576 | tf_op args[0]
  2.0 0.7 copy-done
  2.6 0.7 copy-done.1
  3.3 0.7 copy-done.2
  4.0 0.7 copy-done.3
  4.6 1.0 %route.1 = f32[256,128]{1,0:T(8,128)} custom-call(s32[1,128]{1,0:T(1,128)S(1)} %bitcast.29, s32[1,128]{1,0:T(1,128)S(1)} %copy-done.3, f32[3,1,128]{2,1,0:T(1,128)S(1)} %bitcast.28, f32[5,1,128]{2,1,0:T(1,128)S(1)} %bitcast.27), custom_call_target="tpu_custom_call" | custom-call | tf_op jit(solution)/shard_map/route/pallas_call | solution.py:73
  5.6 7.4 %all-to-all-start = ((f32[16,16,128]{2,1,0:T(8,128)}), f32[16,16,128]{2,1,0:T(8,128)S(1)}, u32[]{:S(2)}, u32[]{:S(2)}) async-start(f32[16,16,128]{2,1,0:T(8,128)} %bitcast.13), calls=%async_computation | async-start | bytes 262144 | tf_op jit(solution)/shard_map/all_to_all | solution.py:775
  13.0 0.7 slice.6
  13.7 0.4 collective-permute-start
  14.1 0.8 %slice.7 = bf16[3,8,64,128]{3,2,1,0:T(8,128)(2,1)} slice(bf16[4,8,64,128]{3,2,1,0:T(8,128)(2,1)S(1)} %bitcast.24), slice={[0:3], [0:8], [0:64], [0:128]} | slice | bytes 786432 | tf_op jit(solution)/shard_map/slice | solution.py:766
  14.9 4.0 %collective-permute-start.1 = (bf16[3,8,64,128]{3,2,1,0:T(8,128)(2,1)}, bf16[3,8,64,128]{3,2,1,0:T(8,128)(2,1)}, u32[]{:S(2)}, u32[]{:S(2)}) collective-permute-start(bf16[3,8,64,128]{3,2,1,0:T(8,128)(2,1)} %slice.7), channel_id=1, source_target_pairs={{1,0},{2,1},{3,2},{4,3},{5,4},{6,5},{7,6},{8,7},{9,8},{10,9},{11,1... | collective-permute-start | bytes 1179656 | tf_op jit(solution)/shard_map/ppermute | solution.py:766
  18.9 0.1 copy.28.bias_ref
  19.1 0.0 copy-start.8
  19.1 0.3 reshape.42
  19.4 0.3 copy.27
  19.7 0.4 reshape.43.weight_ref.conv_weight_ref
  20.1 0.1 pad_add_fusion.place_ref
  20.2 1.2 %copy-done.4 = f32[512,512]{1,0:T(8,128)S(1)} copy-done((f32[512,512]{1,0:T(8,128)S(1)}, f32[512,512]{1,0:T(8,128)}, u32[]{:S(2)}) %copy-start.4) | copy-done | bytes 1048600
  21.4 0.9 %copy-done.5 = f32[64,512]{1,0:T(8,128)S(1)} copy-done((f32[64,512]{1,0:T(8,128)S(1)}, f32[64,512]{1,0:T(8,128)}, u32[]{:S(2)}) %copy-start.5) | copy-done | bytes 131096
  22.3 1.5 %conv_local.1 = (f32[20,64,256]{2,1,0:T(8,128)S(1)}, bf16[64,512]{1,0:T(8,128)(2,1)S(1)}, bf16[64,512]{1,0:T(8,128)(2,1)S(1)}, bf16[512,512]{1,0:T(8,128)(2,1)S(...) custom-call(bf16[4,8,64,128]{3,2,1,0:T(8,128)(2,1)S(1)} %bitcast.25, ...), custom_call_target="tpu_custom_call" | custom-call | flops 3221225472 | bytes 4194304 | tf_op jit(solution)/shard_map/conv_local/pallas_call | solution.py:154
  23.8 0.1 collective-permute-done.left_ref
  23.9 0.6 collective-permute-done.1.right_ref
  24.6 18.1 %encode_decode.1 = (f32[4,328,128]{2,1,0:T(8,128)S(1)}, f32[4,328,128]{2,1,0:T(8,128)S(1)}) custom-call(s32[3]{0:T(128)S(1)} %pad_add_fusion.place_ref, bf16[2,8,64,128]{3,2,1,0:T(8,128)(2,1)} %collective-permute-done.left_ref, bf16[3,8,64,128]{3,2,1,0:T(8,128)(2,1)} %collective-permute-done.1.right_ref, f32[20,64,256]{2,1,0:T(8,128)S(1)} %get-tuple-element.33.partial_ref, ...), custom_call_target="tpu_custom_call" | custom-call | tf_op jit(solution)/shard_map/encode_decode/pallas_call | solution.py:649
  42.7 2.7 %collective-permute-start.2 = (f32[4,328,128]{2,1,0:T(8,128)S(1)}, f32[4,328,128]{2,1,0:T(8,128)S(1)}, u32[]{:S(2)}, u32[]{:S(2)}) collective-permute-start(f32[4,328,128]{2,1,0:T(8,128)S(1)} %get-tuple-element.41), channel_id=1, source_target_pairs={{0,1},{1,0},{2,3},{3,2},{4,5},{5,4},{6,7},{7,6},{8,9},{9,8},{10,11... | collective-permute-start | bytes 2015240 | tf_op jit(solution)/shard_map/ppermute | solution.py:546
  45.3 1.7 %collective-permute-done.2.got_ref = f32[4,328,128]{2,1,0:T(8,128)S(1)} collective-permute-done((f32[4,328,128]{2,1,0:T(8,128)S(1)}, f32[4,328,128]{2,1,0:T(8,128)S(1)}, u32[]{:S(2)}, u32[]{:S(2)}) %collective-permute-start.2) | collective-permute-done | bytes 671776 | tf_op jit(solution)/shard_map/ppermute | solution.py:546
  47.1 0.2 sum_core.1
  47.2 0.2 collective-permute-start.3
  47.4 1.5 %collective-permute-start.4 = (s16[352,128]{1,0:T(8,128)(2,1)S(1)}, s16[352,128]{1,0:T(8,128)(2,1)S(1)}, u32[]{:S(2)}, u32[]{:S(2)}) collective-permute-start(s16[352,128]{1,0:T(8,128)(2,1)S(1)} %get-tuple-element.44), channel_id=1, source_target_pairs={{0,16},{1,17},{2,18},{3,19},{4,20},{5,21},{6,22},{7,23},{8,24},{9,... | collective-permute-start | bytes 270344 | tf_op jit(solution)/shard_map/ppermute | solution.py:546
  48.9 1.9 %collective-permute-start.5 = (s16[352,128]{1,0:T(8,128)(2,1)S(1)}, s16[352,128]{1,0:T(8,128)(2,1)S(1)}, u32[]{:S(2)}, u32[]{:S(2)}) collective-permute-start(s16[352,128]{1,0:T(8,128)(2,1)S(1)} %get-tuple-element.45), channel_id=1, source_target_pairs={{0,18},{1,19},{2,16},{3,17},{4,22},{5,23},{6,20},{7,21},{8,26},{9,... | collective-permute-start | bytes 270344 | tf_op jit(solution)/shard_map/ppermute | solution.py:546
  50.8 1.4 %collective-permute-done.3.refs_0_ = s16[352,128]{1,0:T(8,128)(2,1)S(1)} collective-permute-done((s16[352,128]{1,0:T(8,128)(2,1)S(1)}, s16[352,128]{1,0:T(8,128)(2,1)S(1)}, u32[]{:S(2)}, u32[]{:S(2)}) %collective-permute-start.3) | collective-permute-done | bytes 90144 | tf_op jit(solution)/shard_map/ppermute | solution.py:546
  52.2 0.1 collective-permute-done.4.refs_1_
  52.3 3.0 %collective-permute-done.5.refs_2_ = s16[352,128]{1,0:T(8,128)(2,1)S(1)} collective-permute-done((s16[352,128]{1,0:T(8,128)(2,1)S(1)}, s16[352,128]{1,0:T(8,128)(2,1)S(1)}, u32[]{:S(2)}, u32[]{:S(2)}) %collective-permute-start.5) | collective-permute-done | bytes 90144 | tf_op jit(solution)/shard_map/ppermute | solution.py:546
  55.3 0.1 sum_plane.1.mine_ref
  55.5 0.1 collective-permute-start.6
  55.5 4.5 %collective-permute-done.6.other_ref = s16[352,128]{1,0:T(8,128)(2,1)S(1)} collective-permute-done((s16[352,128]{1,0:T(8,128)(2,1)S(1)}, s16[352,128]{1,0:T(8,128)(2,1)S(1)}, u32[]{:S(2)}, u32[]{:S(2)}) %collective-permute-start.6) | collective-permute-done | bytes 90144 | tf_op jit(solution)/shard_map/ppermute | solution.py:546
  60.1 0.1 sum_line.2.mine_ref
  60.2 1.3 %collective-permute-start.7 = (s16[352,128]{1,0:T(8,128)(2,1)S(1)}, s16[352,128]{1,0:T(8,128)(2,1)S(1)}, u32[]{:S(2)}, u32[]{:S(2)}) collective-permute-start(s16[352,128]{1,0:T(8,128)(2,1)S(1)} %sum_line.2.mine_ref), channel_id=1, source_target_pairs={{0,8},{1,9},{2,10},{3,11},{4,12},{5,13},{6,14},{7,15},{8,0},{9,1},... | collective-permute-start | bytes 270344 | tf_op jit(solution)/shard_map/ppermute | solution.py:546
  61.4 4.6 %collective-permute-done.7.other_ref = s16[352,128]{1,0:T(8,128)(2,1)S(1)} collective-permute-done((s16[352,128]{1,0:T(8,128)(2,1)S(1)}, s16[352,128]{1,0:T(8,128)(2,1)S(1)}, u32[]{:S(2)}, u32[]{:S(2)}) %collective-permute-start.7) | collective-permute-done | bytes 90144 | tf_op jit(solution)/shard_map/ppermute | solution.py:546
  66.1 0.1 sum_line.3.refs_0_
  66.2 1.7 %collective-permute-start.10 = (s16[352,128]{1,0:T(8,128)(2,1)S(1)}, s16[352,128]{1,0:T(8,128)(2,1)S(1)}, u32[]{:S(2)}, u32[]{:S(2)}) collective-permute-start(s16[352,128]{1,0:T(8,128)(2,1)S(1)} %sum_line.3.refs_0_), channel_id=1, source_target_pairs={{0,18},{1,19},{2,16},{3,17},{4,22},{5,23},{6,20},{7,21},{8,26},{9,... | collective-permute-start | bytes 270344 | tf_op jit(solution)/shard_map/ppermute | solution.py:546
  67.9 0.8 collective-permute-start.9
  68.7 1.1 %collective-permute-start.8 = (s16[352,128]{1,0:T(8,128)(2,1)S(1)}, s16[352,128]{1,0:T(8,128)(2,1)S(1)}, u32[]{:S(2)}, u32[]{:S(2)}) collective-permute-start(s16[352,128]{1,0:T(8,128)(2,1)S(1)} %sum_line.3.refs_0_), channel_id=1, source_target_pairs={{0,2},{1,3},{2,0},{3,1},{4,6},{5,7},{6,4},{7,5},{8,10},{9,11},{10,... | collective-permute-start | bytes 270344 | tf_op jit(solution)/shard_map/ppermute | solution.py:546
  69.7 1.9 %collective-permute-done.10.refs_3_ = s16[352,128]{1,0:T(8,128)(2,1)S(1)} collective-permute-done((s16[352,128]{1,0:T(8,128)(2,1)S(1)}, s16[352,128]{1,0:T(8,128)(2,1)S(1)}, u32[]{:S(2)}, u32[]{:S(2)}) %collective-permute-start.10) | collective-permute-done | bytes 90144 | tf_op jit(solution)/shard_map/ppermute | solution.py:546
  71.7 0.7 collective-permute-done.9.refs_2_
  72.4 0.8 collective-permute-done.8.refs_1_
  73.2 0.5 collective-permute-done.13.refs_6_
  73.7 0.8 collective-permute-done.12.refs_5_
  74.5 1.8 %unpack.1 = (f32[5,1,128]{2,1,0:T(1,128)}, f32[64,512]{1,0:T(8,128)}, f32[3,512]{1,0:T(4,128)}, f32[1,512]{1,0:T(1,128)}, f32[512,512]{1,0:T(8,128)}, /*index=5*...) custom-call(s32[3]{0:T(128)S(1)} %pad_add_fusion.place_ref, ...), custom_call_target="tpu_custom_call" | custom-call | tf_op jit(solution)/shard_map/unpack/pallas_call | solution.py:723
  (26 shorter events, 0.1 us)
Async XLA Ops:
  0.6 18.3 %copy-start.12 = (f32[64]{0:T(128)S(1)}, f32[64]{0:T(128)}, u32[]{:S(2)}) copy-start(f32[64]{0:T(128)} %param.16) | copy-start | bytes 772
  0.7 18.4 %copy-start.11 = (bf16[64,1728]{1,0:T(8,128)(2,1)S(1)}, bf16[64,1728]{1,0:T(8,128)(2,1)}, u32[]{:S(2)}) copy-start(bf16[64,1728]{1,0:T(8,128)(2,1)} %param.15) | copy-start | bytes 663556
  2.0 0.7 copy-start
  2.6 0.7 copy-start.1
  3.3 0.7 copy-start.2
  4.0 0.7 copy-start.3
  5.6 18.2 %all-to-all-start = ((f32[16,16,128]{2,1,0:T(8,128)}), f32[16,16,128]{2,1,0:T(8,128)S(1)}, u32[]{:S(2)}, u32[]{:S(2)}) async-start(f32[16,16,128]{2,1,0:T(8,128)} %bitcast.13), calls=%async_computation | async-start | bytes 262144 | tf_op jit(solution)/shard_map/all_to_all | solution.py:775
  13.7 10.2 %collective-permute-start = (bf16[2,8,64,128]{3,2,1,0:T(8,128)(2,1)}, bf16[2,8,64,128]{3,2,1,0:T(8,128)(2,1)}, u32[]{:S(2)}, u32[]{:S(2)}) collective-permute-start(bf16[2,8,64,128]{3,2,1,0:T(8,128)(2,1)} %slice.6), channel_id=1, source_target_pairs={{0,1},{1,2},{2,3},{3,4},{4,5},{5,6},{6,7},{7,8},{8,9},{9,10},{10,1... | collective-permute-start | bytes 786440 | tf_op jit(solution)/shard_map/ppermute | solution.py:765
  14.9 9.6 %collective-permute-start.1 = (bf16[3,8,64,128]{3,2,1,0:T(8,128)(2,1)}, bf16[3,8,64,128]{3,2,1,0:T(8,128)(2,1)}, u32[]{:S(2)}, u32[]{:S(2)}) collective-permute-start(bf16[3,8,64,128]{3,2,1,0:T(8,128)(2,1)} %slice.7), channel_id=1, source_target_pairs={{1,0},{2,1},{3,2},{4,3},{5,4},{6,5},{7,6},{8,7},{9,8},{10,9},{11,1... | collective-permute-start | bytes 1179656 | tf_op jit(solution)/shard_map/ppermute | solution.py:766
  19.0 1.1 %copy-start.6 = (f32[5,512]{1,0:T(8,128)S(1)}, f32[5,512]{1,0:T(8,128)}, u32[]{:S(2)}) copy-start(f32[5,512]{1,0:T(8,128)} %w_out_ref.1) | copy-start | bytes 30724
  19.1 1.1 %copy-start.7 = (f32[3,512]{1,0:T(4,128)S(1)}, f32[3,512]{1,0:T(4,128)}, u32[]{:S(2)}) copy-start(f32[3,512]{1,0:T(4,128)} %w_pos_ref.1) | copy-start | bytes 18436
  19.1 1.1 %copy-start.8 = (f32[512]{0:T(512)S(1)}, f32[512]{0:T(512)}, u32[]{:S(2)}) copy-start(f32[512]{0:T(512)} %param.23) | copy-start | bytes 6148
  19.1 1.1 %copy-start.9 = (f32[512]{0:T(512)S(1)}, f32[512]{0:T(512)}, u32[]{:S(2)}) copy-start(f32[512]{0:T(512)} %param.25) | copy-start | bytes 6148
  19.1 1.1 %copy-start.10 = (f32[5]{0:T(128)S(1)}, f32[5]{0:T(128)}, u32[]{:S(2)}) copy-start(f32[5]{0:T(128)} %param.27) | copy-start | bytes 64
  20.2 1.2 %copy-start.4 = (f32[512,512]{1,0:T(8,128)S(1)}, f32[512,512]{1,0:T(8,128)}, u32[]{:S(2)}) copy-start(f32[512,512]{1,0:T(8,128)} %w_mid_ref.1) | copy-start | bytes 3145732
  21.4 0.9 %copy-start.5 = (f32[64,512]{1,0:T(8,128)S(1)}, f32[64,512]{1,0:T(8,128)}, u32[]{:S(2)}) copy-start(f32[64,512]{1,0:T(8,128)} %w_latent_ref.1) | copy-start | bytes 393220
  42.7 4.4 %collective-permute-start.2 = (f32[4,328,128]{2,1,0:T(8,128)S(1)}, f32[4,328,128]{2,1,0:T(8,128)S(1)}, u32[]{:S(2)}, u32[]{:S(2)}) collective-permute-start(f32[4,328,128]{2,1,0:T(8,128)S(1)} %get-tuple-element.41), channel_id=1, source_target_pairs={{0,1},{1,0},{2,3},{3,2},{4,5},{5,4},{6,7},{7,6},{8,9},{9,8},{10,11... | collective-permute-start | bytes 2015240 | tf_op jit(solution)/shard_map/ppermute | solution.py:546
  47.2 5.0 %collective-permute-start.3 = (s16[352,128]{1,0:T(8,128)(2,1)S(1)}, s16[352,128]{1,0:T(8,128)(2,1)S(1)}, u32[]{:S(2)}, u32[]{:S(2)}) collective-permute-start(s16[352,128]{1,0:T(8,128)(2,1)S(1)} %get-tuple-element.43), channel_id=1, source_target_pairs={{0,2},{1,3},{2,0},{3,1},{4,6},{5,7},{6,4},{7,5},{8,10},{9,11},{10,... | collective-permute-start | bytes 270344 | tf_op jit(solution)/shard_map/ppermute | solution.py:546
  47.4 4.9 %collective-permute-start.4 = (s16[352,128]{1,0:T(8,128)(2,1)S(1)}, s16[352,128]{1,0:T(8,128)(2,1)S(1)}, u32[]{:S(2)}, u32[]{:S(2)}) collective-permute-start(s16[352,128]{1,0:T(8,128)(2,1)S(1)} %get-tuple-element.44), channel_id=1, source_target_pairs={{0,16},{1,17},{2,18},{3,19},{4,20},{5,21},{6,22},{7,23},{8,24},{9,... | collective-permute-start | bytes 270344 | tf_op jit(solution)/shard_map/ppermute | solution.py:546
  48.9 6.4 %collective-permute-start.5 = (s16[352,128]{1,0:T(8,128)(2,1)S(1)}, s16[352,128]{1,0:T(8,128)(2,1)S(1)}, u32[]{:S(2)}, u32[]{:S(2)}) collective-permute-start(s16[352,128]{1,0:T(8,128)(2,1)S(1)} %get-tuple-element.45), channel_id=1, source_target_pairs={{0,18},{1,19},{2,16},{3,17},{4,22},{5,23},{6,20},{7,21},{8,26},{9,... | collective-permute-start | bytes 270344 | tf_op jit(solution)/shard_map/ppermute | solution.py:546
  55.5 4.6 %collective-permute-start.6 = (s16[352,128]{1,0:T(8,128)(2,1)S(1)}, s16[352,128]{1,0:T(8,128)(2,1)S(1)}, u32[]{:S(2)}, u32[]{:S(2)}) collective-permute-start(s16[352,128]{1,0:T(8,128)(2,1)S(1)} %sum_plane.1.mine_ref), channel_id=1, source_target_pairs={{0,4},{1,5},{2,6},{3,7},{4,0},{5,1},{6,2},{7,3},{8,12},{9,13},{10,... | collective-permute-start | bytes 270344 | tf_op jit(solution)/shard_map/ppermute | solution.py:546
  60.2 5.9 %collective-permute-start.7 = (s16[352,128]{1,0:T(8,128)(2,1)S(1)}, s16[352,128]{1,0:T(8,128)(2,1)S(1)}, u32[]{:S(2)}, u32[]{:S(2)}) collective-permute-start(s16[352,128]{1,0:T(8,128)(2,1)S(1)} %sum_line.2.mine_ref), channel_id=1, source_target_pairs={{0,8},{1,9},{2,10},{3,11},{4,12},{5,13},{6,14},{7,15},{8,0},{9,1},... | collective-permute-start | bytes 270344 | tf_op jit(solution)/shard_map/ppermute | solution.py:546
  66.2 5.5 %collective-permute-start.10 = (s16[352,128]{1,0:T(8,128)(2,1)S(1)}, s16[352,128]{1,0:T(8,128)(2,1)S(1)}, u32[]{:S(2)}, u32[]{:S(2)}) collective-permute-start(s16[352,128]{1,0:T(8,128)(2,1)S(1)} %sum_line.3.refs_0_), channel_id=1, source_target_pairs={{0,18},{1,19},{2,16},{3,17},{4,22},{5,23},{6,20},{7,21},{8,26},{9,... | collective-permute-start | bytes 270344 | tf_op jit(solution)/shard_map/ppermute | solution.py:546
  67.9 4.5 %collective-permute-start.9 = (s16[352,128]{1,0:T(8,128)(2,1)S(1)}, s16[352,128]{1,0:T(8,128)(2,1)S(1)}, u32[]{:S(2)}, u32[]{:S(2)}) collective-permute-start(s16[352,128]{1,0:T(8,128)(2,1)S(1)} %sum_line.3.refs_0_), channel_id=1, source_target_pairs={{0,16},{1,17},{2,18},{3,19},{4,20},{5,21},{6,22},{7,23},{8,24},{9,... | collective-permute-start | bytes 270344 | tf_op jit(solution)/shard_map/ppermute | solution.py:546
  68.7 4.5 %collective-permute-start.8 = (s16[352,128]{1,0:T(8,128)(2,1)S(1)}, s16[352,128]{1,0:T(8,128)(2,1)S(1)}, u32[]{:S(2)}, u32[]{:S(2)}) collective-permute-start(s16[352,128]{1,0:T(8,128)(2,1)S(1)} %sum_line.3.refs_0_), channel_id=1, source_target_pairs={{0,2},{1,3},{2,0},{3,1},{4,6},{5,7},{6,4},{7,5},{8,10},{9,11},{10,... | collective-permute-start | bytes 270344 | tf_op jit(solution)/shard_map/ppermute | solution.py:546
  69.7 3.5 %collective-permute-start.11 = (s16[352,128]{1,0:T(8,128)(2,1)S(1)}, s16[352,128]{1,0:T(8,128)(2,1)S(1)}, u32[]{:S(2)}, u32[]{:S(2)}) collective-permute-start(s16[352,128]{1,0:T(8,128)(2,1)S(1)} %sum_line.3.refs_0_), channel_id=1, source_target_pairs={{0,1},{1,0},{2,3},{3,2},{4,5},{5,4},{6,7},{7,6},{8,9},{9,8},{10,11... | collective-permute-start | bytes 270344 | tf_op jit(solution)/shard_map/ppermute | solution.py:546
  71.7 1.5 %collective-permute-start.14 = (s16[352,128]{1,0:T(8,128)(2,1)S(1)}, s16[352,128]{1,0:T(8,128)(2,1)S(1)}, u32[]{:S(2)}, u32[]{:S(2)}) collective-permute-start(s16[352,128]{1,0:T(8,128)(2,1)S(1)} %collective-permute-done.10.refs_3_), channel_id=1, source_target_pairs={{0,1},{1,0},{2,3},{3,2},{4,5},{5,4},{6,7},{7,6},{8,9},{9,8},{10,11... | collective-permute-start | bytes 270344 | tf_op jit(solution)/shard_map/ppermute | solution.py:546
  72.4 1.3 %collective-permute-start.13 = (s16[352,128]{1,0:T(8,128)(2,1)S(1)}, s16[352,128]{1,0:T(8,128)(2,1)S(1)}, u32[]{:S(2)}, u32[]{:S(2)}) collective-permute-start(s16[352,128]{1,0:T(8,128)(2,1)S(1)} %collective-permute-done.9.refs_2_), channel_id=1, source_target_pairs={{0,1},{1,0},{2,3},{3,2},{4,5},{5,4},{6,7},{7,6},{8,9},{9,8},{10,11... | collective-permute-start | bytes 270344 | tf_op jit(solution)/shard_map/ppermute | solution.py:546
  73.2 1.3 %collective-permute-start.12 = (s16[352,128]{1,0:T(8,128)(2,1)S(1)}, s16[352,128]{1,0:T(8,128)(2,1)S(1)}, u32[]{:S(2)}, u32[]{:S(2)}) collective-permute-start(s16[352,128]{1,0:T(8,128)(2,1)S(1)} %collective-permute-done.8.refs_1_), channel_id=1, source_target_pairs={{0,1},{1,0},{2,3},{3,2},{4,5},{5,4},{6,7},{7,6},{8,9},{9,8},{10,11... | collective-permute-start | bytes 270344 | tf_op jit(solution)/shard_map/ppermute | solution.py:546

commit v5 on v4

--- a/solution.py
+++ b/solution.py
@@ -23,6 +23,7 @@
 TN = (((0,), (0,)), ((), ()))
 VMEM = pl.BlockSpec(memory_space=pltpu.VMEM)
 SMEM = pl.BlockSpec(memory_space=pltpu.SMEM)
+HBM = pl.BlockSpec(memory_space=pltpu.HBM)
 
 
 def mul(left, right, dims=NN):
@@ -45,8 +46,21 @@
     return mul(left[0], right[0], dims) + mul(left[0], right[1], dims) + mul(left[1], right[0], dims)
 
 
-def route_kernel(tiles, slots, owner_ref, cell_ref, frac_ref, target_ref, out_ref, words):
+def fetches(sources, targets, sems):
+    copies = [
+        pltpu.make_async_copy(source, target, sems.at[number])
+        for number, (source, target) in enumerate(zip(sources, targets))
+    ]
+    for copy in copies:
+        copy.start()
+    return copies
+
+
+def route_kernel(tiles, slots, *refs):
+    out_ref, owner_ref, cell_ref, frac_ref, target_ref, words, sems = refs[4:]
     queries = owner_ref.shape[1]
+    for copy in fetches(refs[:4], (owner_ref, cell_ref, frac_ref, target_ref), sems):
+        copy.wait()
     owner = owner_ref[...]
     hits = (lax.broadcasted_iota(jnp.int32, (tiles, queries), 0) == owner).astype(F32)
     before = lax.broadcasted_iota(jnp.int32, (queries, queries), 0) < lax.broadcasted_iota(
@@ -73,9 +87,16 @@
     return pl.pallas_call(
         functools.partial(route_kernel, tiles, slots),
         out_shape=jax.ShapeDtypeStruct((tiles * slots, WORDS), F32),
-        in_specs=[VMEM] * 4,
+        in_specs=[HBM] * 4,
         out_specs=VMEM,
-        scratch_shapes=[pltpu.VMEM((WORDS, queries), F32)],
+        scratch_shapes=[
+            pltpu.VMEM(owner.shape, owner.dtype),
+            pltpu.VMEM(cell.shape, cell.dtype),
+            pltpu.VMEM(frac.shape, F32),
+            pltpu.VMEM(target.shape, F32),
+            pltpu.VMEM((WORDS, queries), F32),
+            pltpu.SemaphoreType.DMA((4,)),
+        ],
         compiler_params=pltpu.CompilerParams(vmem_limit_bytes=4 << 20),
         name="route",
     )(owner, cell, frac, target)
@@ -103,24 +124,7 @@
     return jnp.concatenate(sides, axis=1)
 
 
-def local_kernel(
-    here_ref,
-    weight_ref,
-    bias_ref,
-    w_latent_ref,
-    w_pos_ref,
-    bias_one_ref,
-    w_mid_ref,
-    bias_two_ref,
-    w_out_ref,
-    bias_out_ref,
-    partial_ref,
-    latent_high_ref,
-    latent_low_ref,
-    mid_high_ref,
-    mid_low_ref,
-    small_ref,
-):
+def local_kernel(here_ref, weight_ref, bias_ref, partial_ref):
     planes, rows_y = here_ref.shape[0], here_ref.shape[1]
     bias = bias_ref[...]
     for x in range(planes + 1):
@@ -131,40 +135,20 @@
         ]
         for pair in range(rows_y // 2):
             partial_ref[x * (rows_y // 2) + pair] = tap_sum(weight_ref, taps, pair) + bias
-    for source, high_ref, low_ref in (
-        (w_latent_ref, latent_high_ref, latent_low_ref),
-        (w_mid_ref, mid_high_ref, mid_low_ref),
-    ):
-        high, low = halves(source[...])
-        high_ref[...] = high
-        low_ref[...] = low
-    small_ref[...] = jnp.zeros_like(small_ref)
-    small_ref[0:3, :] = w_pos_ref[...]
-    small_ref[3:4, :] = bias_one_ref[...]
-    small_ref[4:5, :] = bias_two_ref[...]
-    small_ref[5:6, 0:5] = bias_out_ref[...]
-    small_ref[8:13, :] = w_out_ref[...]
-
-
-def local_part(here, taps, conv_bias, params):
-    w_latent, w_mid = params[0], params[3]
+
+
+def local_part(here, taps, conv_bias):
     planes, rows_y, channels, rows_z = here.shape
     pairs = (planes + 1) * rows_y // 2
-    split = lambda array: [jax.ShapeDtypeStruct(array.shape, BF16)] * 2
     return pl.pallas_call(
         local_kernel,
-        out_shape=tuple(
-            [jax.ShapeDtypeStruct((pairs, channels, 2 * rows_z), F32)]
-            + split(w_latent)
-            + split(w_mid)
-            + [jax.ShapeDtypeStruct((16, w_mid.shape[0]), F32)]
-        ),
-        in_specs=[VMEM] * 10,
-        out_specs=tuple([VMEM] * 6),
-        compiler_params=pltpu.CompilerParams(vmem_limit_bytes=16 << 20),
+        out_shape=jax.ShapeDtypeStruct((pairs, channels, 2 * rows_z), F32),
+        in_specs=[VMEM] * 3,
+        out_specs=VMEM,
+        compiler_params=pltpu.CompilerParams(vmem_limit_bytes=8 << 20),
         cost_estimate=pl.CostEstimate(flops=3 << 30, bytes_accessed=4 << 20, transcendentals=0),
         name="conv_local",
-    )(here, taps, conv_bias, *params)
+    )(here, taps, conv_bias)
 
 
 def finish_latent(left_ref, right_ref, partial_ref, weight_ref, planes, lat):
@@ -223,11 +207,13 @@
     partial_ref,
     conv_weight_ref,
     words_ref,
-    latent_high,
-    latent_low,
-    mid_high,
-    mid_low,
-    small_ref,
+    w_latent_hbm,
+    w_pos_hbm,
+    bias_one_hbm,
+    w_mid_hbm,
+    bias_two_hbm,
+    w_out_hbm,
+    bias_out_hbm,
     send_ref,
     keep_ref,
     lat,
@@ -245,10 +231,25 @@
     out_t,
     d_out_t,
     packed,
+    mid_high,
+    mid_low,
+    w_latent_ref,
+    w_pos_ref,
+    bias_one_ref,
+    w_mid_ref,
+    bias_two_ref,
+    w_out_ref,
+    bias_out_ref,
+    sems,
 ):
     rows = plan.tiles * plan.slots
-    hidden = mid_high.shape[0]
-    latents = latent_high.shape[0]
+    hidden = w_mid_ref.shape[0]
+    latents = w_latent_ref.shape[0]
+    weights = fetches(
+        (w_latent_hbm, w_pos_hbm, bias_one_hbm, w_mid_hbm, bias_two_hbm, w_out_hbm, bias_out_hbm),
+        (w_latent_ref, w_pos_ref, bias_one_ref, w_mid_ref, bias_two_ref, w_out_ref, bias_out_ref),
+        sems,
+    )
     planes, rows_y, rows_z = plan.planes, left_ref.shape[1], left_ref.shape[3]
     slots = rows // plan.tiles
     my_block = place_ref[0]
@@ -271,11 +272,17 @@
         ),
     )
 
-    z_one[...] = mul(interp, latent_high[...]) + mul(interp, latent_low[...])
-    w_pos = [small_ref[d : d + 1, :] for d in range(3)]
+    for copy in weights:
+        copy.wait()
+    high, low = halves(w_latent_ref[...])
+    z_one[...] = mul(interp, high) + mul(interp, low)
+    high, low = halves(w_mid_ref[...])
+    mid_high[...] = high
+    mid_low[...] = low
+    w_pos = [w_pos_ref[d : d + 1, :] for d in range(3)]
     square = w_pos[0] * w_pos[0] + w_pos[1] * w_pos[1] + w_pos[2] * w_pos[2]
-    bias_one = small_ref[3:4, :]
-    bias_two = small_ref[4:5, :]
+    bias_one = bias_one_ref[...]
+    bias_two = bias_two_ref[...]
 
     def store(index, block, refs, value):
         high, low = halves(value)
@@ -329,7 +336,7 @@
 
     lax.fori_loop(0, rows // BLOCK, layer_two, 0)
 
-    out_fields = small_ref[8:16, :]
+    out_fields = jnp.concatenate([w_out_ref[...], jnp.zeros((3, hidden), F32)], axis=0)
     wo_high, wo_low = halves(out_fields)
     wo_both = jnp.concatenate([out_fields, wo_low.astype(F32)], axis=0).astype(BF16)
     for s in range(5):
@@ -340,7 +347,7 @@
     words_t = words.T
     target = [words_t[4 + f : 5 + f, :] for f in range(5)]
     valid = words_t[9:10, :]
-    value = [out_t[f : f + 1, :] + small_ref[5:6, f : f + 1] for f in range(5)]
+    value = [out_t[f : f + 1, :] + bias_out_ref[0:1, f : f + 1] for f in range(5)]
     grad = [[out_t[8 * (d + 1) + f : 8 * (d + 1) + f + 1, :] for f in range(5)] for d in range(3)]
     laplace = [out_t[32 + f : 33 + f, :] for f in range(5)]
     velocity = value[2:5]
@@ -642,14 +649,14 @@
 
 def main(place, left, right, partial, taps, words, weights, plan):
     rows = plan.tiles * plan.slots
-    hidden = weights[-1].shape[1]
+    hidden = weights[3].shape[0]
     channels = left.shape[2]
     outs = jax.ShapeDtypeStruct((4, plan.rows, LANES), F32)
     wide = lambda kind: pltpu.VMEM((5 * rows, hidden), kind)
     return pl.pallas_call(
         functools.partial(main_kernel, plan),
         out_shape=(outs, outs),
-        in_specs=[SMEM] + [VMEM] * 10,
+        in_specs=[SMEM] + [VMEM] * 5 + [HBM] * 7,
         out_specs=(VMEM, VMEM),
         scratch_shapes=[
             pltpu.VMEM((partial.shape[0], channels, 2 * LANES), BF16),
@@ -667,7 +674,11 @@
             pltpu.VMEM((40, rows), F32),
             pltpu.VMEM((40, rows), F32),
             pltpu.VMEM((8, plan.rows, LANES), F32),
-        ],
+            pltpu.VMEM((hidden, hidden), BF16),
+            pltpu.VMEM((hidden, hidden), BF16),
+        ]
+        + [pltpu.VMEM(weight.shape, F32) for weight in weights]
+        + [pltpu.SemaphoreType.DMA((7,))],
         compiler_params=pltpu.CompilerParams(vmem_limit_bytes=32 << 20),
         name="encode_decode",
     )(place, left, right, partial, taps, words, *weights)
@@ -759,11 +770,16 @@
     place = jnp.stack([plan.my_block(device), my_tile, my_replica]).astype(jnp.int32)
 
     here = fields[0].transpose(1, 2, 0, 3)
-    here, query_owner = lax.optimization_barrier((here, query_owner))
     up = [(i, (i + 1) % tiles) for i in range(tiles)]
     down = [((i + 1) % tiles, i) for i in range(tiles)]
-    left = lax.ppermute(here[-DILATION_RATE:], "tile", up)
-    right = lax.ppermute(here[: DILATION_RATE + 1], "tile", down)
+    to_left, to_right, convolution_weight = lax.optimization_barrier(
+        (here[: DILATION_RATE + 1], here[-DILATION_RATE:], convolution_weight)
+    )
+    taps = convolution_weight.reshape(channels, 3, 3, 3, channels)
+    taps = taps.transpose(1, 3, 0, 2, 4).reshape(3, 3 * channels, 3 * channels)
+    taps, query_owner = lax.optimization_barrier((taps, query_owner))
+    right = lax.ppermute(to_left, "tile", down)
+    left = lax.ppermute(to_right, "tile", up)
     words = route(
         query_owner[:, :, 0],
         query_cell,
@@ -776,10 +792,8 @@
         words.reshape(tiles, plan.slots, WORDS), "tile", split_axis=0, concat_axis=0, tiled=True
     ).reshape(tiles * plan.slots, WORDS)
 
-    taps = convolution_weight.reshape(channels, 3, 3, 3, channels)
-    taps = taps.transpose(1, 3, 0, 2, 4).reshape(3, 3 * channels, 3 * channels)
-    params = (w_latent, w_pos, bias_one[None], w_mid, bias_two[None], w_out, bias_out[None])
-    partial, *weights = local_part(here, taps, convolution_bias[:, None], params)
+    partial = local_part(here, taps, convolution_bias[:, None])
+    weights = (w_latent, w_pos, bias_one[None], w_mid, bias_two[None], w_out, bias_out[None])
     send, keep = main(place, left, right, partial, taps, words, weights, plan)
 
     mine, *others = first_sum(keep, swapped(send, plan, plan.core, 1), plan)

time: 76.7 us -> 73.4 us (0.957)
  waiting for transfers between devices: 20.9 us -> 28 us
  starting transfers between devices: 22.9 us -> 16.9 us
  local copies, waits for them, and re-layouts: 8.64 us -> 3.88 us
    all_to_all x1, waiting for transfers between devices: 0.01 us -> 6.48 us  [body(): lax.all_to_all(words.reshape(tiles, plan.slots, WORDS), 'tile', split_axi...]
    unnamed x27, local copies, waits for them, and re-layouts: 6.12 us -> 1.35 us
    all_to_all x1, starting transfers between devices: 7.39 us -> 3.63 us  [body(): lax.all_to_all(words.reshape(tiles, plan.slots, WORDS), 'tile', split_axi...]
    ppermute x13, starting transfers between devices: 11.1 us -> 7.74 us  [swapped(): lax.ppermute(value, ('replica', 'tile'), [(i, i ^ mask) for i in range(pl...]
    ppermute x13, waiting for transfers between devices: 20.1 us -> 21.5 us  [swapped(): lax.ppermute(value, ('replica', 'tile'), [(i, i ^ mask) for i in range(pl...]
    ppermute x2, starting transfers between devices: 4.44 us -> 5.56 us  [the longest x1 5.06 us: body(): right = lax.ppermute(to_left, 'tile', down)]
  transfers between devices with their start and end apart: 16 -> 16, of which waited for: 13 -> 12; matrix products, arithmetic and copies ran while one was open for 3% -> 2% of each run, Pallas kernels for 2% -> 3%
where the time goes in v5:
time: 73.4 us; the launch traced here: 73.1 us
  waiting for transfers between devices  28 us (38%)
  Pallas kernels  23.3 us (32%)
  starting transfers between devices  16.9 us (23%)
  local copies, waits for them, and re-layouts  3.88 us (5%)
  between operations  0.92 us (1%)
    ppermute x13, waiting for transfers between devices, swapped(): lax.ppermute(value, ('replica', 'tile'), [(i, i ^ mask) for i in range(pl...  21.5 us
    pallas_call x1, Pallas kernels, main(): pl.pallas_call(functools.partial(main_kernel, plan), out_shape=(outs, out...  18.8 us
    ppermute x13, starting transfers between devices, swapped(): lax.ppermute(value, ('replica', 'tile'), [(i, i ^ mask) for i in range(pl...  7.74 us
    all_to_all x1, waiting for transfers between devices, body(): lax.all_to_all(words.reshape(tiles, plan.slots, WORDS), 'tile', split_axi...  6.48 us
    ppermute x1, starting transfers between devices, body(): right = lax.ppermute(to_left, 'tile', down)  5.06 us
    all_to_all x1, starting transfers between devices, body(): lax.all_to_all(words.reshape(tiles, plan.slots, WORDS), 'tile', split_axi...  3.63 us
    pallas_call x1, Pallas kernels, unpack(): pl.pallas_call(functools.partial(unpack_kernel, plan), out_shape=tuple((j...  1.83 us
  transfers between devices with their start and end apart: 16, of which 12 were waited for; matrix products, arithmetic and copies ran while one was open for 2% of the time, Pallas kernels for 3%

profile of v5, /device:TPU:0, one launch (start us, length us, event | category | flops | bytes accessed | tf_op | source)
XLA Modules:
  0.0 73.1 jit_solution(7008747305462442778)
XLA Ops:
  0.7 1.3 %copy.30 = bf16[1,64,4,8,128]{4,1,3,2,0:T(8,128)(2,1)S(1)} copy(bf16[1,64,4,8,128]{4,3,2,1,0:T(8,128)(2,1)} %param.14) | data formatting | bytes 1048576 | tf_op args[0]
  1.9 0.7 slice.9
  2.7 0.8 %slice.8 = bf16[3,8,64,128]{3,2,1,0:T(8,128)(2,1)} slice(bf16[4,8,64,128]{3,2,1,0:T(8,128)(2,1)S(1)} %bitcast.24), slice={[0:3], [0:8], [0:64], [0:128]} | slice | bytes 786432 | tf_op jit(solution)/shard_map/slice | solution.py:776
  3.4 0.5 collective-permute-start
  4.0 5.1 %collective-permute-start.1 = (bf16[3,8,64,128]{3,2,1,0:T(8,128)(2,1)}, bf16[3,8,64,128]{3,2,1,0:T(8,128)(2,1)}, u32[]{:S(2)}, u32[]{:S(2)}) collective-permute-start(bf16[3,8,64,128]{3,2,1,0:T(8,128)(2,1)} %slice.8), channel_id=1, source_target_pairs={{1,0},{2,1},{3,2},{4,3},{5,4},{6,5},{7,6},{8,7},{9,8},{10,9},{11,1... | collective-permute-start | bytes 1179656 | tf_op jit(solution)/shard_map/ppermute | solution.py:781
  9.0 0.3 reshape.42
  9.4 0.0 copy-start.12
  9.4 0.3 copy.27
  9.6 0.4 reshape.43.weight_ref.conv_weight_ref
  10.0 1.0 %route.1 = f32[256,128]{1,0:T(8,128)} custom-call(s32[1,128]{1,0:T(1,128)S(1)} %bitcast.31, s32[1,128]{1,0:T(1,128)S(1)} %copy-done.9, f32[3,1,128]{2,1,0:T(1,128)S(1)} %bitcast.30, f32[5,1,128]{2,1,0:T(1,128)S(1)} %bitcast.27), custom_call_target="tpu_custom_call" | custom-call | tf_op jit(solution)/shard_map/route/pallas_call | solution.py:87
  11.1 3.6 %all-to-all-start = ((f32[16,16,128]{2,1,0:T(8,128)}), f32[16,16,128]{2,1,0:T(8,128)S(1)}, u32[]{:S(2)}, u32[]{:S(2)}) async-start(f32[16,16,128]{2,1,0:T(8,128)} %bitcast.11), calls=%async_computation | async-start | bytes 262144 | tf_op jit(solution)/shard_map/all_to_all | solution.py:791
  14.7 0.1 copy.28.bias_ref
  14.8 0.1 pad_add_fusion.place_ref
  14.9 0.0 copy-start.5
  14.9 0.0 copy-start.6
  14.9 0.0 copy-start.10
  15.0 1.2 %conv_local.1.partial_ref = f32[20,64,256]{2,1,0:T(8,128)S(1)} custom-call(bf16[4,8,64,128]{3,2,1,0:T(8,128)(2,1)S(1)} %bitcast.25, bf16[3,192,192]{2,1,0:T(8,128)(2,1)S(1)} %reshape.43.weight_ref.conv_weight_ref, f32[64,1]{1,0:T(8,128)S(1)} %copy.28.bias_ref), custom_call_target="tpu_custom_call" | custom-call | flops 3221225472 | bytes 4194304 | tf_op jit(solution)/shard_map/conv_local/pallas_call | solution.py:143
  16.2 6.5 %all-to-all-done = f32[16,16,128]{2,1,0:T(8,128)S(1)} async-done(((f32[16,16,128]{2,1,0:T(8,128)}), f32[16,16,128]{2,1,0:T(8,128)S(1)}, u32[]{:S(2)}, u32[]{:S(2)}) %all-to-all-start) | async-done | bytes 131104 | tf_op jit(solution)/shard_map/all_to_all | solution.py:791
  22.6 0.0 collective-permute-done.left_ref
  22.6 0.0 collective-permute-done.1.right_ref
  22.7 18.8 %encode_decode.1 = (f32[4,328,128]{2,1,0:T(8,128)S(1)}, f32[4,328,128]{2,1,0:T(8,128)S(1)}) custom-call(s32[3]{0:T(128)S(1)} %pad_add_fusion.place_ref, bf16[2,8,64,128]{3,2,1,0:T(8,128)(2,1)} %collective-permute-done.left_ref, bf16[3,8,64,128]{3,2,1,0:T(8,128)(2,1)} %collective-permute-done.1.right_ref, f32[20,64,256]{2,1,0:T(8,128)S(1)} %conv_local.1.partial_ref, ...), custom_call_target="tpu_custom_call" | custom-call | tf_op jit(solution)/shard_map/encode_decode/pallas_call | solution.py:656
  41.5 0.1 collective-permute-start.2
  41.6 2.1 %collective-permute-done.2.got_ref = f32[4,328,128]{2,1,0:T(8,128)S(1)} collective-permute-done((f32[4,328,128]{2,1,0:T(8,128)S(1)}, f32[4,328,128]{2,1,0:T(8,128)S(1)}, u32[]{:S(2)}, u32[]{:S(2)}) %collective-permute-start.2) | collective-permute-done | bytes 671776 | tf_op jit(solution)/shard_map/ppermute | solution.py:553
  43.7 0.2 sum_core.1
  43.8 0.1 collective-permute-start.3
  43.9 1.8 %collective-permute-start.4 = (s16[352,128]{1,0:T(8,128)(2,1)S(1)}, s16[352,128]{1,0:T(8,128)(2,1)S(1)}, u32[]{:S(2)}, u32[]{:S(2)}) collective-permute-start(s16[352,128]{1,0:T(8,128)(2,1)S(1)} %get-tuple-element.38), channel_id=1, source_target_pairs={{0,16},{1,17},{2,18},{3,19},{4,20},{5,21},{6,22},{7,23},{8,24},{9,... | collective-permute-start | bytes 270344 | tf_op jit(solution)/shard_map/ppermute | solution.py:553
  45.7 1.7 %collective-permute-start.5 = (s16[352,128]{1,0:T(8,128)(2,1)S(1)}, s16[352,128]{1,0:T(8,128)(2,1)S(1)}, u32[]{:S(2)}, u32[]{:S(2)}) collective-permute-start(s16[352,128]{1,0:T(8,128)(2,1)S(1)} %get-tuple-element.39), channel_id=1, source_target_pairs={{0,18},{1,19},{2,16},{3,17},{4,22},{5,23},{6,20},{7,21},{8,26},{9,... | collective-permute-start | bytes 270344 | tf_op jit(solution)/shard_map/ppermute | solution.py:553
  47.4 1.2 %collective-permute-done.3.refs_0_ = s16[352,128]{1,0:T(8,128)(2,1)S(1)} collective-permute-done((s16[352,128]{1,0:T(8,128)(2,1)S(1)}, s16[352,128]{1,0:T(8,128)(2,1)S(1)}, u32[]{:S(2)}, u32[]{:S(2)}) %collective-permute-start.3) | collective-permute-done | bytes 90144 | tf_op jit(solution)/shard_map/ppermute | solution.py:553
  48.6 0.1 collective-permute-done.4.refs_1_
  48.7 3.1 %collective-permute-done.5.refs_2_ = s16[352,128]{1,0:T(8,128)(2,1)S(1)} collective-permute-done((s16[352,128]{1,0:T(8,128)(2,1)S(1)}, s16[352,128]{1,0:T(8,128)(2,1)S(1)}, u32[]{:S(2)}, u32[]{:S(2)}) %collective-permute-start.5) | collective-permute-done | bytes 90144 | tf_op jit(solution)/shard_map/ppermute | solution.py:553
  51.8 0.1 sum_plane.1.mine_ref
  52.0 0.1 collective-permute-start.6
  52.1 4.5 %collective-permute-done.6.other_ref = s16[352,128]{1,0:T(8,128)(2,1)S(1)} collective-permute-done((s16[352,128]{1,0:T(8,128)(2,1)S(1)}, s16[352,128]{1,0:T(8,128)(2,1)S(1)}, u32[]{:S(2)}, u32[]{:S(2)}) %collective-permute-start.6) | collective-permute-done | bytes 90144 | tf_op jit(solution)/shard_map/ppermute | solution.py:553
  56.6 0.1 sum_line.2.mine_ref
  56.7 0.5 collective-permute-start.7
  57.2 5.4 %collective-permute-done.7.other_ref = s16[352,128]{1,0:T(8,128)(2,1)S(1)} collective-permute-done((s16[352,128]{1,0:T(8,128)(2,1)S(1)}, s16[352,128]{1,0:T(8,128)(2,1)S(1)}, u32[]{:S(2)}, u32[]{:S(2)}) %collective-permute-start.7) | collective-permute-done | bytes 90144 | tf_op jit(solution)/shard_map/ppermute | solution.py:553
  62.6 0.1 sum_line.3.refs_0_
  62.7 1.7 %collective-permute-start.10 = (s16[352,128]{1,0:T(8,128)(2,1)S(1)}, s16[352,128]{1,0:T(8,128)(2,1)S(1)}, u32[]{:S(2)}, u32[]{:S(2)}) collective-permute-start(s16[352,128]{1,0:T(8,128)(2,1)S(1)} %sum_line.3.refs_0_), channel_id=1, source_target_pairs={{0,18},{1,19},{2,16},{3,17},{4,22},{5,23},{6,20},{7,21},{8,26},{9,... | collective-permute-start | bytes 270344 | tf_op jit(solution)/shard_map/ppermute | solution.py:553
  64.4 1.1 %collective-permute-start.9 = (s16[352,128]{1,0:T(8,128)(2,1)S(1)}, s16[352,128]{1,0:T(8,128)(2,1)S(1)}, u32[]{:S(2)}, u32[]{:S(2)}) collective-permute-start(s16[352,128]{1,0:T(8,128)(2,1)S(1)} %sum_line.3.refs_0_), channel_id=1, source_target_pairs={{0,16},{1,17},{2,18},{3,19},{4,20},{5,21},{6,22},{7,23},{8,24},{9,... | collective-permute-start | bytes 270344 | tf_op jit(solution)/shard_map/ppermute | solution.py:553
  65.5 0.8 %collective-permute-start.8 = (s16[352,128]{1,0:T(8,128)(2,1)S(1)}, s16[352,128]{1,0:T(8,128)(2,1)S(1)}, u32[]{:S(2)}, u32[]{:S(2)}) collective-permute-start(s16[352,128]{1,0:T(8,128)(2,1)S(1)} %sum_line.3.refs_0_), channel_id=1, source_target_pairs={{0,2},{1,3},{2,0},{3,1},{4,6},{5,7},{6,4},{7,5},{8,10},{9,11},{10,... | collective-permute-start | bytes 270344 | tf_op jit(solution)/shard_map/ppermute | solution.py:553
  66.3 1.9 %collective-permute-done.10.refs_3_ = s16[352,128]{1,0:T(8,128)(2,1)S(1)} collective-permute-done((s16[352,128]{1,0:T(8,128)(2,1)S(1)}, s16[352,128]{1,0:T(8,128)(2,1)S(1)}, u32[]{:S(2)}, u32[]{:S(2)}) %collective-permute-start.10) | collective-permute-done | bytes 90144 | tf_op jit(solution)/shard_map/ppermute | solution.py:553
  68.2 0.8 %collective-permute-done.9.refs_2_ = s16[352,128]{1,0:T(8,128)(2,1)S(1)} collective-permute-done((s16[352,128]{1,0:T(8,128)(2,1)S(1)}, s16[352,128]{1,0:T(8,128)(2,1)S(1)}, u32[]{:S(2)}, u32[]{:S(2)}) %collective-permute-start.9) | collective-permute-done | bytes 90144 | tf_op jit(solution)/shard_map/ppermute | solution.py:553
  69.0 0.0 collective-permute-start.13
  69.0 1.1 %collective-permute-done.8.refs_1_ = s16[352,128]{1,0:T(8,128)(2,1)S(1)} collective-permute-done((s16[352,128]{1,0:T(8,128)(2,1)S(1)}, s16[352,128]{1,0:T(8,128)(2,1)S(1)}, u32[]{:S(2)}, u32[]{:S(2)}) %collective-permute-start.8) | collective-permute-done | bytes 90144 | tf_op jit(solution)/shard_map/ppermute | solution.py:553
  70.0 0.0 collective-permute-done.14.refs_7_
  70.0 0.2 collective-permute-done.13.refs_6_
  70.2 1.1 %collective-permute-done.12.refs_5_ = s16[352,128]{1,0:T(8,128)(2,1)S(1)} collective-permute-done((s16[352,128]{1,0:T(8,128)(2,1)S(1)}, s16[352,128]{1,0:T(8,128)(2,1)S(1)}, u32[]{:S(2)}, u32[]{:S(2)}) %collective-permute-start.12) | collective-permute-done | bytes 90144 | tf_op jit(solution)/shard_map/ppermute | solution.py:553
  71.3 1.8 %unpack.1 = (f32[5,1,128]{2,1,0:T(1,128)}, f32[64,512]{1,0:T(8,128)}, f32[3,512]{1,0:T(4,128)}, f32[1,512]{1,0:T(1,128)}, f32[512,512]{1,0:T(8,128)}, /*index=5*...) custom-call(s32[3]{0:T(128)S(1)} %pad_add_fusion.place_ref, ...), custom_call_target="tpu_custom_call" | custom-call | tf_op jit(solution)/shard_map/unpack/pallas_call | solution.py:734
  (26 shorter events, 0.1 us)
Async XLA Ops:
  0.6 8.4 %copy-start.11 = (bf16[64,1728]{1,0:T(8,128)(2,1)S(1)}, bf16[64,1728]{1,0:T(8,128)(2,1)}, u32[]{:S(2)}) copy-start(bf16[64,1728]{1,0:T(8,128)(2,1)} %param.15) | copy-start | bytes 663556
  3.4 6.6 %copy-start.4 = (f32[1,5,128]{2,0,1:T(1,128)S(1)}, f32[1,5,128]{2,0,1:T(1,128)}, u32[]{:S(2)}) copy-start(f32[1,5,128]{2,0,1:T(1,128)} %param.20) | copy-start | bytes 7684
  3.4 6.6 %copy-start.7 = (f32[1,3,128]{2,0,1:T(1,128)S(1)}, f32[1,3,128]{2,0,1:T(1,128)}, u32[]{:S(2)}) copy-start(f32[1,3,128]{2,0,1:T(1,128)} %param.19) | copy-start | bytes 4612
  3.4 6.6 %copy-start.8 = (s32[1,128,1]{1,2,0:T(1,128)S(1)}, s32[1,128,1]{1,2,0:T(1,128)}, u32[]{:S(2)}) copy-start(s32[1,128,1]{1,2,0:T(1,128)} %param.17) | copy-start | bytes 1540
  3.4 6.6 %copy-start.9 = (s32[1,128]{1,0:T(1,128)S(1)}, s32[1,128]{1,0:T(1,128)}, u32[]{:S(2)}) copy-start(s32[1,128]{1,0:T(1,128)} %refs_1_.1) | copy-start | bytes 1540
  3.4 19.2 %collective-permute-start = (bf16[2,8,64,128]{3,2,1,0:T(8,128)(2,1)}, bf16[2,8,64,128]{3,2,1,0:T(8,128)(2,1)}, u32[]{:S(2)}, u32[]{:S(2)}) collective-permute-start(bf16[2,8,64,128]{3,2,1,0:T(8,128)(2,1)} %slice.9), channel_id=1, source_target_pairs={{0,1},{1,2},{2,3},{3,4},{4,5},{5,6},{6,7},{7,8},{8,9},{9,10},{10,1... | collective-permute-start | bytes 786440 | tf_op jit(solution)/shard_map/ppermute | solution.py:782
  4.0 18.7 %collective-permute-start.1 = (bf16[3,8,64,128]{3,2,1,0:T(8,128)(2,1)}, bf16[3,8,64,128]{3,2,1,0:T(8,128)(2,1)}, u32[]{:S(2)}, u32[]{:S(2)}) collective-permute-start(bf16[3,8,64,128]{3,2,1,0:T(8,128)(2,1)} %slice.8), channel_id=1, source_target_pairs={{1,0},{2,1},{3,2},{4,3},{5,4},{6,5},{7,6},{8,7},{9,8},{10,9},{11,1... | collective-permute-start | bytes 1179656 | tf_op jit(solution)/shard_map/ppermute | solution.py:781
  9.4 5.4 %copy-start.12 = (f32[64]{0:T(128)S(1)}, f32[64]{0:T(128)}, u32[]{:S(2)}) copy-start(f32[64]{0:T(128)} %param.16) | copy-start | bytes 772
  11.1 11.6 %all-to-all-start = ((f32[16,16,128]{2,1,0:T(8,128)}), f32[16,16,128]{2,1,0:T(8,128)S(1)}, u32[]{:S(2)}, u32[]{:S(2)}) async-start(f32[16,16,128]{2,1,0:T(8,128)} %bitcast.11), calls=%async_computation | async-start | bytes 262144 | tf_op jit(solution)/shard_map/all_to_all | solution.py:791
  14.9 7.8 %copy-start = (f32[512,512]{1,0:T(8,128)S(1)}, f32[512,512]{1,0:T(8,128)}, u32[]{:S(2)}) copy-start(f32[512,512]{1,0:T(8,128)} %w_mid_hbm.1) | copy-start | bytes 3145732
  14.9 7.8 %copy-start.1 = (f32[64,512]{1,0:T(8,128)S(1)}, f32[64,512]{1,0:T(8,128)}, u32[]{:S(2)}) copy-start(f32[64,512]{1,0:T(8,128)} %w_latent_hbm.1) | copy-start | bytes 393220
  14.9 7.8 %copy-start.2 = (f32[5,512]{1,0:T(8,128)S(1)}, f32[5,512]{1,0:T(8,128)}, u32[]{:S(2)}) copy-start(f32[5,512]{1,0:T(8,128)} %w_out_hbm.1) | copy-start | bytes 30724
  14.9 7.8 %copy-start.3 = (f32[3,512]{1,0:T(4,128)S(1)}, f32[3,512]{1,0:T(4,128)}, u32[]{:S(2)}) copy-start(f32[3,512]{1,0:T(4,128)} %w_pos_hbm.1) | copy-start | bytes 18436
  14.9 7.8 %copy-start.5 = (f32[512]{0:T(512)S(1)}, f32[512]{0:T(512)}, u32[]{:S(2)}) copy-start(f32[512]{0:T(512)} %param.23) | copy-start | bytes 6148
  14.9 7.8 %copy-start.6 = (f32[512]{0:T(512)S(1)}, f32[512]{0:T(512)}, u32[]{:S(2)}) copy-start(f32[512]{0:T(512)} %param.25) | copy-start | bytes 6148
  14.9 7.8 %copy-start.10 = (f32[5]{0:T(128)S(1)}, f32[5]{0:T(128)}, u32[]{:S(2)}) copy-start(f32[5]{0:T(128)} %param.27) | copy-start | bytes 64
  41.5 2.2 %collective-permute-start.2 = (f32[4,328,128]{2,1,0:T(8,128)S(1)}, f32[4,328,128]{2,1,0:T(8,128)S(1)}, u32[]{:S(2)}, u32[]{:S(2)}) collective-permute-start(f32[4,328,128]{2,1,0:T(8,128)S(1)} %get-tuple-element.35), channel_id=1, source_target_pairs={{0,1},{1,0},{2,3},{3,2},{4,5},{5,4},{6,7},{7,6},{8,9},{9,8},{10,11... | collective-permute-start | bytes 2015240 | tf_op jit(solution)/shard_map/ppermute | solution.py:553
  43.8 4.7 %collective-permute-start.3 = (s16[352,128]{1,0:T(8,128)(2,1)S(1)}, s16[352,128]{1,0:T(8,128)(2,1)S(1)}, u32[]{:S(2)}, u32[]{:S(2)}) collective-permute-start(s16[352,128]{1,0:T(8,128)(2,1)S(1)} %get-tuple-element.37), channel_id=1, source_target_pairs={{0,2},{1,3},{2,0},{3,1},{4,6},{5,7},{6,4},{7,5},{8,10},{9,11},{10,... | collective-permute-start | bytes 270344 | tf_op jit(solution)/shard_map/ppermute | solution.py:553
  43.9 4.8 %collective-permute-start.4 = (s16[352,128]{1,0:T(8,128)(2,1)S(1)}, s16[352,128]{1,0:T(8,128)(2,1)S(1)}, u32[]{:S(2)}, u32[]{:S(2)}) collective-permute-start(s16[352,128]{1,0:T(8,128)(2,1)S(1)} %get-tuple-element.38), channel_id=1, source_target_pairs={{0,16},{1,17},{2,18},{3,19},{4,20},{5,21},{6,22},{7,23},{8,24},{9,... | collective-permute-start | bytes 270344 | tf_op jit(solution)/shard_map/ppermute | solution.py:553
  45.7 6.1 %collective-permute-start.5 = (s16[352,128]{1,0:T(8,128)(2,1)S(1)}, s16[352,128]{1,0:T(8,128)(2,1)S(1)}, u32[]{:S(2)}, u32[]{:S(2)}) collective-permute-start(s16[352,128]{1,0:T(8,128)(2,1)S(1)} %get-tuple-element.39), channel_id=1, source_target_pairs={{0,18},{1,19},{2,16},{3,17},{4,22},{5,23},{6,20},{7,21},{8,26},{9,... | collective-permute-start | bytes 270344 | tf_op jit(solution)/shard_map/ppermute | solution.py:553
  52.0 4.6 %collective-permute-start.6 = (s16[352,128]{1,0:T(8,128)(2,1)S(1)}, s16[352,128]{1,0:T(8,128)(2,1)S(1)}, u32[]{:S(2)}, u32[]{:S(2)}) collective-permute-start(s16[352,128]{1,0:T(8,128)(2,1)S(1)} %sum_plane.1.mine_ref), channel_id=1, source_target_pairs={{0,4},{1,5},{2,6},{3,7},{4,0},{5,1},{6,2},{7,3},{8,12},{9,13},{10,... | collective-permute-start | bytes 270344 | tf_op jit(solution)/shard_map/ppermute | solution.py:553
  56.7 5.9 %collective-permute-start.7 = (s16[352,128]{1,0:T(8,128)(2,1)S(1)}, s16[352,128]{1,0:T(8,128)(2,1)S(1)}, u32[]{:S(2)}, u32[]{:S(2)}) collective-permute-start(s16[352,128]{1,0:T(8,128)(2,1)S(1)} %sum_line.2.mine_ref), channel_id=1, source_target_pairs={{0,8},{1,9},{2,10},{3,11},{4,12},{5,13},{6,14},{7,15},{8,0},{9,1},... | collective-permute-start | bytes 270344 | tf_op jit(solution)/shard_map/ppermute | solution.py:553
  62.7 5.5 %collective-permute-start.10 = (s16[352,128]{1,0:T(8,128)(2,1)S(1)}, s16[352,128]{1,0:T(8,128)(2,1)S(1)}, u32[]{:S(2)}, u32[]{:S(2)}) collective-permute-start(s16[352,128]{1,0:T(8,128)(2,1)S(1)} %sum_line.3.refs_0_), channel_id=1, source_target_pairs={{0,18},{1,19},{2,16},{3,17},{4,22},{5,23},{6,20},{7,21},{8,26},{9,... | collective-permute-start | bytes 270344 | tf_op jit(solution)/shard_map/ppermute | solution.py:553
  64.4 4.6 %collective-permute-start.9 = (s16[352,128]{1,0:T(8,128)(2,1)S(1)}, s16[352,128]{1,0:T(8,128)(2,1)S(1)}, u32[]{:S(2)}, u32[]{:S(2)}) collective-permute-start(s16[352,128]{1,0:T(8,128)(2,1)S(1)} %sum_line.3.refs_0_), channel_id=1, source_target_pairs={{0,16},{1,17},{2,18},{3,19},{4,20},{5,21},{6,22},{7,23},{8,24},{9,... | collective-permute-start | bytes 270344 | tf_op jit(solution)/shard_map/ppermute | solution.py:553
  65.5 4.5 %collective-permute-start.8 = (s16[352,128]{1,0:T(8,128)(2,1)S(1)}, s16[352,128]{1,0:T(8,128)(2,1)S(1)}, u32[]{:S(2)}, u32[]{:S(2)}) collective-permute-start(s16[352,128]{1,0:T(8,128)(2,1)S(1)} %sum_line.3.refs_0_), channel_id=1, source_target_pairs={{0,2},{1,3},{2,0},{3,1},{4,6},{5,7},{6,4},{7,5},{8,10},{9,11},{10,... | collective-permute-start | bytes 270344 | tf_op jit(solution)/shard_map/ppermute | solution.py:553
  66.3 3.8 %collective-permute-start.11 = (s16[352,128]{1,0:T(8,128)(2,1)S(1)}, s16[352,128]{1,0:T(8,128)(2,1)S(1)}, u32[]{:S(2)}, u32[]{:S(2)}) collective-permute-start(s16[352,128]{1,0:T(8,128)(2,1)S(1)} %sum_line.3.refs_0_), channel_id=1, source_target_pairs={{0,1},{1,0},{2,3},{3,2},{4,5},{5,4},{6,7},{7,6},{8,9},{9,8},{10,11... | collective-permute-start | bytes 270344 | tf_op jit(solution)/shard_map/ppermute | solution.py:553
  68.2 1.8 %collective-permute-start.14 = (s16[352,128]{1,0:T(8,128)(2,1)S(1)}, s16[352,128]{1,0:T(8,128)(2,1)S(1)}, u32[]{:S(2)}, u32[]{:S(2)}) collective-permute-start(s16[352,128]{1,0:T(8,128)(2,1)S(1)} %collective-permute-done.10.refs_3_), channel_id=1, source_target_pairs={{0,1},{1,0},{2,3},{3,2},{4,5},{5,4},{6,7},{7,6},{8,9},{9,8},{10,11... | collective-permute-start | bytes 270344 | tf_op jit(solution)/shard_map/ppermute | solution.py:553
  69.0 1.3 %collective-permute-start.13 = (s16[352,128]{1,0:T(8,128)(2,1)S(1)}, s16[352,128]{1,0:T(8,128)(2,1)S(1)}, u32[]{:S(2)}, u32[]{:S(2)}) collective-permute-start(s16[352,128]{1,0:T(8,128)(2,1)S(1)} %collective-permute-done.9.refs_2_), channel_id=1, source_target_pairs={{0,1},{1,0},{2,3},{3,2},{4,5},{5,4},{6,7},{7,6},{8,9},{9,8},{10,11... | collective-permute-start | bytes 270344 | tf_op jit(solution)/shard_map/ppermute | solution.py:553
  70.0 1.3 %collective-permute-start.12 = (s16[352,128]{1,0:T(8,128)(2,1)S(1)}, s16[352,128]{1,0:T(8,128)(2,1)S(1)}, u32[]{:S(2)}, u32[]{:S(2)}) collective-permute-start(s16[352,128]{1,0:T(8,128)(2,1)S(1)} %collective-permute-done.8.refs_1_), channel_id=1, source_target_pairs={{0,1},{1,0},{2,3},{3,2},{4,5},{5,4},{6,7},{7,6},{8,9},{9,8},{10,11... | collective-permute-start | bytes 270344 | tf_op jit(solution)/shard_map/ppermute | solution.py:553

commit v6 on v5

--- a/solution.py
+++ b/solution.py
@@ -69,15 +69,21 @@
     earlier = mul(hits.astype(BF16), before.astype(F32).astype(BF16))
     slot = jnp.sum(hits * earlier, axis=0, keepdims=True)
     place = owner * slots + slot.astype(jnp.int32)
-    chosen = (lax.broadcasted_iota(jnp.int32, (tiles * slots, queries), 0) == place).astype(F32).astype(BF16)
+    spot = lax.broadcasted_iota(jnp.int32, (tiles * 8, queries), 0)
+    spot = (spot >> 3) * slots + (spot & 7)
+    groups = slots // 8
+    chosen = [jnp.where(spot + 8 * group == place, 1.0, 0.0) for group in range(groups)]
+    chosen = jnp.concatenate(chosen, axis=1).astype(BF16)
     words[...] = jnp.zeros_like(words)
-    words[0:1, :] = cell_ref[...].astype(F32)
-    for d in range(3):
-        words[1 + d : 2 + d, :] = frac_ref[d]
-    for f in range(5):
-        words[4 + f : 5 + f, :] = target_ref[f]
-    words[9:10, :] = jnp.ones((1, queries), F32)
-    words[10:11, :] = lax.broadcasted_iota(jnp.int32, (1, queries), 1).astype(F32)
+    for group in range(groups):
+        row, lanes = 16 * group, slice(group * queries, (group + 1) * queries)
+        words[row : row + 1, lanes] = cell_ref[...].astype(F32)
+        for d in range(3):
+            words[row + 1 + d : row + 2 + d, lanes] = frac_ref[d]
+        for f in range(5):
+            words[row + 4 + f : row + 5 + f, lanes] = target_ref[f]
+        words[row + 9 : row + 10, lanes] = jnp.ones((1, queries), F32)
+        words[row + 10 : row + 11, lanes] = lax.broadcasted_iota(jnp.int32, (1, queries), 1).astype(F32)
     high, middle, low = thirds(words[...])
     out_ref[...] = mul(chosen, high, NT) + mul(chosen, middle, NT) + mul(chosen, low, NT)
 
@@ -86,7 +92,7 @@
     queries = owner.shape[1]
     return pl.pallas_call(
         functools.partial(route_kernel, tiles, slots),
-        out_shape=jax.ShapeDtypeStruct((tiles * slots, WORDS), F32),
+        out_shape=jax.ShapeDtypeStruct((tiles * 8, WORDS), F32),
         in_specs=[HBM] * 4,
         out_specs=VMEM,
         scratch_shapes=[
@@ -94,7 +100,7 @@
             pltpu.VMEM(cell.shape, cell.dtype),
             pltpu.VMEM(frac.shape, F32),
             pltpu.VMEM(target.shape, F32),
-            pltpu.VMEM((WORDS, queries), F32),
+            pltpu.VMEM((WORDS, queries * (slots // 8)), F32),
             pltpu.SemaphoreType.DMA((4,)),
         ],
         compiler_params=pltpu.CompilerParams(vmem_limit_bytes=4 << 20),
@@ -124,35 +130,9 @@
     return jnp.concatenate(sides, axis=1)
 
 
-def local_kernel(here_ref, weight_ref, bias_ref, partial_ref):
+def conv_kernel(left_ref, here_ref, right_ref, weight_ref, bias_ref, lat_ref):
     planes, rows_y = here_ref.shape[0], here_ref.shape[1]
     bias = bias_ref[...]
-    for x in range(planes + 1):
-        taps = [
-            (step, here_ref, x + DILATION_RATE * (step - 1))
-            for step in range(3)
-            if 0 <= x + DILATION_RATE * (step - 1) < planes
-        ]
-        for pair in range(rows_y // 2):
-            partial_ref[x * (rows_y // 2) + pair] = tap_sum(weight_ref, taps, pair) + bias
-
-
-def local_part(here, taps, conv_bias):
-    planes, rows_y, channels, rows_z = here.shape
-    pairs = (planes + 1) * rows_y // 2
-    return pl.pallas_call(
-        local_kernel,
-        out_shape=jax.ShapeDtypeStruct((pairs, channels, 2 * rows_z), F32),
-        in_specs=[VMEM] * 3,
-        out_specs=VMEM,
-        compiler_params=pltpu.CompilerParams(vmem_limit_bytes=8 << 20),
-        cost_estimate=pl.CostEstimate(flops=3 << 30, bytes_accessed=4 << 20, transcendentals=0),
-        name="conv_local",
-    )(here, taps, conv_bias)
-
-
-def finish_latent(left_ref, right_ref, partial_ref, weight_ref, planes, lat):
-    rows_y = left_ref.shape[1]
     for x in range(planes + 1):
         taps = []
         for step in range(3):
@@ -161,10 +141,25 @@
                 taps.append((step, left_ref, plane + left_ref.shape[0]))
             elif plane >= planes:
                 taps.append((step, right_ref, plane - planes))
+            else:
+                taps.append((step, here_ref, plane))
         for pair in range(rows_y // 2):
-            number = x * (rows_y // 2) + pair
-            summed = partial_ref[number] + tap_sum(weight_ref, taps, pair)
-            lat[number] = jax.nn.gelu(summed).astype(BF16)
+            summed = tap_sum(weight_ref, taps, pair) + bias
+            lat_ref[x * (rows_y // 2) + pair] = jax.nn.gelu(summed).astype(BF16)
+
+
+def convolve(left, here, right, taps, conv_bias):
+    planes, rows_y, channels, rows_z = here.shape
+    pairs = (planes + 1) * rows_y // 2
+    return pl.pallas_call(
+        conv_kernel,
+        out_shape=jax.ShapeDtypeStruct((pairs, channels, 2 * rows_z), BF16),
+        in_specs=[VMEM] * 5,
+        out_specs=VMEM,
+        compiler_params=pltpu.CompilerParams(vmem_limit_bytes=8 << 20),
+        cost_estimate=pl.CostEstimate(flops=3 << 30, bytes_accessed=4 << 20, transcendentals=0),
+        name="convolve",
+    )(left, here, right, taps, conv_bias)
 
 
 def interpolate(words, lat, planes, rows_y, rows_z):
@@ -180,16 +175,17 @@
     part_z = jnp.where(spot == base_z, 1.0 - frac[2], 0.0) + jnp.where(
         spot == ((base_z + 1) & (rows_z - 1)), frac[2], 0.0
     )
+    part_yz = []
+    for y in range(rows_y):
+        part_y = jnp.where(
+            base_y == y, 1.0 - frac[1], jnp.where(base_y == (y - 1) % rows_y, frac[1], 0.0)
+        )
+        part_yz.append(part_y * part_z)
     total = None
     for x in range(planes + 1):
         part_x = jnp.where(base_x == x, 1.0 - frac[0], jnp.where(base_x == x - 1, frac[0], 0.0))
         for pair in range(rows_y // 2):
-            sides = []
-            for y in (2 * pair, 2 * pair + 1):
-                part_y = jnp.where(
-                    base_y == y, 1.0 - frac[1], jnp.where(base_y == (y - 1) % rows_y, frac[1], 0.0)
-                )
-                sides.append((part_x * part_y * part_z).astype(BF16))
+            sides = [(part_x * part_yz[2 * pair + half]).astype(BF16) for half in (0, 1)]
             term = mul(jnp.concatenate(sides, axis=1), lat[x * (rows_y // 2) + pair], NT)
             total = term if total is None else total + term
     return total.astype(BF16), base_x, base_y, base_z, frac
@@ -202,10 +198,7 @@
 def main_kernel(
     plan,
     place_ref,
-    left_ref,
-    right_ref,
-    partial_ref,
-    conv_weight_ref,
+    lat,
     words_ref,
     w_latent_hbm,
     w_pos_hbm,
@@ -216,7 +209,6 @@
     bias_out_hbm,
     send_ref,
     keep_ref,
-    lat,
     code,
     pos,
     z_one,
@@ -250,14 +242,17 @@
         (w_latent_ref, w_pos_ref, bias_one_ref, w_mid_ref, bias_two_ref, w_out_ref, bias_out_ref),
         sems,
     )
-    planes, rows_y, rows_z = plan.planes, left_ref.shape[1], left_ref.shape[3]
+    planes, rows_z = plan.planes, lat.shape[2] // 2
+    rows_y = lat.shape[0] // (planes + 1) * 2
     slots = rows // plan.tiles
     my_block = place_ref[0]
     my_tile = place_ref[1]
     my_replica = place_ref[2]
 
-    finish_latent(left_ref, right_ref, partial_ref, conv_weight_ref, planes, lat)
     words = words_ref[...]
+    words = jnp.concatenate(
+        [words] + [pltpu.roll(words, LANES - 16 * group, 1) for group in range(1, slots // 8)], axis=0
+    )
     interp, base_x, base_y, base_z, frac = interpolate(words, lat, planes, rows_y, rows_z)
     code[...] = interp
     global_x = my_tile * planes + base_x
@@ -338,6 +333,7 @@
 
     out_fields = jnp.concatenate([w_out_ref[...], jnp.zeros((3, hidden), F32)], axis=0)
     wo_high, wo_low = halves(out_fields)
+    wo_three = jnp.concatenate([out_fields, wo_low.astype(F32), out_fields], axis=0).astype(BF16)
     wo_both = jnp.concatenate([out_fields, wo_low.astype(F32)], axis=0).astype(BF16)
     for s in range(5):
         span = slice(s * rows, (s + 1) * rows)
@@ -403,8 +399,8 @@
     for s in range(5):
         span = slice(s * rows, (s + 1) * rows)
         wanted = d_out_t[8 * s : 8 * s + 8, :]
-        do_high, do_low = halves(wanted)
-        back[span, :] = mul3((do_high, do_low), (wo_high, wo_low), TN)
+        do_low = halves(wanted)[1].astype(F32)
+        back[span, :] = mul(jnp.concatenate([wanted, wanted, do_low], axis=0).astype(BF16), wo_three, TN)
 
     def second_back(block, total):
         act = fetch(mixed, 0, block)
@@ -506,7 +502,7 @@
         lane == jnp.broadcast_to(words[:, 10:11], (rows, LANES)).astype(jnp.int32), words[:, 9:10], 0.0
     ).astype(BF16)
     fields = jnp.concatenate(value + [jnp.zeros((3, rows), F32)], axis=0)
-    source = lax.broadcasted_iota(jnp.int32, (8, rows), 1) >> (slots.bit_length() - 1)
+    source = (lax.broadcasted_iota(jnp.int32, (8, rows), 1) & (plan.tiles * 8 - 1)) >> 3
     spread = jnp.concatenate([jnp.where(source == t, fields, 0.0) for t in range(plan.tiles)], axis=0)
     high, middle, low = thirds(spread)
     spread = mul(high, chosen) + mul(middle, chosen) + mul(low, chosen)
@@ -647,19 +643,18 @@
     )(*blocks)
 
 
-def main(place, left, right, partial, taps, words, weights, plan):
+def main(place, lat, words, weights, plan):
     rows = plan.tiles * plan.slots
     hidden = weights[3].shape[0]
-    channels = left.shape[2]
+    channels = lat.shape[1]
     outs = jax.ShapeDtypeStruct((4, plan.rows, LANES), F32)
     wide = lambda kind: pltpu.VMEM((5 * rows, hidden), kind)
     return pl.pallas_call(
         functools.partial(main_kernel, plan),
         out_shape=(outs, outs),
-        in_specs=[SMEM] + [VMEM] * 5 + [HBM] * 7,
+        in_specs=[SMEM] + [VMEM] * 2 + [HBM] * 7,
         out_specs=(VMEM, VMEM),
         scratch_shapes=[
-            pltpu.VMEM((partial.shape[0], channels, 2 * LANES), BF16),
             pltpu.VMEM((rows, channels), BF16),
             pltpu.VMEM((rows, LANES), F32),
             pltpu.VMEM((rows, hidden), F32),
@@ -681,7 +676,7 @@
         + [pltpu.SemaphoreType.DMA((7,))],
         compiler_params=pltpu.CompilerParams(vmem_limit_bytes=32 << 20),
         name="encode_decode",
-    )(place, left, right, partial, taps, words, *weights)
+    )(place, lat, words, *weights)
 
 
 def unpack_kernel(plan, place_ref, *refs):
@@ -772,12 +767,11 @@
     here = fields[0].transpose(1, 2, 0, 3)
     up = [(i, (i + 1) % tiles) for i in range(tiles)]
     down = [((i + 1) % tiles, i) for i in range(tiles)]
-    to_left, to_right, convolution_weight = lax.optimization_barrier(
-        (here[: DILATION_RATE + 1], here[-DILATION_RATE:], convolution_weight)
+    to_left, to_right, query_owner = lax.optimization_barrier(
+        (here[: DILATION_RATE + 1], here[-DILATION_RATE:], query_owner)
     )
     taps = convolution_weight.reshape(channels, 3, 3, 3, channels)
     taps = taps.transpose(1, 3, 0, 2, 4).reshape(3, 3 * channels, 3 * channels)
-    taps, query_owner = lax.optimization_barrier((taps, query_owner))
     right = lax.ppermute(to_left, "tile", down)
     left = lax.ppermute(to_right, "tile", up)
     words = route(
@@ -789,12 +783,12 @@
         plan.slots,
     )
     words = lax.all_to_all(
-        words.reshape(tiles, plan.slots, WORDS), "tile", split_axis=0, concat_axis=0, tiled=True
-    ).reshape(tiles * plan.slots, WORDS)
-
-    partial = local_part(here, taps, convolution_bias[:, None])
+        words.reshape(tiles, 8, WORDS), "tile", split_axis=0, concat_axis=0, tiled=True
+    ).reshape(tiles * 8, WORDS)
+
+    lat = convolve(left, here, right, taps, convolution_bias[:, None])
     weights = (w_latent, w_pos, bias_one[None], w_mid, bias_two[None], w_out, bias_out[None])
-    send, keep = main(place, left, right, partial, taps, words, weights, plan)
+    send, keep = main(place, lat, words, weights, plan)
 
     mine, *others = first_sum(keep, swapped(send, plan, plan.core, 1), plan)
     arrived = [swapped(block, plan, plan.plane, step + 1) for step, block in enumerate(others)]

time: 73.4 us -> 72.4 us (0.986)
  waiting for transfers between devices: 28 us -> 25 us
  starting transfers between devices: 16.9 us -> 19.1 us
  Pallas kernels: 23.3 us -> 21.9 us
  local copies, waits for them, and re-layouts: 3.88 us -> 5.05 us
    all_to_all x1, waiting for transfers between devices: 6.48 us -> 3.22 us  [body(): lax.all_to_all(words.reshape(tiles, 8, WORDS), 'tile', split_axis=0, conc...]
    all_to_all x1, starting transfers between devices: 3.63 us -> 5.84 us  [body(): lax.all_to_all(words.reshape(tiles, 8, WORDS), 'tile', split_axis=0, conc...]
    pallas_call x1, Pallas kernels: 18.8 us -> 16.8 us  [main(): pl.pallas_call(functools.partial(main_kernel, plan), out_shape=(outs, out...]
    unnamed x27, local copies, waits for them, and re-layouts: 1.35 us -> 3.26 us
    slice x1, local copies, waits for them, and re-layouts: 0.77 us -> 0.03 us  [body(): here[:DILATION_RATE + 1]]
  transfers between devices with their start and end apart: 16 -> 16, of which waited for: 12 -> 11; matrix products, arithmetic and copies ran while one was open for 2% -> 2% of each run, Pallas kernels for 3% -> 4%
where the time goes in v6:
time: 72.4 us; the launch traced here: 72.1 us
  waiting for transfers between devices  25 us (35%)
  Pallas kernels  21.9 us (30%)
  starting transfers between devices  19.1 us (26%)
  local copies, waits for them, and re-layouts  5.05 us (7%)
  between operations  0.87 us (1%)
    ppermute x13, waiting for transfers between devices, swapped(): lax.ppermute(value, ('replica', 'tile'), [(i, i ^ mask) for i in range(pl...  21.8 us
    pallas_call x1, Pallas kernels, main(): pl.pallas_call(functools.partial(main_kernel, plan), out_shape=(outs, out...  16.8 us
    ppermute x13, starting transfers between devices, swapped(): lax.ppermute(value, ('replica', 'tile'), [(i, i ^ mask) for i in range(pl...  7.87 us
    all_to_all x1, starting transfers between devices, body(): lax.all_to_all(words.reshape(tiles, 8, WORDS), 'tile', split_axis=0, conc...  5.84 us
    ppermute x1, starting transfers between devices, body(): right = lax.ppermute(to_left, 'tile', down)  5.44 us
    unnamed x27, local copies, waits for them, and re-layouts  3.26 us
    all_to_all x1, waiting for transfers between devices, body(): lax.all_to_all(words.reshape(tiles, 8, WORDS), 'tile', split_axis=0, conc...  3.22 us
    pallas_call x1, Pallas kernels, unpack(): pl.pallas_call(functools.partial(unpack_kernel, plan), out_shape=tuple((j...  1.83 us
  transfers between devices with their start and end apart: 16, of which 11 were waited for; matrix products, arithmetic and copies ran while one was open for 2% of the time, Pallas kernels for 4%

profile of v6, /device:TPU:0, one launch (start us, length us, event | category | flops | bytes accessed | tf_op | source)
XLA Modules:
  0.0 72.1 jit_solution(5838072572348302050)
XLA Ops:
  0.6 1.2 %copy.30 = bf16[1,64,4,8,128]{4,1,3,2,0:T(8,128)(2,1)S(1)} copy(bf16[1,64,4,8,128]{4,3,2,1,0:T(8,128)(2,1)} %param.14) | data formatting | bytes 1048576 | tf_op args[0]
  1.9 0.0 copy-start.11
  1.9 0.7 %slice.9 = bf16[2,8,64,128]{3,2,1,0:T(8,128)(2,1)} slice(bf16[4,8,64,128]{3,2,1,0:T(8,128)(2,1)S(1)} %bitcast.24), slice={[2:4], [0:8], [0:64], [0:128]} | slice | bytes 524288 | tf_op jit(solution)/shard_map/slice | solution.py:771
  2.7 5.4 %collective-permute-start.1 = (bf16[3,8,64,128]{3,2,1,0:T(8,128)(2,1)S(1)}, bf16[3,8,64,128]{3,2,1,0:T(8,128)(2,1)S(1)}, u32[]{:S(2)}, u32[]{:S(2)}) collective-permute-start(bf16[3,8,64,128]{3,2,1,0:T(8,128)(2,1)S(1)} %slice.8), channel_id=1, source_target_pairs={{1,0},{2,1},{3,2},{4,3},{5,4},{6,5},{7,6},{8,7},{9,8},{10,9},{11,1... | collective-permute-start | bytes 1179656 | tf_op jit(solution)/shard_map/ppermute | solution.py:775
  8.1 0.0 collective-permute-start
  8.1 0.7 copy-done.7
  8.8 0.0 copy-done.9
  8.8 1.0 %route.1 = f32[128,128]{1,0:T(8,128)} custom-call(s32[1,128]{1,0:T(1,128)S(1)} %bitcast.31, s32[1,128]{1,0:T(1,128)S(1)} %copy-done.9, f32[3,1,128]{2,1,0:T(1,128)S(1)} %bitcast.30, f32[5,1,128]{2,1,0:T(1,128)S(1)} %bitcast.27), custom_call_target="tpu_custom_call" | custom-call | tf_op jit(solution)/shard_map/route/pallas_call | solution.py:93
  9.8 5.8 %all-to-all-start = ((f32[16,8,128]{2,1,0:T(8,128)}), f32[16,8,128]{2,1,0:T(8,128)S(1)}, u32[]{:S(2)}, u32[]{:S(2)}) async-start(f32[16,8,128]{2,1,0:T(8,128)} %bitcast.11), calls=%async_computation | async-start | bytes 131072 | tf_op jit(solution)/shard_map/all_to_all | solution.py:785
  15.7 0.3 reshape.42
  16.0 0.3 copy.27
  16.3 0.4 reshape.43.weight_ref
  16.6 0.0 copy-start.12
  16.6 0.7 copy-done.12
  17.3 0.1 copy.28.bias_ref
  17.4 0.1 pad_add_fusion.place_ref
  17.5 0.0 collective-permute-done.left_ref
  17.5 0.0 copy-start.2
  17.5 0.0 copy-start.3
  17.5 1.8 %convolve.1.lat = bf16[20,64,256]{2,1,0:T(8,128)(2,1)S(1)} custom-call(bf16[2,8,64,128]{3,2,1,0:T(8,128)(2,1)S(1)} %collective-permute-done.left_ref, bf16[4,8,64,128]{3,2,1,0:T(8,128)(2,1)S(1)} %bitcast.25, bf16[3,8,64,128]{3,2,1,0:T(8,128)(2,1)S(1)} %collective-permute-done.1.right_ref, bf16[3,192,192]{2,1,0:T(8,128)(2,1)S(1)} %reshape.43.weight_ref, ...), custom_call_target="tpu_custom_call" | custom-call | flops 3221225472 | bytes 4194304 | tf_op jit(solution)/shard_map/convolve/pallas_call | solution.py:154
  19.3 3.2 %all-to-all-done = f32[16,8,128]{2,1,0:T(8,128)S(1)} async-done(((f32[16,8,128]{2,1,0:T(8,128)}), f32[16,8,128]{2,1,0:T(8,128)S(1)}, u32[]{:S(2)}, u32[]{:S(2)}) %all-to-all-start) | async-done | bytes 65568 | tf_op jit(solution)/shard_map/all_to_all | solution.py:785
  22.6 0.6 copy-done.6
  23.2 0.0 copy-done.5
  23.3 16.8 %encode_decode.1 = (f32[4,328,128]{2,1,0:T(8,128)S(1)}, f32[4,328,128]{2,1,0:T(8,128)S(1)}) custom-call(s32[3]{0:T(128)S(1)} %pad_add_fusion.place_ref, bf16[20,64,256]{2,1,0:T(8,128)(2,1)S(1)} %convolve.1.lat, f32[128,128]{1,0:T(8,128)S(1)} %bitcast.26, f32[64,512]{1,0:T(8,128)S(1)} %copy-done.1, f32[3,512]{1,0:T(4,128)S(1)} %copy-done.3, ...), custom_call_target="tpu_custom_call" | custom-call | tf_op jit(solution)/shard_map/encode_decode/pallas_call | solution.py:652
  40.0 0.1 collective-permute-start.2
  40.1 2.1 %collective-permute-done.2.got_ref = f32[4,328,128]{2,1,0:T(8,128)S(1)} collective-permute-done((f32[4,328,128]{2,1,0:T(8,128)S(1)}, f32[4,328,128]{2,1,0:T(8,128)S(1)}, u32[]{:S(2)}, u32[]{:S(2)}) %collective-permute-start.2) | collective-permute-done | bytes 671776 | tf_op jit(solution)/shard_map/ppermute | solution.py:549
  42.2 0.2 sum_core.1
  42.4 0.2 collective-permute-start.3
  42.6 1.5 %collective-permute-start.4 = (s16[352,128]{1,0:T(8,128)(2,1)S(1)}, s16[352,128]{1,0:T(8,128)(2,1)S(1)}, u32[]{:S(2)}, u32[]{:S(2)}) collective-permute-start(s16[352,128]{1,0:T(8,128)(2,1)S(1)} %get-tuple-element.34), channel_id=1, source_target_pairs={{0,16},{1,17},{2,18},{3,19},{4,20},{5,21},{6,22},{7,23},{8,24},{9,... | collective-permute-start | bytes 270344 | tf_op jit(solution)/shard_map/ppermute | solution.py:549
  44.1 1.9 %collective-permute-start.5 = (s16[352,128]{1,0:T(8,128)(2,1)S(1)}, s16[352,128]{1,0:T(8,128)(2,1)S(1)}, u32[]{:S(2)}, u32[]{:S(2)}) collective-permute-start(s16[352,128]{1,0:T(8,128)(2,1)S(1)} %get-tuple-element.35), channel_id=1, source_target_pairs={{0,18},{1,19},{2,16},{3,17},{4,22},{5,23},{6,20},{7,21},{8,26},{9,... | collective-permute-start | bytes 270344 | tf_op jit(solution)/shard_map/ppermute | solution.py:549
  45.9 1.2 %collective-permute-done.3.refs_0_ = s16[352,128]{1,0:T(8,128)(2,1)S(1)} collective-permute-done((s16[352,128]{1,0:T(8,128)(2,1)S(1)}, s16[352,128]{1,0:T(8,128)(2,1)S(1)}, u32[]{:S(2)}, u32[]{:S(2)}) %collective-permute-start.3) | collective-permute-done | bytes 90144 | tf_op jit(solution)/shard_map/ppermute | solution.py:549
  47.1 0.1 collective-permute-done.4.refs_1_
  47.2 3.1 %collective-permute-done.5.refs_2_ = s16[352,128]{1,0:T(8,128)(2,1)S(1)} collective-permute-done((s16[352,128]{1,0:T(8,128)(2,1)S(1)}, s16[352,128]{1,0:T(8,128)(2,1)S(1)}, u32[]{:S(2)}, u32[]{:S(2)}) %collective-permute-start.5) | collective-permute-done | bytes 90144 | tf_op jit(solution)/shard_map/ppermute | solution.py:549
  50.3 0.1 sum_plane.1.mine_ref
  50.4 0.3 collective-permute-start.6
  50.7 4.3 %collective-permute-done.6.other_ref = s16[352,128]{1,0:T(8,128)(2,1)S(1)} collective-permute-done((s16[352,128]{1,0:T(8,128)(2,1)S(1)}, s16[352,128]{1,0:T(8,128)(2,1)S(1)}, u32[]{:S(2)}, u32[]{:S(2)}) %collective-permute-start.6) | collective-permute-done | bytes 90144 | tf_op jit(solution)/shard_map/ppermute | solution.py:549
  55.0 0.1 sum_line.2.mine_ref
  55.1 0.4 collective-permute-start.7
  55.5 5.7 %collective-permute-done.7.other_ref = s16[352,128]{1,0:T(8,128)(2,1)S(1)} collective-permute-done((s16[352,128]{1,0:T(8,128)(2,1)S(1)}, s16[352,128]{1,0:T(8,128)(2,1)S(1)}, u32[]{:S(2)}, u32[]{:S(2)}) %collective-permute-start.7) | collective-permute-done | bytes 90144 | tf_op jit(solution)/shard_map/ppermute | solution.py:549
  61.2 0.1 sum_line.3.refs_0_
  61.4 1.1 %collective-permute-start.8 = (s16[352,128]{1,0:T(8,128)(2,1)S(1)}, s16[352,128]{1,0:T(8,128)(2,1)S(1)}, u32[]{:S(2)}, u32[]{:S(2)}) collective-permute-start(s16[352,128]{1,0:T(8,128)(2,1)S(1)} %sum_line.3.refs_0_), channel_id=1, source_target_pairs={{0,2},{1,3},{2,0},{3,1},{4,6},{5,7},{6,4},{7,5},{8,10},{9,11},{10,... | collective-permute-start | bytes 270344 | tf_op jit(solution)/shard_map/ppermute | solution.py:549
  62.4 1.1 %collective-permute-start.9 = (s16[352,128]{1,0:T(8,128)(2,1)S(1)}, s16[352,128]{1,0:T(8,128)(2,1)S(1)}, u32[]{:S(2)}, u32[]{:S(2)}) collective-permute-start(s16[352,128]{1,0:T(8,128)(2,1)S(1)} %sum_line.3.refs_0_), channel_id=1, source_target_pairs={{0,16},{1,17},{2,18},{3,19},{4,20},{5,21},{6,22},{7,23},{8,24},{9,... | collective-permute-start | bytes 270344 | tf_op jit(solution)/shard_map/ppermute | solution.py:549
  63.5 1.4 %collective-permute-start.10 = (s16[352,128]{1,0:T(8,128)(2,1)S(1)}, s16[352,128]{1,0:T(8,128)(2,1)S(1)}, u32[]{:S(2)}, u32[]{:S(2)}) collective-permute-start(s16[352,128]{1,0:T(8,128)(2,1)S(1)} %sum_line.3.refs_0_), channel_id=1, source_target_pairs={{0,18},{1,19},{2,16},{3,17},{4,22},{5,23},{6,20},{7,21},{8,26},{9,... | collective-permute-start | bytes 270344 | tf_op jit(solution)/shard_map/ppermute | solution.py:549
  64.9 1.0 %collective-permute-done.8.refs_1_ = s16[352,128]{1,0:T(8,128)(2,1)S(1)} collective-permute-done((s16[352,128]{1,0:T(8,128)(2,1)S(1)}, s16[352,128]{1,0:T(8,128)(2,1)S(1)}, u32[]{:S(2)}, u32[]{:S(2)}) %collective-permute-start.8) | collective-permute-done | bytes 90144 | tf_op jit(solution)/shard_map/ppermute | solution.py:549
  66.0 1.0 %collective-permute-done.9.refs_2_ = s16[352,128]{1,0:T(8,128)(2,1)S(1)} collective-permute-done((s16[352,128]{1,0:T(8,128)(2,1)S(1)}, s16[352,128]{1,0:T(8,128)(2,1)S(1)}, u32[]{:S(2)}, u32[]{:S(2)}) %collective-permute-start.9) | collective-permute-done | bytes 90144 | tf_op jit(solution)/shard_map/ppermute | solution.py:549
  67.0 2.0 %collective-permute-done.10.refs_3_ = s16[352,128]{1,0:T(8,128)(2,1)S(1)} collective-permute-done((s16[352,128]{1,0:T(8,128)(2,1)S(1)}, s16[352,128]{1,0:T(8,128)(2,1)S(1)}, u32[]{:S(2)}, u32[]{:S(2)}) %collective-permute-start.10) | collective-permute-done | bytes 90144 | tf_op jit(solution)/shard_map/ppermute | solution.py:549
  69.0 1.3 %collective-permute-done.14.refs_7_ = s16[352,128]{1,0:T(8,128)(2,1)S(1)} collective-permute-done((s16[352,128]{1,0:T(8,128)(2,1)S(1)}, s16[352,128]{1,0:T(8,128)(2,1)S(1)}, u32[]{:S(2)}, u32[]{:S(2)}) %collective-permute-start.14) | collective-permute-done | bytes 90144 | tf_op jit(solution)/shard_map/ppermute | solution.py:549
  70.2 1.8 %unpack.1 = (f32[5,1,128]{2,1,0:T(1,128)}, f32[64,512]{1,0:T(8,128)}, f32[3,512]{1,0:T(4,128)}, f32[1,512]{1,0:T(1,128)}, f32[512,512]{1,0:T(8,128)}, /*index=5*...) custom-call(s32[3]{0:T(128)S(1)} %pad_add_fusion.place_ref, ...), custom_call_target="tpu_custom_call" | custom-call | tf_op jit(solution)/shard_map/unpack/pallas_call | solution.py:729
  (26 shorter events, 0.1 us)
Async XLA Ops:
  1.9 13.7 %copy-start.11 = (bf16[64,1728]{1,0:T(8,128)(2,1)S(1)}, bf16[64,1728]{1,0:T(8,128)(2,1)}, u32[]{:S(2)}) copy-start(bf16[64,1728]{1,0:T(8,128)(2,1)} %param.15) | copy-start | bytes 663556
  2.7 5.5 %copy-start.4 = (f32[1,5,128]{2,0,1:T(1,128)S(1)}, f32[1,5,128]{2,0,1:T(1,128)}, u32[]{:S(2)}) copy-start(f32[1,5,128]{2,0,1:T(1,128)} %param.20) | copy-start | bytes 7684
  2.7 14.8 %collective-permute-start.1 = (bf16[3,8,64,128]{3,2,1,0:T(8,128)(2,1)S(1)}, bf16[3,8,64,128]{3,2,1,0:T(8,128)(2,1)S(1)}, u32[]{:S(2)}, u32[]{:S(2)}) collective-permute-start(bf16[3,8,64,128]{3,2,1,0:T(8,128)(2,1)S(1)} %slice.8), channel_id=1, source_target_pairs={{1,0},{2,1},{3,2},{4,3},{5,4},{6,5},{7,6},{8,7},{9,8},{10,9},{11,1... | collective-permute-start | bytes 1179656 | tf_op jit(solution)/shard_map/ppermute | solution.py:775
  8.1 9.4 %collective-permute-start = (bf16[2,8,64,128]{3,2,1,0:T(8,128)(2,1)}, bf16[2,8,64,128]{3,2,1,0:T(8,128)(2,1)S(1)}, u32[]{:S(2)}, u32[]{:S(2)}) collective-permute-start(bf16[2,8,64,128]{3,2,1,0:T(8,128)(2,1)} %slice.9), channel_id=1, source_target_pairs={{0,1},{1,2},{2,3},{3,4},{4,5},{5,6},{6,7},{7,8},{8,9},{9,10},{10,1... | collective-permute-start | bytes 786440 | tf_op jit(solution)/shard_map/ppermute | solution.py:776
  8.1 0.7 copy-start.7
  8.1 0.7 copy-start.8
  8.1 0.7 copy-start.9
  9.8 12.7 %all-to-all-start = ((f32[16,8,128]{2,1,0:T(8,128)}), f32[16,8,128]{2,1,0:T(8,128)S(1)}, u32[]{:S(2)}, u32[]{:S(2)}) async-start(f32[16,8,128]{2,1,0:T(8,128)} %bitcast.11), calls=%async_computation | async-start | bytes 131072 | tf_op jit(solution)/shard_map/all_to_all | solution.py:785
  16.6 0.7 copy-start.12
  17.5 5.1 %copy-start = (f32[512,512]{1,0:T(8,128)S(1)}, f32[512,512]{1,0:T(8,128)}, u32[]{:S(2)}) copy-start(f32[512,512]{1,0:T(8,128)} %w_mid_hbm.1) | copy-start | bytes 3145732
  17.5 5.1 %copy-start.1 = (f32[64,512]{1,0:T(8,128)S(1)}, f32[64,512]{1,0:T(8,128)}, u32[]{:S(2)}) copy-start(f32[64,512]{1,0:T(8,128)} %w_latent_hbm.1) | copy-start | bytes 393220
  17.5 5.1 %copy-start.2 = (f32[5,512]{1,0:T(8,128)S(1)}, f32[5,512]{1,0:T(8,128)}, u32[]{:S(2)}) copy-start(f32[5,512]{1,0:T(8,128)} %w_out_hbm.1) | copy-start | bytes 30724
  17.5 5.1 %copy-start.3 = (f32[3,512]{1,0:T(4,128)S(1)}, f32[3,512]{1,0:T(4,128)}, u32[]{:S(2)}) copy-start(f32[3,512]{1,0:T(4,128)} %w_pos_hbm.1) | copy-start | bytes 18436
  22.6 0.7 copy-start.6
  22.6 0.7 copy-start.5
  22.6 0.7 copy-start.10
  40.0 2.2 %collective-permute-start.2 = (f32[4,328,128]{2,1,0:T(8,128)S(1)}, f32[4,328,128]{2,1,0:T(8,128)S(1)}, u32[]{:S(2)}, u32[]{:S(2)}) collective-permute-start(f32[4,328,128]{2,1,0:T(8,128)S(1)} %get-tuple-element.31), channel_id=1, source_target_pairs={{0,1},{1,0},{2,3},{3,2},{4,5},{5,4},{6,7},{7,6},{8,9},{9,8},{10,11... | collective-permute-start | bytes 2015240 | tf_op jit(solution)/shard_map/ppermute | solution.py:549
  42.4 4.7 %collective-permute-start.3 = (s16[352,128]{1,0:T(8,128)(2,1)S(1)}, s16[352,128]{1,0:T(8,128)(2,1)S(1)}, u32[]{:S(2)}, u32[]{:S(2)}) collective-permute-start(s16[352,128]{1,0:T(8,128)(2,1)S(1)} %get-tuple-element.33), channel_id=1, source_target_pairs={{0,2},{1,3},{2,0},{3,1},{4,6},{5,7},{6,4},{7,5},{8,10},{9,11},{10,... | collective-permute-start | bytes 270344 | tf_op jit(solution)/shard_map/ppermute | solution.py:549
  42.6 4.6 %collective-permute-start.4 = (s16[352,128]{1,0:T(8,128)(2,1)S(1)}, s16[352,128]{1,0:T(8,128)(2,1)S(1)}, u32[]{:S(2)}, u32[]{:S(2)}) collective-permute-start(s16[352,128]{1,0:T(8,128)(2,1)S(1)} %get-tuple-element.34), channel_id=1, source_target_pairs={{0,16},{1,17},{2,18},{3,19},{4,20},{5,21},{6,22},{7,23},{8,24},{9,... | collective-permute-start | bytes 270344 | tf_op jit(solution)/shard_map/ppermute | solution.py:549
  44.1 6.2 %collective-permute-start.5 = (s16[352,128]{1,0:T(8,128)(2,1)S(1)}, s16[352,128]{1,0:T(8,128)(2,1)S(1)}, u32[]{:S(2)}, u32[]{:S(2)}) collective-permute-start(s16[352,128]{1,0:T(8,128)(2,1)S(1)} %get-tuple-element.35), channel_id=1, source_target_pairs={{0,18},{1,19},{2,16},{3,17},{4,22},{5,23},{6,20},{7,21},{8,26},{9,... | collective-permute-start | bytes 270344 | tf_op jit(solution)/shard_map/ppermute | solution.py:549
  50.4 4.6 %collective-permute-start.6 = (s16[352,128]{1,0:T(8,128)(2,1)S(1)}, s16[352,128]{1,0:T(8,128)(2,1)S(1)}, u32[]{:S(2)}, u32[]{:S(2)}) collective-permute-start(s16[352,128]{1,0:T(8,128)(2,1)S(1)} %sum_plane.1.mine_ref), channel_id=1, source_target_pairs={{0,4},{1,5},{2,6},{3,7},{4,0},{5,1},{6,2},{7,3},{8,12},{9,13},{10,... | collective-permute-start | bytes 270344 | tf_op jit(solution)/shard_map/ppermute | solution.py:549
  55.1 6.1 %collective-permute-start.7 = (s16[352,128]{1,0:T(8,128)(2,1)S(1)}, s16[352,128]{1,0:T(8,128)(2,1)S(1)}, u32[]{:S(2)}, u32[]{:S(2)}) collective-permute-start(s16[352,128]{1,0:T(8,128)(2,1)S(1)} %sum_line.2.mine_ref), channel_id=1, source_target_pairs={{0,8},{1,9},{2,10},{3,11},{4,12},{5,13},{6,14},{7,15},{8,0},{9,1},... | collective-permute-start | bytes 270344 | tf_op jit(solution)/shard_map/ppermute | solution.py:549
  61.4 4.6 %collective-permute-start.8 = (s16[352,128]{1,0:T(8,128)(2,1)S(1)}, s16[352,128]{1,0:T(8,128)(2,1)S(1)}, u32[]{:S(2)}, u32[]{:S(2)}) collective-permute-start(s16[352,128]{1,0:T(8,128)(2,1)S(1)} %sum_line.3.refs_0_), channel_id=1, source_target_pairs={{0,2},{1,3},{2,0},{3,1},{4,6},{5,7},{6,4},{7,5},{8,10},{9,11},{10,... | collective-permute-start | bytes 270344 | tf_op jit(solution)/shard_map/ppermute | solution.py:549
  62.4 4.5 %collective-permute-start.9 = (s16[352,128]{1,0:T(8,128)(2,1)S(1)}, s16[352,128]{1,0:T(8,128)(2,1)S(1)}, u32[]{:S(2)}, u32[]{:S(2)}) collective-permute-start(s16[352,128]{1,0:T(8,128)(2,1)S(1)} %sum_line.3.refs_0_), channel_id=1, source_target_pairs={{0,16},{1,17},{2,18},{3,19},{4,20},{5,21},{6,22},{7,23},{8,24},{9,... | collective-permute-start | bytes 270344 | tf_op jit(solution)/shard_map/ppermute | solution.py:549
  63.5 5.4 %collective-permute-start.10 = (s16[352,128]{1,0:T(8,128)(2,1)S(1)}, s16[352,128]{1,0:T(8,128)(2,1)S(1)}, u32[]{:S(2)}, u32[]{:S(2)}) collective-permute-start(s16[352,128]{1,0:T(8,128)(2,1)S(1)} %sum_line.3.refs_0_), channel_id=1, source_target_pairs={{0,18},{1,19},{2,16},{3,17},{4,22},{5,23},{6,20},{7,21},{8,26},{9,... | collective-permute-start | bytes 270344 | tf_op jit(solution)/shard_map/ppermute | solution.py:549
  64.9 4.0 %collective-permute-start.11 = (s16[352,128]{1,0:T(8,128)(2,1)S(1)}, s16[352,128]{1,0:T(8,128)(2,1)S(1)}, u32[]{:S(2)}, u32[]{:S(2)}) collective-permute-start(s16[352,128]{1,0:T(8,128)(2,1)S(1)} %sum_line.3.refs_0_), channel_id=1, source_target_pairs={{0,1},{1,0},{2,3},{3,2},{4,5},{5,4},{6,7},{7,6},{8,9},{9,8},{10,11... | collective-permute-start | bytes 270344 | tf_op jit(solution)/shard_map/ppermute | solution.py:549
  66.0 3.0 %collective-permute-start.12 = (s16[352,128]{1,0:T(8,128)(2,1)S(1)}, s16[352,128]{1,0:T(8,128)(2,1)S(1)}, u32[]{:S(2)}, u32[]{:S(2)}) collective-permute-start(s16[352,128]{1,0:T(8,128)(2,1)S(1)} %collective-permute-done.8.refs_1_), channel_id=1, source_target_pairs={{0,1},{1,0},{2,3},{3,2},{4,5},{5,4},{6,7},{7,6},{8,9},{9,8},{10,11... | collective-permute-start | bytes 270344 | tf_op jit(solution)/shard_map/ppermute | solution.py:549
  67.0 2.0 %collective-permute-start.13 = (s16[352,128]{1,0:T(8,128)(2,1)S(1)}, s16[352,128]{1,0:T(8,128)(2,1)S(1)}, u32[]{:S(2)}, u32[]{:S(2)}) collective-permute-start(s16[352,128]{1,0:T(8,128)(2,1)S(1)} %collective-permute-done.9.refs_2_), channel_id=1, source_target_pairs={{0,1},{1,0},{2,3},{3,2},{4,5},{5,4},{6,7},{7,6},{8,9},{9,8},{10,11... | collective-permute-start | bytes 270344 | tf_op jit(solution)/shard_map/ppermute | solution.py:549
  68.9 1.3 %collective-permute-start.14 = (s16[352,128]{1,0:T(8,128)(2,1)S(1)}, s16[352,128]{1,0:T(8,128)(2,1)S(1)}, u32[]{:S(2)}, u32[]{:S(2)}) collective-permute-start(s16[352,128]{1,0:T(8,128)(2,1)S(1)} %collective-permute-done.10.refs_3_), channel_id=1, source_target_pairs={{0,1},{1,0},{2,3},{3,2},{4,5},{5,4},{6,7},{7,6},{8,9},{9,8},{10,11... | collective-permute-start | bytes 270344 | tf_op jit(solution)/shard_map/ppermute | solution.py:549

commit v7 on v6

--- a/solution.py
+++ b/solution.py
@@ -218,6 +218,10 @@
     two_high,
     two_low,
     back,
+    mixed_back,
+    first_high,
+    first_low,
+    sums_ref,
     d_high,
     d_low,
     out_t,
@@ -248,6 +252,7 @@
     my_block = place_ref[0]
     my_tile = place_ref[1]
     my_replica = place_ref[2]
+    always = my_tile >= 0
 
     words = words_ref[...]
     words = jnp.concatenate(
@@ -279,66 +284,88 @@
     bias_one = bias_one_ref[...]
     bias_two = bias_two_ref[...]
 
-    def store(index, block, refs, value):
+    part_rows = rows // 2
+
+    def at(part, index, block=None):
+        first = (part * 5 + index) * part_rows
+        if block is None:
+            return slice(first, first + part_rows)
+        return slice(first + block * BLOCK, first + (block + 1) * BLOCK)
+
+    def rows_at(part, block):
+        first = part * part_rows + block * BLOCK
+        return slice(first, first + BLOCK)
+
+    def store(refs, span, value):
         high, low = halves(value)
-        refs[0][pl.ds(pl.multiple_of(index * rows + block * BLOCK, BLOCK), BLOCK), :] = high
-        refs[1][pl.ds(pl.multiple_of(index * rows + block * BLOCK, BLOCK), BLOCK), :] = low
-
-    def fetch(ref, index, block):
-        return ref[pl.ds(pl.multiple_of(index * rows + block * BLOCK, BLOCK), BLOCK), :]
-
-    def layer_one(block, carry):
-        where = fetch(pos, 0, block)
-        pre = (
-            fetch(z_one, 0, block)
-            + (where[:, 0:1] * w_pos[0] + where[:, 1:2] * w_pos[1] + where[:, 2:3] * w_pos[2])
-            + bias_one
-        )
-        act = jnp.tanh(pre)
-        slope = 1.0 - act * act
-        curve = -2.0 * act * slope
-        z_one[pl.ds(pl.multiple_of(block * BLOCK, BLOCK), BLOCK), :] = act
+        refs[0][span, :] = high
+        refs[1][span, :] = low
+
+    def layer_one(part):
         refs = (one_high, one_low)
-        store(0, block, refs, act)
-        for d in range(3):
-            store(1 + d, block, refs, slope * w_pos[d])
-        store(4, block, refs, curve * square)
-        return carry
-
-    lax.fori_loop(0, rows // BLOCK, layer_one, 0)
-
-    def times_mid(dims, source, result, index, carry):
-        span = pl.ds(pl.multiple_of(index * rows, rows), rows)
-        result[span, :] = mul3((source[0][span, :], source[1][span, :]), (mid_high[...], mid_low[...]), dims)
-        return carry
-
-    lax.fori_loop(0, 5, functools.partial(times_mid, NN, (one_high, one_low), mixed), 0)
-
-    def layer_two(block, carry):
-        act = jnp.tanh(fetch(mixed, 0, block) + bias_two)
-        slope = 1.0 - act * act
-        curve = -2.0 * act * slope
+        for block in range(part_rows // BLOCK):
+            here = rows_at(part, block)
+            where = pos[here, :]
+            pre = (
+                z_one[here, :]
+                + (where[:, 0:1] * w_pos[0] + where[:, 1:2] * w_pos[1] + where[:, 2:3] * w_pos[2])
+                + bias_one
+            )
+            act = jnp.tanh(pre)
+            slope = 1.0 - act * act
+            curve = -2.0 * act * slope
+            z_one[here, :] = act
+            store(refs, at(part, 0, block), act)
+            for d in range(3):
+                store(refs, at(part, 1 + d, block), slope * w_pos[d])
+            store(refs, at(part, 4, block), curve * square)
+
+    def times_mid(dims, source, result, part):
+        for index in range(5):
+            span = at(part, index)
+            left = (source[0][span, :], source[1][span, :])
+            result[span, :] = mul3(left, (mid_high[...], mid_low[...]), dims)
+
+    def layer_two(part):
         refs = (two_high, two_low)
-        store(0, block, refs, act)
-        mixed[pl.ds(pl.multiple_of(block * BLOCK, BLOCK), BLOCK), :] = act
-        norm = None
-        for d in range(3):
-            tangent = fetch(mixed, 1 + d, block)
-            store(1 + d, block, refs, slope * tangent)
-            norm = tangent * tangent if norm is None else norm + tangent * tangent
-        store(4, block, refs, slope * fetch(mixed, 4, block) + curve * norm)
-        return carry
-
-    lax.fori_loop(0, rows // BLOCK, layer_two, 0)
+        for block in range(part_rows // BLOCK):
+            act = jnp.tanh(mixed[at(part, 0, block), :] + bias_two)
+            slope = 1.0 - act * act
+            curve = -2.0 * act * slope
+            store(refs, at(part, 0, block), act)
+            mixed[at(part, 0, block), :] = act
+            norm = None
+            for d in range(3):
+                tangent = mixed[at(part, 1 + d, block), :]
+                store(refs, at(part, 1 + d, block), slope * tangent)
+                norm = tangent * tangent if norm is None else norm + tangent * tangent
+            store(refs, at(part, 4, block), slope * mixed[at(part, 4, block), :] + curve * norm)
 
     out_fields = jnp.concatenate([w_out_ref[...], jnp.zeros((3, hidden), F32)], axis=0)
     wo_high, wo_low = halves(out_fields)
     wo_three = jnp.concatenate([out_fields, wo_low.astype(F32), out_fields], axis=0).astype(BF16)
     wo_both = jnp.concatenate([out_fields, wo_low.astype(F32)], axis=0).astype(BF16)
-    for s in range(5):
-        span = slice(s * rows, (s + 1) * rows)
-        both = mul(wo_both, two_high[span, :], NT)
-        out_t[8 * s : 8 * s + 8, :] = both[:8] + both[8:] + mul(wo_high, two_low[span, :], NT)
+
+    def outputs(part):
+        for s in range(5):
+            span = at(part, s)
+            both = mul(wo_both, two_high[span, :], NT)
+            both = both[:8] + both[8:] + mul(wo_high, two_low[span, :], NT)
+            out_t[8 * s : 8 * s + 8, part * part_rows : (part + 1) * part_rows] = both
+
+    @pl.when(always)
+    def _():
+        layer_one(0)
+        times_mid(NN, (one_high, one_low), mixed, 0)
+        layer_one(1)
+        times_mid(NN, (one_high, one_low), mixed, 1)
+        layer_two(0)
+        layer_two(1)
+
+    @pl.when(always)
+    def _():
+        outputs(0)
+        outputs(1)
 
     words_t = words.T
     target = [words_t[4 + f : 5 + f, :] for f in range(5)]
@@ -396,36 +423,75 @@
     for j in range(3):
         d_out_t[34 + j : 35 + j, :] = -VISCOSITY * d_mom[j]
 
-    for s in range(5):
-        span = slice(s * rows, (s + 1) * rows)
-        wanted = d_out_t[8 * s : 8 * s + 8, :]
-        do_low = halves(wanted)[1].astype(F32)
-        back[span, :] = mul(jnp.concatenate([wanted, wanted, do_low], axis=0).astype(BF16), wo_three, TN)
-
-    def second_back(block, total):
-        act = fetch(mixed, 0, block)
-        slope = 1.0 - act * act
-        curve = -2.0 * act * slope
-        tangent = [fetch(mixed, 1 + d, block) for d in range(3)]
-        cot_t = [fetch(back, 1 + d, block) for d in range(3)]
-        cot_l = fetch(back, 4, block)
+    def out_back(part):
+        for s in range(5):
+            wanted = d_out_t[8 * s : 8 * s + 8, part * part_rows : (part + 1) * part_rows]
+            do_low = halves(wanted)[1].astype(F32)
+            wanted = jnp.concatenate([wanted, wanted, do_low], axis=0).astype(BF16)
+            back[at(part, s), :] = mul(wanted, wo_three, TN)
+
+    def second_back(part, total):
         refs = (d_high, d_low)
-        d_slope = cot_l * fetch(mixed, 4, block)
-        norm = None
-        bent = 2.0 * curve * cot_l
-        for d in range(3):
-            store(1 + d, block, refs, slope * cot_t[d] + bent * tangent[d])
-            d_slope = d_slope + cot_t[d] * tangent[d]
-            norm = tangent[d] * tangent[d] if norm is None else norm + tangent[d] * tangent[d]
-        store(4, block, refs, slope * cot_l)
-        d_curve = cot_l * norm
-        d_slope = d_slope - 2.0 * act * d_curve
-        d_act = fetch(back, 0, block) - 2.0 * slope * d_curve - 2.0 * act * d_slope
-        d_pre = slope * d_act
-        store(0, block, refs, d_pre)
-        return total + folded(d_pre)
-
-    grad_two = lax.fori_loop(0, rows // BLOCK, second_back, jnp.zeros((8, hidden), F32))
+        for block in range(part_rows // BLOCK):
+            act = mixed[at(part, 0, block), :]
+            slope = 1.0 - act * act
+            curve = -2.0 * act * slope
+            cot_l = back[at(part, 4, block), :]
+            d_slope = cot_l * mixed[at(part, 4, block), :]
+            norm = None
+            bent = 2.0 * curve * cot_l
+            for d in range(3):
+                tangent = mixed[at(part, 1 + d, block), :]
+                cot_t = back[at(part, 1 + d, block), :]
+                store(refs, at(part, 1 + d, block), slope * cot_t + bent * tangent)
+                d_slope = d_slope + cot_t * tangent
+                norm = tangent * tangent if norm is None else norm + tangent * tangent
+            store(refs, at(part, 4, block), slope * cot_l)
+            d_curve = cot_l * norm
+            d_slope = d_slope - 2.0 * act * d_curve
+            d_act = back[at(part, 0, block), :] - 2.0 * slope * d_curve - 2.0 * act * d_slope
+            d_pre = slope * d_act
+            store(refs, at(part, 0, block), d_pre)
+            total = total + folded(d_pre)
+        return total
+
+    def first_back(part, sums):
+        for block in range(part_rows // BLOCK):
+            here = rows_at(part, block)
+            act = z_one[here, :]
+            slope = 1.0 - act * act
+            curve = -2.0 * act * slope
+            where = pos[here, :]
+            cot_t = [mixed_back[at(part, 1 + d, block), :] for d in range(3)]
+            cot_l = mixed_back[at(part, 4, block), :]
+            d_curve = cot_l * square
+            d_slope = cot_t[0] * w_pos[0] + cot_t[1] * w_pos[1] + cot_t[2] * w_pos[2] - 2.0 * act * d_curve
+            d_act = mixed_back[at(part, 0, block), :] - 2.0 * slope * d_curve - 2.0 * act * d_slope
+            d_pre = slope * d_act
+            high, low = halves(d_pre)
+            first_high[here, :] = high
+            first_low[here, :] = low
+            sums = (
+                [sums[0] + folded(d_pre)]
+                + [sums[1 + d] + folded(where[:, d : d + 1] * d_pre + slope * cot_t[d]) for d in range(3)]
+                + [sums[4] + folded(curve * cot_l)]
+            )
+        return sums
+
+    @pl.when(always)
+    def _():
+        out_back(0)
+        total = second_back(0, jnp.zeros((8, hidden), F32))
+        out_back(1)
+        sums_ref[5] = second_back(1, total)
+
+    @pl.when(always)
+    def _():
+        times_mid(NT, (d_high, d_low), mixed_back, 0)
+        total = first_back(0, [jnp.zeros((8, hidden), F32)] * 5)
+        times_mid(NT, (d_high, d_low), mixed_back, 1)
+        for number, value in enumerate(first_back(1, total)):
+            sums_ref[number] = value
 
     def put(part, first, value):
         while value.shape[0]:
@@ -445,41 +511,16 @@
             for side in range(2):
                 put(2 * right + side, left * wide, part[:, side * LANES : (side + 1) * LANES])
 
-    lax.fori_loop(0, 5, functools.partial(times_mid, NT, (d_high, d_low), back), 0)
-
-    def first_back(block, totals):
-        act = fetch(z_one, 0, block)
-        slope = 1.0 - act * act
-        curve = -2.0 * act * slope
-        where = fetch(pos, 0, block)
-        cot_t = [fetch(back, 1 + d, block) for d in range(3)]
-        cot_l = fetch(back, 4, block)
-        d_curve = cot_l * square
-        d_slope = cot_t[0] * w_pos[0] + cot_t[1] * w_pos[1] + cot_t[2] * w_pos[2] - 2.0 * act * d_curve
-        d_act = fetch(back, 0, block) - 2.0 * slope * d_curve - 2.0 * act * d_slope
-        d_pre = slope * d_act
-        store(0, block, (d_high, d_low), d_pre)
-        sums = [totals[0] + folded(d_pre)]
-        for d in range(3):
-            sums.append(totals[1 + d] + folded(where[:, d : d + 1] * d_pre + slope * cot_t[d]))
-        sums.append(totals[4] + folded(curve * cot_l))
-        return tuple(sums)
-
-    sums = lax.fori_loop(
-        0, rows // BLOCK, first_back, tuple(jnp.zeros((8, hidden), F32) for _ in range(5))
-    )
+    sums = [sums_ref[number] for number in range(6)]
     d_square = jnp.sum(sums[4], axis=0, keepdims=True)
-    grad_latent = mul(code[...], d_high[0:rows, :], TN) + mul(code[...], d_low[0:rows, :], TN)
-
-    grad_out = None
-    for s in range(5):
-        span = slice(s * rows, (s + 1) * rows)
-        wanted = d_out_t[8 * s : 8 * s + 8, :]
-        do_high, do_low = halves(wanted)
-        do_both = jnp.concatenate([wanted, do_low.astype(F32)], axis=0).astype(BF16)
-        both = mul(do_both, two_high[span, :])
-        term = both[:8] + both[8:] + mul(do_high, two_low[span, :])
-        grad_out = term if grad_out is None else grad_out + term
+    grad_latent = mul(code[...], first_high[...], TN) + mul(code[...], first_low[...], TN)
+
+    parts = [d_out_t[8 * s : 8 * s + 8, p * part_rows : (p + 1) * part_rows] for p in range(2) for s in range(5)]
+    flat = jnp.concatenate(parts, axis=1)
+    fl_high, fl_low = halves(flat)
+    fl_both = jnp.concatenate([flat, fl_low.astype(F32)], axis=0).astype(BF16)
+    grad_out = mul(fl_both, two_high[...])
+    grad_out = grad_out[:8] + grad_out[8:] + mul(fl_high, two_low[...])
 
     lane_row = lax.broadcasted_iota(jnp.int32, (1, hidden), 1)
     last = jnp.where(lane_row == 5, jnp.sum(point_loss), 0.0)
@@ -488,7 +529,7 @@
     grad_pos = [jnp.sum(sums[1 + d], axis=0, keepdims=True) + 2.0 * w_pos[d] * d_square for d in range(3)]
     misc = grad_pos + [
         jnp.sum(sums[0], axis=0, keepdims=True),
-        jnp.sum(grad_two, axis=0, keepdims=True),
+        jnp.sum(sums[5], axis=0, keepdims=True),
         last,
     ]
     misc = jnp.concatenate(misc + [jnp.zeros((2, hidden), F32)], axis=0)
@@ -664,6 +705,10 @@
             wide(BF16),
             wide(BF16),
             wide(F32),
+            wide(F32),
+            pltpu.VMEM((rows, hidden), BF16),
+            pltpu.VMEM((rows, hidden), BF16),
+            pltpu.VMEM((6, 8, hidden), F32),
             wide(BF16),
             wide(BF16),
             pltpu.VMEM((40, rows), F32),

time: 72.4 us -> 71.4 us (0.986)
  Pallas kernels: 21.9 us -> 21 us
    pallas_call x1, Pallas kernels: 16.8 us -> 15.8 us  [main(): pl.pallas_call(functools.partial(main_kernel, plan), out_shape=(outs, out...]
where the time goes in v7:
time: 71.4 us; the launch traced here: 71.1 us
  waiting for transfers between devices  25 us (35%)
  Pallas kernels  21 us (29%)
  starting transfers between devices  19.1 us (27%)
  local copies, waits for them, and re-layouts  5.05 us (7%)
  between operations  0.87 us (1%)
    ppermute x13, waiting for transfers between devices, swapped(): lax.ppermute(value, ('replica', 'tile'), [(i, i ^ mask) for i in range(pl...  21.8 us
    pallas_call x1, Pallas kernels, main(): pl.pallas_call(functools.partial(main_kernel, plan), out_shape=(outs, out...  15.8 us
    ppermute x13, starting transfers between devices, swapped(): lax.ppermute(value, ('replica', 'tile'), [(i, i ^ mask) for i in range(pl...  7.86 us
    all_to_all x1, starting transfers between devices, body(): lax.all_to_all(words.reshape(tiles, 8, WORDS), 'tile', split_axis=0, conc...  5.83 us
    ppermute x1, starting transfers between devices, body(): right = lax.ppermute(to_left, 'tile', down)  5.44 us
    unnamed x27, local copies, waits for them, and re-layouts  3.26 us
    all_to_all x1, waiting for transfers between devices, body(): lax.all_to_all(words.reshape(tiles, 8, WORDS), 'tile', split_axis=0, conc...  3.22 us
    pallas_call x1, Pallas kernels, unpack(): pl.pallas_call(functools.partial(unpack_kernel, plan), out_shape=tuple((j...  1.83 us
  transfers between devices with their start and end apart: 16, of which 11 were waited for; matrix products, arithmetic and copies ran while one was open for 2% of the time, Pallas kernels for 4%

profile of v7, /device:TPU:0, one launch (start us, length us, event | category | flops | bytes accessed | tf_op | source)
XLA Modules:
  0.0 71.1 jit_solution(8734670086336438652)
XLA Ops:
  0.6 1.2 %copy.30 = bf16[1,64,4,8,128]{4,1,3,2,0:T(8,128)(2,1)S(1)} copy(bf16[1,64,4,8,128]{4,3,2,1,0:T(8,128)(2,1)} %param.14) | data formatting | bytes 1048576 | tf_op args[0]
  1.9 0.0 copy-start.11
  1.9 0.7 %slice.9 = bf16[2,8,64,128]{3,2,1,0:T(8,128)(2,1)} slice(bf16[4,8,64,128]{3,2,1,0:T(8,128)(2,1)S(1)} %bitcast.24), slice={[2:4], [0:8], [0:64], [0:128]} | slice | bytes 524288 | tf_op jit(solution)/shard_map/slice | solution.py:816
  2.7 5.4 %collective-permute-start.1 = (bf16[3,8,64,128]{3,2,1,0:T(8,128)(2,1)S(1)}, bf16[3,8,64,128]{3,2,1,0:T(8,128)(2,1)S(1)}, u32[]{:S(2)}, u32[]{:S(2)}) collective-permute-start(bf16[3,8,64,128]{3,2,1,0:T(8,128)(2,1)S(1)} %slice.8), channel_id=1, source_target_pairs={{1,0},{2,1},{3,2},{4,3},{5,4},{6,5},{7,6},{8,7},{9,8},{10,9},{11,1... | collective-permute-start | bytes 1179656 | tf_op jit(solution)/shard_map/ppermute | solution.py:820
  8.1 0.0 collective-permute-start
  8.1 0.7 copy-done.7
  8.8 0.0 copy-done.9
  8.8 1.0 %route.1 = f32[128,128]{1,0:T(8,128)} custom-call(s32[1,128]{1,0:T(1,128)S(1)} %bitcast.31, s32[1,128]{1,0:T(1,128)S(1)} %copy-done.9, f32[3,1,128]{2,1,0:T(1,128)S(1)} %bitcast.30, f32[5,1,128]{2,1,0:T(1,128)S(1)} %bitcast.27), custom_call_target="tpu_custom_call" | custom-call | tf_op jit(solution)/shard_map/route/pallas_call | solution.py:93
  9.8 5.8 %all-to-all-start = ((f32[16,8,128]{2,1,0:T(8,128)}), f32[16,8,128]{2,1,0:T(8,128)S(1)}, u32[]{:S(2)}, u32[]{:S(2)}) async-start(f32[16,8,128]{2,1,0:T(8,128)} %bitcast.11), calls=%async_computation | async-start | bytes 131072 | tf_op jit(solution)/shard_map/all_to_all | solution.py:830
  15.7 0.3 reshape.42
  16.0 0.3 copy.27
  16.3 0.4 reshape.43.weight_ref
  16.6 0.0 copy-start.12
  16.6 0.7 copy-done.12
  17.3 0.1 copy.28.bias_ref
  17.4 0.1 pad_add_fusion.place_ref
  17.5 0.0 collective-permute-done.left_ref
  17.5 0.0 copy-start.2
  17.5 0.0 copy-start.3
  17.5 1.8 %convolve.1.lat = bf16[20,64,256]{2,1,0:T(8,128)(2,1)S(1)} custom-call(bf16[2,8,64,128]{3,2,1,0:T(8,128)(2,1)S(1)} %collective-permute-done.left_ref, bf16[4,8,64,128]{3,2,1,0:T(8,128)(2,1)S(1)} %bitcast.25, bf16[3,8,64,128]{3,2,1,0:T(8,128)(2,1)S(1)} %collective-permute-done.1.right_ref, bf16[3,192,192]{2,1,0:T(8,128)(2,1)S(1)} %reshape.43.weight_ref, ...), custom_call_target="tpu_custom_call" | custom-call | flops 3221225472 | bytes 4194304 | tf_op jit(solution)/shard_map/convolve/pallas_call | solution.py:154
  19.3 3.2 %all-to-all-done = f32[16,8,128]{2,1,0:T(8,128)S(1)} async-done(((f32[16,8,128]{2,1,0:T(8,128)}), f32[16,8,128]{2,1,0:T(8,128)S(1)}, u32[]{:S(2)}, u32[]{:S(2)}) %all-to-all-start) | async-done | bytes 65568 | tf_op jit(solution)/shard_map/all_to_all | solution.py:830
  22.6 0.6 copy-done.6
  23.2 0.0 copy-done.5
  23.2 15.8 %encode_decode.1 = (f32[4,328,128]{2,1,0:T(8,128)S(1)}, f32[4,328,128]{2,1,0:T(8,128)S(1)}) custom-call(s32[3]{0:T(128)S(1)} %pad_add_fusion.place_ref, bf16[20,64,256]{2,1,0:T(8,128)(2,1)S(1)} %convolve.1.lat, f32[128,128]{1,0:T(8,128)S(1)} %bitcast.26, f32[64,512]{1,0:T(8,128)S(1)} %copy-done.1, f32[3,512]{1,0:T(4,128)S(1)} %copy-done.3, ...), custom_call_target="tpu_custom_call" | custom-call | tf_op jit(solution)/shard_map/encode_decode/pallas_call | solution.py:693
  39.1 0.1 collective-permute-start.2
  39.1 2.1 %collective-permute-done.2.got_ref = f32[4,328,128]{2,1,0:T(8,128)S(1)} collective-permute-done((f32[4,328,128]{2,1,0:T(8,128)S(1)}, f32[4,328,128]{2,1,0:T(8,128)S(1)}, u32[]{:S(2)}, u32[]{:S(2)}) %collective-permute-start.2) | collective-permute-done | bytes 671776 | tf_op jit(solution)/shard_map/ppermute | solution.py:590
  41.2 0.2 sum_core.1
  41.4 0.2 collective-permute-start.3
  41.6 1.5 %collective-permute-start.4 = (s16[352,128]{1,0:T(8,128)(2,1)S(1)}, s16[352,128]{1,0:T(8,128)(2,1)S(1)}, u32[]{:S(2)}, u32[]{:S(2)}) collective-permute-start(s16[352,128]{1,0:T(8,128)(2,1)S(1)} %get-tuple-element.34), channel_id=1, source_target_pairs={{0,16},{1,17},{2,18},{3,19},{4,20},{5,21},{6,22},{7,23},{8,24},{9,... | collective-permute-start | bytes 270344 | tf_op jit(solution)/shard_map/ppermute | solution.py:590
  43.1 1.9 %collective-permute-start.5 = (s16[352,128]{1,0:T(8,128)(2,1)S(1)}, s16[352,128]{1,0:T(8,128)(2,1)S(1)}, u32[]{:S(2)}, u32[]{:S(2)}) collective-permute-start(s16[352,128]{1,0:T(8,128)(2,1)S(1)} %get-tuple-element.35), channel_id=1, source_target_pairs={{0,18},{1,19},{2,16},{3,17},{4,22},{5,23},{6,20},{7,21},{8,26},{9,... | collective-permute-start | bytes 270344 | tf_op jit(solution)/shard_map/ppermute | solution.py:590
  45.0 1.2 %collective-permute-done.3.refs_0_ = s16[352,128]{1,0:T(8,128)(2,1)S(1)} collective-permute-done((s16[352,128]{1,0:T(8,128)(2,1)S(1)}, s16[352,128]{1,0:T(8,128)(2,1)S(1)}, u32[]{:S(2)}, u32[]{:S(2)}) %collective-permute-start.3) | collective-permute-done | bytes 90144 | tf_op jit(solution)/shard_map/ppermute | solution.py:590
  46.1 0.1 collective-permute-done.4.refs_1_
  46.2 3.1 %collective-permute-done.5.refs_2_ = s16[352,128]{1,0:T(8,128)(2,1)S(1)} collective-permute-done((s16[352,128]{1,0:T(8,128)(2,1)S(1)}, s16[352,128]{1,0:T(8,128)(2,1)S(1)}, u32[]{:S(2)}, u32[]{:S(2)}) %collective-permute-start.5) | collective-permute-done | bytes 90144 | tf_op jit(solution)/shard_map/ppermute | solution.py:590
  49.3 0.1 sum_plane.1.mine_ref
  49.4 0.3 collective-permute-start.6
  49.7 4.3 %collective-permute-done.6.other_ref = s16[352,128]{1,0:T(8,128)(2,1)S(1)} collective-permute-done((s16[352,128]{1,0:T(8,128)(2,1)S(1)}, s16[352,128]{1,0:T(8,128)(2,1)S(1)}, u32[]{:S(2)}, u32[]{:S(2)}) %collective-permute-start.6) | collective-permute-done | bytes 90144 | tf_op jit(solution)/shard_map/ppermute | solution.py:590
  54.0 0.1 sum_line.2.mine_ref
  54.1 0.4 collective-permute-start.7
  54.5 5.7 %collective-permute-done.7.other_ref = s16[352,128]{1,0:T(8,128)(2,1)S(1)} collective-permute-done((s16[352,128]{1,0:T(8,128)(2,1)S(1)}, s16[352,128]{1,0:T(8,128)(2,1)S(1)}, u32[]{:S(2)}, u32[]{:S(2)}) %collective-permute-start.7) | collective-permute-done | bytes 90144 | tf_op jit(solution)/shard_map/ppermute | solution.py:590
  60.3 0.1 sum_line.3.refs_0_
  60.4 1.1 %collective-permute-start.8 = (s16[352,128]{1,0:T(8,128)(2,1)S(1)}, s16[352,128]{1,0:T(8,128)(2,1)S(1)}, u32[]{:S(2)}, u32[]{:S(2)}) collective-permute-start(s16[352,128]{1,0:T(8,128)(2,1)S(1)} %sum_line.3.refs_0_), channel_id=1, source_target_pairs={{0,2},{1,3},{2,0},{3,1},{4,6},{5,7},{6,4},{7,5},{8,10},{9,11},{10,... | collective-permute-start | bytes 270344 | tf_op jit(solution)/shard_map/ppermute | solution.py:590
  61.5 1.1 %collective-permute-start.9 = (s16[352,128]{1,0:T(8,128)(2,1)S(1)}, s16[352,128]{1,0:T(8,128)(2,1)S(1)}, u32[]{:S(2)}, u32[]{:S(2)}) collective-permute-start(s16[352,128]{1,0:T(8,128)(2,1)S(1)} %sum_line.3.refs_0_), channel_id=1, source_target_pairs={{0,16},{1,17},{2,18},{3,19},{4,20},{5,21},{6,22},{7,23},{8,24},{9,... | collective-permute-start | bytes 270344 | tf_op jit(solution)/shard_map/ppermute | solution.py:590
  62.5 1.4 %collective-permute-start.10 = (s16[352,128]{1,0:T(8,128)(2,1)S(1)}, s16[352,128]{1,0:T(8,128)(2,1)S(1)}, u32[]{:S(2)}, u32[]{:S(2)}) collective-permute-start(s16[352,128]{1,0:T(8,128)(2,1)S(1)} %sum_line.3.refs_0_), channel_id=1, source_target_pairs={{0,18},{1,19},{2,16},{3,17},{4,22},{5,23},{6,20},{7,21},{8,26},{9,... | collective-permute-start | bytes 270344 | tf_op jit(solution)/shard_map/ppermute | solution.py:590
  63.9 1.0 %collective-permute-done.8.refs_1_ = s16[352,128]{1,0:T(8,128)(2,1)S(1)} collective-permute-done((s16[352,128]{1,0:T(8,128)(2,1)S(1)}, s16[352,128]{1,0:T(8,128)(2,1)S(1)}, u32[]{:S(2)}, u32[]{:S(2)}) %collective-permute-start.8) | collective-permute-done | bytes 90144 | tf_op jit(solution)/shard_map/ppermute | solution.py:590
  65.0 1.0 %collective-permute-done.9.refs_2_ = s16[352,128]{1,0:T(8,128)(2,1)S(1)} collective-permute-done((s16[352,128]{1,0:T(8,128)(2,1)S(1)}, s16[352,128]{1,0:T(8,128)(2,1)S(1)}, u32[]{:S(2)}, u32[]{:S(2)}) %collective-permute-start.9) | collective-permute-done | bytes 90144 | tf_op jit(solution)/shard_map/ppermute | solution.py:590
  66.0 2.0 %collective-permute-done.10.refs_3_ = s16[352,128]{1,0:T(8,128)(2,1)S(1)} collective-permute-done((s16[352,128]{1,0:T(8,128)(2,1)S(1)}, s16[352,128]{1,0:T(8,128)(2,1)S(1)}, u32[]{:S(2)}, u32[]{:S(2)}) %collective-permute-start.10) | collective-permute-done | bytes 90144 | tf_op jit(solution)/shard_map/ppermute | solution.py:590
  68.0 1.3 %collective-permute-done.14.refs_7_ = s16[352,128]{1,0:T(8,128)(2,1)S(1)} collective-permute-done((s16[352,128]{1,0:T(8,128)(2,1)S(1)}, s16[352,128]{1,0:T(8,128)(2,1)S(1)}, u32[]{:S(2)}, u32[]{:S(2)}) %collective-permute-start.14) | collective-permute-done | bytes 90144 | tf_op jit(solution)/shard_map/ppermute | solution.py:590
  69.3 1.8 %unpack.1 = (f32[5,1,128]{2,1,0:T(1,128)}, f32[64,512]{1,0:T(8,128)}, f32[3,512]{1,0:T(4,128)}, f32[1,512]{1,0:T(1,128)}, f32[512,512]{1,0:T(8,128)}, /*index=5*...) custom-call(s32[3]{0:T(128)S(1)} %pad_add_fusion.place_ref, ...), custom_call_target="tpu_custom_call" | custom-call | tf_op jit(solution)/shard_map/unpack/pallas_call | solution.py:774
  (26 shorter events, 0.1 us)
Async XLA Ops:
  1.9 13.7 %copy-start.11 = (bf16[64,1728]{1,0:T(8,128)(2,1)S(1)}, bf16[64,1728]{1,0:T(8,128)(2,1)}, u32[]{:S(2)}) copy-start(bf16[64,1728]{1,0:T(8,128)(2,1)} %param.15) | copy-start | bytes 663556
  2.7 5.5 %copy-start.4 = (f32[1,5,128]{2,0,1:T(1,128)S(1)}, f32[1,5,128]{2,0,1:T(1,128)}, u32[]{:S(2)}) copy-start(f32[1,5,128]{2,0,1:T(1,128)} %param.20) | copy-start | bytes 7684
  2.7 14.8 %collective-permute-start.1 = (bf16[3,8,64,128]{3,2,1,0:T(8,128)(2,1)S(1)}, bf16[3,8,64,128]{3,2,1,0:T(8,128)(2,1)S(1)}, u32[]{:S(2)}, u32[]{:S(2)}) collective-permute-start(bf16[3,8,64,128]{3,2,1,0:T(8,128)(2,1)S(1)} %slice.8), channel_id=1, source_target_pairs={{1,0},{2,1},{3,2},{4,3},{5,4},{6,5},{7,6},{8,7},{9,8},{10,9},{11,1... | collective-permute-start | bytes 1179656 | tf_op jit(solution)/shard_map/ppermute | solution.py:820
  8.1 9.4 %collective-permute-start = (bf16[2,8,64,128]{3,2,1,0:T(8,128)(2,1)}, bf16[2,8,64,128]{3,2,1,0:T(8,128)(2,1)S(1)}, u32[]{:S(2)}, u32[]{:S(2)}) collective-permute-start(bf16[2,8,64,128]{3,2,1,0:T(8,128)(2,1)} %slice.9), channel_id=1, source_target_pairs={{0,1},{1,2},{2,3},{3,4},{4,5},{5,6},{6,7},{7,8},{8,9},{9,10},{10,1... | collective-permute-start | bytes 786440 | tf_op jit(solution)/shard_map/ppermute | solution.py:821
  8.1 0.7 copy-start.7
  8.1 0.7 copy-start.8
  8.1 0.7 copy-start.9
  9.8 12.7 %all-to-all-start = ((f32[16,8,128]{2,1,0:T(8,128)}), f32[16,8,128]{2,1,0:T(8,128)S(1)}, u32[]{:S(2)}, u32[]{:S(2)}) async-start(f32[16,8,128]{2,1,0:T(8,128)} %bitcast.11), calls=%async_computation | async-start | bytes 131072 | tf_op jit(solution)/shard_map/all_to_all | solution.py:830
  16.6 0.7 copy-start.12
  17.5 5.1 %copy-start = (f32[512,512]{1,0:T(8,128)S(1)}, f32[512,512]{1,0:T(8,128)}, u32[]{:S(2)}) copy-start(f32[512,512]{1,0:T(8,128)} %w_mid_hbm.1) | copy-start | bytes 3145732
  17.5 5.1 %copy-start.1 = (f32[64,512]{1,0:T(8,128)S(1)}, f32[64,512]{1,0:T(8,128)}, u32[]{:S(2)}) copy-start(f32[64,512]{1,0:T(8,128)} %w_latent_hbm.1) | copy-start | bytes 393220
  17.5 5.1 %copy-start.2 = (f32[5,512]{1,0:T(8,128)S(1)}, f32[5,512]{1,0:T(8,128)}, u32[]{:S(2)}) copy-start(f32[5,512]{1,0:T(8,128)} %w_out_hbm.1) | copy-start | bytes 30724
  17.5 5.1 %copy-start.3 = (f32[3,512]{1,0:T(4,128)S(1)}, f32[3,512]{1,0:T(4,128)}, u32[]{:S(2)}) copy-start(f32[3,512]{1,0:T(4,128)} %w_pos_hbm.1) | copy-start | bytes 18436
  22.5 0.7 copy-start.6
  22.6 0.7 copy-start.5
  22.6 0.7 copy-start.10
  39.1 2.2 %collective-permute-start.2 = (f32[4,328,128]{2,1,0:T(8,128)S(1)}, f32[4,328,128]{2,1,0:T(8,128)S(1)}, u32[]{:S(2)}, u32[]{:S(2)}) collective-permute-start(f32[4,328,128]{2,1,0:T(8,128)S(1)} %get-tuple-element.31), channel_id=1, source_target_pairs={{0,1},{1,0},{2,3},{3,2},{4,5},{5,4},{6,7},{7,6},{8,9},{9,8},{10,11... | collective-permute-start | bytes 2015240 | tf_op jit(solution)/shard_map/ppermute | solution.py:590
  41.4 4.7 %collective-permute-start.3 = (s16[352,128]{1,0:T(8,128)(2,1)S(1)}, s16[352,128]{1,0:T(8,128)(2,1)S(1)}, u32[]{:S(2)}, u32[]{:S(2)}) collective-permute-start(s16[352,128]{1,0:T(8,128)(2,1)S(1)} %get-tuple-element.33), channel_id=1, source_target_pairs={{0,2},{1,3},{2,0},{3,1},{4,6},{5,7},{6,4},{7,5},{8,10},{9,11},{10,... | collective-permute-start | bytes 270344 | tf_op jit(solution)/shard_map/ppermute | solution.py:590
  41.6 4.6 %collective-permute-start.4 = (s16[352,128]{1,0:T(8,128)(2,1)S(1)}, s16[352,128]{1,0:T(8,128)(2,1)S(1)}, u32[]{:S(2)}, u32[]{:S(2)}) collective-permute-start(s16[352,128]{1,0:T(8,128)(2,1)S(1)} %get-tuple-element.34), channel_id=1, source_target_pairs={{0,16},{1,17},{2,18},{3,19},{4,20},{5,21},{6,22},{7,23},{8,24},{9,... | collective-permute-start | bytes 270344 | tf_op jit(solution)/shard_map/ppermute | solution.py:590
  43.1 6.2 %collective-permute-start.5 = (s16[352,128]{1,0:T(8,128)(2,1)S(1)}, s16[352,128]{1,0:T(8,128)(2,1)S(1)}, u32[]{:S(2)}, u32[]{:S(2)}) collective-permute-start(s16[352,128]{1,0:T(8,128)(2,1)S(1)} %get-tuple-element.35), channel_id=1, source_target_pairs={{0,18},{1,19},{2,16},{3,17},{4,22},{5,23},{6,20},{7,21},{8,26},{9,... | collective-permute-start | bytes 270344 | tf_op jit(solution)/shard_map/ppermute | solution.py:590
  49.4 4.6 %collective-permute-start.6 = (s16[352,128]{1,0:T(8,128)(2,1)S(1)}, s16[352,128]{1,0:T(8,128)(2,1)S(1)}, u32[]{:S(2)}, u32[]{:S(2)}) collective-permute-start(s16[352,128]{1,0:T(8,128)(2,1)S(1)} %sum_plane.1.mine_ref), channel_id=1, source_target_pairs={{0,4},{1,5},{2,6},{3,7},{4,0},{5,1},{6,2},{7,3},{8,12},{9,13},{10,... | collective-permute-start | bytes 270344 | tf_op jit(solution)/shard_map/ppermute | solution.py:590
  54.1 6.1 %collective-permute-start.7 = (s16[352,128]{1,0:T(8,128)(2,1)S(1)}, s16[352,128]{1,0:T(8,128)(2,1)S(1)}, u32[]{:S(2)}, u32[]{:S(2)}) collective-permute-start(s16[352,128]{1,0:T(8,128)(2,1)S(1)} %sum_line.2.mine_ref), channel_id=1, source_target_pairs={{0,8},{1,9},{2,10},{3,11},{4,12},{5,13},{6,14},{7,15},{8,0},{9,1},... | collective-permute-start | bytes 270344 | tf_op jit(solution)/shard_map/ppermute | solution.py:590
  60.4 4.6 %collective-permute-start.8 = (s16[352,128]{1,0:T(8,128)(2,1)S(1)}, s16[352,128]{1,0:T(8,128)(2,1)S(1)}, u32[]{:S(2)}, u32[]{:S(2)}) collective-permute-start(s16[352,128]{1,0:T(8,128)(2,1)S(1)} %sum_line.3.refs_0_), channel_id=1, source_target_pairs={{0,2},{1,3},{2,0},{3,1},{4,6},{5,7},{6,4},{7,5},{8,10},{9,11},{10,... | collective-permute-start | bytes 270344 | tf_op jit(solution)/shard_map/ppermute | solution.py:590
  61.5 4.5 %collective-permute-start.9 = (s16[352,128]{1,0:T(8,128)(2,1)S(1)}, s16[352,128]{1,0:T(8,128)(2,1)S(1)}, u32[]{:S(2)}, u32[]{:S(2)}) collective-permute-start(s16[352,128]{1,0:T(8,128)(2,1)S(1)} %sum_line.3.refs_0_), channel_id=1, source_target_pairs={{0,16},{1,17},{2,18},{3,19},{4,20},{5,21},{6,22},{7,23},{8,24},{9,... | collective-permute-start | bytes 270344 | tf_op jit(solution)/shard_map/ppermute | solution.py:590
  62.5 5.4 %collective-permute-start.10 = (s16[352,128]{1,0:T(8,128)(2,1)S(1)}, s16[352,128]{1,0:T(8,128)(2,1)S(1)}, u32[]{:S(2)}, u32[]{:S(2)}) collective-permute-start(s16[352,128]{1,0:T(8,128)(2,1)S(1)} %sum_line.3.refs_0_), channel_id=1, source_target_pairs={{0,18},{1,19},{2,16},{3,17},{4,22},{5,23},{6,20},{7,21},{8,26},{9,... | collective-permute-start | bytes 270344 | tf_op jit(solution)/shard_map/ppermute | solution.py:590
  63.9 4.0 %collective-permute-start.11 = (s16[352,128]{1,0:T(8,128)(2,1)S(1)}, s16[352,128]{1,0:T(8,128)(2,1)S(1)}, u32[]{:S(2)}, u32[]{:S(2)}) collective-permute-start(s16[352,128]{1,0:T(8,128)(2,1)S(1)} %sum_line.3.refs_0_), channel_id=1, source_target_pairs={{0,1},{1,0},{2,3},{3,2},{4,5},{5,4},{6,7},{7,6},{8,9},{9,8},{10,11... | collective-permute-start | bytes 270344 | tf_op jit(solution)/shard_map/ppermute | solution.py:590
  65.0 3.0 %collective-permute-start.12 = (s16[352,128]{1,0:T(8,128)(2,1)S(1)}, s16[352,128]{1,0:T(8,128)(2,1)S(1)}, u32[]{:S(2)}, u32[]{:S(2)}) collective-permute-start(s16[352,128]{1,0:T(8,128)(2,1)S(1)} %collective-permute-done.8.refs_1_), channel_id=1, source_target_pairs={{0,1},{1,0},{2,3},{3,2},{4,5},{5,4},{6,7},{7,6},{8,9},{9,8},{10,11... | collective-permute-start | bytes 270344 | tf_op jit(solution)/shard_map/ppermute | solution.py:590
  66.0 2.0 %collective-permute-start.13 = (s16[352,128]{1,0:T(8,128)(2,1)S(1)}, s16[352,128]{1,0:T(8,128)(2,1)S(1)}, u32[]{:S(2)}, u32[]{:S(2)}) collective-permute-start(s16[352,128]{1,0:T(8,128)(2,1)S(1)} %collective-permute-done.9.refs_2_), channel_id=1, source_target_pairs={{0,1},{1,0},{2,3},{3,2},{4,5},{5,4},{6,7},{7,6},{8,9},{9,8},{10,11... | collective-permute-start | bytes 270344 | tf_op jit(solution)/shard_map/ppermute | solution.py:590
  68.0 1.3 %collective-permute-start.14 = (s16[352,128]{1,0:T(8,128)(2,1)S(1)}, s16[352,128]{1,0:T(8,128)(2,1)S(1)}, u32[]{:S(2)}, u32[]{:S(2)}) collective-permute-start(s16[352,128]{1,0:T(8,128)(2,1)S(1)} %collective-permute-done.10.refs_3_), channel_id=1, source_target_pairs={{0,1},{1,0},{2,3},{3,2},{4,5},{5,4},{6,7},{7,6},{8,9},{9,8},{10,11... | collective-permute-start | bytes 270344 | tf_op jit(solution)/shard_map/ppermute | solution.py:590

commit v8 on v7

--- a/solution.py
+++ b/solution.py
@@ -130,9 +130,37 @@
     return jnp.concatenate(sides, axis=1)
 
 
-def conv_kernel(left_ref, here_ref, right_ref, weight_ref, bias_ref, lat_ref):
-    planes, rows_y = here_ref.shape[0], here_ref.shape[1]
-    bias = bias_ref[...]
+def conv_kernel(
+    left_ref,
+    here_ref,
+    right_ref,
+    taps_ref,
+    bias_ref,
+    bias_one_ref,
+    bias_two_ref,
+    bias_out_ref,
+    lat_ref,
+    small_ref,
+    weight_ref,
+):
+    planes, rows_y, channels = here_ref.shape[:3]
+    taps = taps_ref[...].astype(F32)
+    for step in range(3):
+        rows = []
+        for step_z in range(3):
+            numbers = [9 * step + 3 * step_y + step_z for step_y in range(3)]
+            rows.append(
+                jnp.concatenate([taps[:, n * channels : (n + 1) * channels] for n in numbers], axis=1)
+            )
+        weight_ref[step] = jnp.concatenate(rows, axis=0).astype(BF16)
+    diagonal = lax.broadcasted_iota(jnp.int32, (channels, channels), 0) == lax.broadcasted_iota(
+        jnp.int32, (channels, channels), 1
+    )
+    bias = jnp.sum(jnp.where(diagonal, bias_ref[...], 0.0), axis=1, keepdims=True)
+    small_ref[...] = jnp.zeros_like(small_ref)
+    small_ref[0:1, :] = bias_one_ref[...]
+    small_ref[1:2, :] = bias_two_ref[...]
+    small_ref[2:3, 0:5] = bias_out_ref[...]
     for x in range(planes + 1):
         taps = []
         for step in range(3):
@@ -148,18 +176,22 @@
             lat_ref[x * (rows_y // 2) + pair] = jax.nn.gelu(summed).astype(BF16)
 
 
-def convolve(left, here, right, taps, conv_bias):
+def convolve(left, here, right, taps, conv_bias, biases):
     planes, rows_y, channels, rows_z = here.shape
     pairs = (planes + 1) * rows_y // 2
     return pl.pallas_call(
         conv_kernel,
-        out_shape=jax.ShapeDtypeStruct((pairs, channels, 2 * rows_z), BF16),
-        in_specs=[VMEM] * 5,
-        out_specs=VMEM,
+        out_shape=(
+            jax.ShapeDtypeStruct((pairs, channels, 2 * rows_z), BF16),
+            jax.ShapeDtypeStruct((8, biases[0].shape[1]), F32),
+        ),
+        in_specs=[VMEM] * 8,
+        out_specs=(VMEM, VMEM),
+        scratch_shapes=[pltpu.VMEM((3, 3 * channels, 3 * channels), BF16)],
         compiler_params=pltpu.CompilerParams(vmem_limit_bytes=8 << 20),
         cost_estimate=pl.CostEstimate(flops=3 << 30, bytes_accessed=4 << 20, transcendentals=0),
         name="convolve",
-    )(left, here, right, taps, conv_bias)
+    )(left, here, right, taps, conv_bias, *biases)
 
 
 def interpolate(words, lat, planes, rows_y, rows_z):
@@ -200,13 +232,11 @@
     place_ref,
     lat,
     words_ref,
+    small_ref,
     w_latent_hbm,
     w_pos_hbm,
-    bias_one_hbm,
     w_mid_hbm,
-    bias_two_hbm,
     w_out_hbm,
-    bias_out_hbm,
     send_ref,
     keep_ref,
     code,
@@ -231,19 +261,16 @@
     mid_low,
     w_latent_ref,
     w_pos_ref,
-    bias_one_ref,
     w_mid_ref,
-    bias_two_ref,
     w_out_ref,
-    bias_out_ref,
     sems,
 ):
     rows = plan.tiles * plan.slots
     hidden = w_mid_ref.shape[0]
     latents = w_latent_ref.shape[0]
     weights = fetches(
-        (w_latent_hbm, w_pos_hbm, bias_one_hbm, w_mid_hbm, bias_two_hbm, w_out_hbm, bias_out_hbm),
-        (w_latent_ref, w_pos_ref, bias_one_ref, w_mid_ref, bias_two_ref, w_out_ref, bias_out_ref),
+        (w_latent_hbm, w_pos_hbm, w_mid_hbm, w_out_hbm),
+        (w_latent_ref, w_pos_ref, w_mid_ref, w_out_ref),
         sems,
     )
     planes, rows_z = plan.planes, lat.shape[2] // 2
@@ -281,8 +308,8 @@
     mid_low[...] = low
     w_pos = [w_pos_ref[d : d + 1, :] for d in range(3)]
     square = w_pos[0] * w_pos[0] + w_pos[1] * w_pos[1] + w_pos[2] * w_pos[2]
-    bias_one = bias_one_ref[...]
-    bias_two = bias_two_ref[...]
+    bias_one = small_ref[0:1, :]
+    bias_two = small_ref[1:2, :]
 
     part_rows = rows // 2
 
@@ -360,17 +387,14 @@
         layer_one(1)
         times_mid(NN, (one_high, one_low), mixed, 1)
         layer_two(0)
+        outputs(0)
         layer_two(1)
-
-    @pl.when(always)
-    def _():
-        outputs(0)
         outputs(1)
 
     words_t = words.T
     target = [words_t[4 + f : 5 + f, :] for f in range(5)]
     valid = words_t[9:10, :]
-    value = [out_t[f : f + 1, :] + bias_out_ref[0:1, f : f + 1] for f in range(5)]
+    value = [out_t[f : f + 1, :] + small_ref[2:3, f : f + 1] for f in range(5)]
     grad = [[out_t[8 * (d + 1) + f : 8 * (d + 1) + f + 1, :] for f in range(5)] for d in range(3)]
     laplace = [out_t[32 + f : 33 + f, :] for f in range(5)]
     velocity = value[2:5]
@@ -478,20 +502,6 @@
             )
         return sums
 
-    @pl.when(always)
-    def _():
-        out_back(0)
-        total = second_back(0, jnp.zeros((8, hidden), F32))
-        out_back(1)
-        sums_ref[5] = second_back(1, total)
-
-    @pl.when(always)
-    def _():
-        times_mid(NT, (d_high, d_low), mixed_back, 0)
-        total = first_back(0, [jnp.zeros((8, hidden), F32)] * 5)
-        times_mid(NT, (d_high, d_low), mixed_back, 1)
-        for number, value in enumerate(first_back(1, total)):
-            sums_ref[number] = value
 
     def put(part, first, value):
         while value.shape[0]:
@@ -501,15 +511,29 @@
             first, value = first + count, value[count:]
 
     wide = 2 * LANES
-    for left in range(hidden // wide):
-        for right in range(hidden // wide):
-            lefts = slice(left * wide, (left + 1) * wide)
-            rights = slice(right * wide, (right + 1) * wide)
-            part = mul3(
-                (one_high[:, lefts], one_low[:, lefts]), (d_high[:, rights], d_low[:, rights]), TN
-            )
-            for side in range(2):
-                put(2 * right + side, left * wide, part[:, side * LANES : (side + 1) * LANES])
+    def mid_gradient():
+        for left in range(hidden // wide):
+            for right in range(hidden // wide):
+                lefts = slice(left * wide, (left + 1) * wide)
+                rights = slice(right * wide, (right + 1) * wide)
+                part = mul3(
+                    (one_high[:, lefts], one_low[:, lefts]), (d_high[:, rights], d_low[:, rights]), TN
+                )
+                for side in range(2):
+                    put(2 * right + side, left * wide, part[:, side * LANES : (side + 1) * LANES])
+
+    @pl.when(always)
+    def _():
+        out_back(0)
+        total = second_back(0, jnp.zeros((8, hidden), F32))
+        out_back(1)
+        times_mid(NT, (d_high, d_low), mixed_back, 0)
+        sums_ref[5] = second_back(1, total)
+        times_mid(NT, (d_high, d_low), mixed_back, 1)
+        total = first_back(0, [jnp.zeros((8, hidden), F32)] * 5)
+        mid_gradient()
+        for number, value in enumerate(first_back(1, total)):
+            sums_ref[number] = value
 
     sums = [sums_ref[number] for number in range(6)]
     d_square = jnp.sum(sums[4], axis=0, keepdims=True)
@@ -641,24 +665,27 @@
     return read
 
 
-def first_kernel(plan, keep_ref, got_ref, mine_ref, *out_refs):
+def first_kernel(plan, numbers, keep_ref, got_ref, *refs):
     def reader(block):
         return lambda start, count: (
             keep_ref[block, start : start + count, :] + got_ref[block, start : start + count, :]
         )
 
-    for number, out_ref in enumerate(out_refs):
-        encode(plan, reader(number + 1), out_ref)
-    mine_ref[...] = keep_ref[0] + got_ref[0]
-
-
-def first_sum(keep, got, plan):
+    for number, out_ref in zip(numbers, refs):
+        if number:
+            encode(plan, reader(number), out_ref)
+        else:
+            out_ref[...] = keep_ref[0] + got_ref[0]
+
+
+def first_sum(keep, got, numbers, plan):
     sent = jax.ShapeDtypeStruct((plan.sent_rows, LANES), jnp.int16)
+    own = jax.ShapeDtypeStruct(keep.shape[1:], F32)
     return pl.pallas_call(
-        functools.partial(first_kernel, plan),
-        out_shape=(jax.ShapeDtypeStruct(keep.shape[1:], F32), sent, sent, sent),
+        functools.partial(first_kernel, plan, numbers),
+        out_shape=tuple(sent if number else own for number in numbers),
         in_specs=[VMEM] * 2,
-        out_specs=tuple([VMEM] * 4),
+        out_specs=tuple([VMEM] * len(numbers)),
         compiler_params=pltpu.CompilerParams(vmem_limit_bytes=6 << 20),
         name="sum_core",
     )(keep, got)
@@ -684,16 +711,16 @@
     )(*blocks)
 
 
-def main(place, lat, words, weights, plan):
+def main(place, lat, words, small, weights, plan):
     rows = plan.tiles * plan.slots
-    hidden = weights[3].shape[0]
+    hidden = weights[2].shape[0]
     channels = lat.shape[1]
     outs = jax.ShapeDtypeStruct((4, plan.rows, LANES), F32)
     wide = lambda kind: pltpu.VMEM((5 * rows, hidden), kind)
     return pl.pallas_call(
         functools.partial(main_kernel, plan),
         out_shape=(outs, outs),
-        in_specs=[SMEM] + [VMEM] * 2 + [HBM] * 7,
+        in_specs=[SMEM] + [VMEM] * 3 + [HBM] * 4,
         out_specs=(VMEM, VMEM),
         scratch_shapes=[
             pltpu.VMEM((rows, channels), BF16),
@@ -718,10 +745,10 @@
             pltpu.VMEM((hidden, hidden), BF16),
         ]
         + [pltpu.VMEM(weight.shape, F32) for weight in weights]
-        + [pltpu.SemaphoreType.DMA((7,))],
+        + [pltpu.SemaphoreType.DMA((4,))],
         compiler_params=pltpu.CompilerParams(vmem_limit_bytes=32 << 20),
         name="encode_decode",
-    )(place, lat, words, *weights)
+    )(place, lat, words, small, *weights)
 
 
 def unpack_kernel(plan, place_ref, *refs):
@@ -815,8 +842,6 @@
     to_left, to_right, query_owner = lax.optimization_barrier(
         (here[: DILATION_RATE + 1], here[-DILATION_RATE:], query_owner)
     )
-    taps = convolution_weight.reshape(channels, 3, 3, 3, channels)
-    taps = taps.transpose(1, 3, 0, 2, 4).reshape(3, 3 * channels, 3 * channels)
     right = lax.ppermute(to_left, "tile", down)
     left = lax.ppermute(to_right, "tile", up)
     words = route(
@@ -831,12 +856,16 @@
         words.reshape(tiles, 8, WORDS), "tile", split_axis=0, concat_axis=0, tiled=True
     ).reshape(tiles * 8, WORDS)
 
-    lat = convolve(left, here, right, taps, convolution_bias[:, None])
-    weights = (w_latent, w_pos, bias_one[None], w_mid, bias_two[None], w_out, bias_out[None])
-    send, keep = main(place, lat, words, weights, plan)
-
-    mine, *others = first_sum(keep, swapped(send, plan, plan.core, 1), plan)
-    arrived = [swapped(block, plan, plan.plane, step + 1) for step, block in enumerate(others)]
+    biases = (bias_one[None], bias_two[None], bias_out[None])
+    lat, small = convolve(left, here, right, convolution_weight, convolution_bias[None], biases)
+    weights = (w_latent, w_pos, w_mid, w_out)
+    send, keep = main(place, lat, words, small, weights, plan)
+
+    got = swapped(send, plan, plan.core, 1)
+    (far,) = first_sum(keep, got, (3,), plan)
+    far, keep = lax.optimization_barrier((far, keep))
+    mine, *near = first_sum(keep, got, (0, 1, 2), plan)
+    arrived = [swapped(block, plan, plan.plane, step) for step, block in ((3, far), (1, near[0]), (2, near[1]))]
     block = coded_sum(plane_kernel, [mine] + arrived, plan, "sum_plane")
     for bit in plan.rest:
         block = coded_sum(pair_kernel, [block, swapped(block, plan, [bit], 1)], plan, "sum_line")

time: 71.4 us -> 69.4 us (0.972)
  local copies, waits for them, and re-layouts: 5.05 us -> 2.66 us
    ppermute x1, waiting for transfers between devices: 0.01 us -> 0.85 us  [body(): left = lax.ppermute(to_right, 'tile', up)]
    pallas_call x2 -> x3, Pallas kernels: 1.96 us -> 2.11 us  [the longest x1 1.88 us: convolve(): pl.pallas_call(conv_kernel, out_shape=(jax.ShapeDtypeStruct((pairs, chann...]
  transfers between devices with their start and end apart: 16 -> 16, of which waited for: 11 -> 13; matrix products, arithmetic and copies ran while one was open for 2% -> 0% of each run, Pallas kernels for 4% -> 4%
where the time goes in v8:
time: 69.4 us; the launch traced here: 69.1 us
  waiting for transfers between devices  25.5 us (37%)
  Pallas kernels  20.9 us (30%)
  starting transfers between devices  19.2 us (28%)
  local copies, waits for them, and re-layouts  2.66 us (4%)
  between operations  0.86 us (1%)
    ppermute x13, waiting for transfers between devices, swapped(): lax.ppermute(value, ('replica', 'tile'), [(i, i ^ mask) for i in range(pl...  21.3 us
    pallas_call x1, Pallas kernels, main(): pl.pallas_call(functools.partial(main_kernel, plan), out_shape=(outs, out...  15.6 us
    ppermute x13, starting transfers between devices, swapped(): lax.ppermute(value, ('replica', 'tile'), [(i, i ^ mask) for i in range(pl...  7.88 us
    all_to_all x1, starting transfers between devices, body(): lax.all_to_all(words.reshape(tiles, 8, WORDS), 'tile', split_axis=0, conc...  5.83 us
    ppermute x1, starting transfers between devices, body(): right = lax.ppermute(to_left, 'tile', down)  5.5 us
    all_to_all x1, waiting for transfers between devices, body(): lax.all_to_all(words.reshape(tiles, 8, WORDS), 'tile', split_axis=0, conc...  3.33 us
    unnamed x27, local copies, waits for them, and re-layouts  2.62 us
    pallas_call x1, Pallas kernels, convolve(): pl.pallas_call(conv_kernel, out_shape=(jax.ShapeDtypeStruct((pairs, chann...  1.88 us
  transfers between devices with their start and end apart: 16, of which 13 were waited for; matrix products, arithmetic and copies ran while one was open for 0% of the time, Pallas kernels for 4%

profile of v8, /device:TPU:0, one launch (start us, length us, event | category | flops | bytes accessed | tf_op | source)
XLA Modules:
  0.0 69.1 jit_solution(12470792670624277611)
XLA Ops:
  0.6 1.2 %copy.25 = bf16[1,64,4,8,128]{4,1,3,2,0:T(8,128)(2,1)S(1)} copy(bf16[1,64,4,8,128]{4,3,2,1,0:T(8,128)(2,1)} %param.14) | data formatting | bytes 1048576 | tf_op args[0]
  1.9 0.0 copy-start.8
  2.0 0.0 copy-start.4
  2.0 5.5 %collective-permute-start.1 = (bf16[3,8,64,128]{3,2,1,0:T(8,128)(2,1)S(1)}, bf16[3,8,64,128]{3,2,1,0:T(8,128)(2,1)S(1)}, u32[]{:S(2)}, u32[]{:S(2)}) collective-permute-start(bf16[3,8,64,128]{3,2,1,0:T(8,128)(2,1)S(1)} %slice.8), channel_id=1, source_target_pairs={{1,0},{2,1},{3,2},{4,3},{5,4},{6,5},{7,6},{8,7},{9,8},{10,9},{11,1... | collective-permute-start | bytes 1179656 | tf_op jit(solution)/shard_map/ppermute | solution.py:845
  7.5 0.0 collective-permute-start
  7.5 0.7 copy-done.5
  8.2 0.0 copy-done.7
  8.2 1.0 %route.1 = f32[128,128]{1,0:T(8,128)} custom-call(s32[1,128]{1,0:T(1,128)S(1)} %bitcast.28, s32[1,128]{1,0:T(1,128)S(1)} %copy-done.7, f32[3,1,128]{2,1,0:T(1,128)S(1)} %bitcast.27, f32[5,1,128]{2,1,0:T(1,128)S(1)} %bitcast.26), custom_call_target="tpu_custom_call" | custom-call | tf_op jit(solution)/shard_map/route/pallas_call | solution.py:93
  9.2 5.8 %all-to-all-start = ((f32[16,8,128]{2,1,0:T(8,128)}), f32[16,8,128]{2,1,0:T(8,128)S(1)}, u32[]{:S(2)}, u32[]{:S(2)}) async-start(f32[16,8,128]{2,1,0:T(8,128)} %bitcast.13), calls=%async_computation | async-start | bytes 131072 | tf_op jit(solution)/shard_map/all_to_all | solution.py:855
  15.0 0.0 copy-start.10
  15.0 0.1 pad_add_fusion.place_ref
  15.1 0.8 %collective-permute-done.left_ref = bf16[2,8,64,128]{3,2,1,0:T(8,128)(2,1)S(1)} collective-permute-done((bf16[2,8,64,128]{3,2,1,0:T(8,128)(2,1)S(1)}, bf16[2,8,64,128]{3,2,1,0:T(8,128)(2,1)S(1)}, u32[]{:S(2)}, u32[]{:S(2)}) %collective-permute-start) | collective-permute-done | bytes 262176 | tf_op jit(solution)/shard_map/ppermute | solution.py:846
  16.0 0.0 collective-permute-done.1.right_ref
  16.0 0.7 copy-done.9
  16.7 0.0 copy-start.2
  16.7 0.0 copy-start.3
  16.7 1.9 %convolve.1 = (bf16[20,64,256]{2,1,0:T(8,128)(2,1)S(1)}, f32[8,512]{1,0:T(8,128)S(1)}) custom-call(bf16[2,8,64,128]{3,2,1,0:T(8,128)(2,1)S(1)} %collective-permute-done.left_ref, bf16[4,8,64,128]{3,2,1,0:T(8,128)(2,1)S(1)} %bitcast.24, bf16[3,8,64,128]{3,2,1,0:T(8,128)(2,1)S(1)} %collective-permute-done.1.right_ref, bf16[64,1728]{1,0:T(8,128)(2,1)S(1)} %copy-done.8, ...), custom_call_target="tpu_custom_call" | custom-call | flops 3221225472 | bytes 4194304 | tf_op jit(solution)/shard_map/convolve/pallas_call | solution.py:182
  18.6 3.3 %all-to-all-done = f32[16,8,128]{2,1,0:T(8,128)S(1)} async-done(((f32[16,8,128]{2,1,0:T(8,128)}), f32[16,8,128]{2,1,0:T(8,128)S(1)}, u32[]{:S(2)}, u32[]{:S(2)}) %all-to-all-start) | async-done | bytes 65568 | tf_op jit(solution)/shard_map/all_to_all | solution.py:855
  21.9 15.6 %encode_decode.1 = (f32[4,328,128]{2,1,0:T(8,128)S(1)}, f32[4,328,128]{2,1,0:T(8,128)S(1)}) custom-call(s32[3]{0:T(128)S(1)} %pad_add_fusion.place_ref, bf16[20,64,256]{2,1,0:T(8,128)(2,1)S(1)} %get-tuple-element.32.lat, f32[128,128]{1,0:T(8,128)S(1)} %bitcast.25, f32[8,512]{1,0:T(8,128)S(1)} %get-tuple-element.34.small_ref, f32[64,512]{1,0:T(8,128)S(1)} %copy-done.1, ...), custom_call_target="tpu_custom_call" | custom-call | tf_op jit(solution)/shard_map/encode_decode/pallas_call | solution.py:720
  37.5 0.1 collective-permute-start.2
  37.6 2.1 %collective-permute-done.2.got_ref = f32[4,328,128]{2,1,0:T(8,128)S(1)} collective-permute-done((f32[4,328,128]{2,1,0:T(8,128)S(1)}, f32[4,328,128]{2,1,0:T(8,128)S(1)}, u32[]{:S(2)}, u32[]{:S(2)}) %collective-permute-start.2) | collective-permute-done | bytes 671776 | tf_op jit(solution)/shard_map/ppermute | solution.py:614
  39.7 0.1 sum_core.2
  39.8 0.1 sum_core.3
  40.0 0.2 collective-permute-start.4
  40.1 1.5 %collective-permute-start.5 = (s16[352,128]{1,0:T(8,128)(2,1)S(1)}, s16[352,128]{1,0:T(8,128)(2,1)S(1)}, u32[]{:S(2)}, u32[]{:S(2)}) collective-permute-start(s16[352,128]{1,0:T(8,128)(2,1)S(1)} %get-tuple-element.41), channel_id=1, source_target_pairs={{0,16},{1,17},{2,18},{3,19},{4,20},{5,21},{6,22},{7,23},{8,24},{9,... | collective-permute-start | bytes 270344 | tf_op jit(solution)/shard_map/ppermute | solution.py:614
  41.6 1.9 %collective-permute-start.3 = (s16[352,128]{1,0:T(8,128)(2,1)S(1)}, s16[352,128]{1,0:T(8,128)(2,1)S(1)}, u32[]{:S(2)}, u32[]{:S(2)}) collective-permute-start(s16[352,128]{1,0:T(8,128)(2,1)S(1)} %sum_core.2), channel_id=1, source_target_pairs={{0,18},{1,19},{2,16},{3,17},{4,22},{5,23},{6,20},{7,21},{8,26},{9,... | collective-permute-start | bytes 270344 | tf_op jit(solution)/shard_map/ppermute | solution.py:614
  43.5 1.2 %collective-permute-done.4.refs_1_ = s16[352,128]{1,0:T(8,128)(2,1)S(1)} collective-permute-done((s16[352,128]{1,0:T(8,128)(2,1)S(1)}, s16[352,128]{1,0:T(8,128)(2,1)S(1)}, u32[]{:S(2)}, u32[]{:S(2)}) %collective-permute-start.4) | collective-permute-done | bytes 90144 | tf_op jit(solution)/shard_map/ppermute | solution.py:614
  44.7 0.1 collective-permute-done.5.refs_2_
  44.8 3.1 %collective-permute-done.3.refs_0_ = s16[352,128]{1,0:T(8,128)(2,1)S(1)} collective-permute-done((s16[352,128]{1,0:T(8,128)(2,1)S(1)}, s16[352,128]{1,0:T(8,128)(2,1)S(1)}, u32[]{:S(2)}, u32[]{:S(2)}) %collective-permute-start.3) | collective-permute-done | bytes 90144 | tf_op jit(solution)/shard_map/ppermute | solution.py:614
  47.8 0.1 sum_plane.1.mine_ref
  48.0 0.3 collective-permute-start.6
  48.3 4.3 %collective-permute-done.6.other_ref = s16[352,128]{1,0:T(8,128)(2,1)S(1)} collective-permute-done((s16[352,128]{1,0:T(8,128)(2,1)S(1)}, s16[352,128]{1,0:T(8,128)(2,1)S(1)}, u32[]{:S(2)}, u32[]{:S(2)}) %collective-permute-start.6) | collective-permute-done | bytes 90144 | tf_op jit(solution)/shard_map/ppermute | solution.py:614
  52.6 0.1 sum_line.2.mine_ref
  52.7 0.4 collective-permute-start.7
  53.1 5.7 %collective-permute-done.7.other_ref = s16[352,128]{1,0:T(8,128)(2,1)S(1)} collective-permute-done((s16[352,128]{1,0:T(8,128)(2,1)S(1)}, s16[352,128]{1,0:T(8,128)(2,1)S(1)}, u32[]{:S(2)}, u32[]{:S(2)}) %collective-permute-start.7) | collective-permute-done | bytes 90144 | tf_op jit(solution)/shard_map/ppermute | solution.py:614
  58.8 0.1 sum_line.3.refs_0_
  58.9 1.6 %collective-permute-start.10 = (s16[352,128]{1,0:T(8,128)(2,1)S(1)}, s16[352,128]{1,0:T(8,128)(2,1)S(1)}, u32[]{:S(2)}, u32[]{:S(2)}) collective-permute-start(s16[352,128]{1,0:T(8,128)(2,1)S(1)} %sum_line.3.refs_0_), channel_id=1, source_target_pairs={{0,18},{1,19},{2,16},{3,17},{4,22},{5,23},{6,20},{7,21},{8,26},{9,... | collective-permute-start | bytes 270344 | tf_op jit(solution)/shard_map/ppermute | solution.py:614
  60.5 1.0 %collective-permute-start.9 = (s16[352,128]{1,0:T(8,128)(2,1)S(1)}, s16[352,128]{1,0:T(8,128)(2,1)S(1)}, u32[]{:S(2)}, u32[]{:S(2)}) collective-permute-start(s16[352,128]{1,0:T(8,128)(2,1)S(1)} %sum_line.3.refs_0_), channel_id=1, source_target_pairs={{0,16},{1,17},{2,18},{3,19},{4,20},{5,21},{6,22},{7,23},{8,24},{9,... | collective-permute-start | bytes 270344 | tf_op jit(solution)/shard_map/ppermute | solution.py:614
  61.5 1.0 %collective-permute-start.8 = (s16[352,128]{1,0:T(8,128)(2,1)S(1)}, s16[352,128]{1,0:T(8,128)(2,1)S(1)}, u32[]{:S(2)}, u32[]{:S(2)}) collective-permute-start(s16[352,128]{1,0:T(8,128)(2,1)S(1)} %sum_line.3.refs_0_), channel_id=1, source_target_pairs={{0,2},{1,3},{2,0},{3,1},{4,6},{5,7},{6,4},{7,5},{8,10},{9,11},{10,... | collective-permute-start | bytes 270344 | tf_op jit(solution)/shard_map/ppermute | solution.py:614
  62.5 0.0 collective-permute-start.11
  62.5 1.9 %collective-permute-done.10.refs_3_ = s16[352,128]{1,0:T(8,128)(2,1)S(1)} collective-permute-done((s16[352,128]{1,0:T(8,128)(2,1)S(1)}, s16[352,128]{1,0:T(8,128)(2,1)S(1)}, u32[]{:S(2)}, u32[]{:S(2)}) %collective-permute-start.10) | collective-permute-done | bytes 90144 | tf_op jit(solution)/shard_map/ppermute | solution.py:614
  64.4 0.0 collective-permute-start.14
  64.4 0.6 collective-permute-done.9.refs_2_
  65.1 0.0 collective-permute-start.13
  65.1 1.0 %collective-permute-done.8.refs_1_ = s16[352,128]{1,0:T(8,128)(2,1)S(1)} collective-permute-done((s16[352,128]{1,0:T(8,128)(2,1)S(1)}, s16[352,128]{1,0:T(8,128)(2,1)S(1)}, u32[]{:S(2)}, u32[]{:S(2)}) %collective-permute-start.8) | collective-permute-done | bytes 90144 | tf_op jit(solution)/shard_map/ppermute | solution.py:614
  66.0 0.3 collective-permute-done.13.refs_6_
  66.4 1.0 %collective-permute-done.12.refs_5_ = s16[352,128]{1,0:T(8,128)(2,1)S(1)} collective-permute-done((s16[352,128]{1,0:T(8,128)(2,1)S(1)}, s16[352,128]{1,0:T(8,128)(2,1)S(1)}, u32[]{:S(2)}, u32[]{:S(2)}) %collective-permute-start.12) | collective-permute-done | bytes 90144 | tf_op jit(solution)/shard_map/ppermute | solution.py:614
  67.3 1.8 %unpack.1 = (f32[5,1,128]{2,1,0:T(1,128)}, f32[64,512]{1,0:T(8,128)}, f32[3,512]{1,0:T(4,128)}, f32[1,512]{1,0:T(1,128)}, f32[512,512]{1,0:T(8,128)}, /*index=5*...) custom-call(s32[3]{0:T(128)S(1)} %pad_add_fusion.place_ref, ...), custom_call_target="tpu_custom_call" | custom-call | tf_op jit(solution)/shard_map/unpack/pallas_call | solution.py:801
  (23 shorter events, 0.1 us)
Async XLA Ops:
  1.9 14.1 %copy-start.8 = (bf16[64,1728]{1,0:T(8,128)(2,1)S(1)}, bf16[64,1728]{1,0:T(8,128)(2,1)}, u32[]{:S(2)}) copy-start(bf16[64,1728]{1,0:T(8,128)(2,1)} %taps_ref.1) | copy-start | bytes 663556
  2.0 5.5 %copy-start.4 = (f32[1,5,128]{2,0,1:T(1,128)S(1)}, f32[1,5,128]{2,0,1:T(1,128)}, u32[]{:S(2)}) copy-start(f32[1,5,128]{2,0,1:T(1,128)} %param.20) | copy-start | bytes 7684
  2.0 14.0 %collective-permute-start.1 = (bf16[3,8,64,128]{3,2,1,0:T(8,128)(2,1)S(1)}, bf16[3,8,64,128]{3,2,1,0:T(8,128)(2,1)S(1)}, u32[]{:S(2)}, u32[]{:S(2)}) collective-permute-start(bf16[3,8,64,128]{3,2,1,0:T(8,128)(2,1)S(1)} %slice.8), channel_id=1, source_target_pairs={{1,0},{2,1},{3,2},{4,3},{5,4},{6,5},{7,6},{8,7},{9,8},{10,9},{11,1... | collective-permute-start | bytes 1179656 | tf_op jit(solution)/shard_map/ppermute | solution.py:845
  7.5 8.5 %collective-permute-start = (bf16[2,8,64,128]{3,2,1,0:T(8,128)(2,1)S(1)}, bf16[2,8,64,128]{3,2,1,0:T(8,128)(2,1)S(1)}, u32[]{:S(2)}, u32[]{:S(2)}) collective-permute-start(bf16[2,8,64,128]{3,2,1,0:T(8,128)(2,1)S(1)} %slice.9), channel_id=1, source_target_pairs={{0,1},{1,2},{2,3},{3,4},{4,5},{5,6},{6,7},{7,8},{8,9},{9,10},{10,1... | collective-permute-start | bytes 786440 | tf_op jit(solution)/shard_map/ppermute | solution.py:846
  7.5 0.7 copy-start.5
  7.5 0.7 copy-start.6
  7.5 0.7 copy-start.7
  9.2 12.7 %all-to-all-start = ((f32[16,8,128]{2,1,0:T(8,128)}), f32[16,8,128]{2,1,0:T(8,128)S(1)}, u32[]{:S(2)}, u32[]{:S(2)}) async-start(f32[16,8,128]{2,1,0:T(8,128)} %bitcast.13), calls=%async_computation | async-start | bytes 131072 | tf_op jit(solution)/shard_map/all_to_all | solution.py:855
  15.0 1.0 %copy-start.10 = (f32[512]{0:T(512)S(1)}, f32[512]{0:T(512)}, u32[]{:S(2)}) copy-start(f32[512]{0:T(512)} %param.25) | copy-start | bytes 6148
  16.0 0.7 copy-start.9
  16.0 0.7 copy-start.11
  16.0 0.7 copy-start.12
  16.7 5.3 %copy-start = (f32[512,512]{1,0:T(8,128)S(1)}, f32[512,512]{1,0:T(8,128)}, u32[]{:S(2)}) copy-start(f32[512,512]{1,0:T(8,128)} %w_mid_hbm.1) | copy-start | bytes 3145732
  16.7 5.3 %copy-start.1 = (f32[64,512]{1,0:T(8,128)S(1)}, f32[64,512]{1,0:T(8,128)}, u32[]{:S(2)}) copy-start(f32[64,512]{1,0:T(8,128)} %w_latent_hbm.1) | copy-start | bytes 393220
  16.7 5.3 %copy-start.2 = (f32[5,512]{1,0:T(8,128)S(1)}, f32[5,512]{1,0:T(8,128)}, u32[]{:S(2)}) copy-start(f32[5,512]{1,0:T(8,128)} %w_out_hbm.1) | copy-start | bytes 30724
  16.7 5.2 %copy-start.3 = (f32[3,512]{1,0:T(4,128)S(1)}, f32[3,512]{1,0:T(4,128)}, u32[]{:S(2)}) copy-start(f32[3,512]{1,0:T(4,128)} %w_pos_hbm.1) | copy-start | bytes 18436
  37.5 2.2 %collective-permute-start.2 = (f32[4,328,128]{2,1,0:T(8,128)S(1)}, f32[4,328,128]{2,1,0:T(8,128)S(1)}, u32[]{:S(2)}, u32[]{:S(2)}) collective-permute-start(f32[4,328,128]{2,1,0:T(8,128)S(1)} %get-tuple-element.36), channel_id=1, source_target_pairs={{0,1},{1,0},{2,3},{3,2},{4,5},{5,4},{6,7},{7,6},{8,9},{9,8},{10,11... | collective-permute-start | bytes 2015240 | tf_op jit(solution)/shard_map/ppermute | solution.py:614
  40.0 4.7 %collective-permute-start.4 = (s16[352,128]{1,0:T(8,128)(2,1)S(1)}, s16[352,128]{1,0:T(8,128)(2,1)S(1)}, u32[]{:S(2)}, u32[]{:S(2)}) collective-permute-start(s16[352,128]{1,0:T(8,128)(2,1)S(1)} %get-tuple-element.40), channel_id=1, source_target_pairs={{0,2},{1,3},{2,0},{3,1},{4,6},{5,7},{6,4},{7,5},{8,10},{9,11},{10,... | collective-permute-start | bytes 270344 | tf_op jit(solution)/shard_map/ppermute | solution.py:614
  40.1 4.6 %collective-permute-start.5 = (s16[352,128]{1,0:T(8,128)(2,1)S(1)}, s16[352,128]{1,0:T(8,128)(2,1)S(1)}, u32[]{:S(2)}, u32[]{:S(2)}) collective-permute-start(s16[352,128]{1,0:T(8,128)(2,1)S(1)} %get-tuple-element.41), channel_id=1, source_target_pairs={{0,16},{1,17},{2,18},{3,19},{4,20},{5,21},{6,22},{7,23},{8,24},{9,... | collective-permute-start | bytes 270344 | tf_op jit(solution)/shard_map/ppermute | solution.py:614
  41.6 6.2 %collective-permute-start.3 = (s16[352,128]{1,0:T(8,128)(2,1)S(1)}, s16[352,128]{1,0:T(8,128)(2,1)S(1)}, u32[]{:S(2)}, u32[]{:S(2)}) collective-permute-start(s16[352,128]{1,0:T(8,128)(2,1)S(1)} %sum_core.2), channel_id=1, source_target_pairs={{0,18},{1,19},{2,16},{3,17},{4,22},{5,23},{6,20},{7,21},{8,26},{9,... | collective-permute-start | bytes 270344 | tf_op jit(solution)/shard_map/ppermute | solution.py:614
  48.0 4.6 %collective-permute-start.6 = (s16[352,128]{1,0:T(8,128)(2,1)S(1)}, s16[352,128]{1,0:T(8,128)(2,1)S(1)}, u32[]{:S(2)}, u32[]{:S(2)}) collective-permute-start(s16[352,128]{1,0:T(8,128)(2,1)S(1)} %sum_plane.1.mine_ref), channel_id=1, source_target_pairs={{0,4},{1,5},{2,6},{3,7},{4,0},{5,1},{6,2},{7,3},{8,12},{9,13},{10,... | collective-permute-start | bytes 270344 | tf_op jit(solution)/shard_map/ppermute | solution.py:614
  52.7 6.1 %collective-permute-start.7 = (s16[352,128]{1,0:T(8,128)(2,1)S(1)}, s16[352,128]{1,0:T(8,128)(2,1)S(1)}, u32[]{:S(2)}, u32[]{:S(2)}) collective-permute-start(s16[352,128]{1,0:T(8,128)(2,1)S(1)} %sum_line.2.mine_ref), channel_id=1, source_target_pairs={{0,8},{1,9},{2,10},{3,11},{4,12},{5,13},{6,14},{7,15},{8,0},{9,1},... | collective-permute-start | bytes 270344 | tf_op jit(solution)/shard_map/ppermute | solution.py:614
  58.9 5.5 %collective-permute-start.10 = (s16[352,128]{1,0:T(8,128)(2,1)S(1)}, s16[352,128]{1,0:T(8,128)(2,1)S(1)}, u32[]{:S(2)}, u32[]{:S(2)}) collective-permute-start(s16[352,128]{1,0:T(8,128)(2,1)S(1)} %sum_line.3.refs_0_), channel_id=1, source_target_pairs={{0,18},{1,19},{2,16},{3,17},{4,22},{5,23},{6,20},{7,21},{8,26},{9,... | collective-permute-start | bytes 270344 | tf_op jit(solution)/shard_map/ppermute | solution.py:614
  60.5 4.5 %collective-permute-start.9 = (s16[352,128]{1,0:T(8,128)(2,1)S(1)}, s16[352,128]{1,0:T(8,128)(2,1)S(1)}, u32[]{:S(2)}, u32[]{:S(2)}) collective-permute-start(s16[352,128]{1,0:T(8,128)(2,1)S(1)} %sum_line.3.refs_0_), channel_id=1, source_target_pairs={{0,16},{1,17},{2,18},{3,19},{4,20},{5,21},{6,22},{7,23},{8,24},{9,... | collective-permute-start | bytes 270344 | tf_op jit(solution)/shard_map/ppermute | solution.py:614
  61.5 4.5 %collective-permute-start.8 = (s16[352,128]{1,0:T(8,128)(2,1)S(1)}, s16[352,128]{1,0:T(8,128)(2,1)S(1)}, u32[]{:S(2)}, u32[]{:S(2)}) collective-permute-start(s16[352,128]{1,0:T(8,128)(2,1)S(1)} %sum_line.3.refs_0_), channel_id=1, source_target_pairs={{0,2},{1,3},{2,0},{3,1},{4,6},{5,7},{6,4},{7,5},{8,10},{9,11},{10,... | collective-permute-start | bytes 270344 | tf_op jit(solution)/shard_map/ppermute | solution.py:614
  62.5 3.5 %collective-permute-start.11 = (s16[352,128]{1,0:T(8,128)(2,1)S(1)}, s16[352,128]{1,0:T(8,128)(2,1)S(1)}, u32[]{:S(2)}, u32[]{:S(2)}) collective-permute-start(s16[352,128]{1,0:T(8,128)(2,1)S(1)} %sum_line.3.refs_0_), channel_id=1, source_target_pairs={{0,1},{1,0},{2,3},{3,2},{4,5},{5,4},{6,7},{7,6},{8,9},{9,8},{10,11... | collective-permute-start | bytes 270344 | tf_op jit(solution)/shard_map/ppermute | solution.py:614
  64.4 1.6 %collective-permute-start.14 = (s16[352,128]{1,0:T(8,128)(2,1)S(1)}, s16[352,128]{1,0:T(8,128)(2,1)S(1)}, u32[]{:S(2)}, u32[]{:S(2)}) collective-permute-start(s16[352,128]{1,0:T(8,128)(2,1)S(1)} %collective-permute-done.10.refs_3_), channel_id=1, source_target_pairs={{0,1},{1,0},{2,3},{3,2},{4,5},{5,4},{6,7},{7,6},{8,9},{9,8},{10,11... | collective-permute-start | bytes 270344 | tf_op jit(solution)/shard_map/ppermute | solution.py:614
  65.1 1.3 %collective-permute-start.13 = (s16[352,128]{1,0:T(8,128)(2,1)S(1)}, s16[352,128]{1,0:T(8,128)(2,1)S(1)}, u32[]{:S(2)}, u32[]{:S(2)}) collective-permute-start(s16[352,128]{1,0:T(8,128)(2,1)S(1)} %collective-permute-done.9.refs_2_), channel_id=1, source_target_pairs={{0,1},{1,0},{2,3},{3,2},{4,5},{5,4},{6,7},{7,6},{8,9},{9,8},{10,11... | collective-permute-start | bytes 270344 | tf_op jit(solution)/shard_map/ppermute | solution.py:614
  66.0 1.3 %collective-permute-start.12 = (s16[352,128]{1,0:T(8,128)(2,1)S(1)}, s16[352,128]{1,0:T(8,128)(2,1)S(1)}, u32[]{:S(2)}, u32[]{:S(2)}) collective-permute-start(s16[352,128]{1,0:T(8,128)(2,1)S(1)} %collective-permute-done.8.refs_1_), channel_id=1, source_target_pairs={{0,1},{1,0},{2,3},{3,2},{4,5},{5,4},{6,7},{7,6},{8,9},{9,8},{10,11... | collective-permute-start | bytes 270344 | tf_op jit(solution)/shard_map/ppermute | solution.py:614

commit v9 on v8

--- a/solution.py
+++ b/solution.py
@@ -252,8 +252,7 @@
     first_high,
     first_low,
     sums_ref,
-    d_high,
-    d_low,
+    d_both,
     out_t,
     d_out_t,
     packed,
@@ -348,10 +347,9 @@
             store(refs, at(part, 4, block), curve * square)
 
     def times_mid(dims, source, result, part):
-        for index in range(5):
-            span = at(part, index)
-            left = (source[0][span, :], source[1][span, :])
-            result[span, :] = mul3(left, (mid_high[...], mid_low[...]), dims)
+        span = slice(part * 5 * part_rows, (part + 1) * 5 * part_rows)
+        left = (source[0][span, :], source[1][span, :])
+        result[span, :] = mul3(left, (mid_high[...], mid_low[...]), dims)
 
     def layer_two(part):
         refs = (two_high, two_low)
@@ -455,7 +453,7 @@
             back[at(part, s), :] = mul(wanted, wo_three, TN)
 
     def second_back(part, total):
-        refs = (d_high, d_low)
+        refs = (d_both.at[:, :hidden], d_both.at[:, hidden:])
         for block in range(part_rows // BLOCK):
             act = mixed[at(part, 0, block), :]
             slope = 1.0 - act * act
@@ -513,23 +511,20 @@
     wide = 2 * LANES
     def mid_gradient():
         for left in range(hidden // wide):
-            for right in range(hidden // wide):
-                lefts = slice(left * wide, (left + 1) * wide)
-                rights = slice(right * wide, (right + 1) * wide)
-                part = mul3(
-                    (one_high[:, lefts], one_low[:, lefts]), (d_high[:, rights], d_low[:, rights]), TN
-                )
-                for side in range(2):
-                    put(2 * right + side, left * wide, part[:, side * LANES : (side + 1) * LANES])
+            lefts = slice(left * wide, (left + 1) * wide)
+            both = mul(one_high[:, lefts], d_both[...], TN)
+            both = both[:, :hidden] + both[:, hidden:] + mul(one_low[:, lefts], d_both[:, :hidden], TN)
+            for part in range(hidden // LANES):
+                put(part, left * wide, both[:, part * LANES : (part + 1) * LANES])
 
     @pl.when(always)
     def _():
         out_back(0)
         total = second_back(0, jnp.zeros((8, hidden), F32))
         out_back(1)
-        times_mid(NT, (d_high, d_low), mixed_back, 0)
+        times_mid(NT, (d_both.at[:, :hidden], d_both.at[:, hidden:]), mixed_back, 0)
         sums_ref[5] = second_back(1, total)
-        times_mid(NT, (d_high, d_low), mixed_back, 1)
+        times_mid(NT, (d_both.at[:, :hidden], d_both.at[:, hidden:]), mixed_back, 1)
         total = first_back(0, [jnp.zeros((8, hidden), F32)] * 5)
         mid_gradient()
         for number, value in enumerate(first_back(1, total)):
@@ -736,8 +731,7 @@
             pltpu.VMEM((rows, hidden), BF16),
             pltpu.VMEM((rows, hidden), BF16),
             pltpu.VMEM((6, 8, hidden), F32),
-            wide(BF16),
-            wide(BF16),
+            pltpu.VMEM((5 * rows, 2 * hidden), BF16),
             pltpu.VMEM((40, rows), F32),
             pltpu.VMEM((40, rows), F32),
             pltpu.VMEM((8, plan.rows, LANES), F32),

time: 69.4 us -> 66.4 us (0.957)
  Pallas kernels: 20.9 us -> 17.9 us
    pallas_call x1, Pallas kernels: 15.6 us -> 12.6 us  [main(): pl.pallas_call(functools.partial(main_kernel, plan), out_shape=(outs, out...]
where the time goes in v9:
time: 66.4 us; the launch traced here: 66.1 us
  waiting for transfers between devices  25.4 us (38%)
  starting transfers between devices  19.2 us (29%)
  Pallas kernels  17.9 us (27%)
  local copies, waits for them, and re-layouts  2.66 us (4%)
  between operations  0.86 us (1%)
    ppermute x13, waiting for transfers between devices, swapped(): lax.ppermute(value, ('replica', 'tile'), [(i, i ^ mask) for i in range(pl...  21.3 us
    pallas_call x1, Pallas kernels, main(): pl.pallas_call(functools.partial(main_kernel, plan), out_shape=(outs, out...  12.6 us
    ppermute x13, starting transfers between devices, swapped(): lax.ppermute(value, ('replica', 'tile'), [(i, i ^ mask) for i in range(pl...  7.87 us
    all_to_all x1, starting transfers between devices, body(): lax.all_to_all(words.reshape(tiles, 8, WORDS), 'tile', split_axis=0, conc...  5.83 us
    ppermute x1, starting transfers between devices, body(): right = lax.ppermute(to_left, 'tile', down)  5.5 us
    all_to_all x1, waiting for transfers between devices, body(): lax.all_to_all(words.reshape(tiles, 8, WORDS), 'tile', split_axis=0, conc...  3.33 us
    unnamed x27, local copies, waits for them, and re-layouts  2.62 us
    pallas_call x1, Pallas kernels, convolve(): pl.pallas_call(conv_kernel, out_shape=(jax.ShapeDtypeStruct((pairs, chann...  1.88 us
  transfers between devices with their start and end apart: 16, of which 13 were waited for; matrix products, arithmetic and copies ran while one was open for 0% of the time, Pallas kernels for 4%

profile of v9, /device:TPU:0, one launch (start us, length us, event | category | flops | bytes accessed | tf_op | source)
XLA Modules:
  0.0 66.1 jit_solution(6689142807410292045)
XLA Ops:
  0.6 1.2 %copy.25 = bf16[1,64,4,8,128]{4,1,3,2,0:T(8,128)(2,1)S(1)} copy(bf16[1,64,4,8,128]{4,3,2,1,0:T(8,128)(2,1)} %param.14) | data formatting | bytes 1048576 | tf_op args[0]
  1.9 0.0 copy-start.8
  2.0 0.0 copy-start.4
  2.0 5.5 %collective-permute-start.1 = (bf16[3,8,64,128]{3,2,1,0:T(8,128)(2,1)S(1)}, bf16[3,8,64,128]{3,2,1,0:T(8,128)(2,1)S(1)}, u32[]{:S(2)}, u32[]{:S(2)}) collective-permute-start(bf16[3,8,64,128]{3,2,1,0:T(8,128)(2,1)S(1)} %slice.8), channel_id=1, source_target_pairs={{1,0},{2,1},{3,2},{4,3},{5,4},{6,5},{7,6},{8,7},{9,8},{10,9},{11,1... | collective-permute-start | bytes 1179656 | tf_op jit(solution)/shard_map/ppermute | solution.py:839
  7.5 0.0 collective-permute-start
  7.5 0.7 copy-done.5
  8.2 0.0 copy-done.7
  8.2 1.0 %route.1 = f32[128,128]{1,0:T(8,128)} custom-call(s32[1,128]{1,0:T(1,128)S(1)} %bitcast.28, s32[1,128]{1,0:T(1,128)S(1)} %copy-done.7, f32[3,1,128]{2,1,0:T(1,128)S(1)} %bitcast.27, f32[5,1,128]{2,1,0:T(1,128)S(1)} %bitcast.26), custom_call_target="tpu_custom_call" | custom-call | tf_op jit(solution)/shard_map/route/pallas_call | solution.py:93
  9.2 5.8 %all-to-all-start = ((f32[16,8,128]{2,1,0:T(8,128)}), f32[16,8,128]{2,1,0:T(8,128)S(1)}, u32[]{:S(2)}, u32[]{:S(2)}) async-start(f32[16,8,128]{2,1,0:T(8,128)} %bitcast.13), calls=%async_computation | async-start | bytes 131072 | tf_op jit(solution)/shard_map/all_to_all | solution.py:849
  15.0 0.0 copy-start.10
  15.0 0.1 pad_add_fusion.place_ref
  15.1 0.8 %collective-permute-done.left_ref = bf16[2,8,64,128]{3,2,1,0:T(8,128)(2,1)S(1)} collective-permute-done((bf16[2,8,64,128]{3,2,1,0:T(8,128)(2,1)S(1)}, bf16[2,8,64,128]{3,2,1,0:T(8,128)(2,1)S(1)}, u32[]{:S(2)}, u32[]{:S(2)}) %collective-permute-start) | collective-permute-done | bytes 262176 | tf_op jit(solution)/shard_map/ppermute | solution.py:840
  16.0 0.0 collective-permute-done.1.right_ref
  16.0 0.7 copy-done.9
  16.7 0.0 copy-start.2
  16.7 0.0 copy-start.3
  16.7 1.9 %convolve.1 = (bf16[20,64,256]{2,1,0:T(8,128)(2,1)S(1)}, f32[8,512]{1,0:T(8,128)S(1)}) custom-call(bf16[2,8,64,128]{3,2,1,0:T(8,128)(2,1)S(1)} %collective-permute-done.left_ref, bf16[4,8,64,128]{3,2,1,0:T(8,128)(2,1)S(1)} %bitcast.24, bf16[3,8,64,128]{3,2,1,0:T(8,128)(2,1)S(1)} %collective-permute-done.1.right_ref, bf16[64,1728]{1,0:T(8,128)(2,1)S(1)} %copy-done.8, ...), custom_call_target="tpu_custom_call" | custom-call | flops 3221225472 | bytes 4194304 | tf_op jit(solution)/shard_map/convolve/pallas_call | solution.py:182
  18.6 3.3 %all-to-all-done = f32[16,8,128]{2,1,0:T(8,128)S(1)} async-done(((f32[16,8,128]{2,1,0:T(8,128)}), f32[16,8,128]{2,1,0:T(8,128)S(1)}, u32[]{:S(2)}, u32[]{:S(2)}) %all-to-all-start) | async-done | bytes 65568 | tf_op jit(solution)/shard_map/all_to_all | solution.py:849
  21.9 12.6 %encode_decode.1 = (f32[4,328,128]{2,1,0:T(8,128)S(1)}, f32[4,328,128]{2,1,0:T(8,128)S(1)}) custom-call(s32[3]{0:T(128)S(1)} %pad_add_fusion.place_ref, bf16[20,64,256]{2,1,0:T(8,128)(2,1)S(1)} %get-tuple-element.32.lat, f32[128,128]{1,0:T(8,128)S(1)} %bitcast.25, f32[8,512]{1,0:T(8,128)S(1)} %get-tuple-element.34.small_ref, f32[64,512]{1,0:T(8,128)S(1)} %copy-done.1, ...), custom_call_target="tpu_custom_call" | custom-call | tf_op jit(solution)/shard_map/encode_decode/pallas_call | solution.py:715
  34.5 0.1 collective-permute-start.2
  34.6 2.1 %collective-permute-done.2.got_ref = f32[4,328,128]{2,1,0:T(8,128)S(1)} collective-permute-done((f32[4,328,128]{2,1,0:T(8,128)S(1)}, f32[4,328,128]{2,1,0:T(8,128)S(1)}, u32[]{:S(2)}, u32[]{:S(2)}) %collective-permute-start.2) | collective-permute-done | bytes 671776 | tf_op jit(solution)/shard_map/ppermute | solution.py:609
  36.7 0.1 sum_core.2
  36.8 0.1 sum_core.3
  37.0 0.2 collective-permute-start.4
  37.1 1.5 %collective-permute-start.5 = (s16[352,128]{1,0:T(8,128)(2,1)S(1)}, s16[352,128]{1,0:T(8,128)(2,1)S(1)}, u32[]{:S(2)}, u32[]{:S(2)}) collective-permute-start(s16[352,128]{1,0:T(8,128)(2,1)S(1)} %get-tuple-element.41), channel_id=1, source_target_pairs={{0,16},{1,17},{2,18},{3,19},{4,20},{5,21},{6,22},{7,23},{8,24},{9,... | collective-permute-start | bytes 270344 | tf_op jit(solution)/shard_map/ppermute | solution.py:609
  38.6 1.9 %collective-permute-start.3 = (s16[352,128]{1,0:T(8,128)(2,1)S(1)}, s16[352,128]{1,0:T(8,128)(2,1)S(1)}, u32[]{:S(2)}, u32[]{:S(2)}) collective-permute-start(s16[352,128]{1,0:T(8,128)(2,1)S(1)} %sum_core.2), channel_id=1, source_target_pairs={{0,18},{1,19},{2,16},{3,17},{4,22},{5,23},{6,20},{7,21},{8,26},{9,... | collective-permute-start | bytes 270344 | tf_op jit(solution)/shard_map/ppermute | solution.py:609
  40.5 1.2 %collective-permute-done.4.refs_1_ = s16[352,128]{1,0:T(8,128)(2,1)S(1)} collective-permute-done((s16[352,128]{1,0:T(8,128)(2,1)S(1)}, s16[352,128]{1,0:T(8,128)(2,1)S(1)}, u32[]{:S(2)}, u32[]{:S(2)}) %collective-permute-start.4) | collective-permute-done | bytes 90144 | tf_op jit(solution)/shard_map/ppermute | solution.py:609
  41.7 0.1 collective-permute-done.5.refs_2_
  41.8 3.1 %collective-permute-done.3.refs_0_ = s16[352,128]{1,0:T(8,128)(2,1)S(1)} collective-permute-done((s16[352,128]{1,0:T(8,128)(2,1)S(1)}, s16[352,128]{1,0:T(8,128)(2,1)S(1)}, u32[]{:S(2)}, u32[]{:S(2)}) %collective-permute-start.3) | collective-permute-done | bytes 90144 | tf_op jit(solution)/shard_map/ppermute | solution.py:609
  44.8 0.1 sum_plane.1.mine_ref
  45.0 0.3 collective-permute-start.6
  45.3 4.3 %collective-permute-done.6.other_ref = s16[352,128]{1,0:T(8,128)(2,1)S(1)} collective-permute-done((s16[352,128]{1,0:T(8,128)(2,1)S(1)}, s16[352,128]{1,0:T(8,128)(2,1)S(1)}, u32[]{:S(2)}, u32[]{:S(2)}) %collective-permute-start.6) | collective-permute-done | bytes 90144 | tf_op jit(solution)/shard_map/ppermute | solution.py:609
  49.6 0.1 sum_line.2.mine_ref
  49.7 0.4 collective-permute-start.7
  50.1 5.7 %collective-permute-done.7.other_ref = s16[352,128]{1,0:T(8,128)(2,1)S(1)} collective-permute-done((s16[352,128]{1,0:T(8,128)(2,1)S(1)}, s16[352,128]{1,0:T(8,128)(2,1)S(1)}, u32[]{:S(2)}, u32[]{:S(2)}) %collective-permute-start.7) | collective-permute-done | bytes 90144 | tf_op jit(solution)/shard_map/ppermute | solution.py:609
  55.8 0.1 sum_line.3.refs_0_
  55.9 1.6 %collective-permute-start.10 = (s16[352,128]{1,0:T(8,128)(2,1)S(1)}, s16[352,128]{1,0:T(8,128)(2,1)S(1)}, u32[]{:S(2)}, u32[]{:S(2)}) collective-permute-start(s16[352,128]{1,0:T(8,128)(2,1)S(1)} %sum_line.3.refs_0_), channel_id=1, source_target_pairs={{0,18},{1,19},{2,16},{3,17},{4,22},{5,23},{6,20},{7,21},{8,26},{9,... | collective-permute-start | bytes 270344 | tf_op jit(solution)/shard_map/ppermute | solution.py:609
  57.5 1.0 %collective-permute-start.9 = (s16[352,128]{1,0:T(8,128)(2,1)S(1)}, s16[352,128]{1,0:T(8,128)(2,1)S(1)}, u32[]{:S(2)}, u32[]{:S(2)}) collective-permute-start(s16[352,128]{1,0:T(8,128)(2,1)S(1)} %sum_line.3.refs_0_), channel_id=1, source_target_pairs={{0,16},{1,17},{2,18},{3,19},{4,20},{5,21},{6,22},{7,23},{8,24},{9,... | collective-permute-start | bytes 270344 | tf_op jit(solution)/shard_map/ppermute | solution.py:609
  58.5 1.0 %collective-permute-start.8 = (s16[352,128]{1,0:T(8,128)(2,1)S(1)}, s16[352,128]{1,0:T(8,128)(2,1)S(1)}, u32[]{:S(2)}, u32[]{:S(2)}) collective-permute-start(s16[352,128]{1,0:T(8,128)(2,1)S(1)} %sum_line.3.refs_0_), channel_id=1, source_target_pairs={{0,2},{1,3},{2,0},{3,1},{4,6},{5,7},{6,4},{7,5},{8,10},{9,11},{10,... | collective-permute-start | bytes 270344 | tf_op jit(solution)/shard_map/ppermute | solution.py:609
  59.5 0.0 collective-permute-start.11
  59.5 1.9 %collective-permute-done.10.refs_3_ = s16[352,128]{1,0:T(8,128)(2,1)S(1)} collective-permute-done((s16[352,128]{1,0:T(8,128)(2,1)S(1)}, s16[352,128]{1,0:T(8,128)(2,1)S(1)}, u32[]{:S(2)}, u32[]{:S(2)}) %collective-permute-start.10) | collective-permute-done | bytes 90144 | tf_op jit(solution)/shard_map/ppermute | solution.py:609
  61.4 0.0 collective-permute-start.14
  61.4 0.6 collective-permute-done.9.refs_2_
  62.1 0.0 collective-permute-start.13
  62.1 0.9 %collective-permute-done.8.refs_1_ = s16[352,128]{1,0:T(8,128)(2,1)S(1)} collective-permute-done((s16[352,128]{1,0:T(8,128)(2,1)S(1)}, s16[352,128]{1,0:T(8,128)(2,1)S(1)}, u32[]{:S(2)}, u32[]{:S(2)}) %collective-permute-start.8) | collective-permute-done | bytes 90144 | tf_op jit(solution)/shard_map/ppermute | solution.py:609
  63.0 0.3 collective-permute-done.13.refs_6_
  63.3 1.0 %collective-permute-done.12.refs_5_ = s16[352,128]{1,0:T(8,128)(2,1)S(1)} collective-permute-done((s16[352,128]{1,0:T(8,128)(2,1)S(1)}, s16[352,128]{1,0:T(8,128)(2,1)S(1)}, u32[]{:S(2)}, u32[]{:S(2)}) %collective-permute-start.12) | collective-permute-done | bytes 90144 | tf_op jit(solution)/shard_map/ppermute | solution.py:609
  64.3 1.8 %unpack.1 = (f32[5,1,128]{2,1,0:T(1,128)}, f32[64,512]{1,0:T(8,128)}, f32[3,512]{1,0:T(4,128)}, f32[1,512]{1,0:T(1,128)}, f32[512,512]{1,0:T(8,128)}, /*index=5*...) custom-call(s32[3]{0:T(128)S(1)} %pad_add_fusion.place_ref, ...), custom_call_target="tpu_custom_call" | custom-call | tf_op jit(solution)/shard_map/unpack/pallas_call | solution.py:795
  (23 shorter events, 0.1 us)
Async XLA Ops:
  1.9 14.1 %copy-start.8 = (bf16[64,1728]{1,0:T(8,128)(2,1)S(1)}, bf16[64,1728]{1,0:T(8,128)(2,1)}, u32[]{:S(2)}) copy-start(bf16[64,1728]{1,0:T(8,128)(2,1)} %taps_ref.1) | copy-start | bytes 663556
  2.0 5.5 %copy-start.4 = (f32[1,5,128]{2,0,1:T(1,128)S(1)}, f32[1,5,128]{2,0,1:T(1,128)}, u32[]{:S(2)}) copy-start(f32[1,5,128]{2,0,1:T(1,128)} %param.20) | copy-start | bytes 7684
  2.0 14.0 %collective-permute-start.1 = (bf16[3,8,64,128]{3,2,1,0:T(8,128)(2,1)S(1)}, bf16[3,8,64,128]{3,2,1,0:T(8,128)(2,1)S(1)}, u32[]{:S(2)}, u32[]{:S(2)}) collective-permute-start(bf16[3,8,64,128]{3,2,1,0:T(8,128)(2,1)S(1)} %slice.8), channel_id=1, source_target_pairs={{1,0},{2,1},{3,2},{4,3},{5,4},{6,5},{7,6},{8,7},{9,8},{10,9},{11,1... | collective-permute-start | bytes 1179656 | tf_op jit(solution)/shard_map/ppermute | solution.py:839
  7.5 8.5 %collective-permute-start = (bf16[2,8,64,128]{3,2,1,0:T(8,128)(2,1)S(1)}, bf16[2,8,64,128]{3,2,1,0:T(8,128)(2,1)S(1)}, u32[]{:S(2)}, u32[]{:S(2)}) collective-permute-start(bf16[2,8,64,128]{3,2,1,0:T(8,128)(2,1)S(1)} %slice.9), channel_id=1, source_target_pairs={{0,1},{1,2},{2,3},{3,4},{4,5},{5,6},{6,7},{7,8},{8,9},{9,10},{10,1... | collective-permute-start | bytes 786440 | tf_op jit(solution)/shard_map/ppermute | solution.py:840
  7.5 0.7 %copy-start.5 = (f32[1,3,128]{2,0,1:T(1,128)S(1)}, f32[1,3,128]{2,0,1:T(1,128)}, u32[]{:S(2)}) copy-start(f32[1,3,128]{2,0,1:T(1,128)} %param.19) | copy-start | bytes 4612
  7.5 0.7 %copy-start.6 = (s32[1,128,1]{1,2,0:T(1,128)S(1)}, s32[1,128,1]{1,2,0:T(1,128)}, u32[]{:S(2)}) copy-start(s32[1,128,1]{1,2,0:T(1,128)} %param.17) | copy-start | bytes 1540
  7.5 0.7 %copy-start.7 = (s32[1,128]{1,0:T(1,128)S(1)}, s32[1,128]{1,0:T(1,128)}, u32[]{:S(2)}) copy-start(s32[1,128]{1,0:T(1,128)} %refs_1_.1) | copy-start | bytes 1540
  9.2 12.7 %all-to-all-start = ((f32[16,8,128]{2,1,0:T(8,128)}), f32[16,8,128]{2,1,0:T(8,128)S(1)}, u32[]{:S(2)}, u32[]{:S(2)}) async-start(f32[16,8,128]{2,1,0:T(8,128)} %bitcast.13), calls=%async_computation | async-start | bytes 131072 | tf_op jit(solution)/shard_map/all_to_all | solution.py:849
  15.0 1.0 %copy-start.10 = (f32[512]{0:T(512)S(1)}, f32[512]{0:T(512)}, u32[]{:S(2)}) copy-start(f32[512]{0:T(512)} %param.25) | copy-start | bytes 6148
  16.0 0.7 %copy-start.9 = (f32[512]{0:T(512)S(1)}, f32[512]{0:T(512)}, u32[]{:S(2)}) copy-start(f32[512]{0:T(512)} %param.23) | copy-start | bytes 6148
  16.0 0.7 %copy-start.11 = (f32[64]{0:T(128)S(1)}, f32[64]{0:T(128)}, u32[]{:S(2)}) copy-start(f32[64]{0:T(128)} %param.16) | copy-start | bytes 772
  16.0 0.7 %copy-start.12 = (f32[5]{0:T(128)S(1)}, f32[5]{0:T(128)}, u32[]{:S(2)}) copy-start(f32[5]{0:T(128)} %param.27) | copy-start | bytes 64
  16.7 5.3 %copy-start = (f32[512,512]{1,0:T(8,128)S(1)}, f32[512,512]{1,0:T(8,128)}, u32[]{:S(2)}) copy-start(f32[512,512]{1,0:T(8,128)} %w_mid_hbm.1) | copy-start | bytes 3145732
  16.7 5.3 %copy-start.1 = (f32[64,512]{1,0:T(8,128)S(1)}, f32[64,512]{1,0:T(8,128)}, u32[]{:S(2)}) copy-start(f32[64,512]{1,0:T(8,128)} %w_latent_hbm.1) | copy-start | bytes 393220
  16.7 5.3 %copy-start.2 = (f32[5,512]{1,0:T(8,128)S(1)}, f32[5,512]{1,0:T(8,128)}, u32[]{:S(2)}) copy-start(f32[5,512]{1,0:T(8,128)} %w_out_hbm.1) | copy-start | bytes 30724
  16.7 5.2 %copy-start.3 = (f32[3,512]{1,0:T(4,128)S(1)}, f32[3,512]{1,0:T(4,128)}, u32[]{:S(2)}) copy-start(f32[3,512]{1,0:T(4,128)} %w_pos_hbm.1) | copy-start | bytes 18436
  34.5 2.2 %collective-permute-start.2 = (f32[4,328,128]{2,1,0:T(8,128)S(1)}, f32[4,328,128]{2,1,0:T(8,128)S(1)}, u32[]{:S(2)}, u32[]{:S(2)}) collective-permute-start(f32[4,328,128]{2,1,0:T(8,128)S(1)} %get-tuple-element.36), channel_id=1, source_target_pairs={{0,1},{1,0},{2,3},{3,2},{4,5},{5,4},{6,7},{7,6},{8,9},{9,8},{10,11... | collective-permute-start | bytes 2015240 | tf_op jit(solution)/shard_map/ppermute | solution.py:609
  37.0 4.7 %collective-permute-start.4 = (s16[352,128]{1,0:T(8,128)(2,1)S(1)}, s16[352,128]{1,0:T(8,128)(2,1)S(1)}, u32[]{:S(2)}, u32[]{:S(2)}) collective-permute-start(s16[352,128]{1,0:T(8,128)(2,1)S(1)} %get-tuple-element.40), channel_id=1, source_target_pairs={{0,2},{1,3},{2,0},{3,1},{4,6},{5,7},{6,4},{7,5},{8,10},{9,11},{10,... | collective-permute-start | bytes 270344 | tf_op jit(solution)/shard_map/ppermute | solution.py:609
  37.1 4.6 %collective-permute-start.5 = (s16[352,128]{1,0:T(8,128)(2,1)S(1)}, s16[352,128]{1,0:T(8,128)(2,1)S(1)}, u32[]{:S(2)}, u32[]{:S(2)}) collective-permute-start(s16[352,128]{1,0:T(8,128)(2,1)S(1)} %get-tuple-element.41), channel_id=1, source_target_pairs={{0,16},{1,17},{2,18},{3,19},{4,20},{5,21},{6,22},{7,23},{8,24},{9,... | collective-permute-start | bytes 270344 | tf_op jit(solution)/shard_map/ppermute | solution.py:609
  38.6 6.2 %collective-permute-start.3 = (s16[352,128]{1,0:T(8,128)(2,1)S(1)}, s16[352,128]{1,0:T(8,128)(2,1)S(1)}, u32[]{:S(2)}, u32[]{:S(2)}) collective-permute-start(s16[352,128]{1,0:T(8,128)(2,1)S(1)} %sum_core.2), channel_id=1, source_target_pairs={{0,18},{1,19},{2,16},{3,17},{4,22},{5,23},{6,20},{7,21},{8,26},{9,... | collective-permute-start | bytes 270344 | tf_op jit(solution)/shard_map/ppermute | solution.py:609
  45.0 4.6 %collective-permute-start.6 = (s16[352,128]{1,0:T(8,128)(2,1)S(1)}, s16[352,128]{1,0:T(8,128)(2,1)S(1)}, u32[]{:S(2)}, u32[]{:S(2)}) collective-permute-start(s16[352,128]{1,0:T(8,128)(2,1)S(1)} %sum_plane.1.mine_ref), channel_id=1, source_target_pairs={{0,4},{1,5},{2,6},{3,7},{4,0},{5,1},{6,2},{7,3},{8,12},{9,13},{10,... | collective-permute-start | bytes 270344 | tf_op jit(solution)/shard_map/ppermute | solution.py:609
  49.7 6.1 %collective-permute-start.7 = (s16[352,128]{1,0:T(8,128)(2,1)S(1)}, s16[352,128]{1,0:T(8,128)(2,1)S(1)}, u32[]{:S(2)}, u32[]{:S(2)}) collective-permute-start(s16[352,128]{1,0:T(8,128)(2,1)S(1)} %sum_line.2.mine_ref), channel_id=1, source_target_pairs={{0,8},{1,9},{2,10},{3,11},{4,12},{5,13},{6,14},{7,15},{8,0},{9,1},... | collective-permute-start | bytes 270344 | tf_op jit(solution)/shard_map/ppermute | solution.py:609
  55.9 5.5 %collective-permute-start.10 = (s16[352,128]{1,0:T(8,128)(2,1)S(1)}, s16[352,128]{1,0:T(8,128)(2,1)S(1)}, u32[]{:S(2)}, u32[]{:S(2)}) collective-permute-start(s16[352,128]{1,0:T(8,128)(2,1)S(1)} %sum_line.3.refs_0_), channel_id=1, source_target_pairs={{0,18},{1,19},{2,16},{3,17},{4,22},{5,23},{6,20},{7,21},{8,26},{9,... | collective-permute-start | bytes 270344 | tf_op jit(solution)/shard_map/ppermute | solution.py:609
  57.5 4.5 %collective-permute-start.9 = (s16[352,128]{1,0:T(8,128)(2,1)S(1)}, s16[352,128]{1,0:T(8,128)(2,1)S(1)}, u32[]{:S(2)}, u32[]{:S(2)}) collective-permute-start(s16[352,128]{1,0:T(8,128)(2,1)S(1)} %sum_line.3.refs_0_), channel_id=1, source_target_pairs={{0,16},{1,17},{2,18},{3,19},{4,20},{5,21},{6,22},{7,23},{8,24},{9,... | collective-permute-start | bytes 270344 | tf_op jit(solution)/shard_map/ppermute | solution.py:609
  58.5 4.5 %collective-permute-start.8 = (s16[352,128]{1,0:T(8,128)(2,1)S(1)}, s16[352,128]{1,0:T(8,128)(2,1)S(1)}, u32[]{:S(2)}, u32[]{:S(2)}) collective-permute-start(s16[352,128]{1,0:T(8,128)(2,1)S(1)} %sum_line.3.refs_0_), channel_id=1, source_target_pairs={{0,2},{1,3},{2,0},{3,1},{4,6},{5,7},{6,4},{7,5},{8,10},{9,11},{10,... | collective-permute-start | bytes 270344 | tf_op jit(solution)/shard_map/ppermute | solution.py:609
  59.5 3.5 %collective-permute-start.11 = (s16[352,128]{1,0:T(8,128)(2,1)S(1)}, s16[352,128]{1,0:T(8,128)(2,1)S(1)}, u32[]{:S(2)}, u32[]{:S(2)}) collective-permute-start(s16[352,128]{1,0:T(8,128)(2,1)S(1)} %sum_line.3.refs_0_), channel_id=1, source_target_pairs={{0,1},{1,0},{2,3},{3,2},{4,5},{5,4},{6,7},{7,6},{8,9},{9,8},{10,11... | collective-permute-start | bytes 270344 | tf_op jit(solution)/shard_map/ppermute | solution.py:609
  61.4 1.6 %collective-permute-start.14 = (s16[352,128]{1,0:T(8,128)(2,1)S(1)}, s16[352,128]{1,0:T(8,128)(2,1)S(1)}, u32[]{:S(2)}, u32[]{:S(2)}) collective-permute-start(s16[352,128]{1,0:T(8,128)(2,1)S(1)} %collective-permute-done.10.refs_3_), channel_id=1, source_target_pairs={{0,1},{1,0},{2,3},{3,2},{4,5},{5,4},{6,7},{7,6},{8,9},{9,8},{10,11... | collective-permute-start | bytes 270344 | tf_op jit(solution)/shard_map/ppermute | solution.py:609
  62.1 1.3 %collective-permute-start.13 = (s16[352,128]{1,0:T(8,128)(2,1)S(1)}, s16[352,128]{1,0:T(8,128)(2,1)S(1)}, u32[]{:S(2)}, u32[]{:S(2)}) collective-permute-start(s16[352,128]{1,0:T(8,128)(2,1)S(1)} %collective-permute-done.9.refs_2_), channel_id=1, source_target_pairs={{0,1},{1,0},{2,3},{3,2},{4,5},{5,4},{6,7},{7,6},{8,9},{9,8},{10,11... | collective-permute-start | bytes 270344 | tf_op jit(solution)/shard_map/ppermute | solution.py:609
  63.0 1.3 %collective-permute-start.12 = (s16[352,128]{1,0:T(8,128)(2,1)S(1)}, s16[352,128]{1,0:T(8,128)(2,1)S(1)}, u32[]{:S(2)}, u32[]{:S(2)}) collective-permute-start(s16[352,128]{1,0:T(8,128)(2,1)S(1)} %collective-permute-done.8.refs_1_), channel_id=1, source_target_pairs={{0,1},{1,0},{2,3},{3,2},{4,5},{5,4},{6,7},{7,6},{8,9},{9,8},{10,11... | collective-permute-start | bytes 270344 | tf_op jit(solution)/shard_map/ppermute | solution.py:609

commit v10 on v9

--- a/solution.py
+++ b/solution.py
@@ -57,10 +57,14 @@
 
 
 def route_kernel(tiles, slots, *refs):
-    out_ref, owner_ref, cell_ref, frac_ref, target_ref, words, sems = refs[4:]
+    out_ref, small_ref, *scratch, words, sems = refs[8:]
+    for copy in fetches(refs[:8], scratch, sems):
+        copy.wait()
+    owner_ref, cell_ref, frac_ref, target_ref, *bias_refs = scratch
     queries = owner_ref.shape[1]
-    for copy in fetches(refs[:4], (owner_ref, cell_ref, frac_ref, target_ref), sems):
-        copy.wait()
+    small_ref[...] = jnp.zeros_like(small_ref)
+    for number, ref in enumerate(bias_refs):
+        small_ref[number : number + 1, 0 : ref.shape[1]] = ref[...]
     owner = owner_ref[...]
     hits = (lax.broadcasted_iota(jnp.int32, (tiles, queries), 0) == owner).astype(F32)
     before = lax.broadcasted_iota(jnp.int32, (queries, queries), 0) < lax.broadcasted_iota(
@@ -88,24 +92,22 @@
     out_ref[...] = mul(chosen, high, NT) + mul(chosen, middle, NT) + mul(chosen, low, NT)
 
 
-def route(owner, cell, frac, target, tiles, slots):
-    queries = owner.shape[1]
+def route(inputs, biases, tiles, slots):
+    queries = inputs[0].shape[1]
+    arrays = inputs + biases
     return pl.pallas_call(
         functools.partial(route_kernel, tiles, slots),
-        out_shape=jax.ShapeDtypeStruct((tiles * 8, WORDS), F32),
-        in_specs=[HBM] * 4,
-        out_specs=VMEM,
-        scratch_shapes=[
-            pltpu.VMEM(owner.shape, owner.dtype),
-            pltpu.VMEM(cell.shape, cell.dtype),
-            pltpu.VMEM(frac.shape, F32),
-            pltpu.VMEM(target.shape, F32),
-            pltpu.VMEM((WORDS, queries * (slots // 8)), F32),
-            pltpu.SemaphoreType.DMA((4,)),
-        ],
+        out_shape=(
+            jax.ShapeDtypeStruct((tiles * 8, WORDS), F32),
+            jax.ShapeDtypeStruct((8, biases[0].shape[1]), F32),
+        ),
+        in_specs=[HBM] * 8,
+        out_specs=(VMEM, VMEM),
+        scratch_shapes=[pltpu.VMEM(array.shape, array.dtype) for array in arrays]
+        + [pltpu.VMEM((WORDS, queries * (slots // 8)), F32), pltpu.SemaphoreType.DMA((8,))],
         compiler_params=pltpu.CompilerParams(vmem_limit_bytes=4 << 20),
         name="route",
-    )(owner, cell, frac, target)
+    )(*arrays)
 
 
 def tap_sum(weight_ref, planes, pair):
@@ -135,12 +137,8 @@
     here_ref,
     right_ref,
     taps_ref,
-    bias_ref,
-    bias_one_ref,
-    bias_two_ref,
-    bias_out_ref,
+    small_ref,
     lat_ref,
-    small_ref,
     weight_ref,
 ):
     planes, rows_y, channels = here_ref.shape[:3]
@@ -156,11 +154,7 @@
     diagonal = lax.broadcasted_iota(jnp.int32, (channels, channels), 0) == lax.broadcasted_iota(
         jnp.int32, (channels, channels), 1
     )
-    bias = jnp.sum(jnp.where(diagonal, bias_ref[...], 0.0), axis=1, keepdims=True)
-    small_ref[...] = jnp.zeros_like(small_ref)
-    small_ref[0:1, :] = bias_one_ref[...]
-    small_ref[1:2, :] = bias_two_ref[...]
-    small_ref[2:3, 0:5] = bias_out_ref[...]
+    bias = jnp.sum(jnp.where(diagonal, small_ref[3:4, 0:channels], 0.0), axis=1, keepdims=True)
     for x in range(planes + 1):
         taps = []
         for step in range(3):
@@ -176,22 +170,19 @@
             lat_ref[x * (rows_y // 2) + pair] = jax.nn.gelu(summed).astype(BF16)
 
 
-def convolve(left, here, right, taps, conv_bias, biases):
+def convolve(left, here, right, taps, small):
     planes, rows_y, channels, rows_z = here.shape
     pairs = (planes + 1) * rows_y // 2
     return pl.pallas_call(
         conv_kernel,
-        out_shape=(
-            jax.ShapeDtypeStruct((pairs, channels, 2 * rows_z), BF16),
-            jax.ShapeDtypeStruct((8, biases[0].shape[1]), F32),
-        ),
-        in_specs=[VMEM] * 8,
-        out_specs=(VMEM, VMEM),
+        out_shape=jax.ShapeDtypeStruct((pairs, channels, 2 * rows_z), BF16),
+        in_specs=[VMEM] * 5,
+        out_specs=VMEM,
         scratch_shapes=[pltpu.VMEM((3, 3 * channels, 3 * channels), BF16)],
         compiler_params=pltpu.CompilerParams(vmem_limit_bytes=8 << 20),
         cost_estimate=pl.CostEstimate(flops=3 << 30, bytes_accessed=4 << 20, transcendentals=0),
         name="convolve",
-    )(left, here, right, taps, conv_bias, *biases)
+    )(left, here, right, taps, small)
 
 
 def interpolate(words, lat, planes, rows_y, rows_z):
@@ -369,14 +360,20 @@
     out_fields = jnp.concatenate([w_out_ref[...], jnp.zeros((3, hidden), F32)], axis=0)
     wo_high, wo_low = halves(out_fields)
     wo_three = jnp.concatenate([out_fields, wo_low.astype(F32), out_fields], axis=0).astype(BF16)
-    wo_both = jnp.concatenate([out_fields, wo_low.astype(F32)], axis=0).astype(BF16)
+    wo_both = jnp.concatenate(
+        [out_fields, wo_low.astype(F32), jnp.zeros((LANES - 16, hidden), F32)], axis=0
+    ).astype(BF16)
 
     def outputs(part):
+        span = slice(part * 5 * part_rows, (part + 1) * 5 * part_rows)
+        both = mul(two_high[span, :], wo_both, NT)
+        low = mul(two_low[span, :], wo_both, NT)
         for s in range(5):
-            span = at(part, s)
-            both = mul(wo_both, two_high[span, :], NT)
-            both = both[:8] + both[8:] + mul(wo_high, two_low[span, :], NT)
-            out_t[8 * s : 8 * s + 8, part * part_rows : (part + 1) * part_rows] = both
+            rows_s = slice(s * part_rows, (s + 1) * part_rows)
+            both_t, low_t = both[rows_s].T, low[rows_s].T
+            out_t[8 * s : 8 * s + 8, part * part_rows : (part + 1) * part_rows] = (
+                both_t[0:8] + both_t[8:16] + low_t[0:8]
+            )
 
     @pl.when(always)
     def _():
@@ -446,11 +443,11 @@
         d_out_t[34 + j : 35 + j, :] = -VISCOSITY * d_mom[j]
 
     def out_back(part):
-        for s in range(5):
-            wanted = d_out_t[8 * s : 8 * s + 8, part * part_rows : (part + 1) * part_rows]
-            do_low = halves(wanted)[1].astype(F32)
-            wanted = jnp.concatenate([wanted, wanted, do_low], axis=0).astype(BF16)
-            back[at(part, s), :] = mul(wanted, wo_three, TN)
+        columns = slice(part * part_rows, (part + 1) * part_rows)
+        wanted = jnp.concatenate([d_out_t[8 * s : 8 * s + 8, columns] for s in range(5)], axis=1)
+        do_low = halves(wanted)[1].astype(F32)
+        wanted = jnp.concatenate([wanted, wanted, do_low], axis=0).astype(BF16)
+        back[part * 5 * part_rows : (part + 1) * 5 * part_rows, :] = mul(wanted, wo_three, TN)
 
     def second_back(part, total):
         refs = (d_both.at[:, :hidden], d_both.at[:, hidden:])
@@ -508,14 +505,11 @@
             packed[2 * part + block, row : row + count, :] = value[:count]
             first, value = first + count, value[count:]
 
-    wide = 2 * LANES
     def mid_gradient():
-        for left in range(hidden // wide):
-            lefts = slice(left * wide, (left + 1) * wide)
-            both = mul(one_high[:, lefts], d_both[...], TN)
-            both = both[:, :hidden] + both[:, hidden:] + mul(one_low[:, lefts], d_both[:, :hidden], TN)
-            for part in range(hidden // LANES):
-                put(part, left * wide, both[:, part * LANES : (part + 1) * LANES])
+        both = mul(one_high[...], d_both[...], TN)
+        both = both[:, :hidden] + both[:, hidden:] + mul(one_low[...], d_both[:, :hidden], TN)
+        for part in range(hidden // LANES):
+            put(part, 0, both[:, part * LANES : (part + 1) * LANES])
 
     @pl.when(always)
     def _():
@@ -580,7 +574,7 @@
 
         @pl.when((my_block >> 2) != block // 4)
         def _():
-            send_ref[spot] = packed[block]
+            encode(plan, lambda start, count: packed[block, start : start + count, :], send_ref.at[spot])
 
 
 class Plan:
@@ -662,15 +656,17 @@
 
 def first_kernel(plan, numbers, keep_ref, got_ref, *refs):
     def reader(block):
-        return lambda start, count: (
-            keep_ref[block, start : start + count, :] + got_ref[block, start : start + count, :]
-        )
+        got = decoder(plan, got_ref.at[block])
+        return lambda start, count: keep_ref[block, start : start + count, :] + got(start, count)
 
     for number, out_ref in zip(numbers, refs):
         if number:
             encode(plan, reader(number), out_ref)
         else:
-            out_ref[...] = keep_ref[0] + got_ref[0]
+            read = reader(0)
+            for start in range(0, plan.coded_rows, SUB):
+                out_ref[start : start + SUB, :] = read(start, SUB)
+            out_ref[plan.coded_rows :, :] = read(plan.coded_rows, 8)
 
 
 def first_sum(keep, got, numbers, plan):
@@ -714,7 +710,7 @@
     wide = lambda kind: pltpu.VMEM((5 * rows, hidden), kind)
     return pl.pallas_call(
         functools.partial(main_kernel, plan),
-        out_shape=(outs, outs),
+        out_shape=(jax.ShapeDtypeStruct((4, plan.sent_rows, LANES), jnp.int16), outs),
         in_specs=[SMEM] + [VMEM] * 3 + [HBM] * 4,
         out_specs=(VMEM, VMEM),
         scratch_shapes=[
@@ -838,11 +834,9 @@
     )
     right = lax.ppermute(to_left, "tile", down)
     left = lax.ppermute(to_right, "tile", up)
-    words = route(
-        query_owner[:, :, 0],
-        query_cell,
-        query_frac.transpose(1, 0, 2),
-        target.transpose(1, 0, 2),
+    words, small = route(
+        (query_owner[:, :, 0], query_cell, query_frac.transpose(1, 0, 2), target.transpose(1, 0, 2)),
+        (bias_one[None], bias_two[None], bias_out[None], convolution_bias[None]),
         tiles,
         plan.slots,
     )
@@ -850,8 +844,7 @@
         words.reshape(tiles, 8, WORDS), "tile", split_axis=0, concat_axis=0, tiled=True
     ).reshape(tiles * 8, WORDS)
 
-    biases = (bias_one[None], bias_two[None], bias_out[None])
-    lat, small = convolve(left, here, right, convolution_weight, convolution_bias[None], biases)
+    lat = convolve(left, here, right, convolution_weight, small)
     weights = (w_latent, w_pos, w_mid, w_out)
     send, keep = main(place, lat, words, small, weights, plan)
 

time: 66.4 us -> 66.3 us (level)
  local copies, waits for them, and re-layouts: 2.66 us -> 1.99 us
    all_to_all x1, waiting for transfers between devices: 3.33 us -> 4.09 us  [body(): lax.all_to_all(words.reshape(tiles, 8, WORDS), 'tile', split_axis=0, conc...]
    unnamed x27, local copies, waits for them, and re-layouts: 2.62 us -> 1.95 us
where the time goes in v10:
time: 66.3 us; the launch traced here: 66.1 us
  waiting for transfers between devices  25.7 us (39%)
  starting transfers between devices  19.2 us (29%)
  Pallas kernels  18.2 us (27%)
  local copies, waits for them, and re-layouts  1.99 us (3%)
  between operations  0.89 us (1%)
    ppermute x13, waiting for transfers between devices, swapped(): lax.ppermute(value, ('replica', 'tile'), [(i, i ^ mask) for i in range(pl...  20.8 us
    pallas_call x1, Pallas kernels, main(): pl.pallas_call(functools.partial(main_kernel, plan), out_shape=(jax.Shape...  12.8 us
    ppermute x13, starting transfers between devices, swapped(): lax.ppermute(value, ('replica', 'tile'), [(i, i ^ mask) for i in range(pl...  7.9 us
    all_to_all x1, starting transfers between devices, body(): lax.all_to_all(words.reshape(tiles, 8, WORDS), 'tile', split_axis=0, conc...  5.83 us
    ppermute x1, starting transfers between devices, body(): right = lax.ppermute(to_left, 'tile', down)  5.5 us
    all_to_all x1, waiting for transfers between devices, body(): lax.all_to_all(words.reshape(tiles, 8, WORDS), 'tile', split_axis=0, conc...  4.09 us
    unnamed x27, local copies, waits for them, and re-layouts  1.95 us
    pallas_call x1, Pallas kernels, convolve(): pl.pallas_call(conv_kernel, out_shape=jax.ShapeDtypeStruct((pairs, channe...  1.87 us
  transfers between devices with their start and end apart: 16, of which 13 were waited for; matrix products, arithmetic and copies ran while one was open for 0% of the time, Pallas kernels for 4%

profile of v10, /device:TPU:0, one launch (start us, length us, event | category | flops | bytes accessed | tf_op | source)
XLA Modules:
  0.0 66.1 jit_solution(3327747766652364589)
XLA Ops:
  0.6 1.2 %copy.25 = bf16[1,64,4,8,128]{4,1,3,2,0:T(8,128)(2,1)S(1)} copy(bf16[1,64,4,8,128]{4,3,2,1,0:T(8,128)(2,1)} %param.14) | data formatting | bytes 1048576 | tf_op args[0]
  1.9 0.0 copy-start.6
  1.9 0.0 copy-start.7
  1.9 0.0 copy-start.10
  2.0 0.0 copy-start.11
  2.0 0.0 copy-start.12
  2.0 5.5 %collective-permute-start.1 = (bf16[3,8,64,128]{3,2,1,0:T(8,128)(2,1)S(1)}, bf16[3,8,64,128]{3,2,1,0:T(8,128)(2,1)S(1)}, u32[]{:S(2)}, u32[]{:S(2)}) collective-permute-start(bf16[3,8,64,128]{3,2,1,0:T(8,128)(2,1)S(1)} %slice.8), channel_id=1, source_target_pairs={{1,0},{2,1},{3,2},{4,3},{5,4},{6,5},{7,6},{8,7},{9,8},{10,9},{11,1... | collective-permute-start | bytes 1179656 | tf_op jit(solution)/shard_map/ppermute | solution.py:835
  7.5 0.0 collective-permute-start
  7.5 0.0 copy-start.9
  7.6 0.6 copy-done.4
  8.2 0.0 copy-done.5
  8.2 1.1 %route.1 = (f32[128,128]{1,0:T(8,128)}, f32[8,512]{1,0:T(8,128)S(1)}) custom-call(s32[1,128]{1,0:T(1,128)S(1)} %bitcast.30, s32[1,128]{1,0:T(1,128)S(1)} %copy-done.9, f32[3,1,128]{2,1,0:T(1,128)S(1)} %bitcast.29, f32[5,1,128]{2,1,0:T(1,128)S(1)} %bitcast.26, f32[1,512]{1,0:T(1,128)S(1)} %bitcast.27, f32[1,512]{1,0:T(1,128)S(1)} %bitcast.28, ...), custom_call_target="tpu_custom_call" | custom-call | tf_op jit(solution)/shard_map/route/pallas_call | solution.py:98
  9.3 5.8 %all-to-all-start = ((f32[16,8,128]{2,1,0:T(8,128)}), f32[16,8,128]{2,1,0:T(8,128)S(1)}, u32[]{:S(2)}, u32[]{:S(2)}) async-start(f32[16,8,128]{2,1,0:T(8,128)} %bitcast.13), calls=%async_computation | async-start | bytes 131072 | tf_op jit(solution)/shard_map/all_to_all | solution.py:843
  15.1 0.1 pad_add_fusion.place_ref
  15.2 0.8 %collective-permute-done.left_ref = bf16[2,8,64,128]{3,2,1,0:T(8,128)(2,1)S(1)} collective-permute-done((bf16[2,8,64,128]{3,2,1,0:T(8,128)(2,1)S(1)}, bf16[2,8,64,128]{3,2,1,0:T(8,128)(2,1)S(1)}, u32[]{:S(2)}, u32[]{:S(2)}) %collective-permute-start) | collective-permute-done | bytes 262176 | tf_op jit(solution)/shard_map/ppermute | solution.py:836
  16.0 0.0 collective-permute-done.1.right_ref
  16.0 0.0 copy-start.1
  16.0 0.0 copy-start.2
  16.0 0.0 copy-start.3
  16.1 1.9 %convolve.1.lat = bf16[20,64,256]{2,1,0:T(8,128)(2,1)S(1)} custom-call(bf16[2,8,64,128]{3,2,1,0:T(8,128)(2,1)S(1)} %collective-permute-done.left_ref, bf16[4,8,64,128]{3,2,1,0:T(8,128)(2,1)S(1)} %bitcast.24, bf16[3,8,64,128]{3,2,1,0:T(8,128)(2,1)S(1)} %collective-permute-done.1.right_ref, bf16[64,1728]{1,0:T(8,128)(2,1)S(1)} %copy-done.12, ...), custom_call_target="tpu_custom_call" | custom-call | flops 3221225472 | bytes 4194304 | tf_op jit(solution)/shard_map/convolve/pallas_call | solution.py:176
  17.9 4.1 %all-to-all-done = f32[16,8,128]{2,1,0:T(8,128)S(1)} async-done(((f32[16,8,128]{2,1,0:T(8,128)}), f32[16,8,128]{2,1,0:T(8,128)S(1)}, u32[]{:S(2)}, u32[]{:S(2)}) %all-to-all-start) | async-done | bytes 65568 | tf_op jit(solution)/shard_map/all_to_all | solution.py:843
  22.0 12.8 %encode_decode.1 = (s16[4,352,128]{2,1,0:T(8,128)(2,1)S(1)}, f32[4,328,128]{2,1,0:T(8,128)S(1)}) custom-call(s32[3]{0:T(128)S(1)} %pad_add_fusion.place_ref, bf16[20,64,256]{2,1,0:T(8,128)(2,1)S(1)} %convolve.1.lat, f32[128,128]{1,0:T(8,128)S(1)} %bitcast.25, f32[8,512]{1,0:T(8,128)S(1)} %get-tuple-element.33.small_ref, f32[64,512]{1,0:T(8,128)S(1)} %copy-done.1, ...), custom_call_target="tpu_custom_call" | custom-call | tf_op jit(solution)/shard_map/encode_decode/pallas_call | solution.py:711
  34.9 0.1 collective-permute-start.2
  35.0 1.7 %collective-permute-done.2.got_ref = s16[4,352,128]{2,1,0:T(8,128)(2,1)S(1)} collective-permute-done((s16[4,352,128]{2,1,0:T(8,128)(2,1)S(1)}, s16[4,352,128]{2,1,0:T(8,128)(2,1)S(1)}, u32[]{:S(2)}, u32[]{:S(2)}) %collective-permute-start.2) | collective-permute-done | bytes 360480 | tf_op jit(solution)/shard_map/ppermute | solution.py:603
  36.6 0.1 sum_core.2
  36.7 0.2 sum_core.3
  36.9 0.2 collective-permute-start.4
  37.1 1.5 %collective-permute-start.5 = (s16[352,128]{1,0:T(8,128)(2,1)S(1)}, s16[352,128]{1,0:T(8,128)(2,1)S(1)}, u32[]{:S(2)}, u32[]{:S(2)}) collective-permute-start(s16[352,128]{1,0:T(8,128)(2,1)S(1)} %get-tuple-element.41), channel_id=1, source_target_pairs={{0,16},{1,17},{2,18},{3,19},{4,20},{5,21},{6,22},{7,23},{8,24},{9,... | collective-permute-start | bytes 270344 | tf_op jit(solution)/shard_map/ppermute | solution.py:603
  38.6 1.9 %collective-permute-start.3 = (s16[352,128]{1,0:T(8,128)(2,1)S(1)}, s16[352,128]{1,0:T(8,128)(2,1)S(1)}, u32[]{:S(2)}, u32[]{:S(2)}) collective-permute-start(s16[352,128]{1,0:T(8,128)(2,1)S(1)} %sum_core.2), channel_id=1, source_target_pairs={{0,18},{1,19},{2,16},{3,17},{4,22},{5,23},{6,20},{7,21},{8,26},{9,... | collective-permute-start | bytes 270344 | tf_op jit(solution)/shard_map/ppermute | solution.py:603
  40.5 1.2 %collective-permute-done.4.refs_1_ = s16[352,128]{1,0:T(8,128)(2,1)S(1)} collective-permute-done((s16[352,128]{1,0:T(8,128)(2,1)S(1)}, s16[352,128]{1,0:T(8,128)(2,1)S(1)}, u32[]{:S(2)}, u32[]{:S(2)}) %collective-permute-start.4) | collective-permute-done | bytes 90144 | tf_op jit(solution)/shard_map/ppermute | solution.py:603
  41.6 0.1 collective-permute-done.5.refs_2_
  41.7 3.1 %collective-permute-done.3.refs_0_ = s16[352,128]{1,0:T(8,128)(2,1)S(1)} collective-permute-done((s16[352,128]{1,0:T(8,128)(2,1)S(1)}, s16[352,128]{1,0:T(8,128)(2,1)S(1)}, u32[]{:S(2)}, u32[]{:S(2)}) %collective-permute-start.3) | collective-permute-done | bytes 90144 | tf_op jit(solution)/shard_map/ppermute | solution.py:603
  44.8 0.1 sum_plane.1.mine_ref
  44.9 0.3 collective-permute-start.6
  45.2 4.3 %collective-permute-done.6.other_ref = s16[352,128]{1,0:T(8,128)(2,1)S(1)} collective-permute-done((s16[352,128]{1,0:T(8,128)(2,1)S(1)}, s16[352,128]{1,0:T(8,128)(2,1)S(1)}, u32[]{:S(2)}, u32[]{:S(2)}) %collective-permute-start.6) | collective-permute-done | bytes 90144 | tf_op jit(solution)/shard_map/ppermute | solution.py:603
  49.5 0.1 sum_line.2.mine_ref
  49.6 0.4 collective-permute-start.7
  50.0 5.8 %collective-permute-done.7.other_ref = s16[352,128]{1,0:T(8,128)(2,1)S(1)} collective-permute-done((s16[352,128]{1,0:T(8,128)(2,1)S(1)}, s16[352,128]{1,0:T(8,128)(2,1)S(1)}, u32[]{:S(2)}, u32[]{:S(2)}) %collective-permute-start.7) | collective-permute-done | bytes 90144 | tf_op jit(solution)/shard_map/ppermute | solution.py:603
  55.8 0.1 sum_line.3.refs_0_
  55.9 1.6 %collective-permute-start.10 = (s16[352,128]{1,0:T(8,128)(2,1)S(1)}, s16[352,128]{1,0:T(8,128)(2,1)S(1)}, u32[]{:S(2)}, u32[]{:S(2)}) collective-permute-start(s16[352,128]{1,0:T(8,128)(2,1)S(1)} %sum_line.3.refs_0_), channel_id=1, source_target_pairs={{0,18},{1,19},{2,16},{3,17},{4,22},{5,23},{6,20},{7,21},{8,26},{9,... | collective-permute-start | bytes 270344 | tf_op jit(solution)/shard_map/ppermute | solution.py:603
  57.5 0.9 %collective-permute-start.9 = (s16[352,128]{1,0:T(8,128)(2,1)S(1)}, s16[352,128]{1,0:T(8,128)(2,1)S(1)}, u32[]{:S(2)}, u32[]{:S(2)}) collective-permute-start(s16[352,128]{1,0:T(8,128)(2,1)S(1)} %sum_line.3.refs_0_), channel_id=1, source_target_pairs={{0,16},{1,17},{2,18},{3,19},{4,20},{5,21},{6,22},{7,23},{8,24},{9,... | collective-permute-start | bytes 270344 | tf_op jit(solution)/shard_map/ppermute | solution.py:603
  58.4 1.0 %collective-permute-start.8 = (s16[352,128]{1,0:T(8,128)(2,1)S(1)}, s16[352,128]{1,0:T(8,128)(2,1)S(1)}, u32[]{:S(2)}, u32[]{:S(2)}) collective-permute-start(s16[352,128]{1,0:T(8,128)(2,1)S(1)} %sum_line.3.refs_0_), channel_id=1, source_target_pairs={{0,2},{1,3},{2,0},{3,1},{4,6},{5,7},{6,4},{7,5},{8,10},{9,11},{10,... | collective-permute-start | bytes 270344 | tf_op jit(solution)/shard_map/ppermute | solution.py:603
  59.4 1.9 %collective-permute-done.10.refs_3_ = s16[352,128]{1,0:T(8,128)(2,1)S(1)} collective-permute-done((s16[352,128]{1,0:T(8,128)(2,1)S(1)}, s16[352,128]{1,0:T(8,128)(2,1)S(1)}, u32[]{:S(2)}, u32[]{:S(2)}) %collective-permute-start.10) | collective-permute-done | bytes 90144 | tf_op jit(solution)/shard_map/ppermute | solution.py:603
  61.4 0.6 collective-permute-done.9.refs_2_
  62.0 0.9 %collective-permute-done.8.refs_1_ = s16[352,128]{1,0:T(8,128)(2,1)S(1)} collective-permute-done((s16[352,128]{1,0:T(8,128)(2,1)S(1)}, s16[352,128]{1,0:T(8,128)(2,1)S(1)}, u32[]{:S(2)}, u32[]{:S(2)}) %collective-permute-start.8) | collective-permute-done | bytes 90144 | tf_op jit(solution)/shard_map/ppermute | solution.py:603
  63.0 0.3 collective-permute-done.13.refs_6_
  63.3 0.9 %collective-permute-done.12.refs_5_ = s16[352,128]{1,0:T(8,128)(2,1)S(1)} collective-permute-done((s16[352,128]{1,0:T(8,128)(2,1)S(1)}, s16[352,128]{1,0:T(8,128)(2,1)S(1)}, u32[]{:S(2)}, u32[]{:S(2)}) %collective-permute-start.12) | collective-permute-done | bytes 90144 | tf_op jit(solution)/shard_map/ppermute | solution.py:603
  64.2 1.8 %unpack.1 = (f32[5,1,128]{2,1,0:T(1,128)}, f32[64,512]{1,0:T(8,128)}, f32[3,512]{1,0:T(4,128)}, f32[1,512]{1,0:T(1,128)}, f32[512,512]{1,0:T(8,128)}, /*index=5*...) custom-call(s32[3]{0:T(128)S(1)} %pad_add_fusion.place_ref, ...), custom_call_target="tpu_custom_call" | custom-call | tf_op jit(solution)/shard_map/unpack/pallas_call | solution.py:791
  (23 shorter events, 0.1 us)
Async XLA Ops:
  1.9 5.6 %copy-start.6 = (f32[512]{0:T(512)S(1)}, f32[512]{0:T(512)}, u32[]{:S(2)}) copy-start(f32[512]{0:T(512)} %param.25) | copy-start | bytes 6148
  1.9 5.6 %copy-start.7 = (f32[1,3,128]{2,0,1:T(1,128)S(1)}, f32[1,3,128]{2,0,1:T(1,128)}, u32[]{:S(2)}) copy-start(f32[1,3,128]{2,0,1:T(1,128)} %param.19) | copy-start | bytes 4612
  1.9 5.6 %copy-start.10 = (f32[5]{0:T(128)S(1)}, f32[5]{0:T(128)}, u32[]{:S(2)}) copy-start(f32[5]{0:T(128)} %param.27) | copy-start | bytes 64
  2.0 5.6 %copy-start.11 = (f32[64]{0:T(128)S(1)}, f32[64]{0:T(128)}, u32[]{:S(2)}) copy-start(f32[64]{0:T(128)} %param.16) | copy-start | bytes 772
  2.0 14.0 %copy-start.12 = (bf16[64,1728]{1,0:T(8,128)(2,1)S(1)}, bf16[64,1728]{1,0:T(8,128)(2,1)}, u32[]{:S(2)}) copy-start(bf16[64,1728]{1,0:T(8,128)(2,1)} %taps_ref.1) | copy-start | bytes 663556
  2.0 14.0 %collective-permute-start.1 = (bf16[3,8,64,128]{3,2,1,0:T(8,128)(2,1)S(1)}, bf16[3,8,64,128]{3,2,1,0:T(8,128)(2,1)S(1)}, u32[]{:S(2)}, u32[]{:S(2)}) collective-permute-start(bf16[3,8,64,128]{3,2,1,0:T(8,128)(2,1)S(1)} %slice.8), channel_id=1, source_target_pairs={{1,0},{2,1},{3,2},{4,3},{5,4},{6,5},{7,6},{8,7},{9,8},{10,9},{11,1... | collective-permute-start | bytes 1179656 | tf_op jit(solution)/shard_map/ppermute | solution.py:835
  7.5 8.5 %collective-permute-start = (bf16[2,8,64,128]{3,2,1,0:T(8,128)(2,1)S(1)}, bf16[2,8,64,128]{3,2,1,0:T(8,128)(2,1)S(1)}, u32[]{:S(2)}, u32[]{:S(2)}) collective-permute-start(bf16[2,8,64,128]{3,2,1,0:T(8,128)(2,1)S(1)} %slice.9), channel_id=1, source_target_pairs={{0,1},{1,2},{2,3},{3,4},{4,5},{5,6},{6,7},{7,8},{8,9},{9,10},{10,1... | collective-permute-start | bytes 786440 | tf_op jit(solution)/shard_map/ppermute | solution.py:836
  7.5 0.7 %copy-start.4 = (f32[1,5,128]{2,0,1:T(1,128)S(1)}, f32[1,5,128]{2,0,1:T(1,128)}, u32[]{:S(2)}) copy-start(f32[1,5,128]{2,0,1:T(1,128)} %param.20) | copy-start | bytes 7684
  7.5 0.7 %copy-start.5 = (f32[512]{0:T(512)S(1)}, f32[512]{0:T(512)}, u32[]{:S(2)}) copy-start(f32[512]{0:T(512)} %param.23) | copy-start | bytes 6148
  7.5 0.7 %copy-start.8 = (s32[1,128,1]{1,2,0:T(1,128)S(1)}, s32[1,128,1]{1,2,0:T(1,128)}, u32[]{:S(2)}) copy-start(s32[1,128,1]{1,2,0:T(1,128)} %param.17) | copy-start | bytes 1540
  7.5 0.7 %copy-start.9 = (s32[1,128]{1,0:T(1,128)S(1)}, s32[1,128]{1,0:T(1,128)}, u32[]{:S(2)}) copy-start(s32[1,128]{1,0:T(1,128)} %refs_1_.1) | copy-start | bytes 1540
  9.3 12.7 %all-to-all-start = ((f32[16,8,128]{2,1,0:T(8,128)}), f32[16,8,128]{2,1,0:T(8,128)S(1)}, u32[]{:S(2)}, u32[]{:S(2)}) async-start(f32[16,8,128]{2,1,0:T(8,128)} %bitcast.13), calls=%async_computation | async-start | bytes 131072 | tf_op jit(solution)/shard_map/all_to_all | solution.py:843
  16.0 6.0 %copy-start = (f32[512,512]{1,0:T(8,128)S(1)}, f32[512,512]{1,0:T(8,128)}, u32[]{:S(2)}) copy-start(f32[512,512]{1,0:T(8,128)} %w_mid_hbm.1) | copy-start | bytes 3145732
  16.0 6.0 %copy-start.1 = (f32[64,512]{1,0:T(8,128)S(1)}, f32[64,512]{1,0:T(8,128)}, u32[]{:S(2)}) copy-start(f32[64,512]{1,0:T(8,128)} %w_latent_hbm.1) | copy-start | bytes 393220
  16.0 6.0 %copy-start.2 = (f32[5,512]{1,0:T(8,128)S(1)}, f32[5,512]{1,0:T(8,128)}, u32[]{:S(2)}) copy-start(f32[5,512]{1,0:T(8,128)} %w_out_hbm.1) | copy-start | bytes 30724
  16.0 6.0 %copy-start.3 = (f32[3,512]{1,0:T(4,128)S(1)}, f32[3,512]{1,0:T(4,128)}, u32[]{:S(2)}) copy-start(f32[3,512]{1,0:T(4,128)} %w_pos_hbm.1) | copy-start | bytes 18436
  34.9 1.7 %collective-permute-start.2 = (s16[4,352,128]{2,1,0:T(8,128)(2,1)S(1)}, s16[4,352,128]{2,1,0:T(8,128)(2,1)S(1)}, u32[]{:S(2)}, u32[]{:S(2)}) collective-permute-start(s16[4,352,128]{2,1,0:T(8,128)(2,1)S(1)} %get-tuple-element.36), channel_id=1, source_target_pairs={{0,1},{1,0},{2,3},{3,2},{4,5},{5,4},{6,7},{7,6},{8,9},{9,8},{10,11... | collective-permute-start | bytes 1081352 | tf_op jit(solution)/shard_map/ppermute | solution.py:603
  36.9 4.7 %collective-permute-start.4 = (s16[352,128]{1,0:T(8,128)(2,1)S(1)}, s16[352,128]{1,0:T(8,128)(2,1)S(1)}, u32[]{:S(2)}, u32[]{:S(2)}) collective-permute-start(s16[352,128]{1,0:T(8,128)(2,1)S(1)} %get-tuple-element.40), channel_id=1, source_target_pairs={{0,2},{1,3},{2,0},{3,1},{4,6},{5,7},{6,4},{7,5},{8,10},{9,11},{10,... | collective-permute-start | bytes 270344 | tf_op jit(solution)/shard_map/ppermute | solution.py:603
  37.1 4.6 %collective-permute-start.5 = (s16[352,128]{1,0:T(8,128)(2,1)S(1)}, s16[352,128]{1,0:T(8,128)(2,1)S(1)}, u32[]{:S(2)}, u32[]{:S(2)}) collective-permute-start(s16[352,128]{1,0:T(8,128)(2,1)S(1)} %get-tuple-element.41), channel_id=1, source_target_pairs={{0,16},{1,17},{2,18},{3,19},{4,20},{5,21},{6,22},{7,23},{8,24},{9,... | collective-permute-start | bytes 270344 | tf_op jit(solution)/shard_map/ppermute | solution.py:603
  38.6 6.2 %collective-permute-start.3 = (s16[352,128]{1,0:T(8,128)(2,1)S(1)}, s16[352,128]{1,0:T(8,128)(2,1)S(1)}, u32[]{:S(2)}, u32[]{:S(2)}) collective-permute-start(s16[352,128]{1,0:T(8,128)(2,1)S(1)} %sum_core.2), channel_id=1, source_target_pairs={{0,18},{1,19},{2,16},{3,17},{4,22},{5,23},{6,20},{7,21},{8,26},{9,... | collective-permute-start | bytes 270344 | tf_op jit(solution)/shard_map/ppermute | solution.py:603
  44.9 4.6 %collective-permute-start.6 = (s16[352,128]{1,0:T(8,128)(2,1)S(1)}, s16[352,128]{1,0:T(8,128)(2,1)S(1)}, u32[]{:S(2)}, u32[]{:S(2)}) collective-permute-start(s16[352,128]{1,0:T(8,128)(2,1)S(1)} %sum_plane.1.mine_ref), channel_id=1, source_target_pairs={{0,4},{1,5},{2,6},{3,7},{4,0},{5,1},{6,2},{7,3},{8,12},{9,13},{10,... | collective-permute-start | bytes 270344 | tf_op jit(solution)/shard_map/ppermute | solution.py:603
  49.6 6.2 %collective-permute-start.7 = (s16[352,128]{1,0:T(8,128)(2,1)S(1)}, s16[352,128]{1,0:T(8,128)(2,1)S(1)}, u32[]{:S(2)}, u32[]{:S(2)}) collective-permute-start(s16[352,128]{1,0:T(8,128)(2,1)S(1)} %sum_line.2.mine_ref), channel_id=1, source_target_pairs={{0,8},{1,9},{2,10},{3,11},{4,12},{5,13},{6,14},{7,15},{8,0},{9,1},... | collective-permute-start | bytes 270344 | tf_op jit(solution)/shard_map/ppermute | solution.py:603
  55.9 5.5 %collective-permute-start.10 = (s16[352,128]{1,0:T(8,128)(2,1)S(1)}, s16[352,128]{1,0:T(8,128)(2,1)S(1)}, u32[]{:S(2)}, u32[]{:S(2)}) collective-permute-start(s16[352,128]{1,0:T(8,128)(2,1)S(1)} %sum_line.3.refs_0_), channel_id=1, source_target_pairs={{0,18},{1,19},{2,16},{3,17},{4,22},{5,23},{6,20},{7,21},{8,26},{9,... | collective-permute-start | bytes 270344 | tf_op jit(solution)/shard_map/ppermute | solution.py:603
  57.5 4.5 %collective-permute-start.9 = (s16[352,128]{1,0:T(8,128)(2,1)S(1)}, s16[352,128]{1,0:T(8,128)(2,1)S(1)}, u32[]{:S(2)}, u32[]{:S(2)}) collective-permute-start(s16[352,128]{1,0:T(8,128)(2,1)S(1)} %sum_line.3.refs_0_), channel_id=1, source_target_pairs={{0,16},{1,17},{2,18},{3,19},{4,20},{5,21},{6,22},{7,23},{8,24},{9,... | collective-permute-start | bytes 270344 | tf_op jit(solution)/shard_map/ppermute | solution.py:603
  58.4 4.5 %collective-permute-start.8 = (s16[352,128]{1,0:T(8,128)(2,1)S(1)}, s16[352,128]{1,0:T(8,128)(2,1)S(1)}, u32[]{:S(2)}, u32[]{:S(2)}) collective-permute-start(s16[352,128]{1,0:T(8,128)(2,1)S(1)} %sum_line.3.refs_0_), channel_id=1, source_target_pairs={{0,2},{1,3},{2,0},{3,1},{4,6},{5,7},{6,4},{7,5},{8,10},{9,11},{10,... | collective-permute-start | bytes 270344 | tf_op jit(solution)/shard_map/ppermute | solution.py:603
  59.4 3.5 %collective-permute-start.11 = (s16[352,128]{1,0:T(8,128)(2,1)S(1)}, s16[352,128]{1,0:T(8,128)(2,1)S(1)}, u32[]{:S(2)}, u32[]{:S(2)}) collective-permute-start(s16[352,128]{1,0:T(8,128)(2,1)S(1)} %sum_line.3.refs_0_), channel_id=1, source_target_pairs={{0,1},{1,0},{2,3},{3,2},{4,5},{5,4},{6,7},{7,6},{8,9},{9,8},{10,11... | collective-permute-start | bytes 270344 | tf_op jit(solution)/shard_map/ppermute | solution.py:603
  61.4 1.6 %collective-permute-start.14 = (s16[352,128]{1,0:T(8,128)(2,1)S(1)}, s16[352,128]{1,0:T(8,128)(2,1)S(1)}, u32[]{:S(2)}, u32[]{:S(2)}) collective-permute-start(s16[352,128]{1,0:T(8,128)(2,1)S(1)} %collective-permute-done.10.refs_3_), channel_id=1, source_target_pairs={{0,1},{1,0},{2,3},{3,2},{4,5},{5,4},{6,7},{7,6},{8,9},{9,8},{10,11... | collective-permute-start | bytes 270344 | tf_op jit(solution)/shard_map/ppermute | solution.py:603
  62.0 1.3 %collective-permute-start.13 = (s16[352,128]{1,0:T(8,128)(2,1)S(1)}, s16[352,128]{1,0:T(8,128)(2,1)S(1)}, u32[]{:S(2)}, u32[]{:S(2)}) collective-permute-start(s16[352,128]{1,0:T(8,128)(2,1)S(1)} %collective-permute-done.9.refs_2_), channel_id=1, source_target_pairs={{0,1},{1,0},{2,3},{3,2},{4,5},{5,4},{6,7},{7,6},{8,9},{9,8},{10,11... | collective-permute-start | bytes 270344 | tf_op jit(solution)/shard_map/ppermute | solution.py:603
  62.9 1.3 %collective-permute-start.12 = (s16[352,128]{1,0:T(8,128)(2,1)S(1)}, s16[352,128]{1,0:T(8,128)(2,1)S(1)}, u32[]{:S(2)}, u32[]{:S(2)}) collective-permute-start(s16[352,128]{1,0:T(8,128)(2,1)S(1)} %collective-permute-done.8.refs_1_), channel_id=1, source_target_pairs={{0,1},{1,0},{2,3},{3,2},{4,5},{5,4},{6,7},{7,6},{8,9},{9,8},{10,11... | collective-permute-start | bytes 270344 | tf_op jit(solution)/shard_map/ppermute | solution.py:603

commit v11 on v10

--- a/solution.py
+++ b/solution.py
@@ -133,9 +133,10 @@
 
 
 def conv_kernel(
-    left_ref,
+    place_ref,
+    near_ref,
     here_ref,
-    right_ref,
+    far_ref,
     taps_ref,
     small_ref,
     lat_ref,
@@ -155,34 +156,45 @@
         jnp.int32, (channels, channels), 1
     )
     bias = jnp.sum(jnp.where(diagonal, small_ref[3:4, 0:channels], 0.0), axis=1, keepdims=True)
-    for x in range(planes + 1):
-        taps = []
-        for step in range(3):
-            plane = x + DILATION_RATE * (step - 1)
-            if plane < 0:
-                taps.append((step, left_ref, plane + left_ref.shape[0]))
-            elif plane >= planes:
-                taps.append((step, right_ref, plane - planes))
-            else:
-                taps.append((step, here_ref, plane))
-        for pair in range(rows_y // 2):
-            summed = tap_sum(weight_ref, taps, pair) + bias
-            lat_ref[x * (rows_y // 2) + pair] = jax.nn.gelu(summed).astype(BF16)
-
-
-def convolve(left, here, right, taps, small):
+    def all_planes(left_ref, right_ref):
+        for x in range(planes + 1):
+            taps = []
+            for step in range(3):
+                plane = x + DILATION_RATE * (step - 1)
+                if plane < 0:
+                    taps.append((step, left_ref, plane + left_ref.shape[0]))
+                elif plane >= planes:
+                    taps.append((step, right_ref, plane - planes))
+                else:
+                    taps.append((step, here_ref, plane))
+            for pair in range(rows_y // 2):
+                summed = tap_sum(weight_ref, taps, pair) + bias
+                lat_ref[x * (rows_y // 2) + pair] = jax.nn.gelu(summed).astype(BF16)
+
+    even = (place_ref[1] & 1) == 0
+
+    @pl.when(even)
+    def _():
+        all_planes(far_ref, near_ref)
+
+    @pl.when(jnp.logical_not(even))
+    def _():
+        all_planes(near_ref, far_ref)
+
+
+def convolve(place, near, here, far, taps, small):
     planes, rows_y, channels, rows_z = here.shape
     pairs = (planes + 1) * rows_y // 2
     return pl.pallas_call(
         conv_kernel,
         out_shape=jax.ShapeDtypeStruct((pairs, channels, 2 * rows_z), BF16),
-        in_specs=[VMEM] * 5,
+        in_specs=[SMEM] + [VMEM] * 5,
         out_specs=VMEM,
         scratch_shapes=[pltpu.VMEM((3, 3 * channels, 3 * channels), BF16)],
         compiler_params=pltpu.CompilerParams(vmem_limit_bytes=8 << 20),
         cost_estimate=pl.CostEstimate(flops=3 << 30, bytes_accessed=4 << 20, transcendentals=0),
         name="convolve",
-    )(left, here, right, taps, small)
+    )(place, near, here, far, taps, small)
 
 
 def interpolate(words, lat, planes, rows_y, rows_z):
@@ -827,13 +839,13 @@
     place = jnp.stack([plan.my_block(device), my_tile, my_replica]).astype(jnp.int32)
 
     here = fields[0].transpose(1, 2, 0, 3)
-    up = [(i, (i + 1) % tiles) for i in range(tiles)]
-    down = [((i + 1) % tiles, i) for i in range(tiles)]
-    to_left, to_right, query_owner = lax.optimization_barrier(
-        (here[: DILATION_RATE + 1], here[-DILATION_RATE:], query_owner)
-    )
-    right = lax.ppermute(to_left, "tile", down)
-    left = lax.ppermute(to_right, "tile", up)
+    odd = my_tile & 1
+    count = DILATION_RATE + 1
+    first = lax.dynamic_slice_in_dim(here, (1 - odd) * (here.shape[0] - count), count, axis=0)
+    second = lax.dynamic_slice_in_dim(here, odd * (here.shape[0] - count), count, axis=0)
+    first, second, query_owner = lax.optimization_barrier((first, second, query_owner))
+    near = lax.ppermute(first, "tile", [(i, i ^ 1) for i in range(tiles)])
+    far = lax.ppermute(second, "tile", [(i, (i - 1 + 2 * (i & 1)) % tiles) for i in range(tiles)])
     words, small = route(
         (query_owner[:, :, 0], query_cell, query_frac.transpose(1, 0, 2), target.transpose(1, 0, 2)),
         (bias_one[None], bias_two[None], bias_out[None], convolution_bias[None]),
@@ -844,7 +856,7 @@
         words.reshape(tiles, 8, WORDS), "tile", split_axis=0, concat_axis=0, tiled=True
     ).reshape(tiles * 8, WORDS)
 
-    lat = convolve(left, here, right, convolution_weight, small)
+    lat = convolve(place, near, here, far, convolution_weight, small)
     weights = (w_latent, w_pos, w_mid, w_out)
     send, keep = main(place, lat, words, small, weights, plan)
 

time: 66.3 us -> 65.3 us (0.985)
  starting transfers between devices: 19.2 us -> 17.7 us
  waiting for transfers between devices: 25.7 us -> 24.5 us
  local copies, waits for them, and re-layouts: 1.99 us -> 2.96 us
    all_to_all x1, starting transfers between devices: 5.83 us -> 3.51 us  [body(): lax.all_to_all(words.reshape(tiles, 8, WORDS), 'tile', split_axis=0, conc...]
    another operation x0 -> x1, local copies, waits for them, and re-layouts: none -> 1.24 us
    ppermute x2, waiting for transfers between devices: 0.8 us -> 0.01 us  [the longest x1 0.01 us: body(): near = lax.ppermute(first, 'tile', [(i, i ^ 1) for i in range(tiles)])]
    all_to_all x1, waiting for transfers between devices: 4.09 us -> 3.38 us  [body(): lax.all_to_all(words.reshape(tiles, 8, WORDS), 'tile', split_axis=0, conc...]
    ppermute x2, starting transfers between devices: 5.5 us -> 6.18 us  [the longest x1 5.67 us: body(): lax.ppermute(second, 'tile', [(i, (i - 1 + 2 * (i & 1)) % tiles) for i in...]
    unnamed x27 -> x29, local copies, waits for them, and re-layouts: 1.95 us -> 1.54 us
  transfers between devices with their start and end apart: 16 -> 16, of which waited for: 13 -> 11; matrix products, arithmetic and copies ran while one was open for 0% -> 0% of each run, Pallas kernels for 4% -> 5%
where the time goes in v11:
time: 65.3 us; the launch traced here: 65 us
  waiting for transfers between devices  24.5 us (38%)
  Pallas kernels  18.8 us (29%)
  starting transfers between devices  17.7 us (27%)
  local copies, waits for them, and re-layouts  2.96 us (5%)
  between operations  0.89 us (1%)
    ppermute x13, waiting for transfers between devices, swapped(): lax.ppermute(value, ('replica', 'tile'), [(i, i ^ mask) for i in range(pl...  21.2 us
    pallas_call x1, Pallas kernels, main(): pl.pallas_call(functools.partial(main_kernel, plan), out_shape=(jax.Shape...  12.8 us
    ppermute x13, starting transfers between devices, swapped(): lax.ppermute(value, ('replica', 'tile'), [(i, i ^ mask) for i in range(pl...  8.02 us
    ppermute x1, starting transfers between devices, body(): lax.ppermute(second, 'tile', [(i, (i - 1 + 2 * (i & 1)) % tiles) for i in...  5.67 us
    all_to_all x1, starting transfers between devices, body(): lax.all_to_all(words.reshape(tiles, 8, WORDS), 'tile', split_axis=0, conc...  3.51 us
    all_to_all x1, waiting for transfers between devices, body(): lax.all_to_all(words.reshape(tiles, 8, WORDS), 'tile', split_axis=0, conc...  3.38 us
    pallas_call x1, Pallas kernels, convolve(): pl.pallas_call(conv_kernel, out_shape=jax.ShapeDtypeStruct((pairs, channe...  2.5 us
    pallas_call x1, Pallas kernels, unpack(): pl.pallas_call(functools.partial(unpack_kernel, plan), out_shape=tuple((j...  1.83 us
  transfers between devices with their start and end apart: 16, of which 11 were waited for; matrix products, arithmetic and copies ran while one was open for 0% of the time, Pallas kernels for 5%

profile of v11, /device:TPU:0, one launch (start us, length us, event | category | flops | bytes accessed | tf_op | source)
XLA Modules:
  0.0 65.0 jit_solution(4532102697165644873)
XLA Ops:
  0.6 1.2 %constant_dynamic-slice_fusion = (bf16[1,64,3,8,128]{4,3,2,1,0:T(8,128)(2,1)S(1)}, bf16[1,64,3,8,128]{4,3,2,1,0:T(8,128)(2,1)S(1)}) fusion(bf16[1,64,4,8,128]{4,3,2,1,0:T(8,128)(2,1)} %param.14, s32[]{:T(128)S(6)} %select_n.7, s32[]{:T(128)S(6)} %select_n.6), kind=kLoop, calls=%fused_computation.4 | loop fusion | bytes 1572872 | tf_op jit(solution)/shard_map/dynamic-slice.3
  1.9 0.0 copy-start.6
  1.9 0.0 copy-start.7
  1.9 0.0 copy-start.10
  1.9 0.0 copy-start.11
  1.9 0.0 copy-start.13
  1.9 0.2 copy_bitcast_fusion.1
  2.1 0.5 collective-permute-start
  2.7 5.7 %collective-permute-start.1 = (bf16[3,8,64,128]{3,2,1,0:T(8,128)(2,1)S(1)}, bf16[3,8,64,128]{3,2,1,0:T(8,128)(2,1)S(1)}, u32[]{:S(2)}, u32[]{:S(2)}) collective-permute-start(bf16[3,8,64,128]{3,2,1,0:T(8,128)(2,1)S(1)} %get-tuple-element.31), channel_id=1, source_target_pairs={{0,15},{1,2},{2,1},{3,4},{4,3},{5,6},{6,5},{7,8},{8,7},{9,10},{10,... | collective-permute-start | bytes 1179656 | tf_op jit(solution)/shard_map/ppermute | solution.py:848
  8.4 0.6 copy-done.4
  9.0 0.0 copy-done.5
  9.0 1.1 %route.1 = (f32[128,128]{1,0:T(8,128)}, f32[8,512]{1,0:T(8,128)S(1)}) custom-call(s32[1,128]{1,0:T(1,128)S(1)} %bitcast.36, s32[1,128]{1,0:T(1,128)S(1)} %copy-done.9, f32[3,1,128]{2,1,0:T(1,128)S(1)} %bitcast.35, f32[5,1,128]{2,1,0:T(1,128)S(1)} %bitcast.32, f32[1,512]{1,0:T(1,128)S(1)} %bitcast.33, f32[1,512]{1,0:T(1,128)S(1)} %bitcast.34, ...), custom_call_target="tpu_custom_call" | custom-call | tf_op jit(solution)/shard_map/route/pallas_call | solution.py:98
  10.1 3.5 %all-to-all-start = ((f32[16,8,128]{2,1,0:T(8,128)}), f32[16,8,128]{2,1,0:T(8,128)S(1)}, u32[]{:S(2)}, u32[]{:S(2)}) async-start(f32[16,8,128]{2,1,0:T(8,128)} %bitcast.16), calls=%async_computation | async-start | bytes 131072 | tf_op jit(solution)/shard_map/all_to_all | solution.py:855
  13.6 0.0 copy-start.12
  13.6 0.2 copy.29
  13.9 0.1 pad_add_fusion.place_ref
  13.9 0.0 collective-permute-done.near_ref
  13.9 0.0 collective-permute-done.1.far_ref
  14.0 0.6 copy-done.12
  14.6 2.5 %convolve.1.lat = bf16[20,64,256]{2,1,0:T(8,128)(2,1)S(1)} custom-call(s32[3]{0:T(128)S(1)} %pad_add_fusion.place_ref, bf16[3,8,64,128]{3,2,1,0:T(8,128)(2,1)S(1)} %collective-permute-done.near_ref, bf16[4,8,64,128]{3,2,1,0:T(8,128)(2,1)S(1)} %bitcast.30, bf16[3,8,64,128]{3,2,1,0:T(8,128)(2,1)S(1)} %collective-permute-done.1.far_ref, ...), custom_call_target="tpu_custom_call" | custom-call | flops 3221225472 | bytes 4194304 | tf_op jit(solution)/shard_map/convolve/pallas_call | solution.py:188
  17.1 3.4 %all-to-all-done = f32[16,8,128]{2,1,0:T(8,128)S(1)} async-done(((f32[16,8,128]{2,1,0:T(8,128)}), f32[16,8,128]{2,1,0:T(8,128)S(1)}, u32[]{:S(2)}, u32[]{:S(2)}) %all-to-all-start) | async-done | bytes 65568 | tf_op jit(solution)/shard_map/all_to_all | solution.py:855
  20.5 12.8 %encode_decode.1 = (s16[4,352,128]{2,1,0:T(8,128)(2,1)S(1)}, f32[4,328,128]{2,1,0:T(8,128)S(1)}) custom-call(s32[3]{0:T(128)S(1)} %pad_add_fusion.place_ref, bf16[20,64,256]{2,1,0:T(8,128)(2,1)S(1)} %convolve.1.lat, f32[128,128]{1,0:T(8,128)S(1)} %bitcast.31, f32[8,512]{1,0:T(8,128)S(1)} %get-tuple-element.33.small_ref, f32[64,512]{1,0:T(8,128)S(1)} %copy-done.1, ...), custom_call_target="tpu_custom_call" | custom-call | tf_op jit(solution)/shard_map/encode_decode/pallas_call | solution.py:723
  33.3 0.1 collective-permute-start.2
  33.4 1.7 %collective-permute-done.2.got_ref = s16[4,352,128]{2,1,0:T(8,128)(2,1)S(1)} collective-permute-done((s16[4,352,128]{2,1,0:T(8,128)(2,1)S(1)}, s16[4,352,128]{2,1,0:T(8,128)(2,1)S(1)}, u32[]{:S(2)}, u32[]{:S(2)}) %collective-permute-start.2) | collective-permute-done | bytes 360480 | tf_op jit(solution)/shard_map/ppermute | solution.py:615
  35.1 0.1 sum_core.2
  35.2 0.2 sum_core.3
  35.4 0.2 collective-permute-start.4
  35.5 1.5 %collective-permute-start.5 = (s16[352,128]{1,0:T(8,128)(2,1)S(1)}, s16[352,128]{1,0:T(8,128)(2,1)S(1)}, u32[]{:S(2)}, u32[]{:S(2)}) collective-permute-start(s16[352,128]{1,0:T(8,128)(2,1)S(1)} %get-tuple-element.41), channel_id=1, source_target_pairs={{0,16},{1,17},{2,18},{3,19},{4,20},{5,21},{6,22},{7,23},{8,24},{9,... | collective-permute-start | bytes 270344 | tf_op jit(solution)/shard_map/ppermute | solution.py:615
  37.0 1.9 %collective-permute-start.3 = (s16[352,128]{1,0:T(8,128)(2,1)S(1)}, s16[352,128]{1,0:T(8,128)(2,1)S(1)}, u32[]{:S(2)}, u32[]{:S(2)}) collective-permute-start(s16[352,128]{1,0:T(8,128)(2,1)S(1)} %sum_core.2), channel_id=1, source_target_pairs={{0,18},{1,19},{2,16},{3,17},{4,22},{5,23},{6,20},{7,21},{8,26},{9,... | collective-permute-start | bytes 270344 | tf_op jit(solution)/shard_map/ppermute | solution.py:615
  38.9 1.2 %collective-permute-done.4.refs_1_ = s16[352,128]{1,0:T(8,128)(2,1)S(1)} collective-permute-done((s16[352,128]{1,0:T(8,128)(2,1)S(1)}, s16[352,128]{1,0:T(8,128)(2,1)S(1)}, u32[]{:S(2)}, u32[]{:S(2)}) %collective-permute-start.4) | collective-permute-done | bytes 90144 | tf_op jit(solution)/shard_map/ppermute | solution.py:615
  40.1 0.1 collective-permute-done.5.refs_2_
  40.2 3.1 %collective-permute-done.3.refs_0_ = s16[352,128]{1,0:T(8,128)(2,1)S(1)} collective-permute-done((s16[352,128]{1,0:T(8,128)(2,1)S(1)}, s16[352,128]{1,0:T(8,128)(2,1)S(1)}, u32[]{:S(2)}, u32[]{:S(2)}) %collective-permute-start.3) | collective-permute-done | bytes 90144 | tf_op jit(solution)/shard_map/ppermute | solution.py:615
  43.2 0.1 sum_plane.1.mine_ref
  43.4 0.3 collective-permute-start.6
  43.7 4.3 %collective-permute-done.6.other_ref = s16[352,128]{1,0:T(8,128)(2,1)S(1)} collective-permute-done((s16[352,128]{1,0:T(8,128)(2,1)S(1)}, s16[352,128]{1,0:T(8,128)(2,1)S(1)}, u32[]{:S(2)}, u32[]{:S(2)}) %collective-permute-start.6) | collective-permute-done | bytes 90144 | tf_op jit(solution)/shard_map/ppermute | solution.py:615
  48.0 0.1 sum_line.2.mine_ref
  48.1 0.5 collective-permute-start.7
  48.6 5.6 %collective-permute-done.7.other_ref = s16[352,128]{1,0:T(8,128)(2,1)S(1)} collective-permute-done((s16[352,128]{1,0:T(8,128)(2,1)S(1)}, s16[352,128]{1,0:T(8,128)(2,1)S(1)}, u32[]{:S(2)}, u32[]{:S(2)}) %collective-permute-start.7) | collective-permute-done | bytes 90144 | tf_op jit(solution)/shard_map/ppermute | solution.py:615
  54.2 0.1 sum_line.3.refs_0_
  54.3 1.1 %collective-permute-start.8 = (s16[352,128]{1,0:T(8,128)(2,1)S(1)}, s16[352,128]{1,0:T(8,128)(2,1)S(1)}, u32[]{:S(2)}, u32[]{:S(2)}) collective-permute-start(s16[352,128]{1,0:T(8,128)(2,1)S(1)} %sum_line.3.refs_0_), channel_id=1, source_target_pairs={{0,2},{1,3},{2,0},{3,1},{4,6},{5,7},{6,4},{7,5},{8,10},{9,11},{10,... | collective-permute-start | bytes 270344 | tf_op jit(solution)/shard_map/ppermute | solution.py:615
  55.4 1.1 %collective-permute-start.9 = (s16[352,128]{1,0:T(8,128)(2,1)S(1)}, s16[352,128]{1,0:T(8,128)(2,1)S(1)}, u32[]{:S(2)}, u32[]{:S(2)}) collective-permute-start(s16[352,128]{1,0:T(8,128)(2,1)S(1)} %sum_line.3.refs_0_), channel_id=1, source_target_pairs={{0,16},{1,17},{2,18},{3,19},{4,20},{5,21},{6,22},{7,23},{8,24},{9,... | collective-permute-start | bytes 270344 | tf_op jit(solution)/shard_map/ppermute | solution.py:615
  56.5 1.4 %collective-permute-start.10 = (s16[352,128]{1,0:T(8,128)(2,1)S(1)}, s16[352,128]{1,0:T(8,128)(2,1)S(1)}, u32[]{:S(2)}, u32[]{:S(2)}) collective-permute-start(s16[352,128]{1,0:T(8,128)(2,1)S(1)} %sum_line.3.refs_0_), channel_id=1, source_target_pairs={{0,18},{1,19},{2,16},{3,17},{4,22},{5,23},{6,20},{7,21},{8,26},{9,... | collective-permute-start | bytes 270344 | tf_op jit(solution)/shard_map/ppermute | solution.py:615
  57.9 0.0 collective-permute-start.11
  57.9 1.0 %collective-permute-done.8.refs_1_ = s16[352,128]{1,0:T(8,128)(2,1)S(1)} collective-permute-done((s16[352,128]{1,0:T(8,128)(2,1)S(1)}, s16[352,128]{1,0:T(8,128)(2,1)S(1)}, u32[]{:S(2)}, u32[]{:S(2)}) %collective-permute-start.8) | collective-permute-done | bytes 90144 | tf_op jit(solution)/shard_map/ppermute | solution.py:615
  58.9 1.0 %collective-permute-done.9.refs_2_ = s16[352,128]{1,0:T(8,128)(2,1)S(1)} collective-permute-done((s16[352,128]{1,0:T(8,128)(2,1)S(1)}, s16[352,128]{1,0:T(8,128)(2,1)S(1)}, u32[]{:S(2)}, u32[]{:S(2)}) %collective-permute-start.9) | collective-permute-done | bytes 90144 | tf_op jit(solution)/shard_map/ppermute | solution.py:615
  59.9 2.0 %collective-permute-done.10.refs_3_ = s16[352,128]{1,0:T(8,128)(2,1)S(1)} collective-permute-done((s16[352,128]{1,0:T(8,128)(2,1)S(1)}, s16[352,128]{1,0:T(8,128)(2,1)S(1)}, u32[]{:S(2)}, u32[]{:S(2)}) %collective-permute-start.10) | collective-permute-done | bytes 90144 | tf_op jit(solution)/shard_map/ppermute | solution.py:615
  61.9 1.3 %collective-permute-done.14.refs_7_ = s16[352,128]{1,0:T(8,128)(2,1)S(1)} collective-permute-done((s16[352,128]{1,0:T(8,128)(2,1)S(1)}, s16[352,128]{1,0:T(8,128)(2,1)S(1)}, u32[]{:S(2)}, u32[]{:S(2)}) %collective-permute-start.14) | collective-permute-done | bytes 90144 | tf_op jit(solution)/shard_map/ppermute | solution.py:615
  63.2 1.8 %unpack.1 = (f32[5,1,128]{2,1,0:T(1,128)}, f32[64,512]{1,0:T(8,128)}, f32[3,512]{1,0:T(4,128)}, f32[1,512]{1,0:T(1,128)}, f32[512,512]{1,0:T(8,128)}, /*index=5*...) custom-call(s32[3]{0:T(128)S(1)} %pad_add_fusion.place_ref, ...), custom_call_target="tpu_custom_call" | custom-call | tf_op jit(solution)/shard_map/unpack/pallas_call | solution.py:803
  (25 shorter events, 0.1 us)
Async XLA Ops:
  1.9 6.5 %copy-start.6 = (f32[512]{0:T(512)S(1)}, f32[512]{0:T(512)}, u32[]{:S(2)}) copy-start(f32[512]{0:T(512)} %param.25) | copy-start | bytes 6148
  1.9 6.5 %copy-start.7 = (f32[1,3,128]{2,0,1:T(1,128)S(1)}, f32[1,3,128]{2,0,1:T(1,128)}, u32[]{:S(2)}) copy-start(f32[1,3,128]{2,0,1:T(1,128)} %param.19) | copy-start | bytes 4612
  1.9 6.4 %copy-start.10 = (f32[5]{0:T(128)S(1)}, f32[5]{0:T(128)}, u32[]{:S(2)}) copy-start(f32[5]{0:T(128)} %param.27) | copy-start | bytes 64
  1.9 6.4 %copy-start.11 = (f32[64]{0:T(128)S(1)}, f32[64]{0:T(128)}, u32[]{:S(2)}) copy-start(f32[64]{0:T(128)} %param.16) | copy-start | bytes 772
  1.9 11.7 %copy-start.13 = (bf16[1,64,4,8,128]{4,3,2,1,0:T(8,128)(2,1)S(1)}, bf16[1,64,4,8,128]{4,3,2,1,0:T(8,128)(2,1)}, u32[]{:S(2)}) copy-start(bf16[1,64,4,8,128]{4,3,2,1,0:T(8,128)(2,1)} %param.14) | copy-start | bytes 1572868
  2.1 11.8 %collective-permute-start = (bf16[3,8,64,128]{3,2,1,0:T(8,128)(2,1)S(1)}, bf16[3,8,64,128]{3,2,1,0:T(8,128)(2,1)S(1)}, u32[]{:S(2)}, u32[]{:S(2)}) collective-permute-start(bf16[3,8,64,128]{3,2,1,0:T(8,128)(2,1)S(1)} %get-tuple-element.30), channel_id=1, source_target_pairs={{0,1},{1,0},{2,3},{3,2},{4,5},{5,4},{6,7},{7,6},{8,9},{9,8},{10,11... | collective-permute-start | bytes 1179656 | tf_op jit(solution)/shard_map/ppermute | solution.py:847
  2.7 11.3 %collective-permute-start.1 = (bf16[3,8,64,128]{3,2,1,0:T(8,128)(2,1)S(1)}, bf16[3,8,64,128]{3,2,1,0:T(8,128)(2,1)S(1)}, u32[]{:S(2)}, u32[]{:S(2)}) collective-permute-start(bf16[3,8,64,128]{3,2,1,0:T(8,128)(2,1)S(1)} %get-tuple-element.31), channel_id=1, source_target_pairs={{0,15},{1,2},{2,1},{3,4},{4,3},{5,6},{6,5},{7,8},{8,7},{9,10},{10,... | collective-permute-start | bytes 1179656 | tf_op jit(solution)/shard_map/ppermute | solution.py:848
  8.3 0.7 %copy-start.4 = (f32[1,5,128]{2,0,1:T(1,128)S(1)}, f32[1,5,128]{2,0,1:T(1,128)}, u32[]{:S(2)}) copy-start(f32[1,5,128]{2,0,1:T(1,128)} %param.20) | copy-start | bytes 7684
  8.3 0.7 %copy-start.5 = (f32[512]{0:T(512)S(1)}, f32[512]{0:T(512)}, u32[]{:S(2)}) copy-start(f32[512]{0:T(512)} %param.23) | copy-start | bytes 6148
  8.3 0.7 %copy-start.8 = (s32[1,128,1]{1,2,0:T(1,128)S(1)}, s32[1,128,1]{1,2,0:T(1,128)}, u32[]{:S(2)}) copy-start(s32[1,128,1]{1,2,0:T(1,128)} %param.17) | copy-start | bytes 1540
  8.3 0.7 %copy-start.9 = (s32[1,128]{1,0:T(1,128)S(1)}, s32[1,128]{1,0:T(1,128)}, u32[]{:S(2)}) copy-start(s32[1,128]{1,0:T(1,128)} %refs_1_.1) | copy-start | bytes 1540
  10.1 10.4 %all-to-all-start = ((f32[16,8,128]{2,1,0:T(8,128)}), f32[16,8,128]{2,1,0:T(8,128)S(1)}, u32[]{:S(2)}, u32[]{:S(2)}) async-start(f32[16,8,128]{2,1,0:T(8,128)} %bitcast.16), calls=%async_computation | async-start | bytes 131072 | tf_op jit(solution)/shard_map/all_to_all | solution.py:855
  13.6 0.9 %copy-start.12 = (bf16[64,1728]{1,0:T(8,128)(2,1)S(1)}, bf16[64,1728]{1,0:T(8,128)(2,1)}, u32[]{:S(2)}) copy-start(bf16[64,1728]{1,0:T(8,128)(2,1)} %taps_ref.1) | copy-start | bytes 663556
  14.6 5.9 %copy-start = (f32[512,512]{1,0:T(8,128)S(1)}, f32[512,512]{1,0:T(8,128)}, u32[]{:S(2)}) copy-start(f32[512,512]{1,0:T(8,128)} %w_mid_hbm.1) | copy-start | bytes 3145732
  14.6 5.9 %copy-start.1 = (f32[64,512]{1,0:T(8,128)S(1)}, f32[64,512]{1,0:T(8,128)}, u32[]{:S(2)}) copy-start(f32[64,512]{1,0:T(8,128)} %w_latent_hbm.1) | copy-start | bytes 393220
  14.6 5.9 %copy-start.2 = (f32[5,512]{1,0:T(8,128)S(1)}, f32[5,512]{1,0:T(8,128)}, u32[]{:S(2)}) copy-start(f32[5,512]{1,0:T(8,128)} %w_out_hbm.1) | copy-start | bytes 30724
  14.6 5.9 %copy-start.3 = (f32[3,512]{1,0:T(4,128)S(1)}, f32[3,512]{1,0:T(4,128)}, u32[]{:S(2)}) copy-start(f32[3,512]{1,0:T(4,128)} %w_pos_hbm.1) | copy-start | bytes 18436
  33.3 1.7 %collective-permute-start.2 = (s16[4,352,128]{2,1,0:T(8,128)(2,1)S(1)}, s16[4,352,128]{2,1,0:T(8,128)(2,1)S(1)}, u32[]{:S(2)}, u32[]{:S(2)}) collective-permute-start(s16[4,352,128]{2,1,0:T(8,128)(2,1)S(1)} %get-tuple-element.36), channel_id=1, source_target_pairs={{0,1},{1,0},{2,3},{3,2},{4,5},{5,4},{6,7},{7,6},{8,9},{9,8},{10,11... | collective-permute-start | bytes 1081352 | tf_op jit(solution)/shard_map/ppermute | solution.py:615
  35.4 4.7 %collective-permute-start.4 = (s16[352,128]{1,0:T(8,128)(2,1)S(1)}, s16[352,128]{1,0:T(8,128)(2,1)S(1)}, u32[]{:S(2)}, u32[]{:S(2)}) collective-permute-start(s16[352,128]{1,0:T(8,128)(2,1)S(1)} %get-tuple-element.40), channel_id=1, source_target_pairs={{0,2},{1,3},{2,0},{3,1},{4,6},{5,7},{6,4},{7,5},{8,10},{9,11},{10,... | collective-permute-start | bytes 270344 | tf_op jit(solution)/shard_map/ppermute | solution.py:615
  35.5 4.6 %collective-permute-start.5 = (s16[352,128]{1,0:T(8,128)(2,1)S(1)}, s16[352,128]{1,0:T(8,128)(2,1)S(1)}, u32[]{:S(2)}, u32[]{:S(2)}) collective-permute-start(s16[352,128]{1,0:T(8,128)(2,1)S(1)} %get-tuple-element.41), channel_id=1, source_target_pairs={{0,16},{1,17},{2,18},{3,19},{4,20},{5,21},{6,22},{7,23},{8,24},{9,... | collective-permute-start | bytes 270344 | tf_op jit(solution)/shard_map/ppermute | solution.py:615
  37.0 6.2 %collective-permute-start.3 = (s16[352,128]{1,0:T(8,128)(2,1)S(1)}, s16[352,128]{1,0:T(8,128)(2,1)S(1)}, u32[]{:S(2)}, u32[]{:S(2)}) collective-permute-start(s16[352,128]{1,0:T(8,128)(2,1)S(1)} %sum_core.2), channel_id=1, source_target_pairs={{0,18},{1,19},{2,16},{3,17},{4,22},{5,23},{6,20},{7,21},{8,26},{9,... | collective-permute-start | bytes 270344 | tf_op jit(solution)/shard_map/ppermute | solution.py:615
  43.4 4.6 %collective-permute-start.6 = (s16[352,128]{1,0:T(8,128)(2,1)S(1)}, s16[352,128]{1,0:T(8,128)(2,1)S(1)}, u32[]{:S(2)}, u32[]{:S(2)}) collective-permute-start(s16[352,128]{1,0:T(8,128)(2,1)S(1)} %sum_plane.1.mine_ref), channel_id=1, source_target_pairs={{0,4},{1,5},{2,6},{3,7},{4,0},{5,1},{6,2},{7,3},{8,12},{9,13},{10,... | collective-permute-start | bytes 270344 | tf_op jit(solution)/shard_map/ppermute | solution.py:615
  48.1 6.1 %collective-permute-start.7 = (s16[352,128]{1,0:T(8,128)(2,1)S(1)}, s16[352,128]{1,0:T(8,128)(2,1)S(1)}, u32[]{:S(2)}, u32[]{:S(2)}) collective-permute-start(s16[352,128]{1,0:T(8,128)(2,1)S(1)} %sum_line.2.mine_ref), channel_id=1, source_target_pairs={{0,8},{1,9},{2,10},{3,11},{4,12},{5,13},{6,14},{7,15},{8,0},{9,1},... | collective-permute-start | bytes 270344 | tf_op jit(solution)/shard_map/ppermute | solution.py:615
  54.3 4.6 %collective-permute-start.8 = (s16[352,128]{1,0:T(8,128)(2,1)S(1)}, s16[352,128]{1,0:T(8,128)(2,1)S(1)}, u32[]{:S(2)}, u32[]{:S(2)}) collective-permute-start(s16[352,128]{1,0:T(8,128)(2,1)S(1)} %sum_line.3.refs_0_), channel_id=1, source_target_pairs={{0,2},{1,3},{2,0},{3,1},{4,6},{5,7},{6,4},{7,5},{8,10},{9,11},{10,... | collective-permute-start | bytes 270344 | tf_op jit(solution)/shard_map/ppermute | solution.py:615
  55.4 4.5 %collective-permute-start.9 = (s16[352,128]{1,0:T(8,128)(2,1)S(1)}, s16[352,128]{1,0:T(8,128)(2,1)S(1)}, u32[]{:S(2)}, u32[]{:S(2)}) collective-permute-start(s16[352,128]{1,0:T(8,128)(2,1)S(1)} %sum_line.3.refs_0_), channel_id=1, source_target_pairs={{0,16},{1,17},{2,18},{3,19},{4,20},{5,21},{6,22},{7,23},{8,24},{9,... | collective-permute-start | bytes 270344 | tf_op jit(solution)/shard_map/ppermute | solution.py:615
  56.5 5.4 %collective-permute-start.10 = (s16[352,128]{1,0:T(8,128)(2,1)S(1)}, s16[352,128]{1,0:T(8,128)(2,1)S(1)}, u32[]{:S(2)}, u32[]{:S(2)}) collective-permute-start(s16[352,128]{1,0:T(8,128)(2,1)S(1)} %sum_line.3.refs_0_), channel_id=1, source_target_pairs={{0,18},{1,19},{2,16},{3,17},{4,22},{5,23},{6,20},{7,21},{8,26},{9,... | collective-permute-start | bytes 270344 | tf_op jit(solution)/shard_map/ppermute | solution.py:615
  57.9 4.0 %collective-permute-start.11 = (s16[352,128]{1,0:T(8,128)(2,1)S(1)}, s16[352,128]{1,0:T(8,128)(2,1)S(1)}, u32[]{:S(2)}, u32[]{:S(2)}) collective-permute-start(s16[352,128]{1,0:T(8,128)(2,1)S(1)} %sum_line.3.refs_0_), channel_id=1, source_target_pairs={{0,1},{1,0},{2,3},{3,2},{4,5},{5,4},{6,7},{7,6},{8,9},{9,8},{10,11... | collective-permute-start | bytes 270344 | tf_op jit(solution)/shard_map/ppermute | solution.py:615
  58.9 3.0 %collective-permute-start.12 = (s16[352,128]{1,0:T(8,128)(2,1)S(1)}, s16[352,128]{1,0:T(8,128)(2,1)S(1)}, u32[]{:S(2)}, u32[]{:S(2)}) collective-permute-start(s16[352,128]{1,0:T(8,128)(2,1)S(1)} %collective-permute-done.8.refs_1_), channel_id=1, source_target_pairs={{0,1},{1,0},{2,3},{3,2},{4,5},{5,4},{6,7},{7,6},{8,9},{9,8},{10,11... | collective-permute-start | bytes 270344 | tf_op jit(solution)/shard_map/ppermute | solution.py:615
  59.9 2.0 %collective-permute-start.13 = (s16[352,128]{1,0:T(8,128)(2,1)S(1)}, s16[352,128]{1,0:T(8,128)(2,1)S(1)}, u32[]{:S(2)}, u32[]{:S(2)}) collective-permute-start(s16[352,128]{1,0:T(8,128)(2,1)S(1)} %collective-permute-done.9.refs_2_), channel_id=1, source_target_pairs={{0,1},{1,0},{2,3},{3,2},{4,5},{5,4},{6,7},{7,6},{8,9},{9,8},{10,11... | collective-permute-start | bytes 270344 | tf_op jit(solution)/shard_map/ppermute | solution.py:615
  61.9 1.3 %collective-permute-start.14 = (s16[352,128]{1,0:T(8,128)(2,1)S(1)}, s16[352,128]{1,0:T(8,128)(2,1)S(1)}, u32[]{:S(2)}, u32[]{:S(2)}) collective-permute-start(s16[352,128]{1,0:T(8,128)(2,1)S(1)} %collective-permute-done.10.refs_3_), channel_id=1, source_target_pairs={{0,1},{1,0},{2,3},{3,2},{4,5},{5,4},{6,7},{7,6},{8,9},{9,8},{10,11... | collective-permute-start | bytes 270344 | tf_op jit(solution)/shard_map/ppermute | solution.py:615

commit v12 on v11

--- a/solution.py
+++ b/solution.py
@@ -349,10 +349,9 @@
                 store(refs, at(part, 1 + d, block), slope * w_pos[d])
             store(refs, at(part, 4, block), curve * square)
 
-    def times_mid(dims, source, result, part):
-        span = slice(part * 5 * part_rows, (part + 1) * 5 * part_rows)
-        left = (source[0][span, :], source[1][span, :])
-        result[span, :] = mul3(left, (mid_high[...], mid_low[...]), dims)
+    def times_mid(dims, source, result):
+        left = (source[0][...], source[1][...])
+        result[...] = mul3(left, (mid_high[...], mid_low[...]), dims)
 
     def layer_two(part):
         refs = (two_high, two_low)
@@ -390,9 +389,8 @@
     @pl.when(always)
     def _():
         layer_one(0)
-        times_mid(NN, (one_high, one_low), mixed, 0)
         layer_one(1)
-        times_mid(NN, (one_high, one_low), mixed, 1)
+        times_mid(NN, (one_high, one_low), mixed)
         layer_two(0)
         outputs(0)
         layer_two(1)
@@ -526,11 +524,10 @@
     @pl.when(always)
     def _():
         out_back(0)
+        out_back(1)
         total = second_back(0, jnp.zeros((8, hidden), F32))
-        out_back(1)
-        times_mid(NT, (d_both.at[:, :hidden], d_both.at[:, hidden:]), mixed_back, 0)
         sums_ref[5] = second_back(1, total)
-        times_mid(NT, (d_both.at[:, :hidden], d_both.at[:, hidden:]), mixed_back, 1)
+        times_mid(NT, (d_both.at[:, :hidden], d_both.at[:, hidden:]), mixed_back)
         total = first_back(0, [jnp.zeros((8, hidden), F32)] * 5)
         mid_gradient()
         for number, value in enumerate(first_back(1, total)):
@@ -754,26 +751,36 @@
 
 
 def unpack_kernel(plan, place_ref, *refs):
-    sources, outs, packed = refs[:8], refs[8:-1], refs[-1]
-    prediction_ref, latent_ref, pos_ref, one_ref, mid_ref, two_ref, out_ref, bias_out_ref, loss_ref = outs
+    sources, outs, (packed, mid_part, latent_part, sems) = refs[:8], refs[8:-4], refs[-4:]
+    prediction_ref, latent_hbm, pos_ref, one_ref, mid_hbm, two_ref, out_ref, bias_out_ref, loss_ref = outs
     my_block = place_ref[0]
     device = place_ref[2] * plan.tiles + place_ref[1]
     starts = list(range(0, plan.coded_rows, SUB))
-    for number, ref in enumerate(sources):
-        read = decoder(plan, ref)
-        block = jnp.bitwise_xor(number, my_block)
-        for start in starts:
-            packed[block, start : start + SUB, :] = read(start, SUB)
-        packed[block, plan.coded_rows :, :] = read(plan.coded_rows, 8)
-
-    hidden = mid_ref.shape[0]
-    latents = latent_ref.shape[0]
+    hidden = mid_hbm.shape[0]
     split = plan.main_rows
+    copies = []
+    for half in range(2):
+        for number in range(4):
+            read = decoder(plan, sources[4 * half + number])
+            block = jnp.bitwise_xor(4 * half + number, my_block)
+            for start in starts:
+                packed[block, start : start + SUB, :] = read(start, SUB)
+            packed[block, plan.coded_rows :, :] = read(plan.coded_rows, 8)
+        core = (my_block >> 2) ^ half
+        for part in range(2):
+            lanes = slice(part * LANES, (part + 1) * LANES)
+            upper, lower = packed.at[core * 4 + 2 * part], packed.at[core * 4 + 2 * part + 1]
+            mid_part[half, 0:split, lanes] = upper[0:split, :]
+            mid_part[half, split:, lanes] = lower[0 : hidden - split, :]
+            latent_part[half, :, lanes] = lower[hidden - split : split, :]
+        columns = pl.ds(pl.multiple_of(core * 2 * LANES, 2 * LANES), 2 * LANES)
+        for number, (source, target) in enumerate(((mid_part, mid_hbm), (latent_part, latent_hbm))):
+            copy = pltpu.make_async_copy(source.at[half], target.at[:, columns], sems.at[half, number])
+            copy.start()
+            copies.append(copy)
+
     for part in range(hidden // LANES):
         lanes = slice(part * LANES, (part + 1) * LANES)
-        mid_ref[0:split, lanes] = packed[2 * part, 0:split, :]
-        mid_ref[split:, lanes] = packed[2 * part + 1, 0 : hidden - split, :]
-        latent_ref[:, lanes] = packed[2 * part + 1, hidden - split : split, :]
         misc = packed[2 * part, plan.coded_rows :, :]
         pos_ref[:, lanes] = misc[0:3]
         one_ref[:, lanes] = misc[3:4]
@@ -786,6 +793,8 @@
     fields = packed[device & 7, pl.ds(row, 8), :]
     for f in range(5):
         prediction_ref[f] = fields[f : f + 1]
+    for copy in copies:
+        copy.wait()
 
 
 def unpack(place, blocks, plan, hidden, latents):
@@ -804,8 +813,13 @@
         functools.partial(unpack_kernel, plan),
         out_shape=tuple(jax.ShapeDtypeStruct(shape, F32) for shape in shapes),
         in_specs=[SMEM] + [VMEM] * 8,
-        out_specs=tuple([VMEM] * len(shapes)),
-        scratch_shapes=[pltpu.VMEM((8, plan.rows, LANES), F32)],
+        out_specs=(VMEM, HBM, VMEM, VMEM, HBM, VMEM, VMEM, VMEM, VMEM),
+        scratch_shapes=[
+            pltpu.VMEM((8, plan.rows, LANES), F32),
+            pltpu.VMEM((2, hidden, 2 * LANES), F32),
+            pltpu.VMEM((2, latents, 2 * LANES), F32),
+            pltpu.SemaphoreType.DMA((2, 2)),
+        ],
         compiler_params=pltpu.CompilerParams(vmem_limit_bytes=16 << 20),
         name="unpack",
     )(place, *blocks)

time: 65.3 us -> 66.1 us (1.012)
  no operation moved by 1% of the time
where the time goes in v12:
time: 66.1 us; the launch traced here: 65.8 us
  waiting for transfers between devices  24.6 us (37%)
  Pallas kernels  19.4 us (29%)
  starting transfers between devices  17.7 us (27%)
  local copies, waits for them, and re-layouts  2.96 us (4%)
  between operations  1.05 us (2%)
    ppermute x13, waiting for transfers between devices, swapped(): lax.ppermute(value, ('replica', 'tile'), [(i, i ^ mask) for i in range(pl...  21.2 us
    pallas_call x1, Pallas kernels, main(): pl.pallas_call(functools.partial(main_kernel, plan), out_shape=(jax.Shape...  12.9 us
    ppermute x13, starting transfers between devices, swapped(): lax.ppermute(value, ('replica', 'tile'), [(i, i ^ mask) for i in range(pl...  8 us
    ppermute x1, starting transfers between devices, body(): lax.ppermute(second, 'tile', [(i, (i - 1 + 2 * (i & 1)) % tiles) for i in...  5.67 us
    all_to_all x1, starting transfers between devices, body(): lax.all_to_all(words.reshape(tiles, 8, WORDS), 'tile', split_axis=0, conc...  3.51 us
    all_to_all x1, waiting for transfers between devices, body(): lax.all_to_all(words.reshape(tiles, 8, WORDS), 'tile', split_axis=0, conc...  3.38 us
    pallas_call x1, Pallas kernels, convolve(): pl.pallas_call(conv_kernel, out_shape=jax.ShapeDtypeStruct((pairs, channe...  2.5 us
    pallas_call x1, Pallas kernels, unpack(): pl.pallas_call(functools.partial(unpack_kernel, plan), out_shape=tuple((j...  2.33 us
  transfers between devices with their start and end apart: 16, of which 11 were waited for; matrix products, arithmetic and copies ran while one was open for 0% of the time, Pallas kernels for 5%

profile of v12, /device:TPU:0, one launch (start us, length us, event | category | flops | bytes accessed | tf_op | source)
XLA Modules:
  0.0 65.8 jit_solution(13479909334161382627)
XLA Ops:
  0.6 1.2 %constant_dynamic-slice_fusion = (bf16[1,64,3,8,128]{4,3,2,1,0:T(8,128)(2,1)S(1)}, bf16[1,64,3,8,128]{4,3,2,1,0:T(8,128)(2,1)S(1)}) fusion(bf16[1,64,4,8,128]{4,3,2,1,0:T(8,128)(2,1)} %param.14, s32[]{:T(128)S(6)} %select_n.7, s32[]{:T(128)S(6)} %select_n.6), kind=kLoop, calls=%fused_computation.4 | loop fusion | bytes 1572872 | tf_op jit(solution)/shard_map/dynamic-slice.3
  1.9 0.0 copy-start.6
  1.9 0.0 copy-start.7
  1.9 0.0 copy-start.10
  1.9 0.0 copy-start.11
  1.9 0.0 copy-start.13
  1.9 0.2 copy_bitcast_fusion.1
  2.1 0.5 collective-permute-start
  2.7 5.7 %collective-permute-start.1 = (bf16[3,8,64,128]{3,2,1,0:T(8,128)(2,1)S(1)}, bf16[3,8,64,128]{3,2,1,0:T(8,128)(2,1)S(1)}, u32[]{:S(2)}, u32[]{:S(2)}) collective-permute-start(bf16[3,8,64,128]{3,2,1,0:T(8,128)(2,1)S(1)} %get-tuple-element.31), channel_id=1, source_target_pairs={{0,15},{1,2},{2,1},{3,4},{4,3},{5,6},{6,5},{7,8},{8,7},{9,10},{10,... | collective-permute-start | bytes 1179656 | tf_op jit(solution)/shard_map/ppermute | solution.py:862
  8.4 0.6 copy-done.4
  9.0 0.0 copy-done.5
  9.0 1.1 %route.1 = (f32[128,128]{1,0:T(8,128)}, f32[8,512]{1,0:T(8,128)S(1)}) custom-call(s32[1,128]{1,0:T(1,128)S(1)} %bitcast.36, s32[1,128]{1,0:T(1,128)S(1)} %copy-done.9, f32[3,1,128]{2,1,0:T(1,128)S(1)} %bitcast.35, f32[5,1,128]{2,1,0:T(1,128)S(1)} %bitcast.32, f32[1,512]{1,0:T(1,128)S(1)} %bitcast.33, f32[1,512]{1,0:T(1,128)S(1)} %bitcast.34, ...), custom_call_target="tpu_custom_call" | custom-call | tf_op jit(solution)/shard_map/route/pallas_call | solution.py:98
  10.1 3.5 %all-to-all-start = ((f32[16,8,128]{2,1,0:T(8,128)}), f32[16,8,128]{2,1,0:T(8,128)S(1)}, u32[]{:S(2)}, u32[]{:S(2)}) async-start(f32[16,8,128]{2,1,0:T(8,128)} %bitcast.16), calls=%async_computation | async-start | bytes 131072 | tf_op jit(solution)/shard_map/all_to_all | solution.py:869
  13.6 0.0 copy-start.12
  13.6 0.2 copy.29
  13.9 0.1 pad_add_fusion.place_ref
  13.9 0.0 collective-permute-done.near_ref
  13.9 0.0 collective-permute-done.1.far_ref
  14.0 0.6 copy-done.12
  14.6 2.5 %convolve.1.lat = bf16[20,64,256]{2,1,0:T(8,128)(2,1)S(1)} custom-call(s32[3]{0:T(128)S(1)} %pad_add_fusion.place_ref, bf16[3,8,64,128]{3,2,1,0:T(8,128)(2,1)S(1)} %collective-permute-done.near_ref, bf16[4,8,64,128]{3,2,1,0:T(8,128)(2,1)S(1)} %bitcast.30, bf16[3,8,64,128]{3,2,1,0:T(8,128)(2,1)S(1)} %collective-permute-done.1.far_ref, ...), custom_call_target="tpu_custom_call" | custom-call | flops 3221225472 | bytes 4194304 | tf_op jit(solution)/shard_map/convolve/pallas_call | solution.py:188
  17.1 3.4 %all-to-all-done = f32[16,8,128]{2,1,0:T(8,128)S(1)} async-done(((f32[16,8,128]{2,1,0:T(8,128)}), f32[16,8,128]{2,1,0:T(8,128)S(1)}, u32[]{:S(2)}, u32[]{:S(2)}) %all-to-all-start) | async-done | bytes 65568 | tf_op jit(solution)/shard_map/all_to_all | solution.py:869
  20.5 12.9 %encode_decode.1 = (s16[4,352,128]{2,1,0:T(8,128)(2,1)S(1)}, f32[4,328,128]{2,1,0:T(8,128)S(1)}) custom-call(s32[3]{0:T(128)S(1)} %pad_add_fusion.place_ref, bf16[20,64,256]{2,1,0:T(8,128)(2,1)S(1)} %convolve.1.lat, f32[128,128]{1,0:T(8,128)S(1)} %bitcast.31, f32[8,512]{1,0:T(8,128)S(1)} %get-tuple-element.33.small_ref, f32[64,512]{1,0:T(8,128)S(1)} %copy-done.1, ...), custom_call_target="tpu_custom_call" | custom-call | tf_op jit(solution)/shard_map/encode_decode/pallas_call | solution.py:720
  33.4 0.1 collective-permute-start.2
  33.5 1.7 %collective-permute-done.2.got_ref = s16[4,352,128]{2,1,0:T(8,128)(2,1)S(1)} collective-permute-done((s16[4,352,128]{2,1,0:T(8,128)(2,1)S(1)}, s16[4,352,128]{2,1,0:T(8,128)(2,1)S(1)}, u32[]{:S(2)}, u32[]{:S(2)}) %collective-permute-start.2) | collective-permute-done | bytes 360480 | tf_op jit(solution)/shard_map/ppermute | solution.py:612
  35.2 0.1 sum_core.2
  35.3 0.2 sum_core.3
  35.5 0.2 collective-permute-start.4
  35.6 1.5 %collective-permute-start.5 = (s16[352,128]{1,0:T(8,128)(2,1)S(1)}, s16[352,128]{1,0:T(8,128)(2,1)S(1)}, u32[]{:S(2)}, u32[]{:S(2)}) collective-permute-start(s16[352,128]{1,0:T(8,128)(2,1)S(1)} %get-tuple-element.41), channel_id=1, source_target_pairs={{0,16},{1,17},{2,18},{3,19},{4,20},{5,21},{6,22},{7,23},{8,24},{9,... | collective-permute-start | bytes 270344 | tf_op jit(solution)/shard_map/ppermute | solution.py:612
  37.1 1.9 %collective-permute-start.3 = (s16[352,128]{1,0:T(8,128)(2,1)S(1)}, s16[352,128]{1,0:T(8,128)(2,1)S(1)}, u32[]{:S(2)}, u32[]{:S(2)}) collective-permute-start(s16[352,128]{1,0:T(8,128)(2,1)S(1)} %sum_core.2), channel_id=1, source_target_pairs={{0,18},{1,19},{2,16},{3,17},{4,22},{5,23},{6,20},{7,21},{8,26},{9,... | collective-permute-start | bytes 270344 | tf_op jit(solution)/shard_map/ppermute | solution.py:612
  39.0 1.2 %collective-permute-done.4.refs_1_ = s16[352,128]{1,0:T(8,128)(2,1)S(1)} collective-permute-done((s16[352,128]{1,0:T(8,128)(2,1)S(1)}, s16[352,128]{1,0:T(8,128)(2,1)S(1)}, u32[]{:S(2)}, u32[]{:S(2)}) %collective-permute-start.4) | collective-permute-done | bytes 90144 | tf_op jit(solution)/shard_map/ppermute | solution.py:612
  40.2 0.1 collective-permute-done.5.refs_2_
  40.3 3.1 %collective-permute-done.3.refs_0_ = s16[352,128]{1,0:T(8,128)(2,1)S(1)} collective-permute-done((s16[352,128]{1,0:T(8,128)(2,1)S(1)}, s16[352,128]{1,0:T(8,128)(2,1)S(1)}, u32[]{:S(2)}, u32[]{:S(2)}) %collective-permute-start.3) | collective-permute-done | bytes 90144 | tf_op jit(solution)/shard_map/ppermute | solution.py:612
  43.4 0.1 sum_plane.1.mine_ref
  43.5 0.3 collective-permute-start.6
  43.8 4.3 %collective-permute-done.6.other_ref = s16[352,128]{1,0:T(8,128)(2,1)S(1)} collective-permute-done((s16[352,128]{1,0:T(8,128)(2,1)S(1)}, s16[352,128]{1,0:T(8,128)(2,1)S(1)}, u32[]{:S(2)}, u32[]{:S(2)}) %collective-permute-start.6) | collective-permute-done | bytes 90144 | tf_op jit(solution)/shard_map/ppermute | solution.py:612
  48.1 0.1 sum_line.2.mine_ref
  48.2 0.5 collective-permute-start.7
  48.7 5.6 %collective-permute-done.7.other_ref = s16[352,128]{1,0:T(8,128)(2,1)S(1)} collective-permute-done((s16[352,128]{1,0:T(8,128)(2,1)S(1)}, s16[352,128]{1,0:T(8,128)(2,1)S(1)}, u32[]{:S(2)}, u32[]{:S(2)}) %collective-permute-start.7) | collective-permute-done | bytes 90144 | tf_op jit(solution)/shard_map/ppermute | solution.py:612
  54.3 0.1 sum_line.3.refs_0_
  54.4 1.1 %collective-permute-start.8 = (s16[352,128]{1,0:T(8,128)(2,1)S(1)}, s16[352,128]{1,0:T(8,128)(2,1)S(1)}, u32[]{:S(2)}, u32[]{:S(2)}) collective-permute-start(s16[352,128]{1,0:T(8,128)(2,1)S(1)} %sum_line.3.refs_0_), channel_id=1, source_target_pairs={{0,2},{1,3},{2,0},{3,1},{4,6},{5,7},{6,4},{7,5},{8,10},{9,11},{10,... | collective-permute-start | bytes 270344 | tf_op jit(solution)/shard_map/ppermute | solution.py:612
  55.5 1.1 %collective-permute-start.9 = (s16[352,128]{1,0:T(8,128)(2,1)S(1)}, s16[352,128]{1,0:T(8,128)(2,1)S(1)}, u32[]{:S(2)}, u32[]{:S(2)}) collective-permute-start(s16[352,128]{1,0:T(8,128)(2,1)S(1)} %sum_line.3.refs_0_), channel_id=1, source_target_pairs={{0,16},{1,17},{2,18},{3,19},{4,20},{5,21},{6,22},{7,23},{8,24},{9,... | collective-permute-start | bytes 270344 | tf_op jit(solution)/shard_map/ppermute | solution.py:612
  56.6 1.4 %collective-permute-start.10 = (s16[352,128]{1,0:T(8,128)(2,1)S(1)}, s16[352,128]{1,0:T(8,128)(2,1)S(1)}, u32[]{:S(2)}, u32[]{:S(2)}) collective-permute-start(s16[352,128]{1,0:T(8,128)(2,1)S(1)} %sum_line.3.refs_0_), channel_id=1, source_target_pairs={{0,18},{1,19},{2,16},{3,17},{4,22},{5,23},{6,20},{7,21},{8,26},{9,... | collective-permute-start | bytes 270344 | tf_op jit(solution)/shard_map/ppermute | solution.py:612
  58.0 0.0 collective-permute-start.11
  58.0 1.0 %collective-permute-done.8.refs_1_ = s16[352,128]{1,0:T(8,128)(2,1)S(1)} collective-permute-done((s16[352,128]{1,0:T(8,128)(2,1)S(1)}, s16[352,128]{1,0:T(8,128)(2,1)S(1)}, u32[]{:S(2)}, u32[]{:S(2)}) %collective-permute-start.8) | collective-permute-done | bytes 90144 | tf_op jit(solution)/shard_map/ppermute | solution.py:612
  59.0 1.0 %collective-permute-done.9.refs_2_ = s16[352,128]{1,0:T(8,128)(2,1)S(1)} collective-permute-done((s16[352,128]{1,0:T(8,128)(2,1)S(1)}, s16[352,128]{1,0:T(8,128)(2,1)S(1)}, u32[]{:S(2)}, u32[]{:S(2)}) %collective-permute-start.9) | collective-permute-done | bytes 90144 | tf_op jit(solution)/shard_map/ppermute | solution.py:612
  60.1 2.0 %collective-permute-done.10.refs_3_ = s16[352,128]{1,0:T(8,128)(2,1)S(1)} collective-permute-done((s16[352,128]{1,0:T(8,128)(2,1)S(1)}, s16[352,128]{1,0:T(8,128)(2,1)S(1)}, u32[]{:S(2)}, u32[]{:S(2)}) %collective-permute-start.10) | collective-permute-done | bytes 90144 | tf_op jit(solution)/shard_map/ppermute | solution.py:612
  62.1 1.3 %collective-permute-done.14.refs_7_ = s16[352,128]{1,0:T(8,128)(2,1)S(1)} collective-permute-done((s16[352,128]{1,0:T(8,128)(2,1)S(1)}, s16[352,128]{1,0:T(8,128)(2,1)S(1)}, u32[]{:S(2)}, u32[]{:S(2)}) %collective-permute-start.14) | collective-permute-done | bytes 90144 | tf_op jit(solution)/shard_map/ppermute | solution.py:612
  63.3 2.3 %unpack.1 = (f32[5,1,128]{2,1,0:T(1,128)}, f32[64,512]{1,0:T(8,128)}, f32[3,512]{1,0:T(4,128)}, f32[1,512]{1,0:T(1,128)}, f32[512,512]{1,0:T(8,128)}, /*index=5*...) custom-call(s32[3]{0:T(128)S(1)} %pad_add_fusion.place_ref, ...), custom_call_target="tpu_custom_call" | custom-call | tf_op jit(solution)/shard_map/unpack/pallas_call | solution.py:812
  (25 shorter events, 0.1 us)
Async XLA Ops:
  1.9 6.5 %copy-start.6 = (f32[512]{0:T(512)S(1)}, f32[512]{0:T(512)}, u32[]{:S(2)}) copy-start(f32[512]{0:T(512)} %param.25) | copy-start | bytes 6148
  1.9 6.5 %copy-start.7 = (f32[1,3,128]{2,0,1:T(1,128)S(1)}, f32[1,3,128]{2,0,1:T(1,128)}, u32[]{:S(2)}) copy-start(f32[1,3,128]{2,0,1:T(1,128)} %param.19) | copy-start | bytes 4612
  1.9 6.4 %copy-start.10 = (f32[5]{0:T(128)S(1)}, f32[5]{0:T(128)}, u32[]{:S(2)}) copy-start(f32[5]{0:T(128)} %param.27) | copy-start | bytes 64
  1.9 6.4 %copy-start.11 = (f32[64]{0:T(128)S(1)}, f32[64]{0:T(128)}, u32[]{:S(2)}) copy-start(f32[64]{0:T(128)} %param.16) | copy-start | bytes 772
  1.9 11.7 %copy-start.13 = (bf16[1,64,4,8,128]{4,3,2,1,0:T(8,128)(2,1)S(1)}, bf16[1,64,4,8,128]{4,3,2,1,0:T(8,128)(2,1)}, u32[]{:S(2)}) copy-start(bf16[1,64,4,8,128]{4,3,2,1,0:T(8,128)(2,1)} %param.14) | copy-start | bytes 1572868
  2.1 11.8 %collective-permute-start = (bf16[3,8,64,128]{3,2,1,0:T(8,128)(2,1)S(1)}, bf16[3,8,64,128]{3,2,1,0:T(8,128)(2,1)S(1)}, u32[]{:S(2)}, u32[]{:S(2)}) collective-permute-start(bf16[3,8,64,128]{3,2,1,0:T(8,128)(2,1)S(1)} %get-tuple-element.30), channel_id=1, source_target_pairs={{0,1},{1,0},{2,3},{3,2},{4,5},{5,4},{6,7},{7,6},{8,9},{9,8},{10,11... | collective-permute-start | bytes 1179656 | tf_op jit(solution)/shard_map/ppermute | solution.py:861
  2.7 11.3 %collective-permute-start.1 = (bf16[3,8,64,128]{3,2,1,0:T(8,128)(2,1)S(1)}, bf16[3,8,64,128]{3,2,1,0:T(8,128)(2,1)S(1)}, u32[]{:S(2)}, u32[]{:S(2)}) collective-permute-start(bf16[3,8,64,128]{3,2,1,0:T(8,128)(2,1)S(1)} %get-tuple-element.31), channel_id=1, source_target_pairs={{0,15},{1,2},{2,1},{3,4},{4,3},{5,6},{6,5},{7,8},{8,7},{9,10},{10,... | collective-permute-start | bytes 1179656 | tf_op jit(solution)/shard_map/ppermute | solution.py:862
  8.3 0.7 %copy-start.4 = (f32[1,5,128]{2,0,1:T(1,128)S(1)}, f32[1,5,128]{2,0,1:T(1,128)}, u32[]{:S(2)}) copy-start(f32[1,5,128]{2,0,1:T(1,128)} %param.20) | copy-start | bytes 7684
  8.3 0.7 %copy-start.5 = (f32[512]{0:T(512)S(1)}, f32[512]{0:T(512)}, u32[]{:S(2)}) copy-start(f32[512]{0:T(512)} %param.23) | copy-start | bytes 6148
  8.3 0.7 %copy-start.8 = (s32[1,128,1]{1,2,0:T(1,128)S(1)}, s32[1,128,1]{1,2,0:T(1,128)}, u32[]{:S(2)}) copy-start(s32[1,128,1]{1,2,0:T(1,128)} %param.17) | copy-start | bytes 1540
  8.3 0.7 %copy-start.9 = (s32[1,128]{1,0:T(1,128)S(1)}, s32[1,128]{1,0:T(1,128)}, u32[]{:S(2)}) copy-start(s32[1,128]{1,0:T(1,128)} %refs_1_.1) | copy-start | bytes 1540
  10.1 10.4 %all-to-all-start = ((f32[16,8,128]{2,1,0:T(8,128)}), f32[16,8,128]{2,1,0:T(8,128)S(1)}, u32[]{:S(2)}, u32[]{:S(2)}) async-start(f32[16,8,128]{2,1,0:T(8,128)} %bitcast.16), calls=%async_computation | async-start | bytes 131072 | tf_op jit(solution)/shard_map/all_to_all | solution.py:869
  13.6 0.9 %copy-start.12 = (bf16[64,1728]{1,0:T(8,128)(2,1)S(1)}, bf16[64,1728]{1,0:T(8,128)(2,1)}, u32[]{:S(2)}) copy-start(bf16[64,1728]{1,0:T(8,128)(2,1)} %taps_ref.1) | copy-start | bytes 663556
  14.6 5.9 %copy-start = (f32[512,512]{1,0:T(8,128)S(1)}, f32[512,512]{1,0:T(8,128)}, u32[]{:S(2)}) copy-start(f32[512,512]{1,0:T(8,128)} %w_mid_hbm.1) | copy-start | bytes 3145732
  14.6 5.9 %copy-start.1 = (f32[64,512]{1,0:T(8,128)S(1)}, f32[64,512]{1,0:T(8,128)}, u32[]{:S(2)}) copy-start(f32[64,512]{1,0:T(8,128)} %w_latent_hbm.1) | copy-start | bytes 393220
  14.6 5.9 %copy-start.2 = (f32[5,512]{1,0:T(8,128)S(1)}, f32[5,512]{1,0:T(8,128)}, u32[]{:S(2)}) copy-start(f32[5,512]{1,0:T(8,128)} %w_out_hbm.1) | copy-start | bytes 30724
  14.6 5.9 %copy-start.3 = (f32[3,512]{1,0:T(4,128)S(1)}, f32[3,512]{1,0:T(4,128)}, u32[]{:S(2)}) copy-start(f32[3,512]{1,0:T(4,128)} %w_pos_hbm.1) | copy-start | bytes 18436
  33.4 1.7 %collective-permute-start.2 = (s16[4,352,128]{2,1,0:T(8,128)(2,1)S(1)}, s16[4,352,128]{2,1,0:T(8,128)(2,1)S(1)}, u32[]{:S(2)}, u32[]{:S(2)}) collective-permute-start(s16[4,352,128]{2,1,0:T(8,128)(2,1)S(1)} %get-tuple-element.36), channel_id=1, source_target_pairs={{0,1},{1,0},{2,3},{3,2},{4,5},{5,4},{6,7},{7,6},{8,9},{9,8},{10,11... | collective-permute-start | bytes 1081352 | tf_op jit(solution)/shard_map/ppermute | solution.py:612
  35.5 4.7 %collective-permute-start.4 = (s16[352,128]{1,0:T(8,128)(2,1)S(1)}, s16[352,128]{1,0:T(8,128)(2,1)S(1)}, u32[]{:S(2)}, u32[]{:S(2)}) collective-permute-start(s16[352,128]{1,0:T(8,128)(2,1)S(1)} %get-tuple-element.40), channel_id=1, source_target_pairs={{0,2},{1,3},{2,0},{3,1},{4,6},{5,7},{6,4},{7,5},{8,10},{9,11},{10,... | collective-permute-start | bytes 270344 | tf_op jit(solution)/shard_map/ppermute | solution.py:612
  35.6 4.6 %collective-permute-start.5 = (s16[352,128]{1,0:T(8,128)(2,1)S(1)}, s16[352,128]{1,0:T(8,128)(2,1)S(1)}, u32[]{:S(2)}, u32[]{:S(2)}) collective-permute-start(s16[352,128]{1,0:T(8,128)(2,1)S(1)} %get-tuple-element.41), channel_id=1, source_target_pairs={{0,16},{1,17},{2,18},{3,19},{4,20},{5,21},{6,22},{7,23},{8,24},{9,... | collective-permute-start | bytes 270344 | tf_op jit(solution)/shard_map/ppermute | solution.py:612
  37.1 6.2 %collective-permute-start.3 = (s16[352,128]{1,0:T(8,128)(2,1)S(1)}, s16[352,128]{1,0:T(8,128)(2,1)S(1)}, u32[]{:S(2)}, u32[]{:S(2)}) collective-permute-start(s16[352,128]{1,0:T(8,128)(2,1)S(1)} %sum_core.2), channel_id=1, source_target_pairs={{0,18},{1,19},{2,16},{3,17},{4,22},{5,23},{6,20},{7,21},{8,26},{9,... | collective-permute-start | bytes 270344 | tf_op jit(solution)/shard_map/ppermute | solution.py:612
  43.5 4.6 %collective-permute-start.6 = (s16[352,128]{1,0:T(8,128)(2,1)S(1)}, s16[352,128]{1,0:T(8,128)(2,1)S(1)}, u32[]{:S(2)}, u32[]{:S(2)}) collective-permute-start(s16[352,128]{1,0:T(8,128)(2,1)S(1)} %sum_plane.1.mine_ref), channel_id=1, source_target_pairs={{0,4},{1,5},{2,6},{3,7},{4,0},{5,1},{6,2},{7,3},{8,12},{9,13},{10,... | collective-permute-start | bytes 270344 | tf_op jit(solution)/shard_map/ppermute | solution.py:612
  48.2 6.1 %collective-permute-start.7 = (s16[352,128]{1,0:T(8,128)(2,1)S(1)}, s16[352,128]{1,0:T(8,128)(2,1)S(1)}, u32[]{:S(2)}, u32[]{:S(2)}) collective-permute-start(s16[352,128]{1,0:T(8,128)(2,1)S(1)} %sum_line.2.mine_ref), channel_id=1, source_target_pairs={{0,8},{1,9},{2,10},{3,11},{4,12},{5,13},{6,14},{7,15},{8,0},{9,1},... | collective-permute-start | bytes 270344 | tf_op jit(solution)/shard_map/ppermute | solution.py:612
  54.4 4.6 %collective-permute-start.8 = (s16[352,128]{1,0:T(8,128)(2,1)S(1)}, s16[352,128]{1,0:T(8,128)(2,1)S(1)}, u32[]{:S(2)}, u32[]{:S(2)}) collective-permute-start(s16[352,128]{1,0:T(8,128)(2,1)S(1)} %sum_line.3.refs_0_), channel_id=1, source_target_pairs={{0,2},{1,3},{2,0},{3,1},{4,6},{5,7},{6,4},{7,5},{8,10},{9,11},{10,... | collective-permute-start | bytes 270344 | tf_op jit(solution)/shard_map/ppermute | solution.py:612
  55.5 4.5 %collective-permute-start.9 = (s16[352,128]{1,0:T(8,128)(2,1)S(1)}, s16[352,128]{1,0:T(8,128)(2,1)S(1)}, u32[]{:S(2)}, u32[]{:S(2)}) collective-permute-start(s16[352,128]{1,0:T(8,128)(2,1)S(1)} %sum_line.3.refs_0_), channel_id=1, source_target_pairs={{0,16},{1,17},{2,18},{3,19},{4,20},{5,21},{6,22},{7,23},{8,24},{9,... | collective-permute-start | bytes 270344 | tf_op jit(solution)/shard_map/ppermute | solution.py:612
  56.6 5.4 %collective-permute-start.10 = (s16[352,128]{1,0:T(8,128)(2,1)S(1)}, s16[352,128]{1,0:T(8,128)(2,1)S(1)}, u32[]{:S(2)}, u32[]{:S(2)}) collective-permute-start(s16[352,128]{1,0:T(8,128)(2,1)S(1)} %sum_line.3.refs_0_), channel_id=1, source_target_pairs={{0,18},{1,19},{2,16},{3,17},{4,22},{5,23},{6,20},{7,21},{8,26},{9,... | collective-permute-start | bytes 270344 | tf_op jit(solution)/shard_map/ppermute | solution.py:612
  58.0 4.0 %collective-permute-start.11 = (s16[352,128]{1,0:T(8,128)(2,1)S(1)}, s16[352,128]{1,0:T(8,128)(2,1)S(1)}, u32[]{:S(2)}, u32[]{:S(2)}) collective-permute-start(s16[352,128]{1,0:T(8,128)(2,1)S(1)} %sum_line.3.refs_0_), channel_id=1, source_target_pairs={{0,1},{1,0},{2,3},{3,2},{4,5},{5,4},{6,7},{7,6},{8,9},{9,8},{10,11... | collective-permute-start | bytes 270344 | tf_op jit(solution)/shard_map/ppermute | solution.py:612
  59.0 3.0 %collective-permute-start.12 = (s16[352,128]{1,0:T(8,128)(2,1)S(1)}, s16[352,128]{1,0:T(8,128)(2,1)S(1)}, u32[]{:S(2)}, u32[]{:S(2)}) collective-permute-start(s16[352,128]{1,0:T(8,128)(2,1)S(1)} %collective-permute-done.8.refs_1_), channel_id=1, source_target_pairs={{0,1},{1,0},{2,3},{3,2},{4,5},{5,4},{6,7},{7,6},{8,9},{9,8},{10,11... | collective-permute-start | bytes 270344 | tf_op jit(solution)/shard_map/ppermute | solution.py:612
  60.1 2.0 %collective-permute-start.13 = (s16[352,128]{1,0:T(8,128)(2,1)S(1)}, s16[352,128]{1,0:T(8,128)(2,1)S(1)}, u32[]{:S(2)}, u32[]{:S(2)}) collective-permute-start(s16[352,128]{1,0:T(8,128)(2,1)S(1)} %collective-permute-done.9.refs_2_), channel_id=1, source_target_pairs={{0,1},{1,0},{2,3},{3,2},{4,5},{5,4},{6,7},{7,6},{8,9},{9,8},{10,11... | collective-permute-start | bytes 270344 | tf_op jit(solution)/shard_map/ppermute | solution.py:612
  62.0 1.3 %collective-permute-start.14 = (s16[352,128]{1,0:T(8,128)(2,1)S(1)}, s16[352,128]{1,0:T(8,128)(2,1)S(1)}, u32[]{:S(2)}, u32[]{:S(2)}) collective-permute-start(s16[352,128]{1,0:T(8,128)(2,1)S(1)} %collective-permute-done.10.refs_3_), channel_id=1, source_target_pairs={{0,1},{1,0},{2,3},{3,2},{4,5},{5,4},{6,7},{7,6},{8,9},{9,8},{10,11... | collective-permute-start | bytes 270344 | tf_op jit(solution)/shard_map/ppermute | solution.py:612

commit v13 on v11

--- a/solution.py
+++ b/solution.py
@@ -866,8 +866,10 @@
     mine, *near = first_sum(keep, got, (0, 1, 2), plan)
     arrived = [swapped(block, plan, plan.plane, step) for step, block in ((3, far), (1, near[0]), (2, near[1]))]
     block = coded_sum(plane_kernel, [mine] + arrived, plan, "sum_plane")
-    for bit in plan.rest:
-        block = coded_sum(pair_kernel, [block, swapped(block, plan, [bit], 1)], plan, "sum_line")
+    for bits in zip(plan.rest, reversed(plan.rest)):
+        pairs = [(i, i ^ (1 << bits[i & 1])) for i in range(plan.devices)]
+        other = lax.ppermute(block, ("replica", "tile"), pairs)
+        block = coded_sum(pair_kernel, [block, other], plan, "sum_line")
     blocks = [block] + [swapped(block, plan, plan.plane, step) for step in range(1, 4)]
     blocks = blocks + [swapped(block, plan, plan.core, 1) for block in blocks]
     prediction, g_latent, g_pos, g_one, g_mid, g_two, g_out, g_bias, loss = unpack(

time: 65.3 us -> 65.3 us (level)
    ppermute x0 -> x2, waiting for transfers between devices: none -> 10.3 us  [body(): other = lax.ppermute(block, ('replica', 'tile'), pairs)]
    ppermute x13 -> x11, waiting for transfers between devices: 21.2 us -> 11.3 us  [swapped(): lax.ppermute(value, ('replica', 'tile'), [(i, i ^ mask) for i in range(pl...]
    ppermute x13 -> x11, starting transfers between devices: 8.02 us -> 7.19 us  [swapped(): lax.ppermute(value, ('replica', 'tile'), [(i, i ^ mask) for i in range(pl...]
where the time goes in v13:
time: 65.3 us; the launch traced here: 65 us
  waiting for transfers between devices  25 us (38%)
  Pallas kernels  18.8 us (29%)
  starting transfers between devices  17.3 us (26%)
  local copies, waits for them, and re-layouts  2.96 us (5%)
  between operations  0.9 us (1%)
    pallas_call x1, Pallas kernels, main(): pl.pallas_call(functools.partial(main_kernel, plan), out_shape=(jax.Shape...  12.8 us
    ppermute x11, waiting for transfers between devices, swapped(): lax.ppermute(value, ('replica', 'tile'), [(i, i ^ mask) for i in range(pl...  11.3 us
    ppermute x2, waiting for transfers between devices, body(): other = lax.ppermute(block, ('replica', 'tile'), pairs)  10.3 us
    ppermute x11, starting transfers between devices, swapped(): lax.ppermute(value, ('replica', 'tile'), [(i, i ^ mask) for i in range(pl...  7.19 us
    ppermute x1, starting transfers between devices, body(): lax.ppermute(second, 'tile', [(i, (i - 1 + 2 * (i & 1)) % tiles) for i in...  5.67 us
    all_to_all x1, starting transfers between devices, body(): lax.all_to_all(words.reshape(tiles, 8, WORDS), 'tile', split_axis=0, conc...  3.51 us
    all_to_all x1, waiting for transfers between devices, body(): lax.all_to_all(words.reshape(tiles, 8, WORDS), 'tile', split_axis=0, conc...  3.38 us
    pallas_call x1, Pallas kernels, convolve(): pl.pallas_call(conv_kernel, out_shape=jax.ShapeDtypeStruct((pairs, channe...  2.5 us
  transfers between devices with their start and end apart: 16, of which 11 were waited for; matrix products, arithmetic and copies ran while one was open for 0% of the time, Pallas kernels for 5%

profile of v13, /device:TPU:0, one launch (start us, length us, event | category | flops | bytes accessed | tf_op | source)
XLA Modules:
  0.0 65.0 jit_solution(8897682710552346513)
XLA Ops:
  0.6 1.2 %constant_dynamic-slice_fusion = (bf16[1,64,3,8,128]{4,3,2,1,0:T(8,128)(2,1)S(1)}, bf16[1,64,3,8,128]{4,3,2,1,0:T(8,128)(2,1)S(1)}) fusion(bf16[1,64,4,8,128]{4,3,2,1,0:T(8,128)(2,1)} %param.14, s32[]{:T(128)S(6)} %select_n.7, s32[]{:T(128)S(6)} %select_n.6), kind=kLoop, calls=%fused_computation.4 | loop fusion | bytes 1572872 | tf_op jit(solution)/shard_map/dynamic-slice.3
  1.9 0.0 copy-start.6
  1.9 0.0 copy-start.7
  1.9 0.0 copy-start.10
  1.9 0.0 copy-start.11
  1.9 0.0 copy-start.13
  1.9 0.2 copy_bitcast_fusion.1
  2.1 0.5 collective-permute-start
  2.7 5.7 %collective-permute-start.1 = (bf16[3,8,64,128]{3,2,1,0:T(8,128)(2,1)S(1)}, bf16[3,8,64,128]{3,2,1,0:T(8,128)(2,1)S(1)}, u32[]{:S(2)}, u32[]{:S(2)}) collective-permute-start(bf16[3,8,64,128]{3,2,1,0:T(8,128)(2,1)S(1)} %get-tuple-element.31), channel_id=1, source_target_pairs={{0,15},{1,2},{2,1},{3,4},{4,3},{5,6},{6,5},{7,8},{8,7},{9,10},{10,... | collective-permute-start | bytes 1179656 | tf_op jit(solution)/shard_map/ppermute | solution.py:848
  8.4 0.6 copy-done.4
  9.0 0.0 copy-done.5
  9.0 1.1 %route.1 = (f32[128,128]{1,0:T(8,128)}, f32[8,512]{1,0:T(8,128)S(1)}) custom-call(s32[1,128]{1,0:T(1,128)S(1)} %bitcast.36, s32[1,128]{1,0:T(1,128)S(1)} %copy-done.9, f32[3,1,128]{2,1,0:T(1,128)S(1)} %bitcast.35, f32[5,1,128]{2,1,0:T(1,128)S(1)} %bitcast.32, f32[1,512]{1,0:T(1,128)S(1)} %bitcast.33, f32[1,512]{1,0:T(1,128)S(1)} %bitcast.34, ...), custom_call_target="tpu_custom_call" | custom-call | tf_op jit(solution)/shard_map/route/pallas_call | solution.py:98
  10.1 3.5 %all-to-all-start = ((f32[16,8,128]{2,1,0:T(8,128)}), f32[16,8,128]{2,1,0:T(8,128)S(1)}, u32[]{:S(2)}, u32[]{:S(2)}) async-start(f32[16,8,128]{2,1,0:T(8,128)} %bitcast.16), calls=%async_computation | async-start | bytes 131072 | tf_op jit(solution)/shard_map/all_to_all | solution.py:855
  13.6 0.0 copy-start.12
  13.6 0.2 copy.29
  13.9 0.1 pad_add_fusion.place_ref
  13.9 0.0 collective-permute-done.near_ref
  13.9 0.0 collective-permute-done.1.far_ref
  14.0 0.6 copy-done.12
  14.6 2.5 %convolve.1.lat = bf16[20,64,256]{2,1,0:T(8,128)(2,1)S(1)} custom-call(s32[3]{0:T(128)S(1)} %pad_add_fusion.place_ref, bf16[3,8,64,128]{3,2,1,0:T(8,128)(2,1)S(1)} %collective-permute-done.near_ref, bf16[4,8,64,128]{3,2,1,0:T(8,128)(2,1)S(1)} %bitcast.30, bf16[3,8,64,128]{3,2,1,0:T(8,128)(2,1)S(1)} %collective-permute-done.1.far_ref, ...), custom_call_target="tpu_custom_call" | custom-call | flops 3221225472 | bytes 4194304 | tf_op jit(solution)/shard_map/convolve/pallas_call | solution.py:188
  17.1 3.4 %all-to-all-done = f32[16,8,128]{2,1,0:T(8,128)S(1)} async-done(((f32[16,8,128]{2,1,0:T(8,128)}), f32[16,8,128]{2,1,0:T(8,128)S(1)}, u32[]{:S(2)}, u32[]{:S(2)}) %all-to-all-start) | async-done | bytes 65568 | tf_op jit(solution)/shard_map/all_to_all | solution.py:855
  20.5 12.8 %encode_decode.1 = (s16[4,352,128]{2,1,0:T(8,128)(2,1)S(1)}, f32[4,328,128]{2,1,0:T(8,128)S(1)}) custom-call(s32[3]{0:T(128)S(1)} %pad_add_fusion.place_ref, bf16[20,64,256]{2,1,0:T(8,128)(2,1)S(1)} %convolve.1.lat, f32[128,128]{1,0:T(8,128)S(1)} %bitcast.31, f32[8,512]{1,0:T(8,128)S(1)} %get-tuple-element.33.small_ref, f32[64,512]{1,0:T(8,128)S(1)} %copy-done.1, ...), custom_call_target="tpu_custom_call" | custom-call | tf_op jit(solution)/shard_map/encode_decode/pallas_call | solution.py:723
  33.3 0.1 collective-permute-start.2
  33.4 1.7 %collective-permute-done.2.got_ref = s16[4,352,128]{2,1,0:T(8,128)(2,1)S(1)} collective-permute-done((s16[4,352,128]{2,1,0:T(8,128)(2,1)S(1)}, s16[4,352,128]{2,1,0:T(8,128)(2,1)S(1)}, u32[]{:S(2)}, u32[]{:S(2)}) %collective-permute-start.2) | collective-permute-done | bytes 360480 | tf_op jit(solution)/shard_map/ppermute | solution.py:615
  35.1 0.1 sum_core.2
  35.2 0.2 sum_core.3
  35.4 0.2 collective-permute-start.4
  35.5 1.5 %collective-permute-start.5 = (s16[352,128]{1,0:T(8,128)(2,1)S(1)}, s16[352,128]{1,0:T(8,128)(2,1)S(1)}, u32[]{:S(2)}, u32[]{:S(2)}) collective-permute-start(s16[352,128]{1,0:T(8,128)(2,1)S(1)} %get-tuple-element.41), channel_id=1, source_target_pairs={{0,16},{1,17},{2,18},{3,19},{4,20},{5,21},{6,22},{7,23},{8,24},{9,... | collective-permute-start | bytes 270344 | tf_op jit(solution)/shard_map/ppermute | solution.py:615
  37.0 1.9 %collective-permute-start.3 = (s16[352,128]{1,0:T(8,128)(2,1)S(1)}, s16[352,128]{1,0:T(8,128)(2,1)S(1)}, u32[]{:S(2)}, u32[]{:S(2)}) collective-permute-start(s16[352,128]{1,0:T(8,128)(2,1)S(1)} %sum_core.2), channel_id=1, source_target_pairs={{0,18},{1,19},{2,16},{3,17},{4,22},{5,23},{6,20},{7,21},{8,26},{9,... | collective-permute-start | bytes 270344 | tf_op jit(solution)/shard_map/ppermute | solution.py:615
  38.9 1.2 %collective-permute-done.4.refs_1_ = s16[352,128]{1,0:T(8,128)(2,1)S(1)} collective-permute-done((s16[352,128]{1,0:T(8,128)(2,1)S(1)}, s16[352,128]{1,0:T(8,128)(2,1)S(1)}, u32[]{:S(2)}, u32[]{:S(2)}) %collective-permute-start.4) | collective-permute-done | bytes 90144 | tf_op jit(solution)/shard_map/ppermute | solution.py:615
  40.1 0.1 collective-permute-done.5.refs_2_
  40.2 3.1 %collective-permute-done.3.refs_0_ = s16[352,128]{1,0:T(8,128)(2,1)S(1)} collective-permute-done((s16[352,128]{1,0:T(8,128)(2,1)S(1)}, s16[352,128]{1,0:T(8,128)(2,1)S(1)}, u32[]{:S(2)}, u32[]{:S(2)}) %collective-permute-start.3) | collective-permute-done | bytes 90144 | tf_op jit(solution)/shard_map/ppermute | solution.py:615
  43.2 0.1 sum_plane.1.mine_ref
  43.4 0.3 collective-permute-start.6
  43.7 4.9 %collective-permute-done.6.other_ref = s16[352,128]{1,0:T(8,128)(2,1)S(1)} collective-permute-done((s16[352,128]{1,0:T(8,128)(2,1)S(1)}, s16[352,128]{1,0:T(8,128)(2,1)S(1)}, u32[]{:S(2)}, u32[]{:S(2)}) %collective-permute-start.6) | collective-permute-done | bytes 90144 | tf_op jit(solution)/shard_map/ppermute | solution.py:871
  48.6 0.1 sum_line.2.mine_ref
  48.7 0.1 collective-permute-start.7
  48.7 5.5 %collective-permute-done.7.other_ref = s16[352,128]{1,0:T(8,128)(2,1)S(1)} collective-permute-done((s16[352,128]{1,0:T(8,128)(2,1)S(1)}, s16[352,128]{1,0:T(8,128)(2,1)S(1)}, u32[]{:S(2)}, u32[]{:S(2)}) %collective-permute-start.7) | collective-permute-done | bytes 90144 | tf_op jit(solution)/shard_map/ppermute | solution.py:871
  54.2 0.1 sum_line.3.refs_0_
  54.3 1.1 %collective-permute-start.8 = (s16[352,128]{1,0:T(8,128)(2,1)S(1)}, s16[352,128]{1,0:T(8,128)(2,1)S(1)}, u32[]{:S(2)}, u32[]{:S(2)}) collective-permute-start(s16[352,128]{1,0:T(8,128)(2,1)S(1)} %sum_line.3.refs_0_), channel_id=1, source_target_pairs={{0,2},{1,3},{2,0},{3,1},{4,6},{5,7},{6,4},{7,5},{8,10},{9,11},{10,... | collective-permute-start | bytes 270344 | tf_op jit(solution)/shard_map/ppermute | solution.py:615
  55.4 1.1 %collective-permute-start.9 = (s16[352,128]{1,0:T(8,128)(2,1)S(1)}, s16[352,128]{1,0:T(8,128)(2,1)S(1)}, u32[]{:S(2)}, u32[]{:S(2)}) collective-permute-start(s16[352,128]{1,0:T(8,128)(2,1)S(1)} %sum_line.3.refs_0_), channel_id=1, source_target_pairs={{0,16},{1,17},{2,18},{3,19},{4,20},{5,21},{6,22},{7,23},{8,24},{9,... | collective-permute-start | bytes 270344 | tf_op jit(solution)/shard_map/ppermute | solution.py:615
  56.5 1.4 %collective-permute-start.10 = (s16[352,128]{1,0:T(8,128)(2,1)S(1)}, s16[352,128]{1,0:T(8,128)(2,1)S(1)}, u32[]{:S(2)}, u32[]{:S(2)}) collective-permute-start(s16[352,128]{1,0:T(8,128)(2,1)S(1)} %sum_line.3.refs_0_), channel_id=1, source_target_pairs={{0,18},{1,19},{2,16},{3,17},{4,22},{5,23},{6,20},{7,21},{8,26},{9,... | collective-permute-start | bytes 270344 | tf_op jit(solution)/shard_map/ppermute | solution.py:615
  57.9 0.0 collective-permute-start.11
  57.9 1.0 %collective-permute-done.8.refs_1_ = s16[352,128]{1,0:T(8,128)(2,1)S(1)} collective-permute-done((s16[352,128]{1,0:T(8,128)(2,1)S(1)}, s16[352,128]{1,0:T(8,128)(2,1)S(1)}, u32[]{:S(2)}, u32[]{:S(2)}) %collective-permute-start.8) | collective-permute-done | bytes 90144 | tf_op jit(solution)/shard_map/ppermute | solution.py:615
  58.9 1.0 %collective-permute-done.9.refs_2_ = s16[352,128]{1,0:T(8,128)(2,1)S(1)} collective-permute-done((s16[352,128]{1,0:T(8,128)(2,1)S(1)}, s16[352,128]{1,0:T(8,128)(2,1)S(1)}, u32[]{:S(2)}, u32[]{:S(2)}) %collective-permute-start.9) | collective-permute-done | bytes 90144 | tf_op jit(solution)/shard_map/ppermute | solution.py:615
  59.9 2.0 %collective-permute-done.10.refs_3_ = s16[352,128]{1,0:T(8,128)(2,1)S(1)} collective-permute-done((s16[352,128]{1,0:T(8,128)(2,1)S(1)}, s16[352,128]{1,0:T(8,128)(2,1)S(1)}, u32[]{:S(2)}, u32[]{:S(2)}) %collective-permute-start.10) | collective-permute-done | bytes 90144 | tf_op jit(solution)/shard_map/ppermute | solution.py:615
  61.9 1.3 %collective-permute-done.14.refs_7_ = s16[352,128]{1,0:T(8,128)(2,1)S(1)} collective-permute-done((s16[352,128]{1,0:T(8,128)(2,1)S(1)}, s16[352,128]{1,0:T(8,128)(2,1)S(1)}, u32[]{:S(2)}, u32[]{:S(2)}) %collective-permute-start.14) | collective-permute-done | bytes 90144 | tf_op jit(solution)/shard_map/ppermute | solution.py:615
  63.2 1.8 %unpack.1 = (f32[5,1,128]{2,1,0:T(1,128)}, f32[64,512]{1,0:T(8,128)}, f32[3,512]{1,0:T(4,128)}, f32[1,512]{1,0:T(1,128)}, f32[512,512]{1,0:T(8,128)}, /*index=5*...) custom-call(s32[3]{0:T(128)S(1)} %pad_add_fusion.place_ref, ...), custom_call_target="tpu_custom_call" | custom-call | tf_op jit(solution)/shard_map/unpack/pallas_call | solution.py:803
  (25 shorter events, 0.1 us)
Async XLA Ops:
  1.9 6.5 %copy-start.6 = (f32[512]{0:T(512)S(1)}, f32[512]{0:T(512)}, u32[]{:S(2)}) copy-start(f32[512]{0:T(512)} %param.25) | copy-start | bytes 6148
  1.9 6.5 %copy-start.7 = (f32[1,3,128]{2,0,1:T(1,128)S(1)}, f32[1,3,128]{2,0,1:T(1,128)}, u32[]{:S(2)}) copy-start(f32[1,3,128]{2,0,1:T(1,128)} %param.19) | copy-start | bytes 4612
  1.9 6.4 %copy-start.10 = (f32[5]{0:T(128)S(1)}, f32[5]{0:T(128)}, u32[]{:S(2)}) copy-start(f32[5]{0:T(128)} %param.27) | copy-start | bytes 64
  1.9 6.4 %copy-start.11 = (f32[64]{0:T(128)S(1)}, f32[64]{0:T(128)}, u32[]{:S(2)}) copy-start(f32[64]{0:T(128)} %param.16) | copy-start | bytes 772
  1.9 11.7 %copy-start.13 = (bf16[1,64,4,8,128]{4,3,2,1,0:T(8,128)(2,1)S(1)}, bf16[1,64,4,8,128]{4,3,2,1,0:T(8,128)(2,1)}, u32[]{:S(2)}) copy-start(bf16[1,64,4,8,128]{4,3,2,1,0:T(8,128)(2,1)} %param.14) | copy-start | bytes 1572868
  2.1 11.8 %collective-permute-start = (bf16[3,8,64,128]{3,2,1,0:T(8,128)(2,1)S(1)}, bf16[3,8,64,128]{3,2,1,0:T(8,128)(2,1)S(1)}, u32[]{:S(2)}, u32[]{:S(2)}) collective-permute-start(bf16[3,8,64,128]{3,2,1,0:T(8,128)(2,1)S(1)} %get-tuple-element.30), channel_id=1, source_target_pairs={{0,1},{1,0},{2,3},{3,2},{4,5},{5,4},{6,7},{7,6},{8,9},{9,8},{10,11... | collective-permute-start | bytes 1179656 | tf_op jit(solution)/shard_map/ppermute | solution.py:847
  2.7 11.3 %collective-permute-start.1 = (bf16[3,8,64,128]{3,2,1,0:T(8,128)(2,1)S(1)}, bf16[3,8,64,128]{3,2,1,0:T(8,128)(2,1)S(1)}, u32[]{:S(2)}, u32[]{:S(2)}) collective-permute-start(bf16[3,8,64,128]{3,2,1,0:T(8,128)(2,1)S(1)} %get-tuple-element.31), channel_id=1, source_target_pairs={{0,15},{1,2},{2,1},{3,4},{4,3},{5,6},{6,5},{7,8},{8,7},{9,10},{10,... | collective-permute-start | bytes 1179656 | tf_op jit(solution)/shard_map/ppermute | solution.py:848
  8.3 0.7 %copy-start.4 = (f32[1,5,128]{2,0,1:T(1,128)S(1)}, f32[1,5,128]{2,0,1:T(1,128)}, u32[]{:S(2)}) copy-start(f32[1,5,128]{2,0,1:T(1,128)} %param.20) | copy-start | bytes 7684
  8.3 0.7 %copy-start.5 = (f32[512]{0:T(512)S(1)}, f32[512]{0:T(512)}, u32[]{:S(2)}) copy-start(f32[512]{0:T(512)} %param.23) | copy-start | bytes 6148
  8.3 0.7 %copy-start.8 = (s32[1,128,1]{1,2,0:T(1,128)S(1)}, s32[1,128,1]{1,2,0:T(1,128)}, u32[]{:S(2)}) copy-start(s32[1,128,1]{1,2,0:T(1,128)} %param.17) | copy-start | bytes 1540
  8.3 0.7 %copy-start.9 = (s32[1,128]{1,0:T(1,128)S(1)}, s32[1,128]{1,0:T(1,128)}, u32[]{:S(2)}) copy-start(s32[1,128]{1,0:T(1,128)} %refs_1_.1) | copy-start | bytes 1540
  10.1 10.4 %all-to-all-start = ((f32[16,8,128]{2,1,0:T(8,128)}), f32[16,8,128]{2,1,0:T(8,128)S(1)}, u32[]{:S(2)}, u32[]{:S(2)}) async-start(f32[16,8,128]{2,1,0:T(8,128)} %bitcast.16), calls=%async_computation | async-start | bytes 131072 | tf_op jit(solution)/shard_map/all_to_all | solution.py:855
  13.6 0.9 %copy-start.12 = (bf16[64,1728]{1,0:T(8,128)(2,1)S(1)}, bf16[64,1728]{1,0:T(8,128)(2,1)}, u32[]{:S(2)}) copy-start(bf16[64,1728]{1,0:T(8,128)(2,1)} %taps_ref.1) | copy-start | bytes 663556
  14.6 5.9 %copy-start = (f32[512,512]{1,0:T(8,128)S(1)}, f32[512,512]{1,0:T(8,128)}, u32[]{:S(2)}) copy-start(f32[512,512]{1,0:T(8,128)} %w_mid_hbm.1) | copy-start | bytes 3145732
  14.6 5.9 %copy-start.1 = (f32[64,512]{1,0:T(8,128)S(1)}, f32[64,512]{1,0:T(8,128)}, u32[]{:S(2)}) copy-start(f32[64,512]{1,0:T(8,128)} %w_latent_hbm.1) | copy-start | bytes 393220
  14.6 5.9 %copy-start.2 = (f32[5,512]{1,0:T(8,128)S(1)}, f32[5,512]{1,0:T(8,128)}, u32[]{:S(2)}) copy-start(f32[5,512]{1,0:T(8,128)} %w_out_hbm.1) | copy-start | bytes 30724
  14.6 5.9 %copy-start.3 = (f32[3,512]{1,0:T(4,128)S(1)}, f32[3,512]{1,0:T(4,128)}, u32[]{:S(2)}) copy-start(f32[3,512]{1,0:T(4,128)} %w_pos_hbm.1) | copy-start | bytes 18436
  33.3 1.7 %collective-permute-start.2 = (s16[4,352,128]{2,1,0:T(8,128)(2,1)S(1)}, s16[4,352,128]{2,1,0:T(8,128)(2,1)S(1)}, u32[]{:S(2)}, u32[]{:S(2)}) collective-permute-start(s16[4,352,128]{2,1,0:T(8,128)(2,1)S(1)} %get-tuple-element.36), channel_id=1, source_target_pairs={{0,1},{1,0},{2,3},{3,2},{4,5},{5,4},{6,7},{7,6},{8,9},{9,8},{10,11... | collective-permute-start | bytes 1081352 | tf_op jit(solution)/shard_map/ppermute | solution.py:615
  35.4 4.7 %collective-permute-start.4 = (s16[352,128]{1,0:T(8,128)(2,1)S(1)}, s16[352,128]{1,0:T(8,128)(2,1)S(1)}, u32[]{:S(2)}, u32[]{:S(2)}) collective-permute-start(s16[352,128]{1,0:T(8,128)(2,1)S(1)} %get-tuple-element.40), channel_id=1, source_target_pairs={{0,2},{1,3},{2,0},{3,1},{4,6},{5,7},{6,4},{7,5},{8,10},{9,11},{10,... | collective-permute-start | bytes 270344 | tf_op jit(solution)/shard_map/ppermute | solution.py:615
  35.5 4.6 %collective-permute-start.5 = (s16[352,128]{1,0:T(8,128)(2,1)S(1)}, s16[352,128]{1,0:T(8,128)(2,1)S(1)}, u32[]{:S(2)}, u32[]{:S(2)}) collective-permute-start(s16[352,128]{1,0:T(8,128)(2,1)S(1)} %get-tuple-element.41), channel_id=1, source_target_pairs={{0,16},{1,17},{2,18},{3,19},{4,20},{5,21},{6,22},{7,23},{8,24},{9,... | collective-permute-start | bytes 270344 | tf_op jit(solution)/shard_map/ppermute | solution.py:615
  37.0 6.2 %collective-permute-start.3 = (s16[352,128]{1,0:T(8,128)(2,1)S(1)}, s16[352,128]{1,0:T(8,128)(2,1)S(1)}, u32[]{:S(2)}, u32[]{:S(2)}) collective-permute-start(s16[352,128]{1,0:T(8,128)(2,1)S(1)} %sum_core.2), channel_id=1, source_target_pairs={{0,18},{1,19},{2,16},{3,17},{4,22},{5,23},{6,20},{7,21},{8,26},{9,... | collective-permute-start | bytes 270344 | tf_op jit(solution)/shard_map/ppermute | solution.py:615
  43.4 5.2 %collective-permute-start.6 = (s16[352,128]{1,0:T(8,128)(2,1)S(1)}, s16[352,128]{1,0:T(8,128)(2,1)S(1)}, u32[]{:S(2)}, u32[]{:S(2)}) collective-permute-start(s16[352,128]{1,0:T(8,128)(2,1)S(1)} %sum_plane.1.mine_ref), channel_id=1, source_target_pairs={{0,4},{1,9},{2,6},{3,11},{4,0},{5,13},{6,2},{7,15},{8,12},{9,1},{1... | collective-permute-start | bytes 270344 | tf_op jit(solution)/shard_map/ppermute | solution.py:871
  48.7 5.5 %collective-permute-start.7 = (s16[352,128]{1,0:T(8,128)(2,1)S(1)}, s16[352,128]{1,0:T(8,128)(2,1)S(1)}, u32[]{:S(2)}, u32[]{:S(2)}) collective-permute-start(s16[352,128]{1,0:T(8,128)(2,1)S(1)} %sum_line.2.mine_ref), channel_id=1, source_target_pairs={{0,8},{1,5},{2,10},{3,7},{4,12},{5,1},{6,14},{7,3},{8,0},{9,13},{1... | collective-permute-start | bytes 270344 | tf_op jit(solution)/shard_map/ppermute | solution.py:871
  54.3 4.6 %collective-permute-start.8 = (s16[352,128]{1,0:T(8,128)(2,1)S(1)}, s16[352,128]{1,0:T(8,128)(2,1)S(1)}, u32[]{:S(2)}, u32[]{:S(2)}) collective-permute-start(s16[352,128]{1,0:T(8,128)(2,1)S(1)} %sum_line.3.refs_0_), channel_id=1, source_target_pairs={{0,2},{1,3},{2,0},{3,1},{4,6},{5,7},{6,4},{7,5},{8,10},{9,11},{10,... | collective-permute-start | bytes 270344 | tf_op jit(solution)/shard_map/ppermute | solution.py:615
  55.4 4.5 %collective-permute-start.9 = (s16[352,128]{1,0:T(8,128)(2,1)S(1)}, s16[352,128]{1,0:T(8,128)(2,1)S(1)}, u32[]{:S(2)}, u32[]{:S(2)}) collective-permute-start(s16[352,128]{1,0:T(8,128)(2,1)S(1)} %sum_line.3.refs_0_), channel_id=1, source_target_pairs={{0,16},{1,17},{2,18},{3,19},{4,20},{5,21},{6,22},{7,23},{8,24},{9,... | collective-permute-start | bytes 270344 | tf_op jit(solution)/shard_map/ppermute | solution.py:615
  56.5 5.4 %collective-permute-start.10 = (s16[352,128]{1,0:T(8,128)(2,1)S(1)}, s16[352,128]{1,0:T(8,128)(2,1)S(1)}, u32[]{:S(2)}, u32[]{:S(2)}) collective-permute-start(s16[352,128]{1,0:T(8,128)(2,1)S(1)} %sum_line.3.refs_0_), channel_id=1, source_target_pairs={{0,18},{1,19},{2,16},{3,17},{4,22},{5,23},{6,20},{7,21},{8,26},{9,... | collective-permute-start | bytes 270344 | tf_op jit(solution)/shard_map/ppermute | solution.py:615
  57.9 4.0 %collective-permute-start.11 = (s16[352,128]{1,0:T(8,128)(2,1)S(1)}, s16[352,128]{1,0:T(8,128)(2,1)S(1)}, u32[]{:S(2)}, u32[]{:S(2)}) collective-permute-start(s16[352,128]{1,0:T(8,128)(2,1)S(1)} %sum_line.3.refs_0_), channel_id=1, source_target_pairs={{0,1},{1,0},{2,3},{3,2},{4,5},{5,4},{6,7},{7,6},{8,9},{9,8},{10,11... | collective-permute-start | bytes 270344 | tf_op jit(solution)/shard_map/ppermute | solution.py:615
  58.9 3.0 %collective-permute-start.12 = (s16[352,128]{1,0:T(8,128)(2,1)S(1)}, s16[352,128]{1,0:T(8,128)(2,1)S(1)}, u32[]{:S(2)}, u32[]{:S(2)}) collective-permute-start(s16[352,128]{1,0:T(8,128)(2,1)S(1)} %collective-permute-done.8.refs_1_), channel_id=1, source_target_pairs={{0,1},{1,0},{2,3},{3,2},{4,5},{5,4},{6,7},{7,6},{8,9},{9,8},{10,11... | collective-permute-start | bytes 270344 | tf_op jit(solution)/shard_map/ppermute | solution.py:615
  59.9 2.0 %collective-permute-start.13 = (s16[352,128]{1,0:T(8,128)(2,1)S(1)}, s16[352,128]{1,0:T(8,128)(2,1)S(1)}, u32[]{:S(2)}, u32[]{:S(2)}) collective-permute-start(s16[352,128]{1,0:T(8,128)(2,1)S(1)} %collective-permute-done.9.refs_2_), channel_id=1, source_target_pairs={{0,1},{1,0},{2,3},{3,2},{4,5},{5,4},{6,7},{7,6},{8,9},{9,8},{10,11... | collective-permute-start | bytes 270344 | tf_op jit(solution)/shard_map/ppermute | solution.py:615
  61.9 1.3 %collective-permute-start.14 = (s16[352,128]{1,0:T(8,128)(2,1)S(1)}, s16[352,128]{1,0:T(8,128)(2,1)S(1)}, u32[]{:S(2)}, u32[]{:S(2)}) collective-permute-start(s16[352,128]{1,0:T(8,128)(2,1)S(1)} %collective-permute-done.10.refs_3_), channel_id=1, source_target_pairs={{0,1},{1,0},{2,3},{3,2},{4,5},{5,4},{6,7},{7,6},{8,9},{9,8},{10,11... | collective-permute-start | bytes 270344 | tf_op jit(solution)/shard_map/ppermute | solution.py:615

commit v14 on v13

--- a/solution.py
+++ b/solution.py
@@ -15,7 +15,7 @@
 F32 = jnp.float32
 BF16 = jnp.bfloat16
 LANES = 128
-BLOCK = 32
+BLOCK = 16
 WORDS = 128
 SUB = 32
 NN = (((1,), (0,)), ((), ()))
@@ -870,7 +870,7 @@
         pairs = [(i, i ^ (1 << bits[i & 1])) for i in range(plan.devices)]
         other = lax.ppermute(block, ("replica", "tile"), pairs)
         block = coded_sum(pair_kernel, [block, other], plan, "sum_line")
-    blocks = [block] + [swapped(block, plan, plan.plane, step) for step in range(1, 4)]
+    blocks = [block] + [swapped(block, plan, plan.plane, step) for step in range(3, 0, -1)][::-1]
     blocks = blocks + [swapped(block, plan, plan.core, 1) for block in blocks]
     prediction, g_latent, g_pos, g_one, g_mid, g_two, g_out, g_bias, loss = unpack(
         place, blocks, plan, hidden, channels

time: 65.3 us -> 65.2 us (level)
  no operation moved by 1% of the time
where the time goes in v14:
time: 65.2 us; the launch traced here: 65 us
  waiting for transfers between devices  25 us (38%)
  Pallas kernels  18.8 us (29%)
  starting transfers between devices  17.3 us (27%)
  local copies, waits for them, and re-layouts  2.96 us (5%)
  between operations  0.9 us (1%)
    pallas_call x1, Pallas kernels, main(): pl.pallas_call(functools.partial(main_kernel, plan), out_shape=(jax.Shape...  12.8 us
    ppermute x11, waiting for transfers between devices, swapped(): lax.ppermute(value, ('replica', 'tile'), [(i, i ^ mask) for i in range(pl...  11.3 us
    ppermute x2, waiting for transfers between devices, body(): other = lax.ppermute(block, ('replica', 'tile'), pairs)  10.3 us
    ppermute x11, starting transfers between devices, swapped(): lax.ppermute(value, ('replica', 'tile'), [(i, i ^ mask) for i in range(pl...  7.19 us
    ppermute x1, starting transfers between devices, body(): lax.ppermute(second, 'tile', [(i, (i - 1 + 2 * (i & 1)) % tiles) for i in...  5.67 us
    all_to_all x1, starting transfers between devices, body(): lax.all_to_all(words.reshape(tiles, 8, WORDS), 'tile', split_axis=0, conc...  3.51 us
    all_to_all x1, waiting for transfers between devices, body(): lax.all_to_all(words.reshape(tiles, 8, WORDS), 'tile', split_axis=0, conc...  3.38 us
    pallas_call x1, Pallas kernels, convolve(): pl.pallas_call(conv_kernel, out_shape=jax.ShapeDtypeStruct((pairs, channe...  2.5 us
  transfers between devices with their start and end apart: 16, of which 11 were waited for; matrix products, arithmetic and copies ran while one was open for 0% of the time, Pallas kernels for 5%

profile of v14, /device:TPU:0, one launch (start us, length us, event | category | flops | bytes accessed | tf_op | source)
XLA Modules:
  0.0 65.0 jit_solution(9424340598449773873)
XLA Ops:
  0.6 1.2 %constant_dynamic-slice_fusion = (bf16[1,64,3,8,128]{4,3,2,1,0:T(8,128)(2,1)S(1)}, bf16[1,64,3,8,128]{4,3,2,1,0:T(8,128)(2,1)S(1)}) fusion(bf16[1,64,4,8,128]{4,3,2,1,0:T(8,128)(2,1)} %param.14, s32[]{:T(128)S(6)} %select_n.7, s32[]{:T(128)S(6)} %select_n.6), kind=kLoop, calls=%fused_computation.4 | loop fusion | bytes 1572872 | tf_op jit(solution)/shard_map/dynamic-slice.3
  1.9 0.0 copy-start.6
  1.9 0.0 copy-start.7
  1.9 0.0 copy-start.10
  1.9 0.0 copy-start.11
  1.9 0.0 copy-start.13
  1.9 0.2 copy_bitcast_fusion.1
  2.1 0.5 collective-permute-start
  2.7 5.7 %collective-permute-start.1 = (bf16[3,8,64,128]{3,2,1,0:T(8,128)(2,1)S(1)}, bf16[3,8,64,128]{3,2,1,0:T(8,128)(2,1)S(1)}, u32[]{:S(2)}, u32[]{:S(2)}) collective-permute-start(bf16[3,8,64,128]{3,2,1,0:T(8,128)(2,1)S(1)} %get-tuple-element.31), channel_id=1, source_target_pairs={{0,15},{1,2},{2,1},{3,4},{4,3},{5,6},{6,5},{7,8},{8,7},{9,10},{10,... | collective-permute-start | bytes 1179656 | tf_op jit(solution)/shard_map/ppermute | solution.py:848
  8.4 0.6 copy-done.4
  9.0 0.0 copy-done.5
  9.0 1.1 %route.1 = (f32[128,128]{1,0:T(8,128)}, f32[8,512]{1,0:T(8,128)S(1)}) custom-call(s32[1,128]{1,0:T(1,128)S(1)} %bitcast.36, s32[1,128]{1,0:T(1,128)S(1)} %copy-done.9, f32[3,1,128]{2,1,0:T(1,128)S(1)} %bitcast.35, f32[5,1,128]{2,1,0:T(1,128)S(1)} %bitcast.32, f32[1,512]{1,0:T(1,128)S(1)} %bitcast.33, f32[1,512]{1,0:T(1,128)S(1)} %bitcast.34, ...), custom_call_target="tpu_custom_call" | custom-call | tf_op jit(solution)/shard_map/route/pallas_call | solution.py:98
  10.1 3.5 %all-to-all-start = ((f32[16,8,128]{2,1,0:T(8,128)}), f32[16,8,128]{2,1,0:T(8,128)S(1)}, u32[]{:S(2)}, u32[]{:S(2)}) async-start(f32[16,8,128]{2,1,0:T(8,128)} %bitcast.16), calls=%async_computation | async-start | bytes 131072 | tf_op jit(solution)/shard_map/all_to_all | solution.py:855
  13.6 0.0 copy-start.12
  13.6 0.2 copy.29
  13.9 0.1 pad_add_fusion.place_ref
  13.9 0.0 collective-permute-done.near_ref
  13.9 0.0 collective-permute-done.1.far_ref
  14.0 0.6 copy-done.12
  14.6 2.5 %convolve.1.lat = bf16[20,64,256]{2,1,0:T(8,128)(2,1)S(1)} custom-call(s32[3]{0:T(128)S(1)} %pad_add_fusion.place_ref, bf16[3,8,64,128]{3,2,1,0:T(8,128)(2,1)S(1)} %collective-permute-done.near_ref, bf16[4,8,64,128]{3,2,1,0:T(8,128)(2,1)S(1)} %bitcast.30, bf16[3,8,64,128]{3,2,1,0:T(8,128)(2,1)S(1)} %collective-permute-done.1.far_ref, ...), custom_call_target="tpu_custom_call" | custom-call | flops 3221225472 | bytes 4194304 | tf_op jit(solution)/shard_map/convolve/pallas_call | solution.py:188
  17.1 3.4 %all-to-all-done = f32[16,8,128]{2,1,0:T(8,128)S(1)} async-done(((f32[16,8,128]{2,1,0:T(8,128)}), f32[16,8,128]{2,1,0:T(8,128)S(1)}, u32[]{:S(2)}, u32[]{:S(2)}) %all-to-all-start) | async-done | bytes 65568 | tf_op jit(solution)/shard_map/all_to_all | solution.py:855
  20.5 12.8 %encode_decode.1 = (s16[4,352,128]{2,1,0:T(8,128)(2,1)S(1)}, f32[4,328,128]{2,1,0:T(8,128)S(1)}) custom-call(s32[3]{0:T(128)S(1)} %pad_add_fusion.place_ref, bf16[20,64,256]{2,1,0:T(8,128)(2,1)S(1)} %convolve.1.lat, f32[128,128]{1,0:T(8,128)S(1)} %bitcast.31, f32[8,512]{1,0:T(8,128)S(1)} %get-tuple-element.33.small_ref, f32[64,512]{1,0:T(8,128)S(1)} %copy-done.1, ...), custom_call_target="tpu_custom_call" | custom-call | tf_op jit(solution)/shard_map/encode_decode/pallas_call | solution.py:723
  33.3 0.1 collective-permute-start.2
  33.4 1.7 %collective-permute-done.2.got_ref = s16[4,352,128]{2,1,0:T(8,128)(2,1)S(1)} collective-permute-done((s16[4,352,128]{2,1,0:T(8,128)(2,1)S(1)}, s16[4,352,128]{2,1,0:T(8,128)(2,1)S(1)}, u32[]{:S(2)}, u32[]{:S(2)}) %collective-permute-start.2) | collective-permute-done | bytes 360480 | tf_op jit(solution)/shard_map/ppermute | solution.py:615
  35.0 0.1 sum_core.2
  35.1 0.2 sum_core.3
  35.3 0.2 collective-permute-start.4
  35.5 1.5 %collective-permute-start.5 = (s16[352,128]{1,0:T(8,128)(2,1)S(1)}, s16[352,128]{1,0:T(8,128)(2,1)S(1)}, u32[]{:S(2)}, u32[]{:S(2)}) collective-permute-start(s16[352,128]{1,0:T(8,128)(2,1)S(1)} %get-tuple-element.41), channel_id=1, source_target_pairs={{0,16},{1,17},{2,18},{3,19},{4,20},{5,21},{6,22},{7,23},{8,24},{9,... | collective-permute-start | bytes 270344 | tf_op jit(solution)/shard_map/ppermute | solution.py:615
  37.0 1.9 %collective-permute-start.3 = (s16[352,128]{1,0:T(8,128)(2,1)S(1)}, s16[352,128]{1,0:T(8,128)(2,1)S(1)}, u32[]{:S(2)}, u32[]{:S(2)}) collective-permute-start(s16[352,128]{1,0:T(8,128)(2,1)S(1)} %sum_core.2), channel_id=1, source_target_pairs={{0,18},{1,19},{2,16},{3,17},{4,22},{5,23},{6,20},{7,21},{8,26},{9,... | collective-permute-start | bytes 270344 | tf_op jit(solution)/shard_map/ppermute | solution.py:615
  38.9 1.2 %collective-permute-done.4.refs_1_ = s16[352,128]{1,0:T(8,128)(2,1)S(1)} collective-permute-done((s16[352,128]{1,0:T(8,128)(2,1)S(1)}, s16[352,128]{1,0:T(8,128)(2,1)S(1)}, u32[]{:S(2)}, u32[]{:S(2)}) %collective-permute-start.4) | collective-permute-done | bytes 90144 | tf_op jit(solution)/shard_map/ppermute | solution.py:615
  40.0 0.1 collective-permute-done.5.refs_2_
  40.1 3.1 %collective-permute-done.3.refs_0_ = s16[352,128]{1,0:T(8,128)(2,1)S(1)} collective-permute-done((s16[352,128]{1,0:T(8,128)(2,1)S(1)}, s16[352,128]{1,0:T(8,128)(2,1)S(1)}, u32[]{:S(2)}, u32[]{:S(2)}) %collective-permute-start.3) | collective-permute-done | bytes 90144 | tf_op jit(solution)/shard_map/ppermute | solution.py:615
  43.2 0.1 sum_plane.1.mine_ref
  43.3 0.3 collective-permute-start.6
  43.6 4.9 %collective-permute-done.6.other_ref = s16[352,128]{1,0:T(8,128)(2,1)S(1)} collective-permute-done((s16[352,128]{1,0:T(8,128)(2,1)S(1)}, s16[352,128]{1,0:T(8,128)(2,1)S(1)}, u32[]{:S(2)}, u32[]{:S(2)}) %collective-permute-start.6) | collective-permute-done | bytes 90144 | tf_op jit(solution)/shard_map/ppermute | solution.py:871
  48.5 0.1 sum_line.2.mine_ref
  48.6 0.1 collective-permute-start.7
  48.7 5.5 %collective-permute-done.7.other_ref = s16[352,128]{1,0:T(8,128)(2,1)S(1)} collective-permute-done((s16[352,128]{1,0:T(8,128)(2,1)S(1)}, s16[352,128]{1,0:T(8,128)(2,1)S(1)}, u32[]{:S(2)}, u32[]{:S(2)}) %collective-permute-start.7) | collective-permute-done | bytes 90144 | tf_op jit(solution)/shard_map/ppermute | solution.py:871
  54.1 0.1 sum_line.3.refs_0_
  54.3 1.1 %collective-permute-start.8 = (s16[352,128]{1,0:T(8,128)(2,1)S(1)}, s16[352,128]{1,0:T(8,128)(2,1)S(1)}, u32[]{:S(2)}, u32[]{:S(2)}) collective-permute-start(s16[352,128]{1,0:T(8,128)(2,1)S(1)} %sum_line.3.refs_0_), channel_id=1, source_target_pairs={{0,2},{1,3},{2,0},{3,1},{4,6},{5,7},{6,4},{7,5},{8,10},{9,11},{10,... | collective-permute-start | bytes 270344 | tf_op jit(solution)/shard_map/ppermute | solution.py:615
  55.4 1.1 %collective-permute-start.9 = (s16[352,128]{1,0:T(8,128)(2,1)S(1)}, s16[352,128]{1,0:T(8,128)(2,1)S(1)}, u32[]{:S(2)}, u32[]{:S(2)}) collective-permute-start(s16[352,128]{1,0:T(8,128)(2,1)S(1)} %sum_line.3.refs_0_), channel_id=1, source_target_pairs={{0,16},{1,17},{2,18},{3,19},{4,20},{5,21},{6,22},{7,23},{8,24},{9,... | collective-permute-start | bytes 270344 | tf_op jit(solution)/shard_map/ppermute | solution.py:615
  56.4 1.4 %collective-permute-start.10 = (s16[352,128]{1,0:T(8,128)(2,1)S(1)}, s16[352,128]{1,0:T(8,128)(2,1)S(1)}, u32[]{:S(2)}, u32[]{:S(2)}) collective-permute-start(s16[352,128]{1,0:T(8,128)(2,1)S(1)} %sum_line.3.refs_0_), channel_id=1, source_target_pairs={{0,18},{1,19},{2,16},{3,17},{4,22},{5,23},{6,20},{7,21},{8,26},{9,... | collective-permute-start | bytes 270344 | tf_op jit(solution)/shard_map/ppermute | solution.py:615
  57.8 0.0 collective-permute-start.11
  57.8 1.0 %collective-permute-done.8.refs_1_ = s16[352,128]{1,0:T(8,128)(2,1)S(1)} collective-permute-done((s16[352,128]{1,0:T(8,128)(2,1)S(1)}, s16[352,128]{1,0:T(8,128)(2,1)S(1)}, u32[]{:S(2)}, u32[]{:S(2)}) %collective-permute-start.8) | collective-permute-done | bytes 90144 | tf_op jit(solution)/shard_map/ppermute | solution.py:615
  58.9 1.0 %collective-permute-done.9.refs_2_ = s16[352,128]{1,0:T(8,128)(2,1)S(1)} collective-permute-done((s16[352,128]{1,0:T(8,128)(2,1)S(1)}, s16[352,128]{1,0:T(8,128)(2,1)S(1)}, u32[]{:S(2)}, u32[]{:S(2)}) %collective-permute-start.9) | collective-permute-done | bytes 90144 | tf_op jit(solution)/shard_map/ppermute | solution.py:615
  59.9 2.0 %collective-permute-done.10.refs_3_ = s16[352,128]{1,0:T(8,128)(2,1)S(1)} collective-permute-done((s16[352,128]{1,0:T(8,128)(2,1)S(1)}, s16[352,128]{1,0:T(8,128)(2,1)S(1)}, u32[]{:S(2)}, u32[]{:S(2)}) %collective-permute-start.10) | collective-permute-done | bytes 90144 | tf_op jit(solution)/shard_map/ppermute | solution.py:615
  61.9 1.3 %collective-permute-done.14.refs_7_ = s16[352,128]{1,0:T(8,128)(2,1)S(1)} collective-permute-done((s16[352,128]{1,0:T(8,128)(2,1)S(1)}, s16[352,128]{1,0:T(8,128)(2,1)S(1)}, u32[]{:S(2)}, u32[]{:S(2)}) %collective-permute-start.14) | collective-permute-done | bytes 90144 | tf_op jit(solution)/shard_map/ppermute | solution.py:615
  63.1 1.8 %unpack.1 = (f32[5,1,128]{2,1,0:T(1,128)}, f32[64,512]{1,0:T(8,128)}, f32[3,512]{1,0:T(4,128)}, f32[1,512]{1,0:T(1,128)}, f32[512,512]{1,0:T(8,128)}, /*index=5*...) custom-call(s32[3]{0:T(128)S(1)} %pad_add_fusion.place_ref, ...), custom_call_target="tpu_custom_call" | custom-call | tf_op jit(solution)/shard_map/unpack/pallas_call | solution.py:803
  (25 shorter events, 0.1 us)
Async XLA Ops:
  1.9 6.5 %copy-start.6 = (f32[512]{0:T(512)S(1)}, f32[512]{0:T(512)}, u32[]{:S(2)}) copy-start(f32[512]{0:T(512)} %param.25) | copy-start | bytes 6148
  1.9 6.5 %copy-start.7 = (f32[1,3,128]{2,0,1:T(1,128)S(1)}, f32[1,3,128]{2,0,1:T(1,128)}, u32[]{:S(2)}) copy-start(f32[1,3,128]{2,0,1:T(1,128)} %param.19) | copy-start | bytes 4612
  1.9 6.4 %copy-start.10 = (f32[5]{0:T(128)S(1)}, f32[5]{0:T(128)}, u32[]{:S(2)}) copy-start(f32[5]{0:T(128)} %param.27) | copy-start | bytes 64
  1.9 6.4 %copy-start.11 = (f32[64]{0:T(128)S(1)}, f32[64]{0:T(128)}, u32[]{:S(2)}) copy-start(f32[64]{0:T(128)} %param.16) | copy-start | bytes 772
  1.9 11.7 %copy-start.13 = (bf16[1,64,4,8,128]{4,3,2,1,0:T(8,128)(2,1)S(1)}, bf16[1,64,4,8,128]{4,3,2,1,0:T(8,128)(2,1)}, u32[]{:S(2)}) copy-start(bf16[1,64,4,8,128]{4,3,2,1,0:T(8,128)(2,1)} %param.14) | copy-start | bytes 1572868
  2.1 11.8 %collective-permute-start = (bf16[3,8,64,128]{3,2,1,0:T(8,128)(2,1)S(1)}, bf16[3,8,64,128]{3,2,1,0:T(8,128)(2,1)S(1)}, u32[]{:S(2)}, u32[]{:S(2)}) collective-permute-start(bf16[3,8,64,128]{3,2,1,0:T(8,128)(2,1)S(1)} %get-tuple-element.30), channel_id=1, source_target_pairs={{0,1},{1,0},{2,3},{3,2},{4,5},{5,4},{6,7},{7,6},{8,9},{9,8},{10,11... | collective-permute-start | bytes 1179656 | tf_op jit(solution)/shard_map/ppermute | solution.py:847
  2.7 11.3 %collective-permute-start.1 = (bf16[3,8,64,128]{3,2,1,0:T(8,128)(2,1)S(1)}, bf16[3,8,64,128]{3,2,1,0:T(8,128)(2,1)S(1)}, u32[]{:S(2)}, u32[]{:S(2)}) collective-permute-start(bf16[3,8,64,128]{3,2,1,0:T(8,128)(2,1)S(1)} %get-tuple-element.31), channel_id=1, source_target_pairs={{0,15},{1,2},{2,1},{3,4},{4,3},{5,6},{6,5},{7,8},{8,7},{9,10},{10,... | collective-permute-start | bytes 1179656 | tf_op jit(solution)/shard_map/ppermute | solution.py:848
  8.3 0.7 %copy-start.4 = (f32[1,5,128]{2,0,1:T(1,128)S(1)}, f32[1,5,128]{2,0,1:T(1,128)}, u32[]{:S(2)}) copy-start(f32[1,5,128]{2,0,1:T(1,128)} %param.20) | copy-start | bytes 7684
  8.3 0.7 %copy-start.5 = (f32[512]{0:T(512)S(1)}, f32[512]{0:T(512)}, u32[]{:S(2)}) copy-start(f32[512]{0:T(512)} %param.23) | copy-start | bytes 6148
  8.3 0.7 %copy-start.8 = (s32[1,128,1]{1,2,0:T(1,128)S(1)}, s32[1,128,1]{1,2,0:T(1,128)}, u32[]{:S(2)}) copy-start(s32[1,128,1]{1,2,0:T(1,128)} %param.17) | copy-start | bytes 1540
  8.3 0.7 %copy-start.9 = (s32[1,128]{1,0:T(1,128)S(1)}, s32[1,128]{1,0:T(1,128)}, u32[]{:S(2)}) copy-start(s32[1,128]{1,0:T(1,128)} %refs_1_.1) | copy-start | bytes 1540
  10.1 10.4 %all-to-all-start = ((f32[16,8,128]{2,1,0:T(8,128)}), f32[16,8,128]{2,1,0:T(8,128)S(1)}, u32[]{:S(2)}, u32[]{:S(2)}) async-start(f32[16,8,128]{2,1,0:T(8,128)} %bitcast.16), calls=%async_computation | async-start | bytes 131072 | tf_op jit(solution)/shard_map/all_to_all | solution.py:855
  13.6 0.9 %copy-start.12 = (bf16[64,1728]{1,0:T(8,128)(2,1)S(1)}, bf16[64,1728]{1,0:T(8,128)(2,1)}, u32[]{:S(2)}) copy-start(bf16[64,1728]{1,0:T(8,128)(2,1)} %taps_ref.1) | copy-start | bytes 663556
  14.6 5.9 %copy-start = (f32[512,512]{1,0:T(8,128)S(1)}, f32[512,512]{1,0:T(8,128)}, u32[]{:S(2)}) copy-start(f32[512,512]{1,0:T(8,128)} %w_mid_hbm.1) | copy-start | bytes 3145732
  14.6 5.9 %copy-start.1 = (f32[64,512]{1,0:T(8,128)S(1)}, f32[64,512]{1,0:T(8,128)}, u32[]{:S(2)}) copy-start(f32[64,512]{1,0:T(8,128)} %w_latent_hbm.1) | copy-start | bytes 393220
  14.6 5.9 %copy-start.2 = (f32[5,512]{1,0:T(8,128)S(1)}, f32[5,512]{1,0:T(8,128)}, u32[]{:S(2)}) copy-start(f32[5,512]{1,0:T(8,128)} %w_out_hbm.1) | copy-start | bytes 30724
  14.6 5.9 %copy-start.3 = (f32[3,512]{1,0:T(4,128)S(1)}, f32[3,512]{1,0:T(4,128)}, u32[]{:S(2)}) copy-start(f32[3,512]{1,0:T(4,128)} %w_pos_hbm.1) | copy-start | bytes 18436
  33.3 1.7 %collective-permute-start.2 = (s16[4,352,128]{2,1,0:T(8,128)(2,1)S(1)}, s16[4,352,128]{2,1,0:T(8,128)(2,1)S(1)}, u32[]{:S(2)}, u32[]{:S(2)}) collective-permute-start(s16[4,352,128]{2,1,0:T(8,128)(2,1)S(1)} %get-tuple-element.36), channel_id=1, source_target_pairs={{0,1},{1,0},{2,3},{3,2},{4,5},{5,4},{6,7},{7,6},{8,9},{9,8},{10,11... | collective-permute-start | bytes 1081352 | tf_op jit(solution)/shard_map/ppermute | solution.py:615
  35.3 4.7 %collective-permute-start.4 = (s16[352,128]{1,0:T(8,128)(2,1)S(1)}, s16[352,128]{1,0:T(8,128)(2,1)S(1)}, u32[]{:S(2)}, u32[]{:S(2)}) collective-permute-start(s16[352,128]{1,0:T(8,128)(2,1)S(1)} %get-tuple-element.40), channel_id=1, source_target_pairs={{0,2},{1,3},{2,0},{3,1},{4,6},{5,7},{6,4},{7,5},{8,10},{9,11},{10,... | collective-permute-start | bytes 270344 | tf_op jit(solution)/shard_map/ppermute | solution.py:615
  35.5 4.6 %collective-permute-start.5 = (s16[352,128]{1,0:T(8,128)(2,1)S(1)}, s16[352,128]{1,0:T(8,128)(2,1)S(1)}, u32[]{:S(2)}, u32[]{:S(2)}) collective-permute-start(s16[352,128]{1,0:T(8,128)(2,1)S(1)} %get-tuple-element.41), channel_id=1, source_target_pairs={{0,16},{1,17},{2,18},{3,19},{4,20},{5,21},{6,22},{7,23},{8,24},{9,... | collective-permute-start | bytes 270344 | tf_op jit(solution)/shard_map/ppermute | solution.py:615
  37.0 6.2 %collective-permute-start.3 = (s16[352,128]{1,0:T(8,128)(2,1)S(1)}, s16[352,128]{1,0:T(8,128)(2,1)S(1)}, u32[]{:S(2)}, u32[]{:S(2)}) collective-permute-start(s16[352,128]{1,0:T(8,128)(2,1)S(1)} %sum_core.2), channel_id=1, source_target_pairs={{0,18},{1,19},{2,16},{3,17},{4,22},{5,23},{6,20},{7,21},{8,26},{9,... | collective-permute-start | bytes 270344 | tf_op jit(solution)/shard_map/ppermute | solution.py:615
  43.3 5.2 %collective-permute-start.6 = (s16[352,128]{1,0:T(8,128)(2,1)S(1)}, s16[352,128]{1,0:T(8,128)(2,1)S(1)}, u32[]{:S(2)}, u32[]{:S(2)}) collective-permute-start(s16[352,128]{1,0:T(8,128)(2,1)S(1)} %sum_plane.1.mine_ref), channel_id=1, source_target_pairs={{0,4},{1,9},{2,6},{3,11},{4,0},{5,13},{6,2},{7,15},{8,12},{9,1},{1... | collective-permute-start | bytes 270344 | tf_op jit(solution)/shard_map/ppermute | solution.py:871
  48.6 5.5 %collective-permute-start.7 = (s16[352,128]{1,0:T(8,128)(2,1)S(1)}, s16[352,128]{1,0:T(8,128)(2,1)S(1)}, u32[]{:S(2)}, u32[]{:S(2)}) collective-permute-start(s16[352,128]{1,0:T(8,128)(2,1)S(1)} %sum_line.2.mine_ref), channel_id=1, source_target_pairs={{0,8},{1,5},{2,10},{3,7},{4,12},{5,1},{6,14},{7,3},{8,0},{9,13},{1... | collective-permute-start | bytes 270344 | tf_op jit(solution)/shard_map/ppermute | solution.py:871
  54.3 4.6 %collective-permute-start.8 = (s16[352,128]{1,0:T(8,128)(2,1)S(1)}, s16[352,128]{1,0:T(8,128)(2,1)S(1)}, u32[]{:S(2)}, u32[]{:S(2)}) collective-permute-start(s16[352,128]{1,0:T(8,128)(2,1)S(1)} %sum_line.3.refs_0_), channel_id=1, source_target_pairs={{0,2},{1,3},{2,0},{3,1},{4,6},{5,7},{6,4},{7,5},{8,10},{9,11},{10,... | collective-permute-start | bytes 270344 | tf_op jit(solution)/shard_map/ppermute | solution.py:615
  55.4 4.5 %collective-permute-start.9 = (s16[352,128]{1,0:T(8,128)(2,1)S(1)}, s16[352,128]{1,0:T(8,128)(2,1)S(1)}, u32[]{:S(2)}, u32[]{:S(2)}) collective-permute-start(s16[352,128]{1,0:T(8,128)(2,1)S(1)} %sum_line.3.refs_0_), channel_id=1, source_target_pairs={{0,16},{1,17},{2,18},{3,19},{4,20},{5,21},{6,22},{7,23},{8,24},{9,... | collective-permute-start | bytes 270344 | tf_op jit(solution)/shard_map/ppermute | solution.py:615
  56.4 5.4 %collective-permute-start.10 = (s16[352,128]{1,0:T(8,128)(2,1)S(1)}, s16[352,128]{1,0:T(8,128)(2,1)S(1)}, u32[]{:S(2)}, u32[]{:S(2)}) collective-permute-start(s16[352,128]{1,0:T(8,128)(2,1)S(1)} %sum_line.3.refs_0_), channel_id=1, source_target_pairs={{0,18},{1,19},{2,16},{3,17},{4,22},{5,23},{6,20},{7,21},{8,26},{9,... | collective-permute-start | bytes 270344 | tf_op jit(solution)/shard_map/ppermute | solution.py:615
  57.8 4.0 %collective-permute-start.11 = (s16[352,128]{1,0:T(8,128)(2,1)S(1)}, s16[352,128]{1,0:T(8,128)(2,1)S(1)}, u32[]{:S(2)}, u32[]{:S(2)}) collective-permute-start(s16[352,128]{1,0:T(8,128)(2,1)S(1)} %sum_line.3.refs_0_), channel_id=1, source_target_pairs={{0,1},{1,0},{2,3},{3,2},{4,5},{5,4},{6,7},{7,6},{8,9},{9,8},{10,11... | collective-permute-start | bytes 270344 | tf_op jit(solution)/shard_map/ppermute | solution.py:615
  58.9 3.0 %collective-permute-start.12 = (s16[352,128]{1,0:T(8,128)(2,1)S(1)}, s16[352,128]{1,0:T(8,128)(2,1)S(1)}, u32[]{:S(2)}, u32[]{:S(2)}) collective-permute-start(s16[352,128]{1,0:T(8,128)(2,1)S(1)} %collective-permute-done.8.refs_1_), channel_id=1, source_target_pairs={{0,1},{1,0},{2,3},{3,2},{4,5},{5,4},{6,7},{7,6},{8,9},{9,8},{10,11... | collective-permute-start | bytes 270344 | tf_op jit(solution)/shard_map/ppermute | solution.py:615
  59.9 2.0 %collective-permute-start.13 = (s16[352,128]{1,0:T(8,128)(2,1)S(1)}, s16[352,128]{1,0:T(8,128)(2,1)S(1)}, u32[]{:S(2)}, u32[]{:S(2)}) collective-permute-start(s16[352,128]{1,0:T(8,128)(2,1)S(1)} %collective-permute-done.9.refs_2_), channel_id=1, source_target_pairs={{0,1},{1,0},{2,3},{3,2},{4,5},{5,4},{6,7},{7,6},{8,9},{9,8},{10,11... | collective-permute-start | bytes 270344 | tf_op jit(solution)/shard_map/ppermute | solution.py:615
  61.9 1.3 %collective-permute-start.14 = (s16[352,128]{1,0:T(8,128)(2,1)S(1)}, s16[352,128]{1,0:T(8,128)(2,1)S(1)}, u32[]{:S(2)}, u32[]{:S(2)}) collective-permute-start(s16[352,128]{1,0:T(8,128)(2,1)S(1)} %collective-permute-done.10.refs_3_), channel_id=1, source_target_pairs={{0,1},{1,0},{2,3},{3,2},{4,5},{5,4},{6,7},{7,6},{8,9},{9,8},{10,11... | collective-permute-start | bytes 270344 | tf_op jit(solution)/shard_map/ppermute | solution.py:615

commit v15 on v11

--- a/solution.py
+++ b/solution.py
@@ -15,7 +15,7 @@
 F32 = jnp.float32
 BF16 = jnp.bfloat16
 LANES = 128
-BLOCK = 32
+BLOCK = 16
 WORDS = 128
 SUB = 32
 NN = (((1,), (0,)), ((), ()))

time: 65.3 us -> 65.2 us (level)
  no operation moved by 1% of the time
where the time goes in v15:
time: 65.2 us; the launch traced here: 65 us
  waiting for transfers between devices  24.6 us (38%)
  Pallas kernels  18.8 us (29%)
  starting transfers between devices  17.7 us (27%)
  local copies, waits for them, and re-layouts  2.96 us (5%)
  between operations  0.89 us (1%)
    ppermute x13, waiting for transfers between devices, swapped(): lax.ppermute(value, ('replica', 'tile'), [(i, i ^ mask) for i in range(pl...  21.2 us
    pallas_call x1, Pallas kernels, main(): pl.pallas_call(functools.partial(main_kernel, plan), out_shape=(jax.Shape...  12.8 us
    ppermute x13, starting transfers between devices, swapped(): lax.ppermute(value, ('replica', 'tile'), [(i, i ^ mask) for i in range(pl...  8.01 us
    ppermute x1, starting transfers between devices, body(): lax.ppermute(second, 'tile', [(i, (i - 1 + 2 * (i & 1)) % tiles) for i in...  5.67 us
    all_to_all x1, starting transfers between devices, body(): lax.all_to_all(words.reshape(tiles, 8, WORDS), 'tile', split_axis=0, conc...  3.51 us
    all_to_all x1, waiting for transfers between devices, body(): lax.all_to_all(words.reshape(tiles, 8, WORDS), 'tile', split_axis=0, conc...  3.38 us
    pallas_call x1, Pallas kernels, convolve(): pl.pallas_call(conv_kernel, out_shape=jax.ShapeDtypeStruct((pairs, channe...  2.5 us
    pallas_call x1, Pallas kernels, unpack(): pl.pallas_call(functools.partial(unpack_kernel, plan), out_shape=tuple((j...  1.83 us
  transfers between devices with their start and end apart: 16, of which 11 were waited for; matrix products, arithmetic and copies ran while one was open for 0% of the time, Pallas kernels for 5%

profile of v15, /device:TPU:0, one launch (start us, length us, event | category | flops | bytes accessed | tf_op | source)
XLA Modules:
  0.0 65.0 jit_solution(13311859244990797684)
XLA Ops:
  0.6 1.2 %constant_dynamic-slice_fusion = (bf16[1,64,3,8,128]{4,3,2,1,0:T(8,128)(2,1)S(1)}, bf16[1,64,3,8,128]{4,3,2,1,0:T(8,128)(2,1)S(1)}) fusion(bf16[1,64,4,8,128]{4,3,2,1,0:T(8,128)(2,1)} %param.14, s32[]{:T(128)S(6)} %select_n.7, s32[]{:T(128)S(6)} %select_n.6), kind=kLoop, calls=%fused_computation.4 | loop fusion | bytes 1572872 | tf_op jit(solution)/shard_map/dynamic-slice.3
  1.9 0.0 copy-start.6
  1.9 0.0 copy-start.7
  1.9 0.0 copy-start.10
  1.9 0.0 copy-start.11
  1.9 0.0 copy-start.13
  1.9 0.2 copy_bitcast_fusion.1
  2.1 0.5 collective-permute-start
  2.7 5.7 %collective-permute-start.1 = (bf16[3,8,64,128]{3,2,1,0:T(8,128)(2,1)S(1)}, bf16[3,8,64,128]{3,2,1,0:T(8,128)(2,1)S(1)}, u32[]{:S(2)}, u32[]{:S(2)}) collective-permute-start(bf16[3,8,64,128]{3,2,1,0:T(8,128)(2,1)S(1)} %get-tuple-element.31), channel_id=1, source_target_pairs={{0,15},{1,2},{2,1},{3,4},{4,3},{5,6},{6,5},{7,8},{8,7},{9,10},{10,... | collective-permute-start | bytes 1179656 | tf_op jit(solution)/shard_map/ppermute | solution.py:848
  8.4 0.6 copy-done.4
  9.0 0.0 copy-done.5
  9.0 1.1 %route.1 = (f32[128,128]{1,0:T(8,128)}, f32[8,512]{1,0:T(8,128)S(1)}) custom-call(s32[1,128]{1,0:T(1,128)S(1)} %bitcast.36, s32[1,128]{1,0:T(1,128)S(1)} %copy-done.9, f32[3,1,128]{2,1,0:T(1,128)S(1)} %bitcast.35, f32[5,1,128]{2,1,0:T(1,128)S(1)} %bitcast.32, f32[1,512]{1,0:T(1,128)S(1)} %bitcast.33, f32[1,512]{1,0:T(1,128)S(1)} %bitcast.34, ...), custom_call_target="tpu_custom_call" | custom-call | tf_op jit(solution)/shard_map/route/pallas_call | solution.py:98
  10.1 3.5 %all-to-all-start = ((f32[16,8,128]{2,1,0:T(8,128)}), f32[16,8,128]{2,1,0:T(8,128)S(1)}, u32[]{:S(2)}, u32[]{:S(2)}) async-start(f32[16,8,128]{2,1,0:T(8,128)} %bitcast.16), calls=%async_computation | async-start | bytes 131072 | tf_op jit(solution)/shard_map/all_to_all | solution.py:855
  13.6 0.0 copy-start.12
  13.6 0.2 copy.29
  13.9 0.1 pad_add_fusion.place_ref
  13.9 0.0 collective-permute-done.near_ref
  13.9 0.0 collective-permute-done.1.far_ref
  14.0 0.6 copy-done.12
  14.6 2.5 %convolve.1.lat = bf16[20,64,256]{2,1,0:T(8,128)(2,1)S(1)} custom-call(s32[3]{0:T(128)S(1)} %pad_add_fusion.place_ref, bf16[3,8,64,128]{3,2,1,0:T(8,128)(2,1)S(1)} %collective-permute-done.near_ref, bf16[4,8,64,128]{3,2,1,0:T(8,128)(2,1)S(1)} %bitcast.30, bf16[3,8,64,128]{3,2,1,0:T(8,128)(2,1)S(1)} %collective-permute-done.1.far_ref, ...), custom_call_target="tpu_custom_call" | custom-call | flops 3221225472 | bytes 4194304 | tf_op jit(solution)/shard_map/convolve/pallas_call | solution.py:188
  17.1 3.4 %all-to-all-done = f32[16,8,128]{2,1,0:T(8,128)S(1)} async-done(((f32[16,8,128]{2,1,0:T(8,128)}), f32[16,8,128]{2,1,0:T(8,128)S(1)}, u32[]{:S(2)}, u32[]{:S(2)}) %all-to-all-start) | async-done | bytes 65568 | tf_op jit(solution)/shard_map/all_to_all | solution.py:855
  20.5 12.8 %encode_decode.1 = (s16[4,352,128]{2,1,0:T(8,128)(2,1)S(1)}, f32[4,328,128]{2,1,0:T(8,128)S(1)}) custom-call(s32[3]{0:T(128)S(1)} %pad_add_fusion.place_ref, bf16[20,64,256]{2,1,0:T(8,128)(2,1)S(1)} %convolve.1.lat, f32[128,128]{1,0:T(8,128)S(1)} %bitcast.31, f32[8,512]{1,0:T(8,128)S(1)} %get-tuple-element.33.small_ref, f32[64,512]{1,0:T(8,128)S(1)} %copy-done.1, ...), custom_call_target="tpu_custom_call" | custom-call | tf_op jit(solution)/shard_map/encode_decode/pallas_call | solution.py:723
  33.3 0.1 collective-permute-start.2
  33.4 1.7 %collective-permute-done.2.got_ref = s16[4,352,128]{2,1,0:T(8,128)(2,1)S(1)} collective-permute-done((s16[4,352,128]{2,1,0:T(8,128)(2,1)S(1)}, s16[4,352,128]{2,1,0:T(8,128)(2,1)S(1)}, u32[]{:S(2)}, u32[]{:S(2)}) %collective-permute-start.2) | collective-permute-done | bytes 360480 | tf_op jit(solution)/shard_map/ppermute | solution.py:615
  35.0 0.1 sum_core.2
  35.1 0.2 sum_core.3
  35.3 0.2 collective-permute-start.4
  35.5 1.5 %collective-permute-start.5 = (s16[352,128]{1,0:T(8,128)(2,1)S(1)}, s16[352,128]{1,0:T(8,128)(2,1)S(1)}, u32[]{:S(2)}, u32[]{:S(2)}) collective-permute-start(s16[352,128]{1,0:T(8,128)(2,1)S(1)} %get-tuple-element.41), channel_id=1, source_target_pairs={{0,16},{1,17},{2,18},{3,19},{4,20},{5,21},{6,22},{7,23},{8,24},{9,... | collective-permute-start | bytes 270344 | tf_op jit(solution)/shard_map/ppermute | solution.py:615
  37.0 1.9 %collective-permute-start.3 = (s16[352,128]{1,0:T(8,128)(2,1)S(1)}, s16[352,128]{1,0:T(8,128)(2,1)S(1)}, u32[]{:S(2)}, u32[]{:S(2)}) collective-permute-start(s16[352,128]{1,0:T(8,128)(2,1)S(1)} %sum_core.2), channel_id=1, source_target_pairs={{0,18},{1,19},{2,16},{3,17},{4,22},{5,23},{6,20},{7,21},{8,26},{9,... | collective-permute-start | bytes 270344 | tf_op jit(solution)/shard_map/ppermute | solution.py:615
  38.9 1.2 %collective-permute-done.4.refs_1_ = s16[352,128]{1,0:T(8,128)(2,1)S(1)} collective-permute-done((s16[352,128]{1,0:T(8,128)(2,1)S(1)}, s16[352,128]{1,0:T(8,128)(2,1)S(1)}, u32[]{:S(2)}, u32[]{:S(2)}) %collective-permute-start.4) | collective-permute-done | bytes 90144 | tf_op jit(solution)/shard_map/ppermute | solution.py:615
  40.0 0.1 collective-permute-done.5.refs_2_
  40.1 3.1 %collective-permute-done.3.refs_0_ = s16[352,128]{1,0:T(8,128)(2,1)S(1)} collective-permute-done((s16[352,128]{1,0:T(8,128)(2,1)S(1)}, s16[352,128]{1,0:T(8,128)(2,1)S(1)}, u32[]{:S(2)}, u32[]{:S(2)}) %collective-permute-start.3) | collective-permute-done | bytes 90144 | tf_op jit(solution)/shard_map/ppermute | solution.py:615
  43.2 0.1 sum_plane.1.mine_ref
  43.3 0.3 collective-permute-start.6
  43.6 4.3 %collective-permute-done.6.other_ref = s16[352,128]{1,0:T(8,128)(2,1)S(1)} collective-permute-done((s16[352,128]{1,0:T(8,128)(2,1)S(1)}, s16[352,128]{1,0:T(8,128)(2,1)S(1)}, u32[]{:S(2)}, u32[]{:S(2)}) %collective-permute-start.6) | collective-permute-done | bytes 90144 | tf_op jit(solution)/shard_map/ppermute | solution.py:615
  47.9 0.1 sum_line.2.mine_ref
  48.0 0.5 collective-permute-start.7
  48.5 5.6 %collective-permute-done.7.other_ref = s16[352,128]{1,0:T(8,128)(2,1)S(1)} collective-permute-done((s16[352,128]{1,0:T(8,128)(2,1)S(1)}, s16[352,128]{1,0:T(8,128)(2,1)S(1)}, u32[]{:S(2)}, u32[]{:S(2)}) %collective-permute-start.7) | collective-permute-done | bytes 90144 | tf_op jit(solution)/shard_map/ppermute | solution.py:615
  54.1 0.1 sum_line.3.refs_0_
  54.3 1.1 %collective-permute-start.8 = (s16[352,128]{1,0:T(8,128)(2,1)S(1)}, s16[352,128]{1,0:T(8,128)(2,1)S(1)}, u32[]{:S(2)}, u32[]{:S(2)}) collective-permute-start(s16[352,128]{1,0:T(8,128)(2,1)S(1)} %sum_line.3.refs_0_), channel_id=1, source_target_pairs={{0,2},{1,3},{2,0},{3,1},{4,6},{5,7},{6,4},{7,5},{8,10},{9,11},{10,... | collective-permute-start | bytes 270344 | tf_op jit(solution)/shard_map/ppermute | solution.py:615
  55.4 1.1 %collective-permute-start.9 = (s16[352,128]{1,0:T(8,128)(2,1)S(1)}, s16[352,128]{1,0:T(8,128)(2,1)S(1)}, u32[]{:S(2)}, u32[]{:S(2)}) collective-permute-start(s16[352,128]{1,0:T(8,128)(2,1)S(1)} %sum_line.3.refs_0_), channel_id=1, source_target_pairs={{0,16},{1,17},{2,18},{3,19},{4,20},{5,21},{6,22},{7,23},{8,24},{9,... | collective-permute-start | bytes 270344 | tf_op jit(solution)/shard_map/ppermute | solution.py:615
  56.4 1.4 %collective-permute-start.10 = (s16[352,128]{1,0:T(8,128)(2,1)S(1)}, s16[352,128]{1,0:T(8,128)(2,1)S(1)}, u32[]{:S(2)}, u32[]{:S(2)}) collective-permute-start(s16[352,128]{1,0:T(8,128)(2,1)S(1)} %sum_line.3.refs_0_), channel_id=1, source_target_pairs={{0,18},{1,19},{2,16},{3,17},{4,22},{5,23},{6,20},{7,21},{8,26},{9,... | collective-permute-start | bytes 270344 | tf_op jit(solution)/shard_map/ppermute | solution.py:615
  57.8 0.0 collective-permute-start.11
  57.8 1.0 %collective-permute-done.8.refs_1_ = s16[352,128]{1,0:T(8,128)(2,1)S(1)} collective-permute-done((s16[352,128]{1,0:T(8,128)(2,1)S(1)}, s16[352,128]{1,0:T(8,128)(2,1)S(1)}, u32[]{:S(2)}, u32[]{:S(2)}) %collective-permute-start.8) | collective-permute-done | bytes 90144 | tf_op jit(solution)/shard_map/ppermute | solution.py:615
  58.9 1.0 %collective-permute-done.9.refs_2_ = s16[352,128]{1,0:T(8,128)(2,1)S(1)} collective-permute-done((s16[352,128]{1,0:T(8,128)(2,1)S(1)}, s16[352,128]{1,0:T(8,128)(2,1)S(1)}, u32[]{:S(2)}, u32[]{:S(2)}) %collective-permute-start.9) | collective-permute-done | bytes 90144 | tf_op jit(solution)/shard_map/ppermute | solution.py:615
  59.9 2.0 %collective-permute-done.10.refs_3_ = s16[352,128]{1,0:T(8,128)(2,1)S(1)} collective-permute-done((s16[352,128]{1,0:T(8,128)(2,1)S(1)}, s16[352,128]{1,0:T(8,128)(2,1)S(1)}, u32[]{:S(2)}, u32[]{:S(2)}) %collective-permute-start.10) | collective-permute-done | bytes 90144 | tf_op jit(solution)/shard_map/ppermute | solution.py:615
  61.9 1.3 %collective-permute-done.14.refs_7_ = s16[352,128]{1,0:T(8,128)(2,1)S(1)} collective-permute-done((s16[352,128]{1,0:T(8,128)(2,1)S(1)}, s16[352,128]{1,0:T(8,128)(2,1)S(1)}, u32[]{:S(2)}, u32[]{:S(2)}) %collective-permute-start.14) | collective-permute-done | bytes 90144 | tf_op jit(solution)/shard_map/ppermute | solution.py:615
  63.1 1.8 %unpack.1 = (f32[5,1,128]{2,1,0:T(1,128)}, f32[64,512]{1,0:T(8,128)}, f32[3,512]{1,0:T(4,128)}, f32[1,512]{1,0:T(1,128)}, f32[512,512]{1,0:T(8,128)}, /*index=5*...) custom-call(s32[3]{0:T(128)S(1)} %pad_add_fusion.place_ref, ...), custom_call_target="tpu_custom_call" | custom-call | tf_op jit(solution)/shard_map/unpack/pallas_call | solution.py:803
  (25 shorter events, 0.1 us)
Async XLA Ops:
  1.9 6.5 %copy-start.6 = (f32[512]{0:T(512)S(1)}, f32[512]{0:T(512)}, u32[]{:S(2)}) copy-start(f32[512]{0:T(512)} %param.25) | copy-start | bytes 6148
  1.9 6.5 %copy-start.7 = (f32[1,3,128]{2,0,1:T(1,128)S(1)}, f32[1,3,128]{2,0,1:T(1,128)}, u32[]{:S(2)}) copy-start(f32[1,3,128]{2,0,1:T(1,128)} %param.19) | copy-start | bytes 4612
  1.9 6.4 %copy-start.10 = (f32[5]{0:T(128)S(1)}, f32[5]{0:T(128)}, u32[]{:S(2)}) copy-start(f32[5]{0:T(128)} %param.27) | copy-start | bytes 64
  1.9 6.4 %copy-start.11 = (f32[64]{0:T(128)S(1)}, f32[64]{0:T(128)}, u32[]{:S(2)}) copy-start(f32[64]{0:T(128)} %param.16) | copy-start | bytes 772
  1.9 11.7 %copy-start.13 = (bf16[1,64,4,8,128]{4,3,2,1,0:T(8,128)(2,1)S(1)}, bf16[1,64,4,8,128]{4,3,2,1,0:T(8,128)(2,1)}, u32[]{:S(2)}) copy-start(bf16[1,64,4,8,128]{4,3,2,1,0:T(8,128)(2,1)} %param.14) | copy-start | bytes 1572868
  2.1 11.8 %collective-permute-start = (bf16[3,8,64,128]{3,2,1,0:T(8,128)(2,1)S(1)}, bf16[3,8,64,128]{3,2,1,0:T(8,128)(2,1)S(1)}, u32[]{:S(2)}, u32[]{:S(2)}) collective-permute-start(bf16[3,8,64,128]{3,2,1,0:T(8,128)(2,1)S(1)} %get-tuple-element.30), channel_id=1, source_target_pairs={{0,1},{1,0},{2,3},{3,2},{4,5},{5,4},{6,7},{7,6},{8,9},{9,8},{10,11... | collective-permute-start | bytes 1179656 | tf_op jit(solution)/shard_map/ppermute | solution.py:847
  2.7 11.3 %collective-permute-start.1 = (bf16[3,8,64,128]{3,2,1,0:T(8,128)(2,1)S(1)}, bf16[3,8,64,128]{3,2,1,0:T(8,128)(2,1)S(1)}, u32[]{:S(2)}, u32[]{:S(2)}) collective-permute-start(bf16[3,8,64,128]{3,2,1,0:T(8,128)(2,1)S(1)} %get-tuple-element.31), channel_id=1, source_target_pairs={{0,15},{1,2},{2,1},{3,4},{4,3},{5,6},{6,5},{7,8},{8,7},{9,10},{10,... | collective-permute-start | bytes 1179656 | tf_op jit(solution)/shard_map/ppermute | solution.py:848
  8.3 0.7 %copy-start.4 = (f32[1,5,128]{2,0,1:T(1,128)S(1)}, f32[1,5,128]{2,0,1:T(1,128)}, u32[]{:S(2)}) copy-start(f32[1,5,128]{2,0,1:T(1,128)} %param.20) | copy-start | bytes 7684
  8.3 0.7 %copy-start.5 = (f32[512]{0:T(512)S(1)}, f32[512]{0:T(512)}, u32[]{:S(2)}) copy-start(f32[512]{0:T(512)} %param.23) | copy-start | bytes 6148
  8.3 0.7 %copy-start.8 = (s32[1,128,1]{1,2,0:T(1,128)S(1)}, s32[1,128,1]{1,2,0:T(1,128)}, u32[]{:S(2)}) copy-start(s32[1,128,1]{1,2,0:T(1,128)} %param.17) | copy-start | bytes 1540
  8.3 0.7 %copy-start.9 = (s32[1,128]{1,0:T(1,128)S(1)}, s32[1,128]{1,0:T(1,128)}, u32[]{:S(2)}) copy-start(s32[1,128]{1,0:T(1,128)} %refs_1_.1) | copy-start | bytes 1540
  10.1 10.4 %all-to-all-start = ((f32[16,8,128]{2,1,0:T(8,128)}), f32[16,8,128]{2,1,0:T(8,128)S(1)}, u32[]{:S(2)}, u32[]{:S(2)}) async-start(f32[16,8,128]{2,1,0:T(8,128)} %bitcast.16), calls=%async_computation | async-start | bytes 131072 | tf_op jit(solution)/shard_map/all_to_all | solution.py:855
  13.6 0.9 %copy-start.12 = (bf16[64,1728]{1,0:T(8,128)(2,1)S(1)}, bf16[64,1728]{1,0:T(8,128)(2,1)}, u32[]{:S(2)}) copy-start(bf16[64,1728]{1,0:T(8,128)(2,1)} %taps_ref.1) | copy-start | bytes 663556
  14.6 5.9 %copy-start = (f32[512,512]{1,0:T(8,128)S(1)}, f32[512,512]{1,0:T(8,128)}, u32[]{:S(2)}) copy-start(f32[512,512]{1,0:T(8,128)} %w_mid_hbm.1) | copy-start | bytes 3145732
  14.6 5.9 %copy-start.1 = (f32[64,512]{1,0:T(8,128)S(1)}, f32[64,512]{1,0:T(8,128)}, u32[]{:S(2)}) copy-start(f32[64,512]{1,0:T(8,128)} %w_latent_hbm.1) | copy-start | bytes 393220
  14.6 5.9 %copy-start.2 = (f32[5,512]{1,0:T(8,128)S(1)}, f32[5,512]{1,0:T(8,128)}, u32[]{:S(2)}) copy-start(f32[5,512]{1,0:T(8,128)} %w_out_hbm.1) | copy-start | bytes 30724
  14.6 5.9 %copy-start.3 = (f32[3,512]{1,0:T(4,128)S(1)}, f32[3,512]{1,0:T(4,128)}, u32[]{:S(2)}) copy-start(f32[3,512]{1,0:T(4,128)} %w_pos_hbm.1) | copy-start | bytes 18436
  33.3 1.7 %collective-permute-start.2 = (s16[4,352,128]{2,1,0:T(8,128)(2,1)S(1)}, s16[4,352,128]{2,1,0:T(8,128)(2,1)S(1)}, u32[]{:S(2)}, u32[]{:S(2)}) collective-permute-start(s16[4,352,128]{2,1,0:T(8,128)(2,1)S(1)} %get-tuple-element.36), channel_id=1, source_target_pairs={{0,1},{1,0},{2,3},{3,2},{4,5},{5,4},{6,7},{7,6},{8,9},{9,8},{10,11... | collective-permute-start | bytes 1081352 | tf_op jit(solution)/shard_map/ppermute | solution.py:615
  35.3 4.7 %collective-permute-start.4 = (s16[352,128]{1,0:T(8,128)(2,1)S(1)}, s16[352,128]{1,0:T(8,128)(2,1)S(1)}, u32[]{:S(2)}, u32[]{:S(2)}) collective-permute-start(s16[352,128]{1,0:T(8,128)(2,1)S(1)} %get-tuple-element.40), channel_id=1, source_target_pairs={{0,2},{1,3},{2,0},{3,1},{4,6},{5,7},{6,4},{7,5},{8,10},{9,11},{10,... | collective-permute-start | bytes 270344 | tf_op jit(solution)/shard_map/ppermute | solution.py:615
  35.5 4.6 %collective-permute-start.5 = (s16[352,128]{1,0:T(8,128)(2,1)S(1)}, s16[352,128]{1,0:T(8,128)(2,1)S(1)}, u32[]{:S(2)}, u32[]{:S(2)}) collective-permute-start(s16[352,128]{1,0:T(8,128)(2,1)S(1)} %get-tuple-element.41), channel_id=1, source_target_pairs={{0,16},{1,17},{2,18},{3,19},{4,20},{5,21},{6,22},{7,23},{8,24},{9,... | collective-permute-start | bytes 270344 | tf_op jit(solution)/shard_map/ppermute | solution.py:615
  37.0 6.2 %collective-permute-start.3 = (s16[352,128]{1,0:T(8,128)(2,1)S(1)}, s16[352,128]{1,0:T(8,128)(2,1)S(1)}, u32[]{:S(2)}, u32[]{:S(2)}) collective-permute-start(s16[352,128]{1,0:T(8,128)(2,1)S(1)} %sum_core.2), channel_id=1, source_target_pairs={{0,18},{1,19},{2,16},{3,17},{4,22},{5,23},{6,20},{7,21},{8,26},{9,... | collective-permute-start | bytes 270344 | tf_op jit(solution)/shard_map/ppermute | solution.py:615
  43.3 4.6 %collective-permute-start.6 = (s16[352,128]{1,0:T(8,128)(2,1)S(1)}, s16[352,128]{1,0:T(8,128)(2,1)S(1)}, u32[]{:S(2)}, u32[]{:S(2)}) collective-permute-start(s16[352,128]{1,0:T(8,128)(2,1)S(1)} %sum_plane.1.mine_ref), channel_id=1, source_target_pairs={{0,4},{1,5},{2,6},{3,7},{4,0},{5,1},{6,2},{7,3},{8,12},{9,13},{10,... | collective-permute-start | bytes 270344 | tf_op jit(solution)/shard_map/ppermute | solution.py:615
  48.0 6.1 %collective-permute-start.7 = (s16[352,128]{1,0:T(8,128)(2,1)S(1)}, s16[352,128]{1,0:T(8,128)(2,1)S(1)}, u32[]{:S(2)}, u32[]{:S(2)}) collective-permute-start(s16[352,128]{1,0:T(8,128)(2,1)S(1)} %sum_line.2.mine_ref), channel_id=1, source_target_pairs={{0,8},{1,9},{2,10},{3,11},{4,12},{5,13},{6,14},{7,15},{8,0},{9,1},... | collective-permute-start | bytes 270344 | tf_op jit(solution)/shard_map/ppermute | solution.py:615
  54.3 4.6 %collective-permute-start.8 = (s16[352,128]{1,0:T(8,128)(2,1)S(1)}, s16[352,128]{1,0:T(8,128)(2,1)S(1)}, u32[]{:S(2)}, u32[]{:S(2)}) collective-permute-start(s16[352,128]{1,0:T(8,128)(2,1)S(1)} %sum_line.3.refs_0_), channel_id=1, source_target_pairs={{0,2},{1,3},{2,0},{3,1},{4,6},{5,7},{6,4},{7,5},{8,10},{9,11},{10,... | collective-permute-start | bytes 270344 | tf_op jit(solution)/shard_map/ppermute | solution.py:615
  55.4 4.5 %collective-permute-start.9 = (s16[352,128]{1,0:T(8,128)(2,1)S(1)}, s16[352,128]{1,0:T(8,128)(2,1)S(1)}, u32[]{:S(2)}, u32[]{:S(2)}) collective-permute-start(s16[352,128]{1,0:T(8,128)(2,1)S(1)} %sum_line.3.refs_0_), channel_id=1, source_target_pairs={{0,16},{1,17},{2,18},{3,19},{4,20},{5,21},{6,22},{7,23},{8,24},{9,... | collective-permute-start | bytes 270344 | tf_op jit(solution)/shard_map/ppermute | solution.py:615
  56.4 5.4 %collective-permute-start.10 = (s16[352,128]{1,0:T(8,128)(2,1)S(1)}, s16[352,128]{1,0:T(8,128)(2,1)S(1)}, u32[]{:S(2)}, u32[]{:S(2)}) collective-permute-start(s16[352,128]{1,0:T(8,128)(2,1)S(1)} %sum_line.3.refs_0_), channel_id=1, source_target_pairs={{0,18},{1,19},{2,16},{3,17},{4,22},{5,23},{6,20},{7,21},{8,26},{9,... | collective-permute-start | bytes 270344 | tf_op jit(solution)/shard_map/ppermute | solution.py:615
  57.8 4.0 %collective-permute-start.11 = (s16[352,128]{1,0:T(8,128)(2,1)S(1)}, s16[352,128]{1,0:T(8,128)(2,1)S(1)}, u32[]{:S(2)}, u32[]{:S(2)}) collective-permute-start(s16[352,128]{1,0:T(8,128)(2,1)S(1)} %sum_line.3.refs_0_), channel_id=1, source_target_pairs={{0,1},{1,0},{2,3},{3,2},{4,5},{5,4},{6,7},{7,6},{8,9},{9,8},{10,11... | collective-permute-start | bytes 270344 | tf_op jit(solution)/shard_map/ppermute | solution.py:615
  58.9 3.0 %collective-permute-start.12 = (s16[352,128]{1,0:T(8,128)(2,1)S(1)}, s16[352,128]{1,0:T(8,128)(2,1)S(1)}, u32[]{:S(2)}, u32[]{:S(2)}) collective-permute-start(s16[352,128]{1,0:T(8,128)(2,1)S(1)} %collective-permute-done.8.refs_1_), channel_id=1, source_target_pairs={{0,1},{1,0},{2,3},{3,2},{4,5},{5,4},{6,7},{7,6},{8,9},{9,8},{10,11... | collective-permute-start | bytes 270344 | tf_op jit(solution)/shard_map/ppermute | solution.py:615
  59.9 2.0 %collective-permute-start.13 = (s16[352,128]{1,0:T(8,128)(2,1)S(1)}, s16[352,128]{1,0:T(8,128)(2,1)S(1)}, u32[]{:S(2)}, u32[]{:S(2)}) collective-permute-start(s16[352,128]{1,0:T(8,128)(2,1)S(1)} %collective-permute-done.9.refs_2_), channel_id=1, source_target_pairs={{0,1},{1,0},{2,3},{3,2},{4,5},{5,4},{6,7},{7,6},{8,9},{9,8},{10,11... | collective-permute-start | bytes 270344 | tf_op jit(solution)/shard_map/ppermute | solution.py:615
  61.9 1.3 %collective-permute-start.14 = (s16[352,128]{1,0:T(8,128)(2,1)S(1)}, s16[352,128]{1,0:T(8,128)(2,1)S(1)}, u32[]{:S(2)}, u32[]{:S(2)}) collective-permute-start(s16[352,128]{1,0:T(8,128)(2,1)S(1)} %collective-permute-done.10.refs_3_), channel_id=1, source_target_pairs={{0,1},{1,0},{2,3},{3,2},{4,5},{5,4},{6,7},{7,6},{8,9},{9,8},{10,11... | collective-permute-start | bytes 270344 | tf_op jit(solution)/shard_map/ppermute | solution.py:615
